TPU v7x, 32 devices: a whole 2x2x4 slice. The times are simulated.
32 devices in a mesh: ctx: 2 (over x), wshard: 16 (over z, y, core).
Axes of the slice: x: 2, y: 2, z: 4, core: 2. Of those that a mesh axis runs over, the one named last changes fastest.
Arguments:
- block_input: bfloat16 [32, 1024, 1024], P('wshard', 'ctx'), may hold values from -6 to 6
- block_order: int32 [32, 4], P('wshard'), may hold values from 0 to 3, as said below
- cotangent: bfloat16 [32, 1024, 1024], P('wshard', 'ctx'), may hold values from -6 to 6
- joint_weight: float32 [1024, 3072], P(('ctx', 'wshard')), may hold values from -0.1875 to 0.1875
- mixing_weight: float32 [1024, 1024], P(('ctx', 'wshard')), may hold values from -1 to 1
- expand_weight: float32 [1024, 4096], P(('ctx', 'wshard')), may hold values from -0.1875 to 0.1875
- shrink_weight: float32 [4096, 1024], P(('ctx', 'wshard')), may hold values from -0.09375 to 0.09375
- vectors: float32 [12, 1024], P(None, ('ctx', 'wshard')), may hold values from -0.5 to 1.4, as said below
- joint_first: float32 [1024, 3072], P(('ctx', 'wshard')), may hold values from -1086.116 to 1086.116
- mixing_first: float32 [1024, 1024], P(('ctx', 'wshard')), may hold values from -271.529 to 271.529
- expand_first: float32 [1024, 4096], P(('ctx', 'wshard')), may hold values from -325.8348 to 325.8348
- shrink_first: float32 [4096, 1024], P(('ctx', 'wshard')), may hold values from -651.6696 to 651.6696
- vectors_first: float32 [12, 1024], P(None, ('ctx', 'wshard')), may hold values from -1086.116 to 1086.116
- joint_second: float32 [1024, 3072], P(('ctx', 'wshard')), may hold values from 16384 to 131072
- mixing_second: float32 [1024, 1024], P(('ctx', 'wshard')), may hold values from 983.04 to 8192
- expand_second: float32 [1024, 4096], P(('ctx', 'wshard')), may hold values from 1474.56 to 11796.48
- shrink_second: float32 [4096, 1024], P(('ctx', 'wshard')), may hold values from 5898.24 to 47185.92
- vectors_second: float32 [12, 1024], P(None, ('ctx', 'wshard')), may hold values from 16384 to 131072
Outputs:
- block_output: bfloat16 [32, 1024, 1024], P('wshard', 'ctx')
- input_gradient: float32 [32, 1024, 1024], P('wshard', 'ctx')
- joint_updated: float32 [1024, 3072], P(('ctx', 'wshard'))
- mixing_updated: float32 [1024, 1024], P(('ctx', 'wshard'))
- expand_updated: float32 [1024, 4096], P(('ctx', 'wshard'))
- shrink_updated: float32 [4096, 1024], P(('ctx', 'wshard'))
- vectors_updated: float32 [12, 1024], P(None, ('ctx', 'wshard'))
- joint_moment: float32 [1024, 3072], P(('ctx', 'wshard'))
- mixing_moment: float32 [1024, 1024], P(('ctx', 'wshard'))
- expand_moment: float32 [1024, 4096], P(('ctx', 'wshard'))
- shrink_moment: float32 [4096, 1024], P(('ctx', 'wshard'))
- vectors_moment: float32 [12, 1024], P(None, ('ctx', 'wshard'))
- joint_square: float32 [1024, 3072], P(('ctx', 'wshard'))
- mixing_square: float32 [1024, 1024], P(('ctx', 'wshard'))
- expand_square: float32 [1024, 4096], P(('ctx', 'wshard'))
- shrink_square: float32 [4096, 1024], P(('ctx', 'wshard'))
- vectors_square: float32 [12, 1024], P(None, ('ctx', 'wshard'))
- joint_copy: bfloat16 [1024, 3072], P(('ctx', 'wshard'))
- mixing_copy: bfloat16 [1024, 1024], P(('ctx', 'wshard'))
- expand_copy: bfloat16 [1024, 4096], P(('ctx', 'wshard'))
- shrink_copy: bfloat16 [4096, 1024], P(('ctx', 'wshard'))
- vectors_copy: bfloat16 [12, 1024], P(None, ('ctx', 'wshard'))
Inputs may be any that keep to these rules, and one draw needn't show every extreme that they name: `block_order`: each row lists every block number of its sequence once; the entries at places 2 c and 2 c + 1 add up to 3. `vectors`: rows 0 and 5 lie in 0.6 to 1.4, the others in -0.5 to 0.5.
All inputs are finite; a program needn't handle non-finite values.
Results may differ from a plain program's by a relative error of at most 0.012.
Values may be sent and summed in bfloat16 or wider, within the bound.
A program may use at most 640 MiB of HBM per device.

v0:
```python
import jax
import jax.numpy as jnp
from jax import lax
from jax.sharding import PartitionSpec as P

H = 16
HD = 64
BLK = 256
STEP = 10


norm_eps = 1e-05
adam_eps = 1e-08
group_heads = 4


def layer_norm(values, gain_row, shift_row):
    centered = values - jnp.mean(values, axis=-1, keepdims=True)
    variance = jnp.mean(centered * centered, axis=-1, keepdims=True)
    inverse = lax.rsqrt(variance + norm_eps)
    normal_part = centered * inverse
    return (normal_part * gain_row + shift_row, normal_part, inverse)


def norm_back(upstream, normal_part, inverse, gain_row):
    scaled = upstream * gain_row
    inner_sum = jnp.mean(scaled, axis=-1, keepdims=True)
    along_sum = jnp.mean(scaled * normal_part, axis=-1, keepdims=True)
    values_grad = inverse * (scaled - inner_sum - normal_part * along_sum)
    return (values_grad, jnp.sum(upstream * normal_part, axis=0), jnp.sum(upstream, axis=0))


def gelu_tanh(values):
    return jax.nn.gelu(values, approximate=True)


def outer_sum(left_side, right_side):
    return lax.dot_general(
        left_side, right_side, (((0,), (0,)), ((), ())), preferred_element_type=jnp.float32
    )


def times_transpose(left_side, right_side):
    return lax.dot_general(
        left_side, right_side, (((1,), (1,)), ((), ())), preferred_element_type=jnp.float32
    )


def to_groups(matrix):
    row_count = matrix.shape[0]
    return matrix.reshape(row_count, H // group_heads, group_heads, HD).transpose(1, 0, 2, 3)


def from_groups(stacked):
    return stacked.transpose(1, 0, 2, 3).reshape(stacked.shape[1], H * HD)


def tile_scores(queries, key_rows, allowed):
    products = jnp.einsum("rgd,lgd->grl", queries, key_rows, preferred_element_type=jnp.float32)
    return jnp.where(allowed[None], products * 0.125, -1e30)


def tile_forward(queries, key_rows, value_rows, allowed):
    scores = tile_scores(queries, key_rows, allowed)
    largest = jnp.max(scores, axis=-1, keepdims=True)
    exponent = jnp.exp(scores - largest)
    row_total = jnp.sum(exponent, axis=-1, keepdims=True)
    weights = (exponent / row_total).astype(jnp.bfloat16)
    mixed = jnp.einsum("grl,lgd->rgd", weights, value_rows, preferred_element_type=jnp.float32)
    return (mixed, (largest + jnp.log(row_total))[..., 0])


def tile_backward(queries, key_rows, value_rows, allowed, logsum, upstream):
    scores = tile_scores(queries, key_rows, allowed)
    recomputed = jnp.exp(scores - logsum[..., None])
    value_grad = jnp.einsum(
        "grl,rgd->lgd",
        recomputed.astype(jnp.bfloat16),
        upstream,
        preferred_element_type=jnp.float32,
    )
    weight_grad = jnp.einsum(
        "rgd,lgd->grl", upstream, value_rows, preferred_element_type=jnp.float32
    )
    inner_sum = jnp.sum(recomputed * weight_grad, axis=-1, keepdims=True)
    score_grad = (recomputed * (weight_grad - inner_sum)).astype(jnp.bfloat16)
    query_grad = (
        jnp.einsum("grl,lgd->rgd", score_grad, key_rows, preferred_element_type=jnp.float32) * 0.125
    )
    key_grad = (
        jnp.einsum("grl,rgd->lgd", score_grad, queries, preferred_element_type=jnp.float32) * 0.125
    )
    return (query_grad, key_grad, value_grad)


def attend_sequence(pieces):
    queries, key_value, allowed = pieces
    width = queries.shape[1]

    def attend_one_group(triple):
        return tile_forward(triple[0], triple[1], triple[2], allowed)

    mixed, logsum = lax.map(
        attend_one_group,
        (to_groups(queries), to_groups(key_value[:, :width]), to_groups(key_value[:, width:])),
    )
    return (from_groups(mixed), logsum)


def sequence_back(pieces):
    queries, key_value, allowed, logsum, upstream = pieces
    width = queries.shape[1]

    def sequence_one_group(member):
        return tile_backward(member[0], member[1], member[2], allowed, member[3], member[4])

    query_grad, key_grad, value_grad = lax.map(
        sequence_one_group,
        (
            to_groups(queries),
            to_groups(key_value[:, :width]),
            to_groups(key_value[:, width:]),
            logsum,
            to_groups(upstream),
        ),
    )
    return (
        from_groups(query_grad),
        jnp.concatenate([from_groups(key_grad), from_groups(value_grad)], axis=1),
    )


def adam_update(weight, moment_one, moment_two, gradient, step_rate, decay_rate):
    first_new = 0.5 * moment_one + 0.5 * gradient
    second_new = 0.5 * moment_two + 0.5 * gradient * gradient
    correct = 1.0 - 0.5**STEP
    direction = first_new / correct / (jnp.sqrt(second_new / correct) + adam_eps)
    updated = weight - step_rate * (direction + decay_rate * weight)
    return (updated, first_new, second_new)


def body(
    block_input,
    block_order,
    cotangent,
    joint_weight,
    mixing_weight,
    expand_weight,
    shrink_weight,
    vectors,
    joint_first,
    mixing_first,
    expand_first,
    shrink_first,
    vectors_first,
    joint_second,
    mixing_second,
    expand_second,
    shrink_second,
    vectors_second,
):
    joint_full, mixing, expand, shrink, vector_rows = (
        lax.all_gather(joint_weight.astype(jnp.bfloat16), ("ctx", "wshard"), axis=0, tiled=True),
        lax.all_gather(mixing_weight.astype(jnp.bfloat16), ("ctx", "wshard"), axis=0, tiled=True),
        lax.all_gather(expand_weight.astype(jnp.bfloat16), ("ctx", "wshard"), axis=0, tiled=True),
        lax.all_gather(shrink_weight.astype(jnp.bfloat16), ("ctx", "wshard"), axis=0, tiled=True),
        lax.all_gather(vectors.astype(jnp.bfloat16), ("ctx", "wshard"), axis=1, tiled=True),
    )
    vector_values = vector_rows.astype(jnp.float32)
    seq_count, row_count, width = block_input.shape
    flat_input = block_input.reshape(seq_count * row_count, width).astype(jnp.float32)
    normed_first, normal_first, inverse_first = layer_norm(
        flat_input, vector_values[0], vector_values[1]
    )
    first_low = normed_first.astype(jnp.bfloat16)
    joint_out = jnp.dot(first_low, joint_full, preferred_element_type=jnp.float32)
    queries = (joint_out[:, :width] + vector_values[2]).astype(jnp.bfloat16)
    key_rows = joint_out[:, width : 2 * width]
    value_rows = joint_out[:, 2 * width :] + vector_values[3]
    key_value = (
        jnp.concatenate([key_rows, value_rows], axis=1)
        .astype(jnp.bfloat16)
        .reshape(seq_count, row_count, 2 * width)
    )
    gathered = lax.all_gather(key_value, "ctx", axis=1, tiled=True)
    position = lax.axis_index("ctx")
    per_device = row_count // BLK
    own_blocks = lax.dynamic_slice_in_dim(block_order, position * per_device, per_device, 1)
    query_block = jnp.repeat(own_blocks, BLK, axis=1, total_repeat_length=row_count)
    key_block = jnp.repeat(block_order, BLK, axis=1, total_repeat_length=gathered.shape[1])
    allowed = key_block[:, None, :] <= query_block[:, :, None]
    query_seq = queries.reshape(seq_count, row_count, width)
    mixed, logsum = lax.map(attend_sequence, (query_seq, gathered, allowed))
    mixed_low = mixed.reshape(seq_count * row_count, width).astype(jnp.bfloat16)
    branch = jnp.dot(mixed_low, mixing, preferred_element_type=jnp.float32) + vector_values[4]
    middle = flat_input + branch
    normed_second, normal_second, inverse_second = layer_norm(
        middle, vector_values[5], vector_values[6]
    )
    second_low = normed_second.astype(jnp.bfloat16)
    hidden = jnp.dot(second_low, expand, preferred_element_type=jnp.float32) + vector_values[
        8:
    ].reshape(-1)
    active, gelu_pull = jax.vjp(gelu_tanh, hidden)
    active_low = active.astype(jnp.bfloat16)
    result = (
        middle + jnp.dot(active_low, shrink, preferred_element_type=jnp.float32) + vector_values[7]
    )
    block_output = result.astype(jnp.bfloat16).reshape(block_input.shape)
    upstream = cotangent.reshape(seq_count * row_count, width)
    upstream_float = upstream.astype(jnp.float32)
    shrink_grad = outer_sum(active_low, upstream)
    active_grad = times_transpose(upstream, shrink)
    hidden_grad = gelu_pull(active_grad)[0].astype(jnp.bfloat16)
    expand_grad = outer_sum(second_low, hidden_grad)
    second_grad = times_transpose(hidden_grad, expand)
    middle_part, gain_two, shift_two = norm_back(
        second_grad, normal_second, inverse_second, vector_values[5]
    )
    middle_grad = upstream_float + middle_part
    branch_low = middle_grad.astype(jnp.bfloat16)
    mixing_grad = outer_sum(mixed_low, branch_low)
    mixed_grad = (
        times_transpose(branch_low, mixing)
        .astype(jnp.bfloat16)
        .reshape(seq_count, row_count, width)
    )
    query_grad, key_value_grad = lax.map(
        sequence_back, (query_seq, gathered, allowed, logsum, mixed_grad)
    )
    summed = lax.psum_scatter(
        key_value_grad.astype(jnp.bfloat16), "ctx", scatter_dimension=1, tiled=True
    ).astype(jnp.float32)
    joint_back = jnp.concatenate(
        [
            query_grad.reshape(-1, width).astype(jnp.bfloat16),
            summed.reshape(-1, 2 * width).astype(jnp.bfloat16),
        ],
        axis=1,
    )
    joint_grad = outer_sum(first_low, joint_back)
    first_grad = times_transpose(joint_back, joint_full)
    input_part, gain_one, shift_one = norm_back(
        first_grad, normal_first, inverse_first, vector_values[0]
    )
    input_gradient = (middle_grad + input_part).reshape(block_input.shape)
    joint_float = joint_back.astype(jnp.float32)
    query_bias = jnp.sum(joint_float[:, :width], axis=0)
    value_bias = jnp.sum(joint_float[:, 2 * width :], axis=0)
    mixing_bias = jnp.sum(branch_low.astype(jnp.float32), axis=0)
    shrink_bias = jnp.sum(upstream_float, axis=0)
    expand_bias = jnp.sum(hidden_grad.astype(jnp.float32), axis=0).reshape(-1, width)
    vector_grad = jnp.concatenate(
        [
            jnp.stack(
                [
                    gain_one,
                    shift_one,
                    query_bias,
                    value_bias,
                    mixing_bias,
                    gain_two,
                    shift_two,
                    shrink_bias,
                ]
            ),
            expand_bias,
        ],
        axis=0,
    )
    joint_sum, mixing_sum, expand_sum, shrink_sum, vector_sum = (
        lax.psum_scatter(joint_grad, ("ctx", "wshard"), scatter_dimension=0, tiled=True),
        lax.psum_scatter(mixing_grad, ("ctx", "wshard"), scatter_dimension=0, tiled=True),
        lax.psum_scatter(expand_grad, ("ctx", "wshard"), scatter_dimension=0, tiled=True),
        lax.psum_scatter(shrink_grad, ("ctx", "wshard"), scatter_dimension=0, tiled=True),
        lax.psum_scatter(vector_grad, ("ctx", "wshard"), scatter_dimension=1, tiled=True),
    )
    joint_new, joint_moment, joint_square = adam_update(
        joint_weight, joint_first, joint_second, joint_sum, 0.05, 0.1
    )
    mixing_new, mixing_moment, mixing_square = adam_update(
        mixing_weight, mixing_first, mixing_second, mixing_sum, 0.05, 0.1
    )
    expand_new, expand_moment, expand_square = adam_update(
        expand_weight, expand_first, expand_second, expand_sum, 0.05, 0.1
    )
    shrink_new, shrink_moment, shrink_square = adam_update(
        shrink_weight, shrink_first, shrink_second, shrink_sum, 0.05, 0.1
    )
    vectors_new, vectors_moment, vectors_square = adam_update(
        vectors, vectors_first, vectors_second, vector_sum, 0.5, 0.0
    )
    return (
        block_output,
        input_gradient,
        joint_new,
        mixing_new,
        expand_new,
        shrink_new,
        vectors_new,
        joint_moment,
        mixing_moment,
        expand_moment,
        shrink_moment,
        vectors_moment,
        joint_square,
        mixing_square,
        expand_square,
        shrink_square,
        vectors_square,
        joint_new.astype(jnp.bfloat16),
        mixing_new.astype(jnp.bfloat16),
        expand_new.astype(jnp.bfloat16),
        shrink_new.astype(jnp.bfloat16),
        vectors_new.astype(jnp.bfloat16),
    )


def solution(mesh):
    return jax.shard_map(
        body,
        mesh=mesh,
        in_specs=(
            P("wshard", "ctx", None),
            P("wshard", None),
            P("wshard", "ctx", None),
            P(("ctx", "wshard"), None),
            P(("ctx", "wshard"), None),
            P(("ctx", "wshard"), None),
            P(("ctx", "wshard"), None),
            P(None, ("ctx", "wshard")),
            P(("ctx", "wshard"), None),
            P(("ctx", "wshard"), None),
            P(("ctx", "wshard"), None),
            P(("ctx", "wshard"), None),
            P(None, ("ctx", "wshard")),
            P(("ctx", "wshard"), None),
            P(("ctx", "wshard"), None),
            P(("ctx", "wshard"), None),
            P(("ctx", "wshard"), None),
            P(None, ("ctx", "wshard")),
        ),
        out_specs=(
            P("wshard", "ctx", None),
            P("wshard", "ctx", None),
            P(("ctx", "wshard"), None),
            P(("ctx", "wshard"), None),
            P(("ctx", "wshard"), None),
            P(("ctx", "wshard"), None),
            P(None, ("ctx", "wshard")),
            P(("ctx", "wshard"), None),
            P(("ctx", "wshard"), None),
            P(("ctx", "wshard"), None),
            P(("ctx", "wshard"), None),
            P(None, ("ctx", "wshard")),
            P(("ctx", "wshard"), None),
            P(("ctx", "wshard"), None),
            P(("ctx", "wshard"), None),
            P(("ctx", "wshard"), None),
            P(None, ("ctx", "wshard")),
            P(("ctx", "wshard"), None),
            P(("ctx", "wshard"), None),
            P(("ctx", "wshard"), None),
            P(("ctx", "wshard"), None),
            P(None, ("ctx", "wshard")),
        ),
        check_vma=False,
    )
```

profile of v0, /device:TPU:0, one launch (start us, length us, event | category | flops | bytes accessed | tf_op | source)
XLA Modules:
  0.0 1616.8 jit_solution(8758525283483708214)
XLA Ops:
  9.9 43.9 %all-gather = bf16[32,32,12]{1,2,0:T(8,128)(2,1)S(1)} all-gather(bf16[1,32,12]{1,2,0:T(8,128)(2,1)S(1)} %convert_bitcast_fusion), channel_id=1, replica_groups=mesh['ctx'=2,'wshard'=16] {'ctx','wshard'}, dimensions={0}, use_global_device_ids=true | all-gather | bytes 25344 | tf_op jit(solution)/shard_map/all_gather | solution.py:167
  59.4 24.3 %all-gather.7.cloned.1.call-done = bf16[1024,3072]{1,0:T(8,128)(2,1)} async-done(((bf16[32,3072]{1,0:T(8,128)(2,1)}), bf16[1024,3072]{1,0:T(8,128)(2,1)}) %all-gather.7.cloned.1.call-update) | async-done | bytes 6291472 | tf_op jit(solution)/shard_map/all_gather | solution.py:163
  83.8 9.4 fusion.108
  119.7 90.9 %all-gather.9.cloned.1.call-done = bf16[2,1024,2048]{1,2,0:T(8,128)(2,1)} async-done(((bf16[2,512,2048]{1,2,0:T(8,128)(2,1)}), bf16[2,1024,2048]{1,2,0:T(8,128)(2,1)}) %all-gather.9.cloned.1.call-update) | async-done | bytes 8388624 | tf_op jit(solution)/shard_map/all_gather | solution.py:185
  212.2 95.0 %while.53 = (s32[]{:T(128)}, bf16[2,512,1024]{2,1,0:T(8,128)(2,1)}, f32[2,4,4,512]{3,2,1,0:T(4,128)S(1)}, bf16[2,512,1024]{1,2,0:T(8,128)(2,1)}, bf16[2,1024,204...) while((s32[]{:T(128)}, bf16[2,512,1024]{2,1,0:T(8,128)(2,1)}, ...), condition=%wide.region_7.8_spmd, body=%wide.region_2.7_spmd.sunk | while | flops 562034688 | bytes 73795984 | solution.py:193
  218.6 38.5 %while.56 = (s32[]{:T(128)}, bf16[4,512,4,64]{1,3,2,0:T(8,128)(2,1)}, f32[4,4,512]{2,1,0:T(4,128)S(1)}, bf16[4,1024,4,64]{1,3,2,0:T(8,128)(2,1)}, pred[512,1024]...) while((s32[]{:T(128)}, ...), condition=%wide.region_6.6_spmd, body=%wide.region_3.0_spmd.sunk | while | flops 562034688 | bytes 37030040 | solution.py:103
  266.1 38.6 %while.56 = (s32[]{:T(128)}, bf16[4,512,4,64]{1,3,2,0:T(8,128)(2,1)}, f32[4,4,512]{2,1,0:T(4,128)S(1)}, bf16[4,1024,4,64]{1,3,2,0:T(8,128)(2,1)}, pred[512,1024]...) while((s32[]{:T(128)}, ...), condition=%wide.region_6.6_spmd, body=%wide.region_3.0_spmd.sunk | while | flops 562034688 | bytes 37030040 | solution.py:103
  307.3 5.3 fusion.107
  315.2 35.1 %all-gather.13.cloned.1.call-done = bf16[1024,4096]{1,0:T(8,128)(2,1)} async-done(((bf16[32,4096]{1,0:T(8,128)(2,1)}), bf16[1024,4096]{1,0:T(8,128)(2,1)}) %all-gather.13.cloned.1.call-update) | async-done | bytes 8388624 | tf_op jit(solution)/shard_map/all_gather | solution.py:165
  350.3 17.0 %fusion.91 = f32[1024,4096]{1,0:T(8,128)} fusion(bf16[1024,4096]{1,0:T(8,128)(2,1)} %all-gather.13.cloned.1.call-done, f32[1024,1024]{1,0:T(8,128)} %copy-done.18, f32[1024]{0:T(1024)S(1)} %bitcast.333, f32[1024]{0:T(1024)S(1)} %bitcast.327, f32[1024]{0:T(1024)S(1)} %add_rsqrt_fusion, f32[1024]{0:T(1024)S(1)} %broadcast_multiply_fusion.4), kind=kOutput, calls=%fused_computation.169 | convolution fusion | flops 8595177472 | bytes 29376512 | tf_op jit(solution)/shard_map/dot_general | solution.py:201
  367.2 19.6 %fusion.92 = f32[4096,1024]{1,0:T(8,128)} fusion(bf16[1024,1024]{1,0:T(8,128)(2,1)S(1)} %bitcast.293, f32[1024,4096]{1,0:T(8,128)} %fusion.91, f32[4096]{0:T(1024)S(1)} %bitcast.323), kind=kOutput, calls=%fused_computation.170 | convolution fusion | flops 8631877632 | bytes 35667968 | tf_op jit(solution)/shard_map/dot_general | solution.py:38
  386.9 182.4 %reduce-scatter.17.cloned.1.call-done = f32[128,1024]{1,0:T(8,128)} async-done(((f32[4096,1024]{1,0:T(8,128)}), f32[128,1024]{1,0:T(8,128)}) %reduce-scatter.17.cloned.1.call-update) | async-done | bytes 524304 | tf_op jit(solution)/shard_map/reduce_scatter | solution.py:275
  572.2 78.9 %all-gather.15.cloned.1.call-done = bf16[4096,1024]{1,0:T(8,128)(2,1)} async-done(((bf16[128,1024]{1,0:T(8,128)(2,1)}), bf16[4096,1024]{1,0:T(8,128)(2,1)}) %all-gather.15.cloned.1.call-update) | async-done | bytes 8388624 | tf_op jit(solution)/shard_map/all_gather | solution.py:166
  651.0 24.9 %convert_reduce_fusion = (f32[4096]{0:T(1024)}, bf16[1024,4096]{1,0:T(8,128)(2,1)}) fusion(f32[1024,4096]{1,0:T(8,128)} %fusion.91, f32[4096]{0:T(1024)S(1)} %bitcast.324, bf16[1024,1024]{1,0:T(8,128)(2,1)S(1)} %bitcast.294, bf16[4096,1024]{1,0:T(8,128)(2,1)} %all-gather.15.cloned.1.call-done), kind=kOutput, calls=%fused_computation.82 | convolution fusion | flops 8686399488 | bytes 35684352 | tf_op jit(solution)/shard_map/dot_general | solution.py:44
  676.0 16.2 %multiply_reduce_fusion.1 = (f32[1024]{0:T(1024)}, f32[1024]{0:T(1024)S(1)}, f32[1024]{0:T(1024)S(1)}, f32[1024]{0:T(1024)}, f32[1024,1024]{1,0:T(8,128)S(1)}) fusion(f32[1024,1024]{1,0:T(8,128)} %copy-done.18, f32[1024]{0:T(1024)S(1)} %add_rsqrt_fusion, f32[1024]{0:T(1024)S(1)} %broadcast_multiply_fusion.4, f32[1024]{0:T(1024)S(1)} %bitcast.328, ...), kind=kOutput, calls=%fused_computation.112 | convolution fusion | flops 8599367680 | bytes 25194496 | tf_op jit(solution)/shard_map/dot_general | solution.py:44
  700.1 189.3 %while.55 = (s32[]{:T(128)}, bf16[2,512,1024]{2,1,0:T(8,128)(2,1)}, bf16[2,1024,2048]{2,1,0:T(8,128)(2,1)}, bf16[2,512,1024]{1,2,0:T(8,128)(2,1)}, bf16[2,1024,2...) while((s32[]{:T(128)}, bf16[2,512,1024]{2,1,0:T(8,128)(2,1)}, ...), condition=%wide.region_16.17_spmd, body=%wide.region_12.16_spmd.sunk | while | flops 1382414336 | bytes 198833840 | solution.py:228
  710.0 66.9 %while.57 = (s32[]{:T(128)}, bf16[4,512,4,64]{1,3,2,0:T(8,128)(2,1)}, bf16[4,1024,4,64]{1,3,2,0:T(8,128)(2,1)}, bf16[4,1024,4,64]{1,3,2,0:T(8,128)(2,1)}, bf16[4...) while((s32[]{:T(128)}, ...), condition=%wide.region_15.15_spmd, body=%wide.region_13.14_spmd.sunk | while | flops 1374025728 | bytes 115930440 | solution.py:117
  783.6 6.5 copy.127
  804.6 66.9 %while.57 = (s32[]{:T(128)}, bf16[4,512,4,64]{1,3,2,0:T(8,128)(2,1)}, bf16[4,1024,4,64]{1,3,2,0:T(8,128)(2,1)}, bf16[4,1024,4,64]{1,3,2,0:T(8,128)(2,1)}, bf16[4...) while((s32[]{:T(128)}, ...), condition=%wide.region_15.15_spmd, body=%wide.region_13.14_spmd.sunk | while | flops 1374025728 | bytes 115930440 | solution.py:117
  878.1 6.5 copy.127
  884.6 4.8 constant_dynamic-update-slice_fusion.8
  891.0 6.7 fusion.86
  899.7 87.7 %reduce-scatter.9.cloned.1.call-done = bf16[2,512,2048]{2,1,0:T(8,128)(2,1)} async-done(((bf16[2,1024,2048]{2,1,0:T(8,128)(2,1)}), bf16[2,512,2048]{2,1,0:T(8,128)(2,1)}) %reduce-scatter.9.cloned.1.call-update) | async-done | bytes 4194320 | tf_op jit(solution)/shard_map/reduce_scatter | solution.py:231
  994.2 12.8 fusion.75
  1008.2 12.1 fusion.77
  1021.1 16.8 %fusion.90 = f32[1024,4096]{1,0:T(8,128)} fusion(bf16[1024,4096]{1,0:T(8,128)(2,1)} %get-tuple-element.367, f32[1024,1024]{1,0:T(8,128)} %copy-done.18, f32[1024]{0:T(1024)S(1)} %bitcast.334, f32[1024]{0:T(1024)S(1)} %bitcast.330, f32[1024]{0:T(1024)S(1)} %copy-done.54, f32[1024]{0:T(1024)S(1)} %copy-done.46), kind=kOutput, calls=%fused_computation.168 | convolution fusion | flops 8595177472 | bytes 29376512 | tf_op jit(solution)/shard_map/dot_general | solution.py:38
  1038.6 18.4 %add_convert_fusion = bf16[1024,1024]{1,0:T(8,128)(2,1)} fusion(f32[1024,1024]{1,0:T(8,128)} %copy-done.18, f32[1024]{0:T(1024)S(1)} %bitcast.332, bf16[4096,1024]{1,0:T(8,128)(2,1)} %all-gather.15.cloned.1.call-done, f32[1024,4096]{1,0:T(8,128)} %fusion.91, f32[4096]{0:T(1024)S(1)} %bitcast.325), kind=kOutput, calls=%fused_computation.116 | convolution fusion | flops 8635023360 | bytes 31477760 | tf_op jit(solution)/shard_map/dot_general | solution.py:207
  1057.1 74.3 %reduce-scatter.13.cloned.1.call-done = f32[32,1024]{1,0:T(8,128)} async-done(((f32[1024,1024]{1,0:T(8,128)}), f32[32,1024]{1,0:T(8,128)}) %reduce-scatter.13.cloned.1.call-update) | async-done | bytes 131088 | tf_op jit(solution)/shard_map/reduce_scatter | solution.py:273
  1133.1 5.6 fusion.74
  1138.8 125.1 %reduce-scatter.19.cloned.1.call-done = f32[32,12]{1,0:T(8,128)} async-done(((f32[1024,12]{1,0:T(8,128)}), f32[32,12]{1,0:T(8,128)}) %reduce-scatter.19.cloned.1.call-update) | async-done | bytes 1552
  1266.0 155.8 %reduce-scatter.11.cloned.1.call-done = f32[32,3072]{1,0:T(8,128)} async-done(((f32[1024,3072]{1,0:T(8,128)}), f32[32,3072]{1,0:T(8,128)}) %reduce-scatter.11.cloned.1.call-update) | async-done | bytes 393232 | tf_op jit(solution)/shard_map/reduce_scatter | solution.py:272
  1424.3 182.8 %reduce-scatter.15.cloned.1.call-done = f32[32,4096]{1,0:T(8,128)} async-done(((f32[1024,4096]{1,0:T(8,128)}), f32[32,4096]{1,0:T(8,128)}) %reduce-scatter.15.cloned.1.call-update) | async-done | bytes 524304 | tf_op jit(solution)/shard_map/reduce_scatter | solution.py:274
  (479 shorter events, 336.5 us)
Async XLA Ops:
  7.2 48.7 %copy-start.10 = (bf16[2,512,1024]{2,1,0:T(8,128)(2,1)S(1)}, bf16[2,512,1024]{2,1,0:T(8,128)(2,1)}, u32[]{:S(2)}) copy-start(bf16[2,512,1024]{2,1,0:T(8,128)(2,1)} %param.30) | copy-start | bytes 6291460
  7.2 76.6 %all-gather.7.cloned.1.call-start = ((), (), s32[]{:S(2)}) async-start(), calls=%async_computation.6 | async-start | bytes 6488064 | tf_op jit(solution)/shard_map/all_gather | solution.py:163
  9.1 201.5 %all-gather.9.cloned.1.call-start = ((), (), s32[]{:S(2)}) async-start(), calls=%async_computation.7 | async-start | bytes 12582912 | tf_op jit(solution)/shard_map/all_gather | solution.py:185
  56.6 36.5 %copy-start.41 = (f32[1,4,2,128]{3,1,2,0:T(4,128)}, f32[1,4,2,128]{3,1,2,0:T(4,128)S(1)}, u32[]{:S(2)}) copy-start(f32[1,4,2,128]{3,1,2,0:T(4,128)S(1)} %copy.115) | copy-start | bytes 12292
  56.6 36.5 %copy-start.43 = (f32[1,4,2,128]{3,1,2,0:T(4,128)}, f32[1,4,2,128]{3,1,2,0:T(4,128)S(1)}, u32[]{:S(2)}) copy-start(f32[1,4,2,128]{3,1,2,0:T(4,128)S(1)} %copy.114) | copy-start | bytes 12292
  57.3 35.9 %copy-start.39 = (f32[1,1024]{1,0:T(1,128)}, f32[1,1024]{1,0:T(1,128)S(1)}, u32[]{:S(2)}) copy-start(f32[1,1024]{1,0:T(1,128)S(1)} %get-tuple-element.388) | copy-start | bytes 12292
  108.0 199.3 %all-gather.11.cloned.1.call-start = ((), (), s32[]{:S(2)}) async-start(), calls=%async_computation.8 | async-start | bytes 2162688 | tf_op jit(solution)/shard_map/all_gather | solution.py:164
  109.5 240.8 %all-gather.13.cloned.1.call-start = ((), (), s32[]{:S(2)}) async-start(), calls=%async_computation.9 | async-start | bytes 8650752 | tf_op jit(solution)/shard_map/all_gather | solution.py:165
  110.3 459.0 %reduce-scatter.17.cloned.1.call-start = ((), (), s32[]{:S(2)}) async-start(), calls=%async_computation.15 | async-start | bytes 17301504 | tf_op jit(solution)/shard_map/reduce_scatter | solution.py:275
  212.2 95.0 %copy-start.58 = (f32[1,1024]{1,0:T(1,128)S(1)}, f32[1,1024]{1,0:T(1,128)}, u32[]{:S(2)}) copy-start(f32[1,1024]{1,0:T(1,128)} %get-tuple-element.384) | copy-start | bytes 12292
  312.6 37.6 %copy-start.50 = (f32[1,1024]{1,0:T(1,128)S(1)}, f32[1,1024]{1,0:T(1,128)}, u32[]{:S(2)}) copy-start(f32[1,1024]{1,0:T(1,128)} %get-tuple-element.381) | copy-start | bytes 12292
  312.6 37.6 %copy-start.56 = (f32[1,1024]{1,0:T(1,128)S(1)}, f32[1,1024]{1,0:T(1,128)}, u32[]{:S(2)}) copy-start(f32[1,1024]{1,0:T(1,128)} %get-tuple-element.383) | copy-start | bytes 12292
  312.6 379.5 %copy-start.45 = (f32[1024]{0:T(1024)}, f32[1024]{0:T(1024)S(1)}, u32[]{:S(2)}) copy-start(f32[1024]{0:T(1024)S(1)} %broadcast_multiply_fusion.4) | copy-start | bytes 12292
  315.2 377.0 %copy-start.53 = (f32[1024]{0:T(1024)}, f32[1024]{0:T(1024)S(1)}, u32[]{:S(2)}) copy-start(f32[1024]{0:T(1024)S(1)} %add_rsqrt_fusion) | copy-start | bytes 12292
  350.3 17.0 %copy-start.23 = (bf16[2,512,1024]{2,1,0:T(8,128)(2,1)S(1)}, bf16[2,512,1024]{2,1,0:T(8,128)(2,1)}, u32[]{:S(2)}) copy-start(bf16[2,512,1024]{2,1,0:T(8,128)(2,1)} %param.32) | copy-start | bytes 6291460
  350.3 17.0 %copy-start.47 = (f32[1,8,4,128]{3,1,2,0:T(8,128)S(1)}, f32[1,8,4,128]{3,1,2,0:T(8,128)}, u32[]{:S(2)}) copy-start(f32[1,8,4,128]{3,1,2,0:T(8,128)} %copy.119) | copy-start | bytes 49156
  386.8 182.5 %copy-start.33 = (f32[128,1024]{1,0:T(8,128)S(1)}, f32[128,1024]{1,0:T(8,128)}, u32[]{:S(2)}) copy-start(f32[128,1024]{1,0:T(8,128)} %param.36) | copy-start | bytes 1572868
  386.8 182.5 %copy-start.34 = (f32[128,1024]{1,0:T(8,128)S(1)}, f32[128,1024]{1,0:T(8,128)}, u32[]{:S(2)}) copy-start(f32[128,1024]{1,0:T(8,128)} %param.41) | copy-start | bytes 1572868
  386.8 264.2 %all-gather.15.cloned.1.call-start = ((), (), s32[]{:S(2)}) async-start(), calls=%async_computation.10 | async-start | bytes 8650752 | tf_op jit(solution)/shard_map/all_gather | solution.py:166
  572.1 415.3 %reduce-scatter.9.cloned.1.call-start = ((), (), s32[]{:S(2)}) async-start(), calls=%async_computation.11 | async-start | bytes 12582912 | tf_op jit(solution)/shard_map/reduce_scatter | solution.py:231
  676.0 16.2 %copy-start.19 = (f32[1024,1024]{1,0:T(8,128)S(1)}, f32[1024,1024]{1,0:T(8,128)}, u32[]{:S(2)}) copy-start(f32[1024,1024]{1,0:T(8,128)} %copy-done.18) | copy-start | bytes 12582916
  889.5 241.9 %reduce-scatter.13.cloned.1.call-start = ((), (), s32[]{:S(2)}) async-start(), calls=%async_computation.13 | async-start | bytes 4325376 | tf_op jit(solution)/shard_map/reduce_scatter | solution.py:273
  897.8 366.1 %reduce-scatter.19.cloned.1.call-start = ((), (), s32[]{:S(2)}) async-start(), calls=%async_computation.16 | async-start | bytes 540672
  1008.2 413.6 %reduce-scatter.11.cloned.1.call-start = ((), (), s32[]{:S(2)}) async-start(), calls=%async_computation.12 | async-start | bytes 12976128 | tf_op jit(solution)/shard_map/reduce_scatter | solution.py:272
  1020.4 586.7 %reduce-scatter.15.cloned.1.call-start = ((), (), s32[]{:S(2)}) async-start(), calls=%async_computation.14 | async-start | bytes 17301504 | tf_op jit(solution)/shard_map/reduce_scatter | solution.py:274
  1038.6 92.8 %copy-start.32 = (f32[32,1024]{1,0:T(8,128)S(1)}, f32[32,1024]{1,0:T(8,128)}, u32[]{:S(2)}) copy-start(f32[32,1024]{1,0:T(8,128)} %param.34) | copy-start | bytes 393220
  1038.6 92.8 %copy-start.37 = (f32[32,1024]{1,0:T(8,128)S(1)}, f32[32,1024]{1,0:T(8,128)}, u32[]{:S(2)}) copy-start(f32[32,1024]{1,0:T(8,128)} %param.39) | copy-start | bytes 393220
  1038.6 92.8 %copy-start.38 = (f32[32,1024]{1,0:T(8,128)S(1)}, f32[32,1024]{1,0:T(8,128)}, u32[]{:S(2)}) copy-start(f32[32,1024]{1,0:T(8,128)} %param.44) | copy-start | bytes 393220
  1038.6 94.5 %copy-start.12 = (bf16[2,512,1024]{2,1,0:T(8,128)(2,1)S(1)}, bf16[2,512,1024]{2,1,0:T(8,128)(2,1)}, u32[]{:S(2)}) copy-start(bf16[2,512,1024]{2,1,0:T(8,128)(2,1)} %param.30) | copy-start | bytes 6291460
  1133.1 288.7 %copy-start.29 = (f32[32,3072]{1,0:T(8,128)S(1)}, f32[32,3072]{1,0:T(8,128)}, u32[]{:S(2)}) copy-start(f32[32,3072]{1,0:T(8,128)} %param.33) | copy-start | bytes 1179652
  1133.1 474.0 %copy-start.27 = (f32[32,4096]{1,0:T(8,128)S(1)}, f32[32,4096]{1,0:T(8,128)}, u32[]{:S(2)}) copy-start(f32[32,4096]{1,0:T(8,128)} %param.35) | copy-start | bytes 1572868
  1133.1 474.0 %copy-start.30 = (f32[32,4096]{1,0:T(8,128)S(1)}, f32[32,4096]{1,0:T(8,128)}, u32[]{:S(2)}) copy-start(f32[32,4096]{1,0:T(8,128)} %param.40) | copy-start | bytes 1572868
  (113 other events, 310.9 us)
Sparse Core Ops, SparseCore 0:
  11.5 72.2 all-gather.6
  108.1 102.5 all-gather.8
  214.1 56.4 all-gather.10
  273.9 76.3 all-gather.12
  387.0 182.2 reduce-scatter.16
  572.6 78.4 all-gather.14
  889.6 97.8 reduce-scatter.8
  989.8 141.5 reduce-scatter.12
  1134.3 129.5 reduce-scatter.18
  1269.7 152.0 reduce-scatter.10
  1424.2 182.8 reduce-scatter.14
where the time goes:
time: 1630 us; the launch traced here: 1620 us
  waiting for transfers between devices  1040 us (64%)
  matrix products  315 us (19%)
  local copies, waits for them, and re-layouts  114 us (7%)
  other arithmetic  89.4 us (5%)
  blocking collectives  43.9 us (3%)
    reduce_scatter x1, waiting for transfers between devices, body(): lax.psum_scatter(expand_grad, ('ctx', 'wshard'), scatter_dimension=0, til...  183 us
    reduce_scatter x1, waiting for transfers between devices, body(): lax.psum_scatter(shrink_grad, ('ctx', 'wshard'), scatter_dimension=0, til...  182 us
    reduce_scatter x1, waiting for transfers between devices, body(): lax.psum_scatter(joint_grad, ('ctx', 'wshard'), scatter_dimension=0, tile...  156 us
    unnamed x12, waiting for transfers between devices  125 us
    all_gather x1, waiting for transfers between devices, body(): gathered = lax.all_gather(key_value, 'ctx', axis=1, tiled=True)  90.9 us
    reduce_scatter x1, waiting for transfers between devices, body(): lax.psum_scatter(key_value_grad.astype(jnp.bfloat16), 'ctx', scatter_dime...  87.7 us
    all_gather x1, waiting for transfers between devices, body(): lax.all_gather(shrink_weight.astype(jnp.bfloat16), ('ctx', 'wshard'), axi...  78.9 us
    reduce_scatter x1, waiting for transfers between devices, body(): lax.psum_scatter(mixing_grad, ('ctx', 'wshard'), scatter_dimension=0, til...  74.3 us
  transfers between devices with their start and end apart: 11, of which 10 were waited for; matrix products, arithmetic and copies ran while one was open for 12% of the time, Pallas kernels for 0%

commit v1 on v0

v1 whole, which is shorter than its diff:
```python
import functools

import jax
import jax.numpy as jnp
from jax import lax
from jax.experimental import pallas as pl
from jax.experimental.pallas import tpu as pltpu
from jax.sharding import PartitionSpec as P

H = 16
HD = 64
BLK = 256
STEP = 10
PAIR = 2 * HD

norm_eps = 1e-05
adam_eps = 1e-08
group_heads = 4
score_scale = 0.125 * 1.4426950408889634
gelu_root = 0.7978845608028654
gelu_cubic = 0.044715
low = jnp.bfloat16
axes = ("ctx", "wshard")
small_cost = pl.CostEstimate(flops=1024, bytes_accessed=1024, transcendentals=0)


def nt(a,b):
    return lax.dot_general(a,b,(((1,),(1,)),((),())),preferred_element_type=jnp.float32)
def nn(a,b):
    return jnp.dot(a,b,preferred_element_type=jnp.float32)

def rows_of(place):
    return pl.ds(pl.multiple_of(place*BLK,BLK),BLK)

def attend_kernel(blocks, place_ref, q_ref, k_ref, v_ref, o_ref, lse_ref):
    seq=pl.program_id(0)
    lane=lax.broadcasted_iota(jnp.int32,(1,PAIR),1)
    masks=[lane<HD, lane>=HD]
    for i in range(blocks):
        rows=rows_of(place_ref[seq,i])
        qi=q_ref[rows,:]
        outs=[]
        for h in range(2):
            qh=jnp.where(masks[h],qi,jnp.zeros_like(qi))
            ss=[nt(qh,k_ref[rows_of(place_ref[seq,j]),:])*score_scale for j in range(i+1)]
            top=ss[0]
            for s in ss[1:]: top=jnp.maximum(top,s)
            top=jnp.max(top,axis=1,keepdims=True)
            ps=[jnp.exp2(s-top) for s in ss]
            tot=ps[0]
            for p in ps[1:]: tot=tot+p
            tot=jnp.sum(tot,axis=1,keepdims=True)
            acc=None
            for j in range(i+1):
                t=nn(ps[j].astype(jnp.bfloat16),v_ref[rows_of(place_ref[seq,j]),:])
                acc=t if acc is None else acc+t
            outs.append(acc*(1.0/tot))
            lse=top+jnp.log2(tot)
            lse_ref[h:h+1,rows]=jnp.transpose(jnp.broadcast_to(lse,(BLK,PAIR)))[0:1,:]
        o_ref[rows,:]=jnp.where(masks[0],outs[0],outs[1]).astype(o_ref.dtype)

def attend(place, qkv):
    tokens,width3=qkv.shape
    seqs,blocks=place.shape
    length=tokens//seqs
    width=width3//3
    pairs=width//PAIR
    spec=lambda part: pl.BlockSpec((length,PAIR),lambda s,p,place:(s,part*pairs+p))
    return pl.pallas_call(
        functools.partial(attend_kernel,blocks),
        grid_spec=pltpu.PrefetchScalarGridSpec(
            num_scalar_prefetch=1,grid=(seqs,pairs),
            in_specs=[spec(0),spec(1),spec(2)],
            out_specs=[pl.BlockSpec((length,PAIR),lambda s,p,place:(s,p)),
                       pl.BlockSpec((None,None,8,length),lambda s,p,place:(s,p,0,0))]),
        out_shape=[jax.ShapeDtypeStruct((tokens,width),jnp.bfloat16),
                   jax.ShapeDtypeStruct((seqs,pairs,8,length),jnp.float32)],
        compiler_params=pltpu.CompilerParams(vmem_limit_bytes=48<<20),
        cost_estimate=small_cost,
        name="attend",
    )(place,qkv,qkv,qkv)

def attend_back_kernel(blocks, place_ref, q_ref, k_ref, v_ref, do_ref, lse_ref, dq_ref, dk_ref, dv_ref, kt, dk_acc, dv_acc):
    seq=pl.program_id(0)
    lane=lax.broadcasted_iota(jnp.int32,(1,PAIR),1)
    masks=[lane<HD, lane>=HD]
    for j in range(blocks):
        kt[j]=jnp.transpose(k_ref[rows_of(place_ref[seq,j]),:])
    for i in range(blocks):
        rows=rows_of(place_ref[seq,i])
        qi=q_ref[rows,:]
        doi=do_ref[rows,:]
        dqts=[]
        for h in range(2):
            qh=jnp.where(masks[h],qi,jnp.zeros_like(qi))
            doh=jnp.where(masks[h],doi,jnp.zeros_like(doi))
            lse=lse_ref[h:h+1,rows]
            pts=[];dpts=[];delta=None
            for j in range(i+1):
                rj=rows_of(place_ref[seq,j])
                pt=jnp.exp2(nt(k_ref[rj,:],qh)*score_scale-lse)
                dpt=nt(v_ref[rj,:],doh)
                d=jnp.sum(pt*dpt,axis=0,keepdims=True)
                delta=d if delta is None else delta+d
                pts.append(pt);dpts.append(dpt)
            dqt=None
            for j in range(i+1):
                pb=pts[j].astype(jnp.bfloat16)
                ds=(pts[j]*(dpts[j]-delta)).astype(jnp.bfloat16)
                dv=nn(pb,doh)
                dk=nn(ds,qh)
                if i==j and h==0:
                    dv_acc[j]=dv; dk_acc[j]=dk
                else:
                    dv_acc[j]+=dv; dk_acc[j]+=dk
                t=nn(kt[j,h*HD:(h+1)*HD,:],ds)
                dqt=t if dqt is None else dqt+t
            dqts.append(dqt)
        dq_ref[rows,:]=(jnp.transpose(jnp.concatenate(dqts,axis=0))*0.125).astype(dq_ref.dtype)
    for j in range(blocks):
        rows=rows_of(place_ref[seq,j])
        dk_ref[rows,:]=(dk_acc[j]*0.125).astype(dk_ref.dtype)
        dv_ref[rows,:]=dv_acc[j].astype(dv_ref.dtype)

def attend_back(place, qkv, upstream, lse):
    tokens,width3=qkv.shape
    seqs,blocks=place.shape
    length=tokens//seqs
    width=width3//3
    pairs=width//PAIR
    spec=lambda part: pl.BlockSpec((length,PAIR),lambda s,p,place:(s,part*pairs+p))
    one=pl.BlockSpec((length,PAIR),lambda s,p,place:(s,p))
    return pl.pallas_call(
        functools.partial(attend_back_kernel,blocks),
        grid_spec=pltpu.PrefetchScalarGridSpec(
            num_scalar_prefetch=1,grid=(seqs,pairs),
            in_specs=[spec(0),spec(1),spec(2),one,pl.BlockSpec((None,None,8,length),lambda s,p,place:(s,p,0,0))],
            out_specs=[one,one,one],
            scratch_shapes=[pltpu.VMEM((blocks,PAIR,BLK),jnp.bfloat16),pltpu.VMEM((blocks,BLK,PAIR),jnp.float32),pltpu.VMEM((blocks,BLK,PAIR),jnp.float32)]),
        out_shape=[jax.ShapeDtypeStruct((tokens,width),jnp.bfloat16)]*3,
        compiler_params=pltpu.CompilerParams(vmem_limit_bytes=48<<20),
        cost_estimate=small_cost,
        name="attend_back",
    )(place,qkv,qkv,qkv,upstream,lse)


def mlp_kernel(first, rows_step, c_ref, dy_ref, we_ref, ws_ref, be_ref, *rest):
    if first:
        y_ref, dc_ref, gwe_ref, gws_ref, gbe_ref, ct, act_all, du_all = rest
    else:
        y_in, dc_in, y_ref, dc_ref, gwe_ref, gws_ref, gbe_ref, ct, act_all, du_all, sem = rest
    step=pl.program_id(0)
    tokens=c_ref.shape[0]
    @pl.when(step==0)
    def _():
        ct[...]=jnp.transpose(c_ref[...])
        if first:
            y_ref[...]=jnp.zeros_like(y_ref)
            dc_ref[...]=jnp.zeros_like(dc_ref)
        else:
            a=pltpu.make_async_copy(y_in,y_ref,sem.at[0]); b=pltpu.make_async_copy(dc_in,dc_ref,sem.at[1])
            a.start(); b.start(); a.wait(); b.wait()
    we=we_ref[...]; ws=ws_ref[...]
    total=None
    for r in range(tokens//rows_step):
        rows=pl.ds(r*rows_step,rows_step)
        u=nn(c_ref[rows,:],we)+be_ref[...]
        t2=u*u
        th=jnp.tanh(gelu_root*u*(1.0+gelu_cubic*t2))
        half=0.5+0.5*th
        act=(u*half).astype(jnp.bfloat16)
        slope=half+(0.5*gelu_root)*u*(1.0-th*th)*(1.0+(3*gelu_cubic)*t2)
        du=(nt(dy_ref[rows,:],ws)*slope).astype(jnp.bfloat16)
        act_all[rows,:]=act; du_all[rows,:]=du
        y_ref[rows,:]+=nn(act,ws)
        dc_ref[rows,:]+=nt(du,we)
        s=jnp.sum(du.astype(jnp.float32),axis=0,keepdims=True)
        total=s if total is None else total+s
    gbe_ref[...]=total
    gwe_ref[...]=nn(ct[...],du_all[...]).astype(gwe_ref.dtype)
    gws_ref[...]=lax.dot_general(act_all[...],dy_ref[...],(((0,),(0,)),((),())),preferred_element_type=jnp.float32).astype(gws_ref.dtype)

def mlp(c,dy,we,ws,be,before=None,tile=256,rows_step=256):
    tokens,width=c.shape
    hidden=we.shape[1]
    whole=pl.BlockSpec((tokens,width),lambda t:(0,0))
    specs=[whole,whole,pl.BlockSpec((width,tile),lambda t:(0,t)),pl.BlockSpec((tile,width),lambda t:(t,0)),pl.BlockSpec((1,tile),lambda t:(0,t))]
    args=[c,dy,we,ws,be]
    scratch=[pltpu.VMEM((width,tokens),jnp.bfloat16),pltpu.VMEM((tokens,tile),jnp.bfloat16),pltpu.VMEM((tokens,tile),jnp.bfloat16)]
    if before is not None:
        specs+=[pl.BlockSpec(memory_space=pl.ANY)]*2
        args+=list(before)
        scratch+=[pltpu.SemaphoreType.DMA((2,))]
    return pl.pallas_call(
        functools.partial(mlp_kernel,before is None,rows_step),
        grid=(hidden//tile,),
        in_specs=specs,
        out_specs=[whole,whole,pl.BlockSpec((width,tile),lambda t:(0,t)),pl.BlockSpec((tile,width),lambda t:(t,0)),pl.BlockSpec((1,tile),lambda t:(0,t))],
        out_shape=[jax.ShapeDtypeStruct((tokens,width),jnp.float32)]*2+[jax.ShapeDtypeStruct((width,hidden),jnp.bfloat16),jax.ShapeDtypeStruct((hidden,width),jnp.bfloat16),jax.ShapeDtypeStruct((1,hidden),jnp.float32)],
        scratch_shapes=scratch,
        compiler_params=pltpu.CompilerParams(vmem_limit_bytes=56<<20),
        cost_estimate=small_cost,
        name="mlp",
    )(*args)


def layer_norm(values, gain_row, shift_row):
    centered = values - jnp.mean(values, axis=-1, keepdims=True)
    variance = jnp.mean(centered * centered, axis=-1, keepdims=True)
    inverse = lax.rsqrt(variance + norm_eps)
    normal_part = centered * inverse
    return (normal_part * gain_row + shift_row, normal_part, inverse)


def norm_back(upstream, normal_part, inverse, gain_row):
    scaled = upstream * gain_row
    inner_sum = jnp.mean(scaled, axis=-1, keepdims=True)
    along_sum = jnp.mean(scaled * normal_part, axis=-1, keepdims=True)
    values_grad = inverse * (scaled - inner_sum - normal_part * along_sum)
    return (values_grad, jnp.sum(upstream * normal_part, axis=0), jnp.sum(upstream, axis=0))


def outer_sum(left_side, right_side):
    return lax.dot_general(
        left_side, right_side, (((0,), (0,)), ((), ())), preferred_element_type=jnp.float32
    )


def adam_update(weight, moment_one, moment_two, gradient, step_rate, decay_rate):
    first_new = 0.5 * moment_one + 0.5 * gradient
    second_new = 0.5 * moment_two + 0.5 * gradient * gradient
    correct = 1.0 - 0.5**STEP
    direction = first_new / correct / (jnp.sqrt(second_new / correct) + adam_eps)
    updated = weight - step_rate * (direction + decay_rate * weight)
    return (updated, first_new, second_new)


def to_groups(matrix):
    row_count = matrix.shape[0]
    return matrix.reshape(row_count, H // group_heads, group_heads, HD).transpose(1, 0, 2, 3)


def from_groups(stacked):
    return stacked.transpose(1, 0, 2, 3).reshape(stacked.shape[1], H * HD)


def tile_scores(queries, key_rows, allowed):
    products = jnp.einsum("rgd,lgd->grl", queries, key_rows, preferred_element_type=jnp.float32)
    return jnp.where(allowed[None], products * 0.125, -1e30)


def tile_forward(queries, key_rows, value_rows, allowed):
    scores = tile_scores(queries, key_rows, allowed)
    largest = jnp.max(scores, axis=-1, keepdims=True)
    exponent = jnp.exp(scores - largest)
    row_total = jnp.sum(exponent, axis=-1, keepdims=True)
    weights = (exponent / row_total).astype(low)
    mixed = jnp.einsum("grl,lgd->rgd", weights, value_rows, preferred_element_type=jnp.float32)
    return (mixed, (largest + jnp.log(row_total))[..., 0])


def tile_backward(queries, key_rows, value_rows, allowed, logsum, upstream):
    scores = tile_scores(queries, key_rows, allowed)
    recomputed = jnp.exp(scores - logsum[..., None])
    value_grad = jnp.einsum(
        "grl,rgd->lgd", recomputed.astype(low), upstream, preferred_element_type=jnp.float32
    )
    weight_grad = jnp.einsum(
        "rgd,lgd->grl", upstream, value_rows, preferred_element_type=jnp.float32
    )
    inner_sum = jnp.sum(recomputed * weight_grad, axis=-1, keepdims=True)
    score_grad = (recomputed * (weight_grad - inner_sum)).astype(low)
    query_grad = (
        jnp.einsum("grl,lgd->rgd", score_grad, key_rows, preferred_element_type=jnp.float32) * 0.125
    )
    key_grad = (
        jnp.einsum("grl,rgd->lgd", score_grad, queries, preferred_element_type=jnp.float32) * 0.125
    )
    return (query_grad, key_grad, value_grad)


def spread_forward(queries, key_value, allowed):
    def one_sequence(pieces):
        queries, key_value, allowed = pieces
        width = queries.shape[1]
        mixed, logsum = lax.map(
            lambda triple: tile_forward(triple[0], triple[1], triple[2], allowed),
            (to_groups(queries), to_groups(key_value[:, :width]), to_groups(key_value[:, width:])),
        )
        return (from_groups(mixed), logsum)

    return lax.map(one_sequence, (queries, key_value, allowed))


def spread_backward(queries, key_value, allowed, logsum, upstream):
    def one_sequence(pieces):
        queries, key_value, allowed, logsum, upstream = pieces
        width = queries.shape[1]
        query_grad, key_grad, value_grad = lax.map(
            lambda member: tile_backward(
                member[0], member[1], member[2], allowed, member[3], member[4]
            ),
            (
                to_groups(queries),
                to_groups(key_value[:, :width]),
                to_groups(key_value[:, width:]),
                logsum,
                to_groups(upstream),
            ),
        )
        return (
            from_groups(query_grad),
            jnp.concatenate([from_groups(key_grad), from_groups(value_grad)], axis=1),
        )

    return lax.map(one_sequence, (queries, key_value, allowed, logsum, upstream))


class Slice:
    def __init__(self, ctx_size, wshard_size):
        rest = wshard_size // 2
        self.sizes = {"c": ctx_size, "z": 4, "y": rest // 4, "k": 2}

    def here(self):
        flat = lax.axis_index(axes)
        found = {}
        for name in ("k", "y", "z", "c"):
            found[name] = flat % self.sizes[name]
            flat = flat // self.sizes[name]
        return found

    def shift(self, value, name, by):
        pairs = []
        sizes = self.sizes
        for c in range(sizes["c"]):
            for z in range(sizes["z"]):
                for y in range(sizes["y"]):
                    for k in range(sizes["k"]):
                        spot = {"c": c, "z": z, "y": y, "k": k}
                        goal = dict(spot)
                        goal[name] = (spot[name] + by) % sizes[name]
                        pairs.append((self.flat(spot), self.flat(goal)))
        return lax.ppermute(value, axes, pairs)

    def flat(self, spot):
        sizes = self.sizes
        return ((spot["c"] * sizes["z"] + spot["z"]) * sizes["y"] + spot["y"]) * sizes["k"] + spot[
            "k"
        ]

    def stack(self, array, name, here):
        size = self.sizes[name]
        parts = [array] + [self.shift(array, name, by) for by in range(1, size)]
        if size > 4:
            ordered = [parts[(-place) % size] for place in range(size)]
            return jnp.roll(jnp.stack(ordered), here[name], axis=0)
        return jnp.stack(
            [lax.select_n((here[name] - place) % size, *parts) if size > 2 else
             jnp.where(here[name] == place, parts[0], parts[1]) for place in range(size)]
        )

    def reach(self, pieces, name):
        grown = list(pieces)
        for by in range(1, self.sizes[name]):
            for array, place in pieces:
                moved = dict(place)
                moved[name] = (place[name] - by) % self.sizes[name]
                grown.append((self.shift(array, name, by), moved))
        return grown

    def gather_split(self, stacked, cut, here):
        sizes = self.sizes
        depth, rows, columns = stacked.shape
        out = jnp.zeros((sizes["c"], depth, sizes["y"], rows, columns), stacked.dtype)
        for low_column, high_column, order in ((0, cut, "cy"), (cut, columns, "yc")):
            pieces = [(stacked[:, :, low_column:high_column], here)]
            for name in order:
                pieces = self.reach(pieces, name)
            for array, place in pieces:
                out = lax.dynamic_update_slice(
                    out, array[None, :, None], (place["c"], 0, place["y"], 0, low_column)
                )
        return out.reshape(-1, columns)

    def gather_deep(self, block, here):
        sizes = self.sizes
        stacked = jnp.moveaxis(self.stack(self.stack(block, "c", here), "z", here), 0, 1)
        out = jnp.zeros(stacked.shape[:2] + (sizes["y"],) + block.shape, block.dtype)
        for array, place in self.reach([(stacked, here)], "y"):
            out = lax.dynamic_update_slice(
                out, array[:, :, None], (0, 0, place["y"], 0, 0)
            )
        return out.reshape(-1, block.shape[1])

    def send_terms(self, value, name, place, here):
        size = self.sizes[name]
        own = lax.dynamic_index_in_dim(value, here[name], place, False)
        moved = [
            self.shift(
                lax.dynamic_index_in_dim(value, (here[name] + by) % size, place, False), name, by
            )
            for by in range(1, size)
        ]
        return own, moved

    def add_terms(self, terms, kind=low):
        own, moved = terms
        total = own.astype(jnp.float32)
        for other in moved:
            total = total + other.astype(jnp.float32)
        return total.astype(kind)

    def everywhere(self, value):
        for name in ("k", "c", "y", "z"):
            total = value
            for by in range(1, self.sizes[name]):
                total = total + self.shift(value, name, by)
            value = total
        return value


def tie(value, *others):
    return lax.optimization_barrier((value, others))[0]


def by_core(core, first, second, axis):
    return jnp.where(
        core == 0,
        jnp.concatenate([first, second], axis=axis),
        jnp.concatenate([second, first], axis=axis),
    )


def pick(core, array, axis):
    return (
        lax.dynamic_index_in_dim(array, core, axis, False),
        lax.dynamic_index_in_dim(array, 1 - core, axis, False),
    )


def body(
    grid,
    block_input,
    block_order,
    cotangent,
    joint_weight,
    mixing_weight,
    expand_weight,
    shrink_weight,
    vectors,
    joint_first,
    mixing_first,
    expand_first,
    shrink_first,
    vectors_first,
    joint_second,
    mixing_second,
    expand_second,
    shrink_second,
    vectors_second,
):
    here = grid.here()
    core, ctx = here["k"], here["c"]
    ctx_size = grid.sizes["c"]
    seq_count, row_count, width = block_input.shape
    half = width // 2
    hidden_width = expand_weight.shape[1]
    slot = shrink_weight.shape[0]
    whole_sequences = ctx_size == seq_count
    tokens = seq_count * row_count
    row_blocks = row_count // BLK

    def to_sequence(rows):
        if not whole_sequences:
            return rows.reshape(tokens, width)
        parts = [lax.dynamic_index_in_dim(rows, ctx, 0, False)]
        for by in range(1, ctx_size):
            sent = lax.dynamic_index_in_dim(rows, (ctx + by) % ctx_size, 0, False)
            parts.append(grid.shift(sent, "c", by))
        return jnp.concatenate(parts, axis=0)

    def from_sequence(rows, kind):
        if not whole_sequences:
            return rows.astype(kind).reshape(seq_count, row_count, width)
        parts = [rows[:row_count].astype(kind)]
        for by in range(1, ctx_size):
            sent = rows[by * row_count : (by + 1) * row_count].astype(low)
            parts.append(grid.shift(sent, "c", -by).astype(kind))
        stacked = jnp.stack(parts)
        if ctx_size == 2:
            return jnp.where(ctx == 0, stacked, stacked[::-1])
        return jnp.roll(stacked, ctx, axis=0)

    def halves(shard, outer, inner):
        own, other = pick(core, shard.astype(low).reshape(shard.shape[0], outer, 2, inner), 2)
        return own.reshape(shard.shape[0], -1), other.reshape(shard.shape[0], -1)

    def rows_of_chip(own, other):
        return by_core(core, own, grid.shift(other, "k", 1), 0)

    part = vectors.shape[1]
    table = jnp.pad(vectors.T.astype(low), ((0, 0), (0, 128 - vectors.shape[0])))
    joint_halves = halves(joint_weight, 3, half)
    joint_block = rows_of_chip(
        *[jnp.concatenate([table, piece], axis=1) for piece in joint_halves]
    )
    joint_stack = grid.stack(joint_block, "z", here)
    input_rows = to_sequence(block_input).astype(jnp.float32)
    joint_and_table = grid.gather_split(joint_stack, 128 + 3 * half // 2, here)
    joint_own = joint_and_table[:, 128:]
    vector_values = joint_and_table[:, : vectors.shape[0]].T.astype(jnp.float32)
    joint_other = grid.shift(joint_own, "k", 1)

    mixing_shard, expand_shard, shrink_shard, cotangent = tie(
        (mixing_weight, expand_weight, shrink_weight, cotangent), joint_stack
    )
    mixing_own = grid.gather_split(
        grid.stack(rows_of_chip(*halves(mixing_shard, 1, half)), "z", here), half // 2, here
    )
    mixing_full = by_core(core, mixing_own, grid.shift(mixing_own, "k", 1), 1)
    expand_own = grid.gather_deep(
        rows_of_chip(*halves(expand_shard, hidden_width // (2 * slot), slot)), here
    )
    expand_other = grid.shift(expand_own, "k", 1)
    shrink_own = grid.gather_split(
        grid.stack(shrink_shard.astype(low), "z", here), half, here
    )
    shrink_other = grid.shift(shrink_own, "k", 1)
    upstream = to_sequence(cotangent)

    normed_first, normal_first, inverse_first = layer_norm(
        input_rows, vector_values[0], vector_values[1]
    )
    first_low = normed_first.astype(low)
    query_bias = pick(core, vector_values[2].reshape(2, half), 0)
    value_bias = pick(core, vector_values[3].reshape(2, half), 0)

    def project(weight, query_shift, value_shift):
        shift = jnp.concatenate([query_shift, jnp.zeros_like(query_shift), value_shift])
        return (jnp.dot(first_low, weight, preferred_element_type=jnp.float32) + shift).astype(low)

    joint_out_own = project(joint_own, query_bias[0], value_bias[0])
    joint_out_other = project(joint_other, query_bias[1], value_bias[1])
    if whole_sequences:
        order = lax.dynamic_slice_in_dim(block_order, ctx, 1, 0)[0]
        stored = jnp.arange(order.shape[0], dtype=jnp.int32)
        moved = ((ctx - stored // row_blocks) % ctx_size) * row_blocks + stored % row_blocks
        place = jnp.sum(
            jnp.where(order[None, :] == stored[:, None], moved[None, :], 0), axis=1
        )[None].astype(jnp.int32)
        mixed_own, logsum_own = attend(place, joint_out_own)
        mixed_other, logsum_other = attend(place, joint_out_other)
    else:
        joined = [
            by_core(
                core,
                joint_out_own[:, part * half : (part + 1) * half],
                joint_out_other[:, part * half : (part + 1) * half],
                1,
            ).reshape(seq_count, row_count, width)
            for part in range(3)
        ]
        queries = joined[0]
        key_value = lax.all_gather(
            jnp.concatenate(joined[1:], axis=2), "ctx", axis=1, tiled=True
        )
        own_blocks = lax.dynamic_slice_in_dim(block_order, ctx * row_blocks, row_blocks, 1)
        query_block = jnp.repeat(own_blocks, BLK, axis=1, total_repeat_length=row_count)
        key_block = jnp.repeat(block_order, BLK, axis=1, total_repeat_length=key_value.shape[1])
        allowed = key_block[:, None, :] <= query_block[:, :, None]
        mixed, logsum = spread_forward(queries, key_value, allowed)
        mixed_own, mixed_other = pick(core, mixed.astype(low).reshape(tokens, 2, half), 1)
    mixing_rows = pick(core, mixing_full.reshape(2, half, width), 0)
    branch = (
        jnp.dot(mixed_own, mixing_rows[0], preferred_element_type=jnp.float32)
        + jnp.dot(mixed_other, mixing_rows[1], preferred_element_type=jnp.float32)
        + vector_values[4]
    )
    middle = input_rows + branch
    normed_second, normal_second, inverse_second = layer_norm(
        middle, vector_values[5], vector_values[6]
    )
    second_low = normed_second.astype(low)

    hidden_bias = pick(core, vector_values[8:].reshape(hidden_width // (2 * slot), 2, slot), 1)
    result, second_grad, expand_grad_other, shrink_grad_other, hidden_bias_other = mlp(
        second_low, upstream, expand_other, shrink_other, hidden_bias[1].reshape(1, -1)
    )
    expand_moved = grid.shift(expand_grad_other, "k", 1)
    shrink_moved = grid.shift(shrink_grad_other, "k", 1)
    result, second_grad, expand_grad_own, shrink_grad_own, hidden_bias_own = mlp(
        second_low,
        upstream,
        expand_own,
        shrink_own,
        hidden_bias[0].reshape(1, -1),
        before=(result, second_grad),
    )

    def by_device(own, moved):
        sizes = grid.sizes
        total = grid.add_terms((own, [moved]))
        return total.reshape(sizes["c"], sizes["z"], sizes["y"], -1, own.shape[-1])

    def join_columns(part, outer, inner):
        rows = part.shape[0] // 2
        own, other = pick(core, part.reshape(2, rows, outer, inner), 0)
        return by_core(core, own[:, :, None], grid.shift(other, "k", 1)[:, :, None], 2).reshape(
            rows, 2 * outer * inner
        )

    def split_one(value, cut):
        return (
            grid.send_terms(value[..., :cut], "y", 2, here),
            grid.send_terms(value[..., cut:], "c", 0, here),
        )

    def split_two(terms):
        return (
            grid.send_terms(grid.add_terms(terms[0]), "c", 0, here),
            grid.send_terms(grid.add_terms(terms[1]), "y", 1, here),
        )

    def split_three(terms):
        joined = jnp.concatenate([grid.add_terms(terms[0]), grid.add_terms(terms[1])], axis=-1)
        return grid.send_terms(joined, "z", 0, here)

    shrink_terms = split_one(by_device(shrink_grad_own, shrink_moved), half)
    expand_terms = grid.send_terms(by_device(expand_grad_own, expand_moved), "y", 2, here)
    block_output = from_sequence(middle + result + vector_values[7], low)

    upstream_float = upstream.astype(jnp.float32)
    middle_part, gain_two, shift_two = norm_back(
        second_grad, normal_second, inverse_second, vector_values[5]
    )
    middle_grad = upstream_float + middle_part
    branch_low = middle_grad.astype(low)
    mixing_grad = by_core(
        core,
        outer_sum(mixed_own, branch_low).astype(low),
        outer_sum(mixed_other, branch_low).astype(low),
        0,
    )
    mixing_grad_own, mixing_grad_other = pick(core, mixing_grad.reshape(width, 2, half), 1)
    mixing_moved = grid.shift(mixing_grad_other, "k", 1)
    mixed_grad_other = nt(branch_low, mixing_rows[1]).astype(low)
    mixed_grad_own = nt(branch_low, mixing_rows[0]).astype(low)
    mixing_terms = split_one(by_device(mixing_grad_own, mixing_moved), half // 2)
    if whole_sequences:
        mixed_grad_other = tie(mixed_grad_other, mixing_moved)
        joint_back_other = jnp.concatenate(
            attend_back(place, joint_out_other, mixed_grad_other, logsum_other), axis=1
        )
        joint_grad_other = outer_sum(first_low, joint_back_other).astype(low)
        joint_moved = grid.shift(joint_grad_other, "k", 1)
        shrink_terms = split_two(shrink_terms)
        expand_terms = grid.send_terms(grid.add_terms(expand_terms), "z", 1, here)
        mixing_terms = split_two(mixing_terms)
        mixed_grad_own = tie(
            mixed_grad_own,
            joint_grad_other,
            block_output,
            [terms[0] for terms in shrink_terms + mixing_terms],
            expand_terms[0],
        )
        joint_back_own = jnp.concatenate(
            attend_back(place, joint_out_own, mixed_grad_own, logsum_own), axis=1
        )
    else:
        mixed_grad = by_core(core, mixed_grad_own, mixed_grad_other, 1)
        query_grad, key_value_grad = spread_backward(
            queries, key_value, allowed, logsum, mixed_grad.reshape(seq_count, row_count, width)
        )
        summed = lax.psum_scatter(
            key_value_grad.astype(low), "ctx", scatter_dimension=1, tiled=True
        )
        pieces = [query_grad.astype(low), summed[..., :width], summed[..., width:]]
        both = [pick(core, piece.reshape(tokens, 2, half), 1) for piece in pieces]
        joint_back_own = jnp.concatenate([piece[0] for piece in both], axis=1)
        joint_back_other = jnp.concatenate([piece[1] for piece in both], axis=1)
        joint_grad_other = outer_sum(first_low, joint_back_other).astype(low)
        joint_moved = grid.shift(joint_grad_other, "k", 1)
        shrink_terms = split_two(shrink_terms)
        expand_terms = grid.send_terms(grid.add_terms(expand_terms), "z", 1, here)
        mixing_terms = split_two(mixing_terms)
    joint_grad_own = outer_sum(first_low, joint_back_own).astype(low)
    joint_terms = split_one(by_device(joint_grad_own, joint_moved), 3 * half // 2)
    shrink_terms = split_three(shrink_terms)
    expand_terms = grid.send_terms(grid.add_terms(expand_terms), "c", 0, here)
    mixing_terms = split_three(mixing_terms)
    joint_back_own = tie(
        joint_back_own,
        [terms[0] for terms in joint_terms],
        shrink_terms[0],
        expand_terms[0],
        mixing_terms[0],
    )
    first_grad = nt(joint_back_other, joint_other) + nt(joint_back_own, joint_own)
    input_part, gain_one, shift_one = norm_back(
        first_grad, normal_first, inverse_first, vector_values[0]
    )
    input_gradient = from_sequence(middle_grad + input_part, jnp.float32)
    shrink_sum = grid.add_terms(shrink_terms, jnp.float32)
    expand_sum = join_columns(
        grid.add_terms(expand_terms, jnp.float32), hidden_width // (2 * slot), slot
    )
    mixing_sum = join_columns(grid.add_terms(mixing_terms, jnp.float32), 1, half)
    joint_terms = split_three(split_two(joint_terms))
    joint_sum = join_columns(grid.add_terms(joint_terms, jnp.float32), 3, half)

    def column_sum(rows):
        return jnp.sum(rows.astype(jnp.float32), axis=0)

    back_sums = [column_sum(joint_back_own), column_sum(joint_back_other)]
    query_bias_grad = by_core(core, back_sums[0][:half], back_sums[1][:half], 0)
    value_bias_grad = by_core(core, back_sums[0][2 * half :], back_sums[1][2 * half :], 0)
    hidden_bias_grad = by_core(
        core,
        hidden_bias_own.reshape(-1, 1, slot),
        hidden_bias_other.reshape(-1, 1, slot),
        1,
    ).reshape(-1, width)
    vector_grad = jnp.concatenate(
        [
            jnp.stack(
                [
                    gain_one,
                    shift_one,
                    query_bias_grad,
                    value_bias_grad,
                    column_sum(branch_low),
                    gain_two,
                    shift_two,
                    column_sum(upstream),
                ]
            ),
            hidden_bias_grad,
        ],
        axis=0,
    )
    vector_sum = lax.dynamic_slice_in_dim(
        grid.everywhere(vector_grad),
        lax.axis_index(axes) * part,
        part,
        1,
    )
    joint_new, joint_moment, joint_square = adam_update(
        joint_weight, joint_first, joint_second, joint_sum, 0.05, 0.1
    )
    mixing_new, mixing_moment, mixing_square = adam_update(
        mixing_weight, mixing_first, mixing_second, mixing_sum, 0.05, 0.1
    )
    expand_new, expand_moment, expand_square = adam_update(
        expand_weight, expand_first, expand_second, expand_sum, 0.05, 0.1
    )
    shrink_new, shrink_moment, shrink_square = adam_update(
        shrink_weight, shrink_first, shrink_second, shrink_sum, 0.05, 0.1
    )
    vectors_new, vectors_moment, vectors_square = adam_update(
        vectors, vectors_first, vectors_second, vector_sum, 0.5, 0.0
    )
    return (
        block_output,
        input_gradient,
        joint_new,
        mixing_new,
        expand_new,
        shrink_new,
        vectors_new,
        joint_moment,
        mixing_moment,
        expand_moment,
        shrink_moment,
        vectors_moment,
        joint_square,
        mixing_square,
        expand_square,
        shrink_square,
        vectors_square,
        joint_new.astype(low),
        mixing_new.astype(low),
        expand_new.astype(low),
        shrink_new.astype(low),
        vectors_new.astype(low),
    )


def solution(mesh):
    grid = Slice(mesh.shape["ctx"], mesh.shape["wshard"])
    rows = P("wshard", "ctx", None)
    matrix = P(axes, None)
    table = P(None, axes)
    parameters = (matrix, matrix, matrix, matrix, table)
    return jax.shard_map(
        functools.partial(body, grid),
        mesh=mesh,
        in_specs=(rows, P("wshard", None), rows) + parameters * 3,
        out_specs=(rows, rows) + parameters * 4,
        check_vma=False,
    )
```

time: 1630 us -> 721 us (0.44)
  waiting for transfers between devices: 1040 us -> 230 us
  matrix products: 315 us -> 48 us
  Pallas kernels: 0 us -> 155 us
  starting transfers between devices: 1.09 us -> 123 us
  blocking collectives: 43.9 us -> 0 us
  local copies, waits for them, and re-layouts: 114 us -> 75.1 us
    reduce_scatter x5 -> x0, waiting for transfers between devices: 683 us -> none  [the longest x1 183 us: body(): lax.psum_scatter(expand_grad, ('ctx', 'wshard'), scatter_dimension=0, til...]
    ppermute x0 -> x82, waiting for transfers between devices: none -> 230 us  [shift(): return lax.ppermute(value, axes, pairs)]
    all_gather x5 -> x0, waiting for transfers between devices: 229 us -> none  [the longest x1 90.9 us: body(): gathered = lax.all_gather(key_value, 'ctx', axis=1, tiled=True)]
    dot_general x64 -> x8, matrix products: 259 us -> 35.7 us  [the longest x4 17.7 us: nt(): lax.dot_general(a, b, (((1,), (1,)), ((), ())), preferred_element_type=jn...]
    pallas_call x0 -> x6, Pallas kernels: none -> 155 us  [the longest x2 82.7 us: mlp(): pl.pallas_call(functools.partial(mlp_kernel, before is None, rows_step),...]
    unnamed x12 -> x0, waiting for transfers between devices: 125 us -> none
    ppermute x0 -> x82, starting transfers between devices: none -> 123 us  [shift(): return lax.ppermute(value, axes, pairs)]
    all_gather x1 -> x0, blocking collectives: 43.9 us -> none  [body(): lax.all_gather(vectors.astype(jnp.bfloat16), ('ctx', 'wshard'), axis=1, t...]
  transfers between devices with their start and end apart: 11 -> 82, of which waited for: 10 -> 25; matrix products, arithmetic and copies ran while one was open for 12% -> 24% of each run, Pallas kernels for 0% -> 10%
where the time goes in v1:
time: 721 us; the launch traced here: 711 us
  waiting for transfers between devices  230 us (32%)
  Pallas kernels  155 us (21%)
  starting transfers between devices  123 us (17%)
  other arithmetic  76.2 us (11%)
  local copies, waits for them, and re-layouts  75.1 us (10%)
  matrix products  48 us (7%)
    ppermute x82, waiting for transfers between devices, shift(): return lax.ppermute(value, axes, pairs)  230 us
    ppermute x82, starting transfers between devices, shift(): return lax.ppermute(value, axes, pairs)  123 us
    pallas_call x2, Pallas kernels, mlp(): pl.pallas_call(functools.partial(mlp_kernel, before is None, rows_step),...  82.7 us
    pallas_call x2, Pallas kernels, attend_back(): pl.pallas_call(functools.partial(attend_back_kernel, blocks), grid_spec=p...  42.6 us
    pallas_call x2, Pallas kernels, attend(): pl.pallas_call(functools.partial(attend_kernel, blocks), grid_spec=pltpu....  30.1 us
    dynamic_update_slice x24, local copies, waits for them, and re-layouts, gather_split(): lax.dynamic_update_slice(out, array[None, :, None], (place['c'], 0, place...  25 us
    convert_element_type x18, other arithmetic, add_terms(): return total.astype(kind)  20.2 us
    dot_general x4, matrix products, nt(): lax.dot_general(a, b, (((1,), (1,)), ((), ())), preferred_element_type=jn...  17.7 us
  transfers between devices with their start and end apart: 82, of which 25 were waited for; matrix products, arithmetic and copies ran while one was open for 24% of the time, Pallas kernels for 10%

profile of v1, /device:TPU:0, one launch (start us, length us, event | category | flops | bytes accessed | tf_op | source)
XLA Modules:
  0.0 711.2 jit_solution(16382805099676606636)
XLA Ops:
  20.1 8.3 %collective-permute-done.3 = bf16[64,1664]{1,0:T(8,128)(2,1)S(1)} collective-permute-done((bf16[64,1664]{1,0:T(8,128)(2,1)S(1)}, bf16[64,1664]{1,0:T(8,128)(2,1)S(1)}, u32[]{:S(2)}, u32[]{:S(2)}) %collective-permute-start.3) | collective-permute-done | bytes 213024 | tf_op jit(solution)/shard_map/ppermute | solution.py:343
  31.4 5.0 collective-permute-start.30
  54.9 5.3 collective-permute-done.15
  75.6 7.5 %collective-permute-done.17 = bf16[4,64,256]{2,1,0:T(8,128)(2,1)S(1)} collective-permute-done((bf16[4,64,256]{2,1,0:T(8,128)(2,1)S(1)}, bf16[4,64,256]{2,1,0:T(8,128)(2,1)S(1)}, u32[]{:S(2)}, u32[]{:S(2)}) %collective-permute-start.17) | collective-permute-done | bytes 131104 | tf_op jit(solution)/shard_map/ppermute | solution.py:343
  104.0 5.4 collective-permute-done.33
  111.8 7.2 %collective-permute-done.34 = bf16[4,128,512]{2,1,0:T(8,128)(2,1)S(1)} collective-permute-done((bf16[4,128,512]{2,1,0:T(8,128)(2,1)S(1)}, bf16[4,128,512]{2,1,0:T(8,128)(2,1)S(1)}, u32[]{:S(2)}, u32[]{:S(2)}) %collective-permute-start.34) | collective-permute-done | bytes 524320 | tf_op jit(solution)/shard_map/ppermute | solution.py:343
  119.0 11.3 %collective-permute-start.28 = (bf16[2,64,2048]{2,1,0:T(8,128)(2,1)S(1)}, bf16[2,64,2048]{2,1,0:T(8,128)(2,1)S(1)}, u32[]{:S(2)}, u32[]{:S(2)}) collective-permute-start(bf16[2,64,2048]{2,1,0:T(8,128)(2,1)S(1)} %pad_maximum_fusion.7), channel_id=1, source_target_pairs={{0,12},{1,13},{2,14},{3,15},{4,0},{5,1},{6,2},{7,3},{8,4},{9,5},{1... | collective-permute-start | bytes 1572872 | tf_op jit(solution)/shard_map/ppermute | solution.py:343
  137.9 8.2 %collective-permute-done.28 = bf16[2,64,2048]{2,1,0:T(8,128)(2,1)S(1)} collective-permute-done((bf16[2,64,2048]{2,1,0:T(8,128)(2,1)S(1)}, bf16[2,64,2048]{2,1,0:T(8,128)(2,1)S(1)}, u32[]{:S(2)}, u32[]{:S(2)}) %collective-permute-start.28) | collective-permute-done | bytes 524320 | tf_op jit(solution)/shard_map/ppermute | solution.py:343
  153.4 30.0 %collective-permute-done.10 = bf16[4,64,768]{2,1,0:T(8,128)(2,1)S(1)} collective-permute-done((bf16[4,64,768]{2,1,0:T(8,128)(2,1)S(1)}, bf16[4,64,768]{2,1,0:T(8,128)(2,1)S(1)}, u32[]{:S(2)}, u32[]{:S(2)}) %collective-permute-start.10) | collective-permute-done | bytes 393248 | tf_op jit(solution)/shard_map/ppermute | solution.py:343
  206.4 11.8 %collective-permute-done.29 = bf16[2,4,64,2048]{3,2,0,1:T(8,128)(2,1)} collective-permute-done((bf16[2,4,64,2048]{3,2,0,1:T(8,128)(2,1)}, bf16[2,4,64,2048]{3,2,0,1:T(8,128)(2,1)}, u32[]{:S(2)}, u32[]{:S(2)}) %collective-permute-start.29) | collective-permute-done | bytes 2097184 | tf_op jit(solution)/shard_map/ppermute | solution.py:343
  221.4 6.9 add_convert_fusion.4.q_ref.k_ref.v_ref
  228.3 15.0 %attend.2 = (bf16[1024,512]{1,0:T(8,128)(2,1)S(1)}, f32[1,4,8,1024]{3,2,1,0:T(8,128)S(1)}) custom-call(s32[1,4]{1,0:T(1,128)S(1)} %bitcast.387, bf16[1024,1536]{1,0:T(8,128)(2,1)S(1)} %add_convert_fusion.4.q_ref.k_ref.v_ref, bf16[1024,1536]{1,0:T(8,128)(2,1)S(1)} %add_convert_fusion.4.q_ref.k_ref.v_ref, ...), custom_call_target="tpu_custom_call" | custom-call | flops 1024 | bytes 1024 | tf_op jit(solution)/shard_map/attend/pallas_call | solution.py:69
  253.6 7.6 %add_convert_fusion.3.q_ref.k_ref.v_ref = bf16[1024,1536]{1,0:T(8,128)(2,1)S(1)} fusion(bf16[1024,1536]{1,0:T(8,128)(2,1)} %collective-permute-done.22, f32[1536]{0:T(1024)S(1)} %get-tuple-element.205, f32[1024]{0:T(1024)S(1)} %get-tuple-element.90, f32[1024]{0:T(1024)S(1)} %get-tuple-element.91, f32[1024]{0:T(1024)S(1)} %add_rsqrt_fusion.1, ...), kind=kOutput, calls=%fused_computation.6 | convolution fusion | flops 3233808384 | bytes 8411136 | tf_op jit(solution)/shard_map/dot_general | solution.py:540
  262.5 15.2 %attend.3 = (bf16[1024,512]{1,0:T(8,128)(2,1)S(1)}, f32[1,4,8,1024]{3,2,1,0:T(8,128)S(1)}) custom-call(s32[1,4]{1,0:T(1,128)S(1)} %bitcast.388, bf16[1024,1536]{1,0:T(8,128)(2,1)S(1)} %add_convert_fusion.3.q_ref.k_ref.v_ref, bf16[1024,1536]{1,0:T(8,128)(2,1)S(1)} %add_convert_fusion.3.q_ref.k_ref.v_ref, ...), custom_call_target="tpu_custom_call" | custom-call | flops 1024 | bytes 1024 | tf_op jit(solution)/shard_map/attend/pallas_call | solution.py:69
  282.6 40.0 %mlp.2 = (f32[1024,1024]{1,0:T(8,128)}, f32[1024,1024]{1,0:T(8,128)}, bf16[1024,2048]{1,0:T(8,128)(2,1)}, bf16[2048,1024]{1,0:T(8,128)(2,1)}, f32[1,2048]{1,0:T(1,128)}) custom-call(bf16[1024,1024]{1,0:T(8,128)(2,1)} %add_convert_fusion.6.c_ref, bf16[1024,1024]{1,0:T(8,128)(2,1)} %pad_maximum_fusion.2.dy_ref, ...), custom_call_target="tpu_custom_call" | custom-call | flops 1024 | bytes 1024 | tf_op jit(solution)/shard_map/mlp/pallas_call | solution.py:194
  322.6 42.7 %mlp.3 = (f32[1024,1024]{1,0:T(8,128)}, f32[1024,1024]{1,0:T(8,128)}, bf16[1024,2048]{1,0:T(8,128)(2,1)}, bf16[2048,1024]{1,0:T(8,128)(2,1)}, f32[1,2048]{1,0:T(1,128)}) custom-call(bf16[1024,1024]{1,0:T(8,128)(2,1)} %add_convert_fusion.6.c_ref, bf16[1024,1024]{1,0:T(8,128)(2,1)} %pad_maximum_fusion.2.dy_ref, bf16[1024,2048]{1,0:T(8,128)(2,1)} %bitcast.67.we_ref, ...), custom_call_target="tpu_custom_call" | custom-call | flops 1024 | bytes 1024 | tf_op jit(solution)/shard_map/mlp/pallas_call | solution.py:194
  369.7 6.9 convert_reduce_fusion.4
  394.9 21.3 %attend_back.2 = (bf16[1024,512]{1,0:T(8,128)(2,1)S(1)}, bf16[1024,512]{1,0:T(8,128)(2,1)S(1)}, bf16[1024,512]{1,0:T(8,128)(2,1)S(1)}) custom-call(s32[1,4]{1,0:T(1,128)S(1)} %bitcast.389, bf16[1024,1536]{1,0:T(8,128)(2,1)} %copy-done.3, bf16[1024,1536]{1,0:T(8,128)(2,1)} %copy-done.3, bf16[1024,1536]{1,0:T(8,128)(2,1)} %copy-done.3, ...), custom_call_target="tpu_custom_call" | custom-call | flops 1024 | bytes 1024 | tf_op jit(solution)/shard_map/attend_back/pallas_call | solution.py:133
  418.1 5.5 convolution_convert_fusion.1
  425.5 6.9 fusion.106
  458.5 14.3 %collective-permute-done.45 = bf16[4,2,128,512]{3,2,1,0:T(8,128)(2,1)S(1)} collective-permute-done((bf16[4,2,128,512]{3,2,1,0:T(8,128)(2,1)S(1)}, bf16[4,2,128,512]{3,2,1,0:T(8,128)(2,1)S(1)}, u32[]{:S(2)}, u32[]{:S(2)}) %collective-permute-start.45) | collective-permute-done | bytes 1048608 | tf_op jit(solution)/shard_map/ppermute | solution.py:343
  479.3 50.0 %collective-permute-done.52 = bf16[4,128,512]{2,1,0:T(8,128)(2,1)S(1)} collective-permute-done((bf16[4,128,512]{2,1,0:T(8,128)(2,1)S(1)}, bf16[4,128,512]{2,1,0:T(8,128)(2,1)S(1)}, u32[]{:S(2)}, u32[]{:S(2)}) %collective-permute-start.52) | collective-permute-done | bytes 524320 | tf_op jit(solution)/shard_map/ppermute | solution.py:343
  540.8 7.4 %collective-permute-start.54 = (bf16[2,64,2048]{2,1,0:T(8,128)(2,1)S(1)}, bf16[2,64,2048]{2,1,0:T(8,128)(2,1)S(1)}, u32[]{:S(2)}, u32[]{:S(2)}) collective-permute-start(bf16[2,64,2048]{2,1,0:T(8,128)(2,1)S(1)} %get-tuple-element.144), channel_id=1, source_target_pairs={{0,8},{1,9},{2,10},{3,11},{4,12},{5,13},{6,14},{7,15},{8,0},{9,1},... | collective-permute-start | bytes 1572872 | tf_op jit(solution)/shard_map/ppermute | solution.py:343
  548.2 17.3 %collective-permute-done.74 = bf16[128,1024]{1,0:T(8,128)(2,1)S(1)} collective-permute-done((bf16[128,1024]{1,0:T(8,128)(2,1)S(1)}, bf16[128,1024]{1,0:T(8,128)(2,1)S(1)}, u32[]{:S(2)}, u32[]{:S(2)}) %collective-permute-start.74) | collective-permute-done | bytes 262176 | tf_op jit(solution)/shard_map/ppermute | solution.py:343
  567.9 18.9 %collective-permute-done.54 = bf16[2,64,2048]{2,1,0:T(8,128)(2,1)S(1)} collective-permute-done((bf16[2,64,2048]{2,1,0:T(8,128)(2,1)S(1)}, bf16[2,64,2048]{2,1,0:T(8,128)(2,1)S(1)}, u32[]{:S(2)}, u32[]{:S(2)}) %collective-permute-start.54) | collective-permute-done | bytes 524320 | tf_op jit(solution)/shard_map/ppermute | solution.py:343
  588.9 21.3 %attend_back.3 = (bf16[1024,512]{1,0:T(8,128)(2,1)S(1)}, bf16[1024,512]{1,0:T(8,128)(2,1)S(1)}, bf16[1024,512]{1,0:T(8,128)(2,1)S(1)}) custom-call(s32[1,4]{1,0:T(1,128)S(1)} %bitcast.390, bf16[1024,1536]{1,0:T(8,128)(2,1)} %copy-done.2, bf16[1024,1536]{1,0:T(8,128)(2,1)} %copy-done.2, bf16[1024,1536]{1,0:T(8,128)(2,1)} %copy-done.2, ...), custom_call_target="tpu_custom_call" | custom-call | flops 1024 | bytes 1024 | tf_op jit(solution)/shard_map/attend_back/pallas_call | solution.py:133
  628.3 11.1 %collective-permute-done.59 = bf16[2,4,64,768]{3,2,1,0:T(8,128)(2,1)} collective-permute-done((bf16[2,4,64,768]{3,2,1,0:T(8,128)(2,1)}, bf16[2,4,64,768]{3,2,1,0:T(8,128)(2,1)}, u32[]{:S(2)}, u32[]{:S(2)}) %collective-permute-start.59) | collective-permute-done | bytes 786464 | tf_op jit(solution)/shard_map/ppermute | solution.py:343
  641.4 8.3 %fusion.12 = (f32[1024]{0:T(1024)S(1)}, f32[1024]{0:T(1024)S(1)}, f32[1024]{0:T(1024)S(1)}, f32[1024]{0:T(1024)S(1)}, f32[1024,1024]{1,0:T(8,128)}) fusion(f32[1024]{0:T(1024)S(1)} %copy-done.50, f32[1024]{0:T(1024)S(1)} %broadcast_multiply_fusion.5, bf16[512,1024]{1,0:T(8,128)(2,1)S(1)} %copy-done.18, bf16[512,1024]{1,0:T(8,128)(2,1)S(1)} %copy-done.11, ...), kind=kOutput, calls=%fused_computation.25 | convolution fusion | flops 3235901440 | bytes 16805888 | tf_op jit(solution)/shard_map/dot_general | solution.py:28
  659.1 6.0 collective-permute-done.77
  666.6 11.1 %collective-permute-start.63 = (bf16[64,1536]{1,0:T(8,128)(2,1)S(1)}, bf16[64,1536]{1,0:T(8,128)(2,1)S(1)}, u32[]{:S(2)}, u32[]{:S(2)}) collective-permute-start(bf16[64,1536]{1,0:T(8,128)(2,1)S(1)} %get-tuple-element.173), channel_id=1, source_target_pairs={{0,4},{1,5},{2,6},{3,7},{4,8},{5,9},{6,10},{7,11},{8,12},{9,13},{1... | collective-permute-start | bytes 589832 | tf_op jit(solution)/shard_map/ppermute | solution.py:343
  684.2 7.7 %collective-permute-start.80 = (f32[12,1024]{1,0:T(8,128)S(1)}, f32[12,1024]{1,0:T(8,128)}, u32[]{:S(2)}, u32[]{:S(2)}) collective-permute-start(f32[12,1024]{1,0:T(8,128)S(1)} %add.742), channel_id=1, source_target_pairs={{0,8},{1,9},{2,10},{3,11},{4,12},{5,13},{6,14},{7,15},{8,0},{9,1},... | collective-permute-start | bytes 147464 | tf_op jit(solution)/shard_map/ppermute | solution.py:343
  692.4 7.5 %collective-permute-start.81 = (f32[12,1024]{1,0:T(8,128)S(1)}, f32[12,1024]{1,0:T(8,128)}, u32[]{:S(2)}, u32[]{:S(2)}) collective-permute-start(f32[12,1024]{1,0:T(8,128)S(1)} %add.742), channel_id=1, source_target_pairs={{0,12},{1,13},{2,14},{3,15},{4,0},{5,1},{6,2},{7,3},{8,4},{9,5},{1... | collective-permute-start | bytes 147464 | tf_op jit(solution)/shard_map/ppermute | solution.py:343
  (480 shorter events, 259.7 us)
Async XLA Ops:
  7.2 94.1 %collective-permute-start = (bf16[512,1024]{1,0:T(8,128)(2,1)}, bf16[512,1024]{1,0:T(8,128)(2,1)S(1)}, u32[]{:S(2)}, u32[]{:S(2)}) collective-permute-start(bf16[512,1024]{1,0:T(8,128)(2,1)} %get-tuple-element.155), channel_id=1, source_target_pairs={{0,16},{1,17},{2,18},{3,19},{4,20},{5,21},{6,22},{7,23},{8,24},{9,... | collective-permute-start | bytes 3145736 | tf_op jit(solution)/shard_map/ppermute | solution.py:343
  31.4 35.1 %collective-permute-start.30 = (bf16[128,1024]{1,0:T(8,128)(2,1)}, bf16[128,1024]{1,0:T(8,128)(2,1)}, u32[]{:S(2)}, u32[]{:S(2)}) collective-permute-start(bf16[128,1024]{1,0:T(8,128)(2,1)} %convert_element_type.343), channel_id=1, source_target_pairs={{0,4},{1,5},{2,6},{3,7},{4,8},{5,9},{6,10},{7,11},{8,12},{9,13},{1... | collective-permute-start | bytes 786440 | tf_op jit(solution)/shard_map/ppermute | solution.py:343
  65.4 33.2 %collective-permute-start.5 = (bf16[4,64,896]{2,1,0:T(8,128)(2,1)S(1)}, bf16[4,64,896]{2,1,0:T(8,128)(2,1)S(1)}, u32[]{:S(2)}, u32[]{:S(2)}) collective-permute-start(bf16[4,64,896]{2,1,0:T(8,128)(2,1)S(1)} %copy-done.40), channel_id=1, source_target_pairs={{0,16},{1,17},{2,18},{3,19},{4,20},{5,21},{6,22},{7,23},{8,24},{9,... | collective-permute-start | bytes 1376264 | tf_op jit(solution)/shard_map/ppermute | solution.py:343
  66.5 33.4 %collective-permute-start.6 = (bf16[4,64,896]{2,1,0:T(8,128)(2,1)S(1)}, bf16[4,64,896]{2,1,0:T(8,128)(2,1)S(1)}, u32[]{:S(2)}, u32[]{:S(2)}) collective-permute-start(bf16[4,64,896]{2,1,0:T(8,128)(2,1)S(1)} %copy-done.40), channel_id=1, source_target_pairs={{0,2},{1,3},{2,0},{3,1},{4,6},{5,7},{6,4},{7,5},{8,10},{9,11},{10,... | collective-permute-start | bytes 1376264 | tf_op jit(solution)/shard_map/ppermute | solution.py:343
  95.8 38.5 %collective-permute-start.8 = (bf16[4,64,768]{2,1,0:T(8,128)(2,1)S(1)}, bf16[4,64,768]{2,1,0:T(8,128)(2,1)S(1)}, u32[]{:S(2)}, u32[]{:S(2)}) collective-permute-start(bf16[4,64,768]{2,1,0:T(8,128)(2,1)S(1)} %copy-done.41), channel_id=1, source_target_pairs={{0,2},{1,3},{2,0},{3,1},{4,6},{5,7},{6,4},{7,5},{8,10},{9,11},{10,... | collective-permute-start | bytes 1179656 | tf_op jit(solution)/shard_map/ppermute | solution.py:343
  100.0 36.0 %collective-permute-start.26 = (bf16[2,64,2048]{2,1,0:T(8,128)(2,1)S(1)}, bf16[2,64,2048]{2,1,0:T(8,128)(2,1)S(1)}, u32[]{:S(2)}, u32[]{:S(2)}) collective-permute-start(bf16[2,64,2048]{2,1,0:T(8,128)(2,1)S(1)} %pad_maximum_fusion.7), channel_id=1, source_target_pairs={{0,4},{1,5},{2,6},{3,7},{4,8},{5,9},{6,10},{7,11},{8,12},{9,13},{1... | collective-permute-start | bytes 1572872 | tf_op jit(solution)/shard_map/ppermute | solution.py:343
  101.3 36.1 %collective-permute-start.27 = (bf16[2,64,2048]{2,1,0:T(8,128)(2,1)S(1)}, bf16[2,64,2048]{2,1,0:T(8,128)(2,1)S(1)}, u32[]{:S(2)}, u32[]{:S(2)}) collective-permute-start(bf16[2,64,2048]{2,1,0:T(8,128)(2,1)S(1)} %pad_maximum_fusion.7), channel_id=1, source_target_pairs={{0,8},{1,9},{2,10},{3,11},{4,12},{5,13},{6,14},{7,15},{8,0},{9,1},... | collective-permute-start | bytes 1572872 | tf_op jit(solution)/shard_map/ppermute | solution.py:343
  134.3 112.8 %collective-permute-start.23 = (bf16[512,1024]{1,0:T(8,128)(2,1)}, bf16[512,1024]{1,0:T(8,128)(2,1)}, u32[]{:S(2)}, u32[]{:S(2)}) collective-permute-start(bf16[512,1024]{1,0:T(8,128)(2,1)} %get-tuple-element.153), channel_id=1, source_target_pairs={{0,16},{1,17},{2,18},{3,19},{4,20},{5,21},{6,22},{7,23},{8,24},{9,... | collective-permute-start | bytes 3145736 | tf_op jit(solution)/shard_map/ppermute | solution.py:343
  137.4 64.7 %collective-permute-start.37 = (bf16[4,128,512]{2,1,0:T(8,128)(2,1)}, bf16[4,128,512]{2,1,0:T(8,128)(2,1)}, u32[]{:S(2)}, u32[]{:S(2)}) collective-permute-start(bf16[4,128,512]{2,1,0:T(8,128)(2,1)} %get-tuple-element.163), channel_id=1, source_target_pairs={{0,16},{1,17},{2,18},{3,19},{4,20},{5,21},{6,22},{7,23},{8,24},{9,... | collective-permute-start | bytes 1572872 | tf_op jit(solution)/shard_map/ppermute | solution.py:343
  146.1 37.3 %collective-permute-start.10 = (bf16[4,64,768]{2,1,0:T(8,128)(2,1)S(1)}, bf16[4,64,768]{2,1,0:T(8,128)(2,1)S(1)}, u32[]{:S(2)}, u32[]{:S(2)}) collective-permute-start(bf16[4,64,768]{2,1,0:T(8,128)(2,1)S(1)} %collective-permute-done.8), channel_id=1, source_target_pairs={{0,16},{1,17},{2,18},{3,19},{4,20},{5,21},{6,22},{7,23},{8,24},{9,... | collective-permute-start | bytes 1179656 | tf_op jit(solution)/shard_map/ppermute | solution.py:343
  147.3 50.1 %collective-permute-start.35 = (bf16[4,128,512]{2,1,0:T(8,128)(2,1)}, bf16[4,128,512]{2,1,0:T(8,128)(2,1)}, u32[]{:S(2)}, u32[]{:S(2)}) collective-permute-start(bf16[4,128,512]{2,1,0:T(8,128)(2,1)} %collective-permute-done.33), channel_id=1, source_target_pairs={{0,2},{1,3},{2,0},{3,1},{4,6},{5,7},{6,4},{7,5},{8,10},{9,11},{10,... | collective-permute-start | bytes 1572872 | tf_op jit(solution)/shard_map/ppermute | solution.py:343
  149.1 55.4 %collective-permute-start.38 = (bf16[4,128,512]{2,1,0:T(8,128)(2,1)}, bf16[4,128,512]{2,1,0:T(8,128)(2,1)}, u32[]{:S(2)}, u32[]{:S(2)}) collective-permute-start(bf16[4,128,512]{2,1,0:T(8,128)(2,1)} %collective-permute-done.36), channel_id=1, source_target_pairs={{0,16},{1,17},{2,18},{3,19},{4,20},{5,21},{6,22},{7,23},{8,24},{9,... | collective-permute-start | bytes 1572872 | tf_op jit(solution)/shard_map/ppermute | solution.py:343
  183.4 34.8 %collective-permute-start.29 = (bf16[2,4,64,2048]{3,2,0,1:T(8,128)(2,1)}, bf16[2,4,64,2048]{3,2,0,1:T(8,128)(2,1)}, u32[]{:S(2)}, u32[]{:S(2)}) collective-permute-start(bf16[2,4,64,2048]{3,2,0,1:T(8,128)(2,1)} %get-tuple-element.147), channel_id=1, source_target_pairs={{0,2},{1,3},{2,0},{3,1},{4,6},{5,7},{6,4},{7,5},{8,10},{9,11},{10,... | collective-permute-start | bytes 6291464 | tf_op jit(solution)/shard_map/ppermute | solution.py:343
  197.4 56.1 %collective-permute-start.22 = (bf16[1024,1536]{1,0:T(8,128)(2,1)}, bf16[1024,1536]{1,0:T(8,128)(2,1)}, u32[]{:S(2)}, u32[]{:S(2)}) collective-permute-start(bf16[1024,1536]{1,0:T(8,128)(2,1)} %slice.134), channel_id=1, source_target_pairs={{0,1},{1,0},{2,3},{3,2},{4,5},{5,4},{6,7},{7,6},{8,9},{9,8},{10,11... | collective-permute-start | bytes 9437192 | tf_op jit(solution)/shard_map/ppermute | solution.py:343
  202.1 48.2 %collective-permute-start.21 = (bf16[1024,512]{1,0:T(8,128)(2,1)}, bf16[1024,512]{1,0:T(8,128)(2,1)}, u32[]{:S(2)}, u32[]{:S(2)}) collective-permute-start(bf16[1024,512]{1,0:T(8,128)(2,1)} %bitcast.50), channel_id=1, source_target_pairs={{0,1},{1,0},{2,3},{3,2},{4,5},{5,4},{6,7},{7,6},{8,9},{9,8},{10,11... | collective-permute-start | bytes 3145736 | tf_op jit(solution)/shard_map/ppermute | solution.py:343
  206.4 76.2 %collective-permute-start.40 = (bf16[2048,1024]{1,0:T(8,128)(2,1)}, bf16[2048,1024]{1,0:T(8,128)(2,1)}, u32[]{:S(2)}, u32[]{:S(2)}) collective-permute-start(bf16[2048,1024]{1,0:T(8,128)(2,1)} %bitcast.88.ws_ref), channel_id=1, source_target_pairs={{0,1},{1,0},{2,3},{3,2},{4,5},{5,4},{6,7},{7,6},{8,9},{9,8},{10,11... | collective-permute-start | bytes 12582920 | tf_op jit(solution)/shard_map/ppermute | solution.py:343
  221.4 61.2 %collective-permute-start.39 = (bf16[1024,2048]{1,0:T(8,128)(2,1)}, bf16[1024,2048]{1,0:T(8,128)(2,1)}, u32[]{:S(2)}, u32[]{:S(2)}) collective-permute-start(bf16[1024,2048]{1,0:T(8,128)(2,1)} %bitcast.67.we_ref), channel_id=1, source_target_pairs={{0,1},{1,0},{2,3},{3,2},{4,5},{5,4},{6,7},{7,6},{8,9},{9,8},{10,11... | collective-permute-start | bytes 12582920 | tf_op jit(solution)/shard_map/ppermute | solution.py:343
  383.6 67.2 %collective-permute-start.48 = (bf16[1024,2048]{1,0:T(8,128)(2,1)}, bf16[1024,2048]{1,0:T(8,128)(2,1)}, u32[]{:S(2)}, u32[]{:S(2)}) collective-permute-start(bf16[1024,2048]{1,0:T(8,128)(2,1)} %get-tuple-element.67), channel_id=1, source_target_pairs={{0,1},{1,0},{2,3},{3,2},{4,5},{5,4},{6,7},{7,6},{8,9},{9,8},{10,11... | collective-permute-start | bytes 12582920 | tf_op jit(solution)/shard_map/ppermute | solution.py:343
  383.6 61.7 %collective-permute-start.43 = (bf16[2048,1024]{1,0:T(8,128)(2,1)}, bf16[2048,1024]{1,0:T(8,128)(2,1)}, u32[]{:S(2)}, u32[]{:S(2)}) collective-permute-start(bf16[2048,1024]{1,0:T(8,128)(2,1)} %get-tuple-element.65), channel_id=1, source_target_pairs={{0,1},{1,0},{2,3},{3,2},{4,5},{5,4},{6,7},{7,6},{8,9},{9,8},{10,11... | collective-permute-start | bytes 12582920 | tf_op jit(solution)/shard_map/ppermute | solution.py:343
  385.9 30.6 %collective-permute-start.41 = (bf16[512,1024]{1,0:T(8,128)(2,1)S(1)}, bf16[512,1024]{1,0:T(8,128)(2,1)}, u32[]{:S(2)}, u32[]{:S(2)}) collective-permute-start(bf16[512,1024]{1,0:T(8,128)(2,1)S(1)} %get-tuple-element.146), channel_id=1, source_target_pairs={{0,16},{1,17},{2,18},{3,19},{4,20},{5,21},{6,22},{7,23},{8,24},{9,... | collective-permute-start | bytes 3145736 | tf_op jit(solution)/shard_map/ppermute | solution.py:343
  391.7 41.7 %collective-permute-start.47 = (bf16[4,2,64,256]{3,2,1,0:T(8,128)(2,1)}, bf16[4,2,64,256]{3,2,1,0:T(8,128)(2,1)}, u32[]{:S(2)}, u32[]{:S(2)}) collective-permute-start(bf16[4,2,64,256]{3,2,1,0:T(8,128)(2,1)} %dynamic-slice_bitcast_fusion.23), channel_id=1, source_target_pairs={{0,16},{1,17},{2,18},{3,19},{4,20},{5,21},{6,22},{7,23},{8,24},{9,... | collective-permute-start | bytes 786440 | tf_op jit(solution)/shard_map/ppermute | solution.py:343
  393.3 42.0 %collective-permute-start.46 = (bf16[2,4,64,256]{3,2,1,0:T(8,128)(2,1)S(1)}, bf16[2,4,64,256]{3,2,1,0:T(8,128)(2,1)}, u32[]{:S(2)}, u32[]{:S(2)}) collective-permute-start(bf16[2,4,64,256]{3,2,1,0:T(8,128)(2,1)S(1)} %dynamic-slice_bitcast_fusion.24), channel_id=1, source_target_pairs={{0,2},{1,3},{2,0},{3,1},{4,6},{5,7},{6,4},{7,5},{8,10},{9,11},{10,... | collective-permute-start | bytes 786440 | tf_op jit(solution)/shard_map/ppermute | solution.py:343
  456.5 158.2 %collective-permute-start.50 = (bf16[1024,1536]{1,0:T(8,128)(2,1)}, bf16[1024,1536]{1,0:T(8,128)(2,1)}, u32[]{:S(2)}, u32[]{:S(2)}) collective-permute-start(bf16[1024,1536]{1,0:T(8,128)(2,1)} %convolution_convert_fusion.1), channel_id=1, source_target_pairs={{0,1},{1,0},{2,3},{3,2},{4,5},{5,4},{6,7},{7,6},{8,9},{9,8},{10,11... | collective-permute-start | bytes 9437192 | tf_op jit(solution)/shard_map/ppermute | solution.py:343
  456.6 78.3 %collective-permute-start.49 = (bf16[2,4,64,2048]{3,2,1,0:T(8,128)(2,1)S(1)}, bf16[2,4,64,2048]{3,2,1,0:T(8,128)(2,1)S(1)}, u32[]{:S(2)}, u32[]{:S(2)}) collective-permute-start(bf16[2,4,64,2048]{3,2,1,0:T(8,128)(2,1)S(1)} %dynamic-slice_bitcast_fusion), channel_id=1, source_target_pairs={{0,2},{1,3},{2,0},{3,1},{4,6},{5,7},{6,4},{7,5},{8,10},{9,11},{10,... | collective-permute-start | bytes 6291464 | tf_op jit(solution)/shard_map/ppermute | solution.py:343
  473.2 56.1 %collective-permute-start.52 = (bf16[4,128,512]{2,1,0:T(8,128)(2,1)S(1)}, bf16[4,128,512]{2,1,0:T(8,128)(2,1)S(1)}, u32[]{:S(2)}, u32[]{:S(2)}) collective-permute-start(bf16[4,128,512]{2,1,0:T(8,128)(2,1)S(1)} %dynamic-slice_bitcast_fusion.13), channel_id=1, source_target_pairs={{0,2},{1,3},{2,0},{3,1},{4,6},{5,7},{6,4},{7,5},{8,10},{9,11},{10,... | collective-permute-start | bytes 1572872 | tf_op jit(solution)/shard_map/ppermute | solution.py:343
  477.3 52.1 %collective-permute-start.51 = (bf16[4,128,512]{2,1,0:T(8,128)(2,1)S(1)}, bf16[4,128,512]{2,1,0:T(8,128)(2,1)S(1)}, u32[]{:S(2)}, u32[]{:S(2)}) collective-permute-start(bf16[4,128,512]{2,1,0:T(8,128)(2,1)S(1)} %dynamic-slice_bitcast_fusion.14), channel_id=1, source_target_pairs={{0,16},{1,17},{2,18},{3,19},{4,20},{5,21},{6,22},{7,23},{8,24},{9,... | collective-permute-start | bytes 1572872 | tf_op jit(solution)/shard_map/ppermute | solution.py:343
  530.3 35.2 %collective-permute-start.74 = (bf16[128,1024]{1,0:T(8,128)(2,1)S(1)}, bf16[128,1024]{1,0:T(8,128)(2,1)S(1)}, u32[]{:S(2)}, u32[]{:S(2)}) collective-permute-start(bf16[128,1024]{1,0:T(8,128)(2,1)S(1)} %get-tuple-element.159), channel_id=1, source_target_pairs={{0,8},{1,9},{2,10},{3,11},{4,12},{5,13},{6,14},{7,15},{8,0},{9,1},... | collective-permute-start | bytes 786440 | tf_op jit(solution)/shard_map/ppermute | solution.py:343
  531.6 34.7 %collective-permute-start.75 = (bf16[128,1024]{1,0:T(8,128)(2,1)S(1)}, bf16[128,1024]{1,0:T(8,128)(2,1)S(1)}, u32[]{:S(2)}, u32[]{:S(2)}) collective-permute-start(bf16[128,1024]{1,0:T(8,128)(2,1)S(1)} %get-tuple-element.160), channel_id=1, source_target_pairs={{0,12},{1,13},{2,14},{3,15},{4,0},{5,1},{6,2},{7,3},{8,4},{9,5},{1... | collective-permute-start | bytes 786440 | tf_op jit(solution)/shard_map/ppermute | solution.py:343
  535.8 32.1 %collective-permute-start.53 = (bf16[2,64,2048]{2,1,0:T(8,128)(2,1)S(1)}, bf16[2,64,2048]{2,1,0:T(8,128)(2,1)S(1)}, u32[]{:S(2)}, u32[]{:S(2)}) collective-permute-start(bf16[2,64,2048]{2,1,0:T(8,128)(2,1)S(1)} %get-tuple-element.142), channel_id=1, source_target_pairs={{0,4},{1,5},{2,6},{3,7},{4,8},{5,9},{6,10},{7,11},{8,12},{9,13},{1... | collective-permute-start | bytes 1572872 | tf_op jit(solution)/shard_map/ppermute | solution.py:343
  540.8 46.0 %collective-permute-start.54 = (bf16[2,64,2048]{2,1,0:T(8,128)(2,1)S(1)}, bf16[2,64,2048]{2,1,0:T(8,128)(2,1)S(1)}, u32[]{:S(2)}, u32[]{:S(2)}) collective-permute-start(bf16[2,64,2048]{2,1,0:T(8,128)(2,1)S(1)} %get-tuple-element.144), channel_id=1, source_target_pairs={{0,8},{1,9},{2,10},{3,11},{4,12},{5,13},{6,14},{7,15},{8,0},{9,1},... | collective-permute-start | bytes 1572872 | tf_op jit(solution)/shard_map/ppermute | solution.py:343
  587.2 30.7 %collective-permute-start.71 = (bf16[64,2048]{1,0:T(8,128)(2,1)S(1)}, bf16[64,2048]{1,0:T(8,128)(2,1)S(1)}, u32[]{:S(2)}, u32[]{:S(2)}) collective-permute-start(bf16[64,2048]{1,0:T(8,128)(2,1)S(1)} %dynamic-slice_bitcast_fusion.21), channel_id=1, source_target_pairs={{0,16},{1,17},{2,18},{3,19},{4,20},{5,21},{6,22},{7,23},{8,24},{9,... | collective-permute-start | bytes 786440 | tf_op jit(solution)/shard_map/ppermute | solution.py:343
  622.0 27.8 %collective-permute-start.61 = (bf16[4,2,64,768]{3,2,0,1:T(8,128)(2,1)}, bf16[4,2,64,768]{3,2,0,1:T(8,128)(2,1)}, u32[]{:S(2)}, u32[]{:S(2)}) collective-permute-start(bf16[4,2,64,768]{3,2,0,1:T(8,128)(2,1)} %bitcast.380), channel_id=1, source_target_pairs={{0,16},{1,17},{2,18},{3,19},{4,20},{5,21},{6,22},{7,23},{8,24},{9,... | collective-permute-start | bytes 2359304 | tf_op jit(solution)/shard_map/ppermute | solution.py:343
  (116 other events, 1844.9 us)

commit v2 on v1

v2 whole, which is shorter than its diff:
```python
import functools

import jax
import jax.numpy as jnp
from jax import lax
from jax.experimental import pallas as pl
from jax.experimental.pallas import tpu as pltpu
from jax.sharding import PartitionSpec as P

H = 16
HD = 64
BLK = 256
STEP = 10
PAIR = 2 * HD

norm_eps = 1e-05
adam_eps = 1e-08
group_heads = 4
score_scale = 0.125 * 1.4426950408889634
gelu_root = 0.7978845608028654
gelu_cubic = 0.044715
low = jnp.bfloat16
axes = ("ctx", "wshard")
small_cost = pl.CostEstimate(flops=1024, bytes_accessed=1024, transcendentals=0)


def nt(a,b):
    return lax.dot_general(a,b,(((1,),(1,)),((),())),preferred_element_type=jnp.float32)
def nn(a,b):
    return jnp.dot(a,b,preferred_element_type=jnp.float32)

def arrange_kernel(place_ref, rows_ref, out_ref):
    out_ref[...] = rows_ref[...]


def arrange(place, rows):
    columns = rows.shape[1]
    return pl.pallas_call(
        arrange_kernel,
        grid_spec=pltpu.PrefetchScalarGridSpec(
            num_scalar_prefetch=1,
            grid=(place.shape[0],),
            in_specs=[pl.BlockSpec((BLK, columns), lambda i, place: (place[i], 0))],
            out_specs=pl.BlockSpec((BLK, columns), lambda i, place: (i, 0)),
        ),
        out_shape=jax.ShapeDtypeStruct(rows.shape, rows.dtype),
        cost_estimate=small_cost,
        name="arrange",
    )(place, rows)


def block_rows(block):
    return pl.ds(block * BLK, BLK)


def thirds(ref):
    return [ref.at[:, pl.ds(part * PAIR, PAIR)] for part in range(3)]


def attend_pair(blocks, projected, o_ref, lse_ref, between):
    q_ref, k_ref, v_ref = thirds(projected)
    lane = lax.broadcasted_iota(jnp.int32, (1, PAIR), 1)
    masks = [lane < HD, lane >= HD]
    for i in range(blocks):
        between(i)
        rows = block_rows(i)
        queries = q_ref[rows, :]
        outs = []
        for h in range(2):
            masked = jnp.where(masks[h], queries, jnp.zeros_like(queries))
            scores = [nt(masked, k_ref[block_rows(j), :]) * score_scale for j in range(i + 1)]
            top = scores[0]
            for score in scores[1:]:
                top = jnp.maximum(top, score)
            top = jnp.max(top, axis=1, keepdims=True)
            weights = [jnp.exp2(score - top) for score in scores]
            total = weights[0]
            for weight in weights[1:]:
                total = total + weight
            total = jnp.sum(total, axis=1, keepdims=True)
            mixed = nn(weights[0].astype(low), v_ref[block_rows(0), :])
            for j in range(1, i + 1):
                mixed = mixed + nn(weights[j].astype(low), v_ref[block_rows(j), :])
            outs.append(mixed * (1.0 / total))
            logsum = jnp.broadcast_to(top + jnp.log2(total), (BLK, PAIR))
            lse_ref[h : h + 1, rows] = jnp.transpose(logsum)[0:1, :]
        o_ref[rows, :] = jnp.where(masks[0], outs[0], outs[1]).astype(o_ref.dtype)


def attend_back_pair(
    blocks, projected, do_ref, lse_ref, back_ref, turned, key_sum, value_sum, between
):
    q_ref, k_ref, v_ref = thirds(projected)
    dq_ref, dk_ref, dv_ref = thirds(back_ref)
    lane = lax.broadcasted_iota(jnp.int32, (1, PAIR), 1)
    masks = [lane < HD, lane >= HD]
    for j in range(blocks):
        turned[j] = jnp.transpose(k_ref[block_rows(j), :])
    for i in range(blocks):
        between(i)
        rows = block_rows(i)
        queries, upstream = q_ref[rows, :], do_ref[rows, :]
        query_grads = []
        for h in range(2):
            masked = jnp.where(masks[h], queries, jnp.zeros_like(queries))
            pulled = jnp.where(masks[h], upstream, jnp.zeros_like(upstream))
            logsum = lse_ref[h : h + 1, rows]
            weights, pulls, inner = [], [], None
            for j in range(i + 1):
                weight = jnp.exp2(nt(k_ref[block_rows(j), :], masked) * score_scale - logsum)
                pull = nt(v_ref[block_rows(j), :], pulled)
                along = jnp.sum(weight * pull, axis=0, keepdims=True)
                inner = along if inner is None else inner + along
                weights.append(weight)
                pulls.append(pull)
            query_grad = None
            for j in range(i + 1):
                score_grad = (weights[j] * (pulls[j] - inner)).astype(low)
                value_grad = nn(weights[j].astype(low), pulled)
                key_grad = nn(score_grad, masked)
                if i == j and h == 0:
                    value_sum[j] = value_grad
                    key_sum[j] = key_grad
                else:
                    value_sum[j] += value_grad
                    key_sum[j] += key_grad
                piece = nn(turned[j, h * HD : (h + 1) * HD, :], score_grad)
                query_grad = piece if query_grad is None else query_grad + piece
            query_grads.append(query_grad)
        joined = jnp.transpose(jnp.concatenate(query_grads, axis=0))
        dq_ref[rows, :] = (joined * 0.125).astype(dq_ref.dtype)
    for j in range(blocks):
        dk_ref[block_rows(j), :] = (key_sum[j] * 0.125).astype(dk_ref.dtype)
        dv_ref[block_rows(j), :] = value_sum[j].astype(dv_ref.dtype)


def hooks(step, schedule):
    def between(block):
        for when, where, action in schedule:
            if where == block:
                pl.when(step == when)(action)

    return between


any_place = pl.BlockSpec(memory_space=pl.ANY)
whole_vmem = pl.BlockSpec(memory_space=pltpu.VMEM)


def mlp_kernel(first, rows_step, c_ref, dy_ref, we_ref, ws_ref, be_ref, *rest):
    if first:
        y_ref, dc_ref, gwe_ref, gws_ref, gbe_ref, ct, act_all, du_all = rest
    else:
        y_in, dc_in, y_ref, dc_ref, gwe_ref, gws_ref, gbe_ref, ct, act_all, du_all, sem = rest
    step=pl.program_id(0)
    tokens=c_ref.shape[0]
    @pl.when(step==0)
    def _():
        ct[...]=jnp.transpose(c_ref[...])
        if first:
            y_ref[...]=jnp.zeros_like(y_ref)
            dc_ref[...]=jnp.zeros_like(dc_ref)
        else:
            a=pltpu.make_async_copy(y_in,y_ref,sem.at[0]); b=pltpu.make_async_copy(dc_in,dc_ref,sem.at[1])
            a.start(); b.start(); a.wait(); b.wait()
    we=we_ref[...]; ws=ws_ref[...]
    total=None
    for r in range(tokens//rows_step):
        rows=pl.ds(r*rows_step,rows_step)
        u=nn(c_ref[rows,:],we)+be_ref[...]
        t2=u*u
        th=jnp.tanh(gelu_root*u*(1.0+gelu_cubic*t2))
        half=0.5+0.5*th
        act=(u*half).astype(jnp.bfloat16)
        slope=half+(0.5*gelu_root)*u*(1.0-th*th)*(1.0+(3*gelu_cubic)*t2)
        du=(nt(dy_ref[rows,:],ws)*slope).astype(jnp.bfloat16)
        act_all[rows,:]=act; du_all[rows,:]=du
        y_ref[rows,:]+=nn(act,ws)
        dc_ref[rows,:]+=nt(du,we)
        s=jnp.sum(du.astype(jnp.float32),axis=0,keepdims=True)
        total=s if total is None else total+s
    gbe_ref[...]=total
    gwe_ref[...]=nn(ct[...],du_all[...]).astype(gwe_ref.dtype)
    gws_ref[...]=lax.dot_general(act_all[...],dy_ref[...],(((0,),(0,)),((),())),preferred_element_type=jnp.float32).astype(gws_ref.dtype)

def mlp(c,dy,we,ws,be,before=None,tile=256,rows_step=256):
    tokens,width=c.shape
    hidden=we.shape[1]
    whole=pl.BlockSpec((tokens,width),lambda t:(0,0))
    specs=[whole,whole,pl.BlockSpec((width,tile),lambda t:(0,t)),pl.BlockSpec((tile,width),lambda t:(t,0)),pl.BlockSpec((1,tile),lambda t:(0,t))]
    args=[c,dy,we,ws,be]
    scratch=[pltpu.VMEM((width,tokens),jnp.bfloat16),pltpu.VMEM((tokens,tile),jnp.bfloat16),pltpu.VMEM((tokens,tile),jnp.bfloat16)]
    if before is not None:
        specs+=[pl.BlockSpec(memory_space=pl.ANY)]*2
        args+=list(before)
        scratch+=[pltpu.SemaphoreType.DMA((2,))]
    return pl.pallas_call(
        functools.partial(mlp_kernel,before is None,rows_step),
        grid=(hidden//tile,),
        in_specs=specs,
        out_specs=[whole,whole,pl.BlockSpec((width,tile),lambda t:(0,t)),pl.BlockSpec((tile,width),lambda t:(t,0)),pl.BlockSpec((1,tile),lambda t:(0,t))],
        out_shape=[jax.ShapeDtypeStruct((tokens,width),jnp.float32)]*2+[jax.ShapeDtypeStruct((width,hidden),jnp.bfloat16),jax.ShapeDtypeStruct((hidden,width),jnp.bfloat16),jax.ShapeDtypeStruct((1,hidden),jnp.float32)],
        scratch_shapes=scratch,
        compiler_params=pltpu.CompilerParams(vmem_limit_bytes=56<<20),
        cost_estimate=small_cost,
        name="mlp",
    )(*args)


MESH = pl.DeviceIdType.MESH


class Spot:
    def __init__(self, sizes):
        self.sizes = sizes
        ctx, shard = lax.axis_index("ctx"), lax.axis_index("wshard")
        self.c = ctx
        self.k = shard % 2
        self.y = (shard // 2) % 2
        self.z = shard // 4

    def device(self, name, by=1):
        c, z, y, k = self.c, self.z, self.y, self.k
        if name == "c":
            c = 1 - c
        if name == "y":
            y = 1 - y
        if name == "k":
            k = 1 - k
        if name == "z":
            z = (z + by) % self.sizes["z"]
        return (c, (z * 2 + y) * 2 + k)

    def meet(self, names):
        barrier = pltpu.get_barrier_semaphore()
        partners = []
        for name in names:
            for by in range(1, self.sizes[name]):
                partners.append(self.device(name, by))
        for partner in partners:
            pl.semaphore_signal(barrier, inc=1, device_id=partner, device_id_type=MESH)
        pl.semaphore_wait(barrier, len(partners))


class Mover:
    def __init__(self, spot, sems):
        self.spot, self.sems, self.count = spot, sems, 0

    def copy(self, source, target, name, by=1):
        number = self.count
        self.count += 1
        return pltpu.make_async_remote_copy(
            src_ref=source,
            dst_ref=target,
            send_sem=self.sems.at[0, number],
            recv_sem=self.sems.at[1, number],
            device_id=self.spot.device(name, by),
            device_id_type=MESH,
        )

    def local(self, source, target):
        number = self.count
        self.count += 1
        return pltpu.make_async_copy(source, target, self.sems.at[0, number])


def start(copies):
    for copy in copies:
        copy.start()


def wait(copies):
    for copy in copies:
        copy.wait()


def span(first, size):
    return pl.ds(pl.multiple_of(first, 128), size)


class GatherJob:
    def __init__(self, mover, half, offset, width, cut, core=True):
        spot = mover.spot
        c, z, y = spot.c, spot.z, spot.y

        def part(ci, zi, yi, first, size):
            return half.at[ci, zi, yi, :, span(offset + first, size)]

        every = slice(None)
        self.along_z = []
        for by in range(1, spot.sizes["z"]):
            block = part(c, z, y, 0, width)
            self.along_z.append(mover.copy(block, block, "z", by))
        self.near, self.far = [], []
        for first, size, one, two in ((0, cut, "c", "y"), (cut, width - cut, "y", "c")):
            if size == 0:
                continue
            block = part(c, every, y, first, size)
            self.near.append(mover.copy(block, block, one))
            self.near.append(mover.copy(block, block, two))
            block = part(1 - c if one == "c" else c, every, 1 - y if one == "y" else y, first, size)
            self.far.append(mover.copy(block, block, two))
        self.core = [[], [], []]
        if core:
            for stage, ci, yi in ((0, c, y), (1, 1 - c, y), (1, c, 1 - y), (2, 1 - c, 1 - y)):
                block = part(ci, every, yi, 0, width)
                self.core[stage].append(mover.copy(block, block, "k"))


def first_rows(mover, halves, out, width):
    spot = mover.spot
    rows = halves.shape[1]
    block = out.at[spot.c, spot.z, spot.y, pl.ds(pl.multiple_of(spot.k * rows, rows), rows)]
    return [
        mover.local(halves.at[spot.k], block.at[:, span(spot.k * width, width)]),
        mover.copy(halves.at[1 - spot.k], block.at[:, span((1 - spot.k) * width, width)], "k"),
    ]


class ReduceJob:
    def __init__(self, mover, mine, theirs, cut, scratch):
        self.spot = spot = mover.spot
        self.cut = cut
        (self.total, self.other, self.by_y, self.by_c, self.then_c, self.then_y, self.by_z) = scratch
        self.width = width = self.total.shape[-1]
        c, z, y = spot.c, spot.z, spot.y
        depth = spot.sizes["z"]
        every, left, right = slice(None), pl.ds(0, cut), pl.ds(cut, width - cut)
        total = self.total
        self.first = [mover.local(mine, total), mover.copy(theirs, self.other, "k")]
        self.near = [
            mover.copy(total.at[every, every, 1 - y, every, left], self.by_y, "y"),
            mover.copy(total.at[1 - c, every, every, every, right], self.by_c, "c"),
        ]
        self.far = [
            mover.copy(total.at[1 - c, every, y, every, left], self.then_c, "c"),
            mover.copy(total.at[c, every, 1 - y, every, right], self.then_y, "y"),
        ]
        self.along_z = [
            mover.copy(total.at[c, (z + by) % depth, y], self.by_z.at[by - 1], "z", by)
            for by in range(1, depth)
        ]

    @staticmethod
    def scratch(sizes, rows, width, cut):
        c, z, y = sizes["c"], sizes["z"], sizes["y"]
        shapes = [
            (c, z, y, rows, width),
            (c, z, y, rows, width),
            (c, z, rows, cut),
            (z, y, rows, width - cut),
            (z, rows, cut),
            (z, rows, width - cut),
            (z - 1, rows, width),
        ]
        return [pltpu.VMEM(shape, low) for shape in shapes]

    def add(self, where, extra):
        self.total[where] = (
            self.total[where].astype(jnp.float32) + extra.astype(jnp.float32)
        ).astype(low)

    def add_first(self):
        sizes = self.spot.sizes
        for c in range(sizes["c"]):
            for y in range(sizes["y"]):

                @pl.loop(0, sizes["z"])
                def _(z):
                    self.add((c, z, y), self.other[c, z, y])

    def add_near(self):
        spot, cut = self.spot, self.cut
        left, right = pl.ds(0, cut), pl.ds(cut, self.width - cut)

        @pl.loop(0, spot.sizes["z"])
        def _(z):
            for c in range(spot.sizes["c"]):
                self.add((c, z, spot.y, slice(None), left), self.by_y[c, z])
            for y in range(spot.sizes["y"]):
                self.add((spot.c, z, y, slice(None), right), self.by_c[z, y])

    def add_far(self):
        spot, cut = self.spot, self.cut
        left, right = pl.ds(0, cut), pl.ds(cut, self.width - cut)

        @pl.loop(0, spot.sizes["z"])
        def _(z):
            self.add((spot.c, z, spot.y, slice(None), left), self.then_c[z])
            self.add((spot.c, z, spot.y, slice(None), right), self.then_y[z])

    def result(self):
        spot = self.spot
        value = self.total[spot.c, spot.z, spot.y].astype(jnp.float32)
        for by in range(spot.sizes["z"] - 1):
            value = value + self.by_z[by].astype(jnp.float32)
        return value


def begin_kernel(sizes, *refs):
    (
        joint_halves, table, mixing_halves, expand_a, expand_b, shrink_a, shrink_b,
        joint, tables, mixing, grown_a, grown_b, shrunk_a, shrunk_b, sems,
    ) = refs
    spot = Spot(sizes)
    mover = Mover(spot, sems)
    c, z, y, k = spot.c, spot.z, spot.y, spot.k
    width, half = joint_halves.shape[2], mixing_halves.shape[2]
    rows = table.shape[0]
    joint_first = first_rows(mover, joint_halves, joint, width)
    spread = tables.at[c, z, y, pl.ds(pl.multiple_of(k * rows, rows), rows)]
    joint_first += [mover.local(table, spread), mover.copy(table, spread, "k")]
    later_first = first_rows(mover, mixing_halves, mixing, half)
    later_first += first_rows(mover, expand_a, grown_a, expand_a.shape[2])
    later_first += first_rows(mover, expand_b, grown_b, expand_b.shape[2])
    later_first += [
        mover.local(shrink_a, shrunk_a.at[k, c, z, y]),
        mover.local(shrink_b, shrunk_b.at[k, c, z, y]),
    ]
    job = GatherJob(mover, joint, k * width, width, width // 2)
    thin = GatherJob(mover, tables, 0, tables.shape[-1], tables.shape[-1], core=False)
    later = later_jobs(mover, mixing, grown_a, grown_b, shrunk_a, shrunk_b)[:3]
    spot.meet(("k", "c", "y", "z"))
    start(joint_first + later_first)
    wait(joint_first)
    start(thin.along_z + job.along_z)
    wait(later_first)
    wait(thin.along_z + job.along_z)
    start(thin.near + job.near + job.core[0])
    for each in later:
        start(each.along_z)
    wait(thin.near + job.near)
    start(thin.far + job.far + job.core[1])
    wait(thin.far + job.far)
    start(job.core[2])
    for each in later:
        wait(each.along_z)
    wait(job.core[0] + job.core[1] + job.core[2])


def later_jobs(mover, mixing, grown_a, grown_b, shrunk_a, shrunk_b):
    k = mover.spot.k
    half, grown, width = mixing.shape[-1] // 2, grown_a.shape[-1] // 2, shrunk_a.shape[-1]
    return [
        GatherJob(mover, mixing, k * half, half, half // 2),
        GatherJob(mover, shrunk_a.at[k], 0, width, width // 2),
        GatherJob(mover, grown_a, k * grown, grown, grown // 2),
        GatherJob(mover, shrunk_b.at[k], 0, width, width // 2),
        GatherJob(mover, grown_b, k * grown, grown, grown // 2),
    ]


def later_shapes(sizes, pieces):
    joint_halves, table, mixing_halves, expand_a, expand_b, shrink_a, shrink_b = pieces
    lead = (sizes["c"], sizes["z"], sizes["y"])
    rows = 2 * table.shape[0]

    def shape(*dims):
        return jax.ShapeDtypeStruct(dims, low)

    grown, shrunk = (*lead, rows, 2 * expand_a.shape[2]), (2, *lead, *shrink_a.shape)
    return [
        shape(*lead, rows, 2 * joint_halves.shape[2]),
        shape(*lead, rows, table.shape[1]),
        shape(*lead, rows, 2 * mixing_halves.shape[2]),
        shape(*grown),
        shape(*grown),
        shape(*shrunk),
        shape(*shrunk),
    ]


def begin(sizes, pieces):
    return pl.pallas_call(
        functools.partial(begin_kernel, sizes),
        in_specs=[whole_vmem] * 7,
        out_specs=[any_place] * 7,
        out_shape=later_shapes(sizes, pieces),
        scratch_shapes=[pltpu.SemaphoreType.DMA((2, 96))],
        compiler_params=pltpu.CompilerParams(
            collective_id=1, has_side_effects=True, vmem_limit_bytes=16 << 20
        ),
        cost_estimate=small_cost,
        name="begin",
    )(*pieces)


def attend_kernel(sizes, blocks, *refs):
    projected, o_ref, lse_ref = refs[0], refs[6], refs[7]
    outs, sems = refs[8:13], refs[13]
    spot = Spot(sizes)
    mover = Mover(spot, sems)
    mixing, shrink_a, expand_a, shrink_b, expand_b = later_jobs(mover, *outs)
    soon, then = [mixing, shrink_a, expand_a], [shrink_b, expand_b]

    def open_all():
        spot.meet(("k", "c", "y", "z"))
        for job in soon:
            start(job.near + job.core[0])
        for job in then:
            start(job.along_z)

    def soon_far():
        for job in soon:
            wait(job.near)
            start(job.far + job.core[1])

    def then_near():
        for job in then:
            wait(job.along_z)
            start(job.near + job.core[0])

    def soon_core():
        for job in soon:
            wait(job.far)
            start(job.core[2])

    def close_all():
        for job in then:
            wait(job.near)
            start(job.far + job.core[1])
        for job in then:
            wait(job.far)
            start(job.core[2])
        for job in soon + then:
            for stage in job.core:
                wait(stage)

    step = pl.program_id(0)
    schedule = [(0, 0, open_all), (5, 0, then_near), (6, 0, soon_far), (7, 3, soon_core)]
    attend_pair(blocks, projected, o_ref, lse_ref, hooks(step, schedule))
    pl.when(step == pl.num_programs(0) - 1)(close_all)


def attend(sizes, blocks, projected, outs):
    tokens, width = projected.shape[0], projected.shape[1] // 3
    pairs = width // PAIR
    return pl.pallas_call(
        functools.partial(attend_kernel, sizes, blocks),
        grid=(pairs,),
        in_specs=[pl.BlockSpec((tokens, 3 * PAIR), lambda g: (0, g))] + [any_place] * 5,
        out_specs=[
            pl.BlockSpec((tokens, PAIR), lambda g: (0, g)),
            pl.BlockSpec((None, 8, tokens), lambda g: (g, 0, 0)),
        ]
        + [any_place] * 5,
        out_shape=[
            jax.ShapeDtypeStruct((tokens, width), low),
            jax.ShapeDtypeStruct((pairs, 8, tokens), jnp.float32),
        ]
        + [jax.ShapeDtypeStruct(out.shape, out.dtype) for out in outs],
        input_output_aliases={1 + number: 2 + number for number in range(5)},
        scratch_shapes=[pltpu.SemaphoreType.DMA((2, 80))],
        compiler_params=pltpu.CompilerParams(
            collective_id=2, has_side_effects=True, vmem_limit_bytes=48 << 20
        ),
        cost_estimate=small_cost,
        name="attend",
    )(projected, *outs)


def core_halves(grad, k, width, first=0, size=None):
    size = width if size is None else size
    every = slice(None)
    return [
        grad.at[every, every, every, every, span(half * width + first, size)]
        for half in (k, 1 - k)
    ]


class Finish:
    def __init__(self, mover, summed, arrived):
        self.k = mover.spot.k
        self.summed, self.arrived = summed, arrived
        rows = arrived.shape[0]
        self.rows = rows
        away = summed.at[pl.ds(pl.multiple_of((1 - self.k) * rows, rows), rows)]
        self.copies = [mover.copy(away, arrived, "k")]

    def write(self, out, columns=slice(None)):
        rows = self.rows
        kept = pl.ds(pl.multiple_of(self.k * rows, rows), rows)
        out[self.k, :, columns] = self.summed[kept, :]
        out[1 - self.k, :, columns] = self.arrived[...]


def attend_back_kernel(sizes, blocks, *refs):
    projected, upstream, lse_ref = refs[:3]
    mixing, expand_a, shrink_a, expand_b, shrink_b = refs[3:8]
    back_ref = refs[8]
    mixing_out, expand_a_out, shrink_a_out, expand_b_out, shrink_b_out = refs[9:14]
    turned, key_sum, value_sum, sems = refs[14:18]
    scratch = [refs[18 + 7 * number : 25 + 7 * number] for number in range(5)]
    tails = [refs[53 + 2 * number : 55 + 2 * number] for number in range(3)]
    spot = Spot(sizes)
    mover = Mover(spot, sems)
    k = spot.k
    half, grown, width = mixing.shape[-1] // 2, expand_a.shape[-1] // 2, shrink_a.shape[-1]
    m = ReduceJob(mover, *core_halves(mixing, k, half), half // 2, scratch[0])
    ea = ReduceJob(mover, *core_halves(expand_a, k, grown), grown // 2, scratch[1])
    sa = ReduceJob(mover, shrink_a.at[k], shrink_a.at[1 - k], width // 2, scratch[2])
    eb = ReduceJob(mover, *core_halves(expand_b, k, grown), grown // 2, scratch[3])
    sb = ReduceJob(mover, shrink_b.at[k], shrink_b.at[1 - k], width // 2, scratch[4])
    ends = [Finish(mover, *tail) for tail in tails]

    def open_all():
        spot.meet(("k", "c", "y", "z"))
        for job in (sa, ea, m, sb, eb):
            start(job.first)

    def near(*jobs):
        for job in jobs:
            wait(job.first)
            job.add_first()
            start(job.near)

    def far(*jobs):
        for job in jobs:
            wait(job.near)
            job.add_near()
            start(job.far)

    def along_z(*jobs):
        for job in jobs:
            wait(job.far)
            job.add_far()
            start(job.along_z)

    def close_all():
        along_z(sa, ea)
        far(m, sb, eb)
        for job, end in ((ea, ends[1]),):
            wait(job.along_z)
            end.summed[...] = job.result()
            start(end.copies)
        wait(sa.along_z)
        shrink_a_out[...] = sa.result()
        along_z(m, sb, eb)
        for job, end in ((m, ends[0]), (eb, ends[2])):
            wait(job.along_z)
            end.summed[...] = job.result()
            start(end.copies)
        wait(sb.along_z)
        shrink_b_out[...] = sb.result()
        for end, out in zip(ends, (mixing_out, expand_a_out, expand_b_out)):
            wait(end.copies)
            end.write(out)

    step = pl.program_id(0)
    schedule = [
        (0, 0, open_all),
        (1, 3, lambda: near(sa, ea)),
        (4, 0, lambda: near(m, sb, eb)),
        (6, 3, lambda: far(sa, ea)),
    ]
    attend_back_pair(
        blocks, projected, upstream, lse_ref, back_ref, turned, key_sum, value_sum,
        hooks(step, schedule),
    )
    pl.when(step == pl.num_programs(0) - 1)(close_all)


def attend_back(sizes, blocks, projected, upstream, lse, grads):
    tokens, width = upstream.shape
    pairs = width // PAIR
    mixing, expand_a, shrink_a, expand_b, shrink_b = grads
    rows = mixing.shape[3]
    own = rows // 2
    half, grown, full = mixing.shape[-1] // 2, expand_a.shape[-1] // 2, shrink_a.shape[-1]
    triple = pl.BlockSpec((tokens, 3 * PAIR), lambda g: (0, g))
    finals = [(2, own, half), (2, own, grown), (rows, full), (2, own, grown), (rows, full)]
    scratch = [
        pltpu.VMEM((blocks, PAIR, BLK), low),
        pltpu.VMEM((blocks, BLK, PAIR), jnp.float32),
        pltpu.VMEM((blocks, BLK, PAIR), jnp.float32),
        pltpu.SemaphoreType.DMA((2, 48)),
    ]
    for columns in (half, grown, full, grown, full):
        scratch += ReduceJob.scratch(sizes, rows, columns, columns // 2)
    for columns in (half, grown, grown):
        scratch += [
            pltpu.VMEM((rows, columns), jnp.float32),
            pltpu.VMEM((own, columns), jnp.float32),
        ]
    return pl.pallas_call(
        functools.partial(attend_back_kernel, sizes, blocks),
        grid=(pairs,),
        in_specs=[
            triple,
            pl.BlockSpec((tokens, PAIR), lambda g: (0, g)),
            pl.BlockSpec((None, 8, tokens), lambda g: (g, 0, 0)),
        ]
        + [any_place] * 5,
        out_specs=[triple] + [whole_vmem] * 5,
        out_shape=[jax.ShapeDtypeStruct(projected.shape, low)]
        + [jax.ShapeDtypeStruct(final, jnp.float32) for final in finals],
        scratch_shapes=scratch,
        compiler_params=pltpu.CompilerParams(
            collective_id=3, has_side_effects=True, vmem_limit_bytes=56 << 20
        ),
        cost_estimate=small_cost,
        name="attend_back",
    )(projected, upstream, lse, *grads)


def end_kernel(sizes, joint, vector, out, vector_out, sems, steps, arrived, *scratch):
    spot = Spot(sizes)
    mover = Mover(spot, sems)
    width = joint.shape[-1] // 2
    part = width // 2
    jobs, ends = [], []
    for number in range(2):
        refs = scratch[9 * number : 9 * number + 9]
        halves = core_halves(joint, spot.k, width, number * part, part)
        jobs.append(ReduceJob(mover, *halves, part // 2, refs[:7]))
        ends.append(Finish(mover, *refs[7:]))
    hops = [
        mover.copy(steps.at[number], arrived.at[number], name)
        for number, name in enumerate(("k", "c", "y"))
    ]
    spread = [
        mover.copy(steps.at[3], arrived.at[2 + by], "z", by) for by in range(1, sizes["z"])
    ]
    spot.meet(("k", "c", "y", "z"))
    start(jobs[0].first)
    steps[0] = vector[...]
    start(hops[:1])
    start(jobs[1].first)

    def hop(number):
        wait([hops[number]])
        steps[number + 1] = steps[number] + arrived[number]
        start([hops[number + 1]] if number < 2 else spread)

    wait(jobs[0].first)
    jobs[0].add_first()
    start(jobs[0].near)
    hop(0)
    wait(jobs[1].first)
    jobs[1].add_first()
    start(jobs[1].near)
    hop(1)
    wait(jobs[0].near)
    jobs[0].add_near()
    start(jobs[0].far)
    hop(2)
    wait(jobs[1].near)
    jobs[1].add_near()
    start(jobs[1].far)
    for job in jobs:
        wait(job.far)
        job.add_far()
        start(job.along_z)
    wait(spread)
    total = steps[3]
    for by in range(1, sizes["z"]):
        total = total + arrived[2 + by]
    vector_out[...] = total
    for job, end in zip(jobs, ends):
        wait(job.along_z)
        end.summed[...] = job.result()
        start(end.copies)
    for number, end in enumerate(ends):
        wait(end.copies)
        end.write(out, pl.ds(number * part, part))


def end(sizes, joint, vector):
    rows, width = joint.shape[3], joint.shape[4] // 2
    part = width // 2
    scratch = [
        pltpu.SemaphoreType.DMA((2, 40)),
        pltpu.VMEM((4, *vector.shape), jnp.float32),
        pltpu.VMEM((2 + sizes["z"], *vector.shape), jnp.float32),
    ]
    for number in range(2):
        scratch += ReduceJob.scratch(sizes, rows, part, part // 2)
        scratch += [
            pltpu.VMEM((rows, part), jnp.float32),
            pltpu.VMEM((rows // 2, part), jnp.float32),
        ]
    return pl.pallas_call(
        functools.partial(end_kernel, sizes),
        in_specs=[any_place, whole_vmem],
        out_specs=[whole_vmem] * 2,
        out_shape=[
            jax.ShapeDtypeStruct((2, rows // 2, width), jnp.float32),
            jax.ShapeDtypeStruct(vector.shape, jnp.float32),
        ],
        scratch_shapes=scratch,
        compiler_params=pltpu.CompilerParams(
            collective_id=4, has_side_effects=True, vmem_limit_bytes=32 << 20
        ),
        cost_estimate=small_cost,
        name="end",
    )(joint, vector)


def layer_norm(values, gain_row, shift_row):
    centered = values - jnp.mean(values, axis=-1, keepdims=True)
    variance = jnp.mean(centered * centered, axis=-1, keepdims=True)
    inverse = lax.rsqrt(variance + norm_eps)
    normal_part = centered * inverse
    return (normal_part * gain_row + shift_row, normal_part, inverse)


def norm_back(upstream, normal_part, inverse, gain_row):
    scaled = upstream * gain_row
    inner_sum = jnp.mean(scaled, axis=-1, keepdims=True)
    along_sum = jnp.mean(scaled * normal_part, axis=-1, keepdims=True)
    values_grad = inverse * (scaled - inner_sum - normal_part * along_sum)
    return (values_grad, jnp.sum(upstream * normal_part, axis=0), jnp.sum(upstream, axis=0))


def outer_sum(left_side, right_side):
    return lax.dot_general(
        left_side, right_side, (((0,), (0,)), ((), ())), preferred_element_type=jnp.float32
    )


def adam_update(weight, moment_one, moment_two, gradient, step_rate, decay_rate):
    first_new = 0.5 * moment_one + 0.5 * gradient
    second_new = 0.5 * moment_two + 0.5 * gradient * gradient
    correct = 1.0 - 0.5**STEP
    direction = first_new / correct / (jnp.sqrt(second_new / correct) + adam_eps)
    updated = weight - step_rate * (direction + decay_rate * weight)
    return (updated, first_new, second_new)


def to_groups(matrix):
    row_count = matrix.shape[0]
    return matrix.reshape(row_count, H // group_heads, group_heads, HD).transpose(1, 0, 2, 3)


def from_groups(stacked):
    return stacked.transpose(1, 0, 2, 3).reshape(stacked.shape[1], H * HD)


def tile_scores(queries, key_rows, allowed):
    products = jnp.einsum("rgd,lgd->grl", queries, key_rows, preferred_element_type=jnp.float32)
    return jnp.where(allowed[None], products * 0.125, -1e30)


def tile_forward(queries, key_rows, value_rows, allowed):
    scores = tile_scores(queries, key_rows, allowed)
    largest = jnp.max(scores, axis=-1, keepdims=True)
    exponent = jnp.exp(scores - largest)
    row_total = jnp.sum(exponent, axis=-1, keepdims=True)
    weights = (exponent / row_total).astype(low)
    mixed = jnp.einsum("grl,lgd->rgd", weights, value_rows, preferred_element_type=jnp.float32)
    return (mixed, (largest + jnp.log(row_total))[..., 0])


def tile_backward(queries, key_rows, value_rows, allowed, logsum, upstream):
    scores = tile_scores(queries, key_rows, allowed)
    recomputed = jnp.exp(scores - logsum[..., None])
    value_grad = jnp.einsum(
        "grl,rgd->lgd", recomputed.astype(low), upstream, preferred_element_type=jnp.float32
    )
    weight_grad = jnp.einsum(
        "rgd,lgd->grl", upstream, value_rows, preferred_element_type=jnp.float32
    )
    inner_sum = jnp.sum(recomputed * weight_grad, axis=-1, keepdims=True)
    score_grad = (recomputed * (weight_grad - inner_sum)).astype(low)
    query_grad = (
        jnp.einsum("grl,lgd->rgd", score_grad, key_rows, preferred_element_type=jnp.float32) * 0.125
    )
    key_grad = (
        jnp.einsum("grl,rgd->lgd", score_grad, queries, preferred_element_type=jnp.float32) * 0.125
    )
    return (query_grad, key_grad, value_grad)


def spread_forward(queries, key_value, allowed):
    def one_sequence(pieces):
        queries, key_value, allowed = pieces
        width = queries.shape[1]
        mixed, logsum = lax.map(
            lambda triple: tile_forward(triple[0], triple[1], triple[2], allowed),
            (to_groups(queries), to_groups(key_value[:, :width]), to_groups(key_value[:, width:])),
        )
        return (from_groups(mixed), logsum)

    return lax.map(one_sequence, (queries, key_value, allowed))


def spread_backward(queries, key_value, allowed, logsum, upstream):
    def one_sequence(pieces):
        queries, key_value, allowed, logsum, upstream = pieces
        width = queries.shape[1]
        query_grad, key_grad, value_grad = lax.map(
            lambda member: tile_backward(
                member[0], member[1], member[2], allowed, member[3], member[4]
            ),
            (
                to_groups(queries),
                to_groups(key_value[:, :width]),
                to_groups(key_value[:, width:]),
                logsum,
                to_groups(upstream),
            ),
        )
        return (
            from_groups(query_grad),
            jnp.concatenate([from_groups(key_grad), from_groups(value_grad)], axis=1),
        )

    return lax.map(one_sequence, (queries, key_value, allowed, logsum, upstream))


class Slice:
    def __init__(self, ctx_size, wshard_size):
        rest = wshard_size // 2
        self.sizes = {"c": ctx_size, "z": 4, "y": rest // 4, "k": 2}

    def here(self):
        flat = lax.axis_index(axes)
        found = {}
        for name in ("k", "y", "z", "c"):
            found[name] = flat % self.sizes[name]
            flat = flat // self.sizes[name]
        return found

    def shift(self, value, name, by):
        pairs = []
        sizes = self.sizes
        for c in range(sizes["c"]):
            for z in range(sizes["z"]):
                for y in range(sizes["y"]):
                    for k in range(sizes["k"]):
                        spot = {"c": c, "z": z, "y": y, "k": k}
                        goal = dict(spot)
                        goal[name] = (spot[name] + by) % sizes[name]
                        pairs.append((self.flat(spot), self.flat(goal)))
        return lax.ppermute(value, axes, pairs)

    def flat(self, spot):
        sizes = self.sizes
        return ((spot["c"] * sizes["z"] + spot["z"]) * sizes["y"] + spot["y"]) * sizes["k"] + spot[
            "k"
        ]

    def stack(self, array, name, here):
        size = self.sizes[name]
        parts = [array] + [self.shift(array, name, by) for by in range(1, size)]
        if size > 4:
            ordered = [parts[(-place) % size] for place in range(size)]
            return jnp.roll(jnp.stack(ordered), here[name], axis=0)
        return jnp.stack(
            [lax.select_n((here[name] - place) % size, *parts) if size > 2 else
             jnp.where(here[name] == place, parts[0], parts[1]) for place in range(size)]
        )

    def reach(self, pieces, name):
        grown = list(pieces)
        for by in range(1, self.sizes[name]):
            for array, place in pieces:
                moved = dict(place)
                moved[name] = (place[name] - by) % self.sizes[name]
                grown.append((self.shift(array, name, by), moved))
        return grown

    def gather_split(self, stacked, cut, here):
        sizes = self.sizes
        depth, rows, columns = stacked.shape
        out = jnp.zeros((sizes["c"], depth, sizes["y"], rows, columns), stacked.dtype)
        for low_column, high_column, order in ((0, cut, "cy"), (cut, columns, "yc")):
            pieces = [(stacked[:, :, low_column:high_column], here)]
            for name in order:
                pieces = self.reach(pieces, name)
            for array, place in pieces:
                out = lax.dynamic_update_slice(
                    out, array[None, :, None], (place["c"], 0, place["y"], 0, low_column)
                )
        return out.reshape(-1, columns)

    def send_terms(self, value, name, place, here):
        size = self.sizes[name]
        own = lax.dynamic_index_in_dim(value, here[name], place, False)
        moved = [
            self.shift(
                lax.dynamic_index_in_dim(value, (here[name] + by) % size, place, False), name, by
            )
            for by in range(1, size)
        ]
        return own, moved

    def add_terms(self, terms, kind=low):
        own, moved = terms
        total = own.astype(jnp.float32)
        for other in moved:
            total = total + other.astype(jnp.float32)
        return total.astype(kind)

    def everywhere(self, value):
        for name in ("k", "c", "y", "z"):
            total = value
            for by in range(1, self.sizes[name]):
                total = total + self.shift(value, name, by)
            value = total
        return value


def tie(value, *others):
    return lax.optimization_barrier((value, others))[0]


def by_core(core, first, second, axis):
    return jnp.where(
        core == 0,
        jnp.concatenate([first, second], axis=axis),
        jnp.concatenate([second, first], axis=axis),
    )


def pick(core, array, axis):
    return (
        lax.dynamic_index_in_dim(array, core, axis, False),
        lax.dynamic_index_in_dim(array, 1 - core, axis, False),
    )


def gather_far(grid, here, pieces):
    joint_halves, table, mixing_halves, expand_a, expand_b, shrink_a, shrink_b = pieces
    core = here["k"]

    def chip_rows(halves):
        own, other = pick(core, halves, 0)
        return by_core(core, own, grid.shift(other, "k", 1), 0)

    def everyone(block):
        width = block.shape[1]
        return grid.gather_split(grid.stack(block, "z", here), width // 2, here)

    def both(block, axis):
        own = everyone(block)
        return by_core(core, own, grid.shift(own, "k", 1), axis)

    return (
        both(chip_rows(joint_halves), 1),
        everyone(by_core(core, table, grid.shift(table, "k", 1), 0)),
        both(chip_rows(mixing_halves), 1),
        both(chip_rows(expand_a), 1),
        both(chip_rows(expand_b), 1),
        both(shrink_a, 0),
        both(shrink_b, 0),
    )


def reduce_far(grid, here, gradient, by_rows):
    core = here["k"]
    sizes = grid.sizes
    if by_rows:
        own, other = pick(core, gradient.reshape(2, -1, gradient.shape[1]), 0)
    else:
        own, other = pick(core, gradient.reshape(gradient.shape[0], 2, -1), 1)
    total = grid.add_terms((own, [grid.shift(other, "k", 1)]))
    total = total.reshape(sizes["c"], sizes["z"], sizes["y"], -1, own.shape[-1])
    for name, place in (("y", 2), ("c", 0)):
        total = grid.add_terms(grid.send_terms(total, name, place, here))
    total = grid.add_terms(grid.send_terms(total, "z", 0, here), jnp.float32)
    if by_rows:
        return total
    kept, other = pick(core, total.reshape(2, -1, total.shape[1]), 0)
    return by_core(core, kept[None], grid.shift(other, "k", 1)[None], 0)


def body(
    grid,
    block_input,
    block_order,
    cotangent,
    joint_weight,
    mixing_weight,
    expand_weight,
    shrink_weight,
    vectors,
    joint_first,
    mixing_first,
    expand_first,
    shrink_first,
    vectors_first,
    joint_second,
    mixing_second,
    expand_second,
    shrink_second,
    vectors_second,
):
    here = grid.here()
    sizes = grid.sizes
    ctx, ctx_size = here["c"], sizes["c"]
    seq_count, row_count, width = block_input.shape
    half = width // 2
    pairs = H // 2
    hidden_width = expand_weight.shape[1]
    own_rows = joint_weight.shape[0]
    slot = shrink_weight.shape[0]
    sub = slot // 2
    chips = hidden_width // (2 * slot)
    tokens = seq_count * row_count
    row_blocks = row_count // BLK
    near = ctx_size == 2 and seq_count == 2 and sizes["y"] == 2 and own_rows % 32 == 0

    def to_sequence(rows):
        if not near:
            return rows.reshape(tokens, width)
        sent = lax.dynamic_index_in_dim(rows, 1 - ctx, 0, False)
        kept = lax.dynamic_index_in_dim(rows, ctx, 0, False)
        return jnp.concatenate([kept, grid.shift(sent, "c", 1)], axis=0)

    def from_sequence(rows, kind):
        if not near:
            return rows.astype(kind).reshape(seq_count, row_count, width)
        kept = rows[:row_count].astype(kind)
        arrived = grid.shift(rows[row_count:].astype(low), "c", 1).astype(kind)
        return by_core(ctx, kept[None], arrived[None], 0)

    def hidden_sets(shard):
        parts = shard.astype(low).reshape(own_rows, chips, 2, 2, sub)
        return [
            parts[:, :, :, number].transpose(2, 0, 1, 3).reshape(2, own_rows, chips * sub)
            for number in range(2)
        ]

    joint_halves = (
        joint_weight.astype(low)
        .reshape(own_rows, 3, 2, pairs // 2, PAIR)
        .transpose(2, 0, 3, 1, 4)
        .reshape(2, own_rows, 3 * half)
    )
    table = jnp.pad(vectors.T.astype(low), ((0, 0), (0, 128 - vectors.shape[0])))
    mixing_halves = mixing_weight.astype(low).reshape(own_rows, 2, half).transpose(1, 0, 2)
    shrink_low = shrink_weight.astype(low)
    pieces = [joint_halves, table, mixing_halves, *hidden_sets(expand_weight)]
    pieces += [shrink_low[:sub], shrink_low[sub:]]
    input_rows = to_sequence(block_input)
    upstream = to_sequence(cotangent)
    if near:
        joint, tables, *later = begin(sizes, pieces)
    else:
        joint, tables, mixing, expand_a, expand_b, shrink_a, shrink_b = gather_far(
            grid, here, pieces
        )
    joint = joint.reshape(width, 3 * width)
    vector_values = (
        tables.reshape(width, -1)[:, : vectors.shape[0]].T.astype(jnp.float32)
    )

    if near:
        order = lax.dynamic_slice_in_dim(block_order, ctx, 1, 0)[0]
        blocks = order.shape[0]
        stored = jnp.arange(blocks, dtype=jnp.int32)
        moved = jnp.where(stored // row_blocks == ctx, 0, row_blocks) + stored % row_blocks
        place = jnp.sum(jnp.where(order[None, :] == stored[:, None], moved[None, :], 0), axis=1)
        back = jnp.sum(jnp.where(moved[None, :] == stored[:, None], order[None, :], 0), axis=1)
        place, back = place.astype(jnp.int32), back.astype(jnp.int32)
        input_rows = arrange(place, input_rows)
        upstream = arrange(place, upstream)
    input_rows = input_rows.astype(jnp.float32)
    normed_first, normal_first, inverse_first = layer_norm(
        input_rows, vector_values[0], vector_values[1]
    )
    first_low = normed_first.astype(low)
    joint_shift = jnp.stack(
        [
            vector_values[2].reshape(pairs, PAIR),
            jnp.zeros((pairs, PAIR), jnp.float32),
            vector_values[3].reshape(pairs, PAIR),
        ],
        axis=1,
    ).reshape(-1)
    projected = (nn(first_low, joint) + joint_shift).astype(low)
    if near:
        mixed_low, logsum, mixing, expand_a, expand_b, shrink_a, shrink_b = attend(
            sizes, blocks, projected, later
        )
    else:
        by_part = projected.reshape(seq_count, row_count, pairs, 3, PAIR)
        queries, keys, values = [
            by_part[:, :, :, part].reshape(seq_count, row_count, width) for part in range(3)
        ]
        key_value = lax.all_gather(
            jnp.concatenate([keys, values], axis=2), "ctx", axis=1, tiled=True
        )
        own_blocks = lax.dynamic_slice_in_dim(block_order, ctx * row_blocks, row_blocks, 1)
        query_block = jnp.repeat(own_blocks, BLK, axis=1, total_repeat_length=row_count)
        key_block = jnp.repeat(block_order, BLK, axis=1, total_repeat_length=key_value.shape[1])
        allowed = key_block[:, None, :] <= query_block[:, :, None]
        mixed, logsum = spread_forward(queries, key_value, allowed)
        mixed_low = mixed.astype(low).reshape(tokens, width)
    mixing = mixing.reshape(width, width)
    expands = [expand.reshape(width, -1) for expand in (expand_a, expand_b)]
    shrinks = [shrink.reshape(-1, width) for shrink in (shrink_a, shrink_b)]
    middle = input_rows + (nn(mixed_low, mixing) + vector_values[4])
    normed_second, normal_second, inverse_second = layer_norm(
        middle, vector_values[5], vector_values[6]
    )
    second_low = normed_second.astype(low)

    hidden_bias = vector_values[8:].reshape(chips, 2, 2, sub)
    before, hidden_grads, hidden_bias_grads = None, [], []
    for number in range(2):
        bias = hidden_bias[:, :, number].transpose(1, 0, 2).reshape(1, -1)
        result, second_grad, expand_grad, shrink_grad, bias_grad = mlp(
            second_low, upstream, expands[number], shrinks[number], bias, before=before
        )
        before = (result, second_grad)
        hidden_grads += [expand_grad, shrink_grad]
        hidden_bias_grads.append(bias_grad.reshape(2, chips, 1, sub).transpose(1, 0, 2, 3))
    block_output = (middle + result + vector_values[7]).astype(low)
    if near:
        block_output = arrange(back, block_output)
    block_output = from_sequence(block_output, low)

    upstream_float = upstream.astype(jnp.float32)
    middle_part, gain_two, shift_two = norm_back(
        second_grad, normal_second, inverse_second, vector_values[5]
    )
    middle_grad = upstream_float + middle_part
    branch_low = middle_grad.astype(low)
    mixing_grad = outer_sum(mixed_low, branch_low).astype(low)
    mixed_grad = nt(branch_low, mixing).astype(low)
    if near:
        lead = (sizes["c"], sizes["z"], sizes["y"])
        grads = [mixing_grad.reshape(*lead, -1, width)]
        for number in range(2):
            expand_grad, shrink_grad = hidden_grads[2 * number : 2 * number + 2]
            grads.append(expand_grad.reshape(*lead, -1, expand_grad.shape[1]))
            grads.append(shrink_grad.reshape(2, *lead, -1, width))
        joint_back, mixing_part, *hidden_parts = attend_back(
            sizes, blocks, projected, mixed_grad, logsum, grads
        )
    else:
        query_grad, key_value_grad = spread_backward(
            queries, key_value, allowed, logsum, mixed_grad.reshape(seq_count, row_count, width)
        )
        summed = lax.psum_scatter(
            key_value_grad.astype(low), "ctx", scatter_dimension=1, tiled=True
        )
        parts = [query_grad.astype(low), summed[..., :width], summed[..., width:]]
        joint_back = jnp.stack(
            [part.reshape(tokens, pairs, PAIR) for part in parts], axis=2
        ).reshape(tokens, 3 * width)
        mixing_part = reduce_far(grid, here, mixing_grad, False)
        hidden_parts = [
            reduce_far(grid, here, grad, number % 2 == 1)
            for number, grad in enumerate(hidden_grads)
        ]
    joint_grad = outer_sum(first_low, joint_back).astype(low)
    first_grad = nt(joint_back, joint)
    input_part, gain_one, shift_one = norm_back(
        first_grad, normal_first, inverse_first, vector_values[0]
    )
    input_gradient = middle_grad + input_part
    if near:
        input_gradient = arrange(back, input_gradient)
    input_gradient = from_sequence(input_gradient, jnp.float32)

    def column_sum(rows):
        return jnp.sum(rows.astype(jnp.float32), axis=0)

    joint_sums = column_sum(joint_back).reshape(pairs, 3, PAIR)
    vector_grad = jnp.concatenate(
        [
            jnp.stack(
                [
                    gain_one,
                    shift_one,
                    joint_sums[:, 0].reshape(-1),
                    joint_sums[:, 2].reshape(-1),
                    column_sum(branch_low),
                    gain_two,
                    shift_two,
                    column_sum(upstream),
                ]
            ),
            jnp.concatenate(hidden_bias_grads, axis=2).reshape(-1, width),
        ],
        axis=0,
    )
    if near:
        joint_part, vector_sum = end(
            sizes,
            joint_grad.reshape(*lead, -1, 3 * width),
            jnp.pad(vector_grad, ((0, -vector_grad.shape[0] % 8), (0, 0))),
        )
    else:
        joint_part = reduce_far(grid, here, joint_grad, False)
        vector_sum = grid.everywhere(vector_grad)
    vector_sum = lax.dynamic_slice(
        vector_sum, (0, lax.axis_index(axes) * vectors.shape[1]), vectors.shape
    )
    joint_sum = (
        joint_part.reshape(2, own_rows, pairs // 2, 3, PAIR)
        .transpose(1, 3, 0, 2, 4)
        .reshape(joint_weight.shape)
    )
    mixing_sum = mixing_part.transpose(1, 0, 2).reshape(mixing_weight.shape)
    expand_sum = jnp.stack(
        [part.reshape(2, own_rows, chips, sub) for part in hidden_parts[0::2]], axis=0
    )
    expand_sum = expand_sum.transpose(2, 3, 1, 0, 4).reshape(expand_weight.shape)
    shrink_sum = jnp.concatenate(hidden_parts[1::2], axis=0)
    joint_new, joint_moment, joint_square = adam_update(
        joint_weight, joint_first, joint_second, joint_sum, 0.05, 0.1
    )
    mixing_new, mixing_moment, mixing_square = adam_update(
        mixing_weight, mixing_first, mixing_second, mixing_sum, 0.05, 0.1
    )
    expand_new, expand_moment, expand_square = adam_update(
        expand_weight, expand_first, expand_second, expand_sum, 0.05, 0.1
    )
    shrink_new, shrink_moment, shrink_square = adam_update(
        shrink_weight, shrink_first, shrink_second, shrink_sum, 0.05, 0.1
    )
    vectors_new, vectors_moment, vectors_square = adam_update(
        vectors, vectors_first, vectors_second, vector_sum, 0.5, 0.0
    )
    return (
        block_output,
        input_gradient,
        joint_new,
        mixing_new,
        expand_new,
        shrink_new,
        vectors_new,
        joint_moment,
        mixing_moment,
        expand_moment,
        shrink_moment,
        vectors_moment,
        joint_square,
        mixing_square,
        expand_square,
        shrink_square,
        vectors_square,
        joint_new.astype(low),
        mixing_new.astype(low),
        expand_new.astype(low),
        shrink_new.astype(low),
        vectors_new.astype(low),
    )


def solution(mesh):
    grid = Slice(mesh.shape["ctx"], mesh.shape["wshard"])
    rows = P("wshard", "ctx", None)
    matrix = P(axes, None)
    table = P(None, axes)
    parameters = (matrix, matrix, matrix, matrix, table)
    return jax.shard_map(
        functools.partial(body, grid),
        mesh=mesh,
        in_specs=(rows, P("wshard", None), rows) + parameters * 3,
        out_specs=(rows, rows) + parameters * 4,
        check_vma=False,
    )
```

time: 721 us -> 608 us (0.84)
  Pallas kernels: 155 us -> 453 us
  waiting for transfers between devices: 230 us -> 0.01 us
  starting transfers between devices: 123 us -> 4.98 us
  local copies, waits for them, and re-layouts: 75.1 us -> 48.1 us
  other arithmetic: 76.2 us -> 50.1 us
    pallas_call x4 -> x8, Pallas kernels: 72.7 us -> 370 us  [the longest x1 125 us: attend_back(): pl.pallas_call(functools.partial(attend_back_kernel, sizes, blocks), grid...]
    ppermute x82 -> x4, waiting for transfers between devices: 230 us -> 0.01 us  [shift(): return lax.ppermute(value, axes, pairs)]
    ppermute x82 -> x4, starting transfers between devices: 123 us -> 4.98 us  [shift(): return lax.ppermute(value, axes, pairs)]
    dynamic_update_slice x26 -> x0, local copies, waits for them, and re-layouts: 29.7 us -> none  [the longest x24 25 us: gather_split(): lax.dynamic_update_slice(out, array[None, :, None], (place['c'], 0, place...]
    convert_element_type x23 -> x5, other arithmetic: 24 us -> 0.1 us  [the longest x1 0.03 us: body(): shrink_low = shrink_weight.astype(low)]
    unnamed x145 -> x98, local copies, waits for them, and re-layouts: 4.5 us -> 16.3 us
    slice x14 -> x6, local copies, waits for them, and re-layouts: 13.3 us -> 4.14 us  [the longest x1 2.88 us: from_sequence(): arrived = grid.shift(rows[row_count:].astype(low), 'c', 1).astype(kind)]
    reshape x6 -> x20, local copies, waits for them, and re-layouts: 1.28 us -> 9.23 us  [the longest x1 2.96 us: body(): expand_sum.transpose(2, 3, 1, 0, 4).reshape(expand_weight.shape)]
  transfers between devices with their start and end apart: 82 -> 4, of which waited for: 25 -> 0; matrix products, arithmetic and copies ran while one was open for 24% -> 10% of each run, Pallas kernels for 10% -> 38%
where the time goes in v2:
time: 608 us; the launch traced here: 604 us
  Pallas kernels  453 us (75%)
  other arithmetic  50.1 us (8%)
  local copies, waits for them, and re-layouts  48.1 us (8%)
  matrix products  45.9 us (8%)
    pallas_call x1, Pallas kernels, attend_back(): pl.pallas_call(functools.partial(attend_back_kernel, sizes, blocks), grid...  125 us
    pallas_call x1, Pallas kernels, attend(): pl.pallas_call(functools.partial(attend_kernel, sizes, blocks), grid=(pai...  89.6 us
    pallas_call x2, Pallas kernels, mlp(): pl.pallas_call(functools.partial(mlp_kernel, before is None, rows_step),...  82.6 us
    pallas_call x1, Pallas kernels, begin(): pl.pallas_call(functools.partial(begin_kernel, sizes), in_specs=[whole_vm...  74.7 us
    pallas_call x1, Pallas kernels, end(): pl.pallas_call(functools.partial(end_kernel, sizes), in_specs=[any_place,...  62.7 us
    pallas_call x4, Pallas kernels, arrange(): pl.pallas_call(arrange_kernel, grid_spec=pltpu.PrefetchScalarGridSpec(num...  18.9 us
    unnamed x98, local copies, waits for them, and re-layouts  16.3 us
    dot_general x2, matrix products, outer_sum(): lax.dot_general(left_side, right_side, (((0,), (0,)), ((), ())), preferre...  16.1 us
  transfers between devices with their start and end apart: 4, of which 0 were waited for; matrix products, arithmetic and copies ran while one was open for 10% of the time, Pallas kernels for 38%

profile of v2, /device:TPU:0, one launch (start us, length us, event | category | flops | bytes accessed | tf_op | source)
XLA Modules:
  0.0 604.0 jit_solution(2493725397702030094)
XLA Ops:
  0.8 3.2 dynamic-slice_bitcast_fusion.3
  4.0 2.9 collective-permute-start
  11.4 74.7 %begin.1 = (bf16[2,4,2,64,3072]{4,3,2,1,0:T(8,128)(2,1)S(1)}, bf16[2,4,2,64,128]{4,3,2,1,0:T(8,128)(2,1)S(1)}, bf16[2,4,2,64,1024]{4,3,2,1,0:T(8,128)(2,1)S(1)},...) custom-call(bf16[2,32,1536]{2,1,0:T(8,128)(2,1)S(1)} %reshape.199.re, ...), custom_call_target="tpu_custom_call" | custom-call | flops 1024 | bytes 1024 | tf_op jit(solution)/shard_map/begin/pallas_call | solution.py:474
  94.1 2.7 copy-done.8
  99.3 3.0 pad_maximum_fusion.rows_ref
  102.3 4.5 arrange.4
  111.2 11.8 %add_convert_fusion.refs_0_ = bf16[1024,3072]{1,0:T(8,128)(2,1)} fusion(f32[3072]{0:T(1024)S(1)} %add.214, bf16[1024,3072]{1,0:T(8,128)(2,1)} %bitcast.111, bf16[1024,1024]{1,0:T(8,128)(2,1)S(1)} %copy-done.13, f32[1024]{0:T(1024)S(1)} %bitcast.147, f32[1024]{0:T(1024)S(1)} %bitcast.135, f32[1024]{0:T(1024)S(1)} %add_rsqrt_fusion.1, ...), kind=kOutput, calls=%fused_computation.1 | convolution fusion | flops 6455033856 | bytes 14708736 | tf_op jit(solution)/shard_map/dot_general | solution.py:30
  123.0 89.6 %attend.1 = (bf16[1024,1024]{1,0:T(8,128)(2,1)S(1)}, f32[8,8,1024]{2,1,0:T(8,128)S(1)}, bf16[2,4,2,64,1024]{4,3,2,1,0:T(8,128)(2,1)S(1)}, bf16[2,4,2,64,2048]{4,...) custom-call(bf16[1024,3072]{1,0:T(8,128)(2,1)} %add_convert_fusion.r, ...), custom_call_target="tpu_custom_call", output_to_operand_aliasing={{2}: (1, {}), {3}: (2, {}), {4}: (3, {}), {5}: (4, {}), {6}... | custom-call | flops 1024 | bytes 1024 | tf_op jit(solution)/shard_map/attend/pallas_call | solution.py:538
  212.6 2.5 fusion.39
  217.2 2.8 pad_maximum_fusion.1.rows_ref
  220.0 4.5 arrange.5.dy_ref
  224.4 4.2 add_convert_fusion.2.c_ref
  228.7 40.0 %mlp.2 = (f32[1024,1024]{1,0:T(8,128)}, f32[1024,1024]{1,0:T(8,128)}, bf16[1024,2048]{1,0:T(8,128)(2,1)}, bf16[2048,1024]{1,0:T(8,128)(2,1)}, f32[1,2048]{1,0:T(1,128)}) custom-call(bf16[1024,1024]{1,0:T(8,128)(2,1)} %add_convert_fusion.2.c_ref, bf16[1024,1024]{1,0:T(8,128)(2,1)} %arrange.5.dy_ref, bf16[1024,2048]{1,0:T(8,128)(2,1)} %bitcast.104, ...), custom_call_target="tpu_custom_call" | custom-call | flops 1024 | bytes 1024 | tf_op jit(solution)/shard_map/mlp/pallas_call | solution.py:197
  268.7 42.7 %mlp.3 = (f32[1024,1024]{1,0:T(8,128)}, f32[1024,1024]{1,0:T(8,128)}, bf16[1024,2048]{1,0:T(8,128)(2,1)}, bf16[2048,1024]{1,0:T(8,128)(2,1)}, f32[1,2048]{1,0:T(1,128)}) custom-call(bf16[1024,1024]{1,0:T(8,128)(2,1)} %add_convert_fusion.2.c_ref, bf16[1024,1024]{1,0:T(8,128)(2,1)} %arrange.5.dy_ref, bf16[1024,2048]{1,0:T(8,128)(2,1)} %bitcast.102, ...), custom_call_target="tpu_custom_call" | custom-call | flops 1024 | bytes 1024 | tf_op jit(solution)/shard_map/mlp/pallas_call | solution.py:197
  311.4 4.5 multiply_reduce_fusion
  315.9 5.6 convert_reduce_fusion.3
  321.5 3.8 convolution_convert_fusion.2.refs_1_
  325.3 3.8 convolution_convert_fusion.1
  329.0 124.5 %attend_back.1 = (bf16[1024,3072]{1,0:T(8,128)(2,1)}, f32[2,32,512]{2,1,0:T(8,128)}, f32[2,32,1024]{2,1,0:T(8,128)}, f32[64,1024]{1,0:T(8,128)}, f32[2,32,1024]{2,1,0:T(8,128)}, /*index=5*/f32[64,1024]{1,0:T(8,128)}) custom-call(bf16[1024,3072]{1,0:T(8,128)(2,1)} %add_convert_fusion.refs_0_, bf16[1024,1024]{1,0:T(8,128)(2,1)} %convolution_convert_fusion.2.refs_1_, ...), custom_call_target="tpu_custom_call" | custom-call | flops 1024 | bytes 1024 | tf_op jit(solution)/shard_map/attend_back/pallas_call | solution.py:685
  453.6 11.8 %fusion.12 = (f32[1024]{0:T(1024)}, f32[1024]{0:T(1024)S(1)}, f32[1024]{0:T(1024)S(1)}, f32[1024]{0:T(1024)}, f32[1024,1024]{1,0:T(8,128)S(1)}) fusion(bf16[1024,1024]{1,0:T(8,128)(2,1)} %arrange.4, f32[1024]{0:T(1024)S(1)} %add_rsqrt_fusion.1, f32[1024]{0:T(1024)S(1)} %broadcast_multiply_fusion.5, f32[1024]{0:T(1024)S(1)} %bitcast.136, ...), kind=kOutput, calls=%fused_computation.20 | convolution fusion | flops 6452932608 | bytes 18903040 | tf_op jit(solution)/shard_map/dot_general | solution.py:28
  465.4 2.9 fusion.11.rows_ref
  468.3 5.4 arrange.7
  473.7 2.9 slice.118
  478.4 12.3 %convolution_convert_fusion = bf16[1024,3072]{1,0:T(8,128)(2,1)} fusion(bf16[1024,3072]{1,0:T(8,128)(2,1)} %get-tuple-element.76, bf16[1024,1024]{1,0:T(8,128)(2,1)S(1)} %copy-done.15, f32[1024]{0:T(1024)S(1)} %bitcast.148, f32[1024]{0:T(1024)S(1)} %bitcast.138, f32[1024]{0:T(1024)S(1)} %add_rsqrt_fusion.1, f32[1024]{0:T(1024)S(1)} %broadcast_multiply_fusion.5), kind=kOutput, calls=%fused_computation.5 | convolution fusion | flops 6451888128 | bytes 14696448 | tf_op jit(solution)/shard_map/dot_general | solution.py:816
  491.7 4.6 arrange.6
  496.3 2.7 slice_bitcast_fusion.1
  511.8 3.0 reshape.227
  518.7 3.0 fusion.29
  523.6 2.8 copy-done.6
  526.3 62.7 %end.1 = (f32[2,32,1536]{2,1,0:T(8,128)S(1)}, f32[16,1024]{1,0:T(8,128)S(1)}) custom-call(bf16[2,4,2,64,3072]{4,3,2,1,0:T(8,128)(2,1)S(1)} %bitcast.106, f32[16,1024]{1,0:T(8,128)S(1)} %pad.9.vector), custom_call_target="tpu_custom_call" | custom-call | flops 1024 | bytes 1024 | tf_op jit(solution)/shard_map/end/pallas_call | solution.py:782
  593.6 2.6 fusion.33
  596.2 3.4 maximum_select_fusion.1
  (179 shorter events, 51.0 us)
Async XLA Ops:
  0.7 98.0 %copy-start = (s32[2,4]{1,0:T(2,128)S(1)}, s32[2,4]{1,0:T(2,128)}, u32[]{:S(2)}) copy-start(s32[2,4]{1,0:T(2,128)} %param.19) | copy-start | bytes 100
  0.7 6.3 %copy-start.21 = (bf16[2,512,1024]{2,1,0:T(8,128)(2,1)S(1)}, bf16[2,512,1024]{2,1,0:T(8,128)(2,1)}, u32[]{:S(2)}) copy-start(bf16[2,512,1024]{2,1,0:T(8,128)(2,1)} %param.20) | copy-start | bytes 6291460
  0.8 7.7 %copy-start.25 = (f32[32,3072]{1,0:T(8,128)S(1)}, f32[32,3072]{1,0:T(8,128)}, u32[]{:S(2)}) copy-start(f32[32,3072]{1,0:T(8,128)} %param.21) | copy-start | bytes 1179652
  0.8 8.1 %copy-start.34 = (f32[12,32]{1,0:T(8,128)S(1)}, f32[12,32]{1,0:T(8,128)}, u32[]{:S(2)}) copy-start(f32[12,32]{1,0:T(8,128)} %param.25) | copy-start | bytes 4612
  0.8 8.2 %copy-start.28 = (f32[32,1024]{1,0:T(8,128)S(1)}, f32[32,1024]{1,0:T(8,128)}, u32[]{:S(2)}) copy-start(f32[32,1024]{1,0:T(8,128)} %param.22) | copy-start | bytes 393220
  4.0 5.0 copy-start.22
  4.0 95.3 %collective-permute-start = (bf16[512,1024]{1,0:T(8,128)(2,1)}, bf16[512,1024]{1,0:T(8,128)(2,1)}, u32[]{:S(2)}, u32[]{:S(2)}) collective-permute-start(bf16[512,1024]{1,0:T(8,128)(2,1)} %get-tuple-element.125), channel_id=1, source_target_pairs={{0,16},{1,17},{2,18},{3,19},{4,20},{5,21},{6,22},{7,23},{8,24},{9,... | collective-permute-start | bytes 3145736 | tf_op jit(solution)/shard_map/ppermute | solution.py:935
  8.4 207.3 %collective-permute-start.1 = (bf16[512,1024]{1,0:T(8,128)(2,1)}, bf16[512,1024]{1,0:T(8,128)(2,1)}, u32[]{:S(2)}, u32[]{:S(2)}) collective-permute-start(bf16[512,1024]{1,0:T(8,128)(2,1)} %get-tuple-element.123), channel_id=1, source_target_pairs={{0,16},{1,17},{2,18},{3,19},{4,20},{5,21},{6,22},{7,23},{8,24},{9,... | collective-permute-start | bytes 3145736 | tf_op jit(solution)/shard_map/ppermute | solution.py:935
  215.1 4.8 copy-start.11
  268.7 42.7 %copy-start.12 = (f32[1024,1024]{1,0:T(8,128)S(1)}, f32[1024,1024]{1,0:T(8,128)}, u32[]{:S(2)}) copy-start(f32[1024,1024]{1,0:T(8,128)} %copy-done.11) | copy-start | bytes 12582916
  325.3 128.3 %slice-start = ((s8[6291456]{0:T(1024)(128)(4,1)}), s8[4194304]{0:T(1024)(128)(4,1)S(1)}, s32[]{:S(2)}) async-start(s8[6291456]{0:T(1024)(128)(4,1)} %bitcast.112), calls=%async_computation | async-start | bytes 8388608
  329.0 124.6 %slice-start.1 = ((s8[6291456]{0:T(1024)(128)(4,1)}), s8[2097152]{0:T(1024)(128)(4,1)S(1)}, s32[]{:S(2)}) async-start(s8[6291456]{0:T(1024)(128)(4,1)} %bitcast.112), calls=%async_computation.1 | async-start | bytes 4194304
  453.6 11.8 %copy-start.14 = (bf16[1024,1024]{1,0:T(8,128)(2,1)S(1)}, bf16[1024,1024]{1,0:T(8,128)(2,1)}, u32[]{:S(2)}) copy-start(bf16[1024,1024]{1,0:T(8,128)(2,1)} %arrange.4) | copy-start | bytes 6291460
  453.6 11.8 %copy-start.18 = (f32[1024,1024]{1,0:T(8,128)S(1)}, f32[1024,1024]{1,0:T(8,128)}, u32[]{:S(2)}) copy-start(f32[1024,1024]{1,0:T(8,128)} %copy-done.17) | copy-start | bytes 12582916
  476.5 14.2 %slice-start.2 = ((s8[6291456]{0:T(1024)(128)(4,1)}), s8[4194304]{0:T(1024)(128)(4,1)S(1)}, s32[]{:S(2)}) async-start(s8[6291456]{0:T(1024)(128)(4,1)} %bitcast.115), calls=%async_computation.2 | async-start | bytes 8388608
  478.4 12.3 %slice-start.3 = ((s8[6291456]{0:T(1024)(128)(4,1)}), s8[2097152]{0:T(1024)(128)(4,1)S(1)}, s32[]{:S(2)}) async-start(s8[6291456]{0:T(1024)(128)(4,1)} %bitcast.115), calls=%async_computation.3 | async-start | bytes 4194304
  491.7 10.5 %copy-start.41 = (f32[1,2048]{1,0:T(1,128)S(1)}, f32[1,2048]{1,0:T(1,128)}, u32[]{:S(2)}) copy-start(f32[1,2048]{1,0:T(1,128)} %get-tuple-element.78) | copy-start | bytes 24580
  491.7 11.8 %copy-start.40 = (f32[1,2048]{1,0:T(1,128)S(1)}, f32[1,2048]{1,0:T(1,128)}, u32[]{:S(2)}) copy-start(f32[1,2048]{1,0:T(1,128)} %get-tuple-element.77) | copy-start | bytes 24580
  491.7 13.2 %copy-start.31 = (f32[2,32,512]{2,1,0:T(8,128)S(1)}, f32[2,32,512]{2,1,0:T(8,128)}, u32[]{:S(2)}) copy-start(f32[2,32,512]{2,1,0:T(8,128)} %get-tuple-element.80) | copy-start | bytes 393220
  499.0 97.2 %collective-permute-start.2 = (bf16[512,1024]{1,0:T(8,128)(2,1)}, bf16[512,1024]{1,0:T(8,128)(2,1)}, u32[]{:S(2)}, u32[]{:S(2)}) collective-permute-start(bf16[512,1024]{1,0:T(8,128)(2,1)} %get-tuple-element.121), channel_id=1, source_target_pairs={{0,16},{1,17},{2,18},{3,19},{4,20},{5,21},{6,22},{7,23},{8,24},{9,... | collective-permute-start | bytes 3145736 | tf_op jit(solution)/shard_map/ppermute | solution.py:935
  499.5 100.2 %collective-permute-start.3 = (bf16[512,1024]{1,0:T(8,128)(2,1)}, bf16[512,1024]{1,0:T(8,128)(2,1)}, u32[]{:S(2)}, u32[]{:S(2)}) collective-permute-start(bf16[512,1024]{1,0:T(8,128)(2,1)} %slice.118), channel_id=1, source_target_pairs={{0,16},{1,17},{2,18},{3,19},{4,20},{5,21},{6,22},{7,23},{8,24},{9,... | collective-permute-start | bytes 3145736 | tf_op jit(solution)/shard_map/ppermute | solution.py:935
  504.9 11.9 %copy-start.29 = (f32[32,1024]{1,0:T(8,128)S(1)}, f32[32,1024]{1,0:T(8,128)}, u32[]{:S(2)}) copy-start(f32[32,1024]{1,0:T(8,128)} %param.22) | copy-start | bytes 393220
  504.9 11.9 %copy-start.30 = (f32[32,1024]{1,0:T(8,128)S(1)}, f32[32,1024]{1,0:T(8,128)}, u32[]{:S(2)}) copy-start(f32[32,1024]{1,0:T(8,128)} %param.27) | copy-start | bytes 393220
  514.8 6.9 %copy-start.24 = (f32[128,1024]{1,0:T(8,128)S(1)}, f32[128,1024]{1,0:T(8,128)}, u32[]{:S(2)}) copy-start(f32[128,1024]{1,0:T(8,128)} %param.24) | copy-start | bytes 1572868
  514.8 6.9 %copy-start.26 = (f32[128,1024]{1,0:T(8,128)S(1)}, f32[128,1024]{1,0:T(8,128)}, u32[]{:S(2)}) copy-start(f32[128,1024]{1,0:T(8,128)} %param.29) | copy-start | bytes 1572868
  514.8 6.9 %copy-start.27 = (f32[128,1024]{1,0:T(8,128)S(1)}, f32[128,1024]{1,0:T(8,128)}, u32[]{:S(2)}) copy-start(f32[128,1024]{1,0:T(8,128)} %param.34) | copy-start | bytes 1572868
  516.8 6.4 %copy-start.32 = (f32[2,16,1,64]{3,2,0,1:T(1,128)S(1)}, f32[2,16,1,64]{3,2,0,1:T(1,128)}, u32[]{:S(2)}) copy-start(f32[2,16,1,64]{3,2,0,1:T(1,128)} %copy.127) | copy-start | bytes 24580
  516.9 6.4 %copy-start.33 = (f32[2,16,1,64]{3,2,0,1:T(1,128)S(1)}, f32[2,16,1,64]{3,2,0,1:T(1,128)}, u32[]{:S(2)}) copy-start(f32[2,16,1,64]{3,2,0,1:T(1,128)} %copy.128) | copy-start | bytes 24580
  518.6 4.8 copy-start.38
  518.6 4.8 copy-start.39
  518.6 4.8 copy-start.42
  518.6 4.8 copy-start.43
  (20 other events, 67.5 us)

commit v3 on v2

v3 whole, which is shorter than its diff:
```python
import functools

import jax
import jax.numpy as jnp
from jax import lax
from jax.experimental import pallas as pl
from jax.experimental.pallas import tpu as pltpu
from jax.sharding import PartitionSpec as P

H = 16
HD = 64
BLK = 256
STEP = 10
PAIR = 2 * HD

norm_eps = 1e-05
adam_eps = 1e-08
group_heads = 4
score_scale = 0.125 * 1.4426950408889634
gelu_root = 0.7978845608028654
gelu_cubic = 0.044715
low = jnp.bfloat16
axes = ("ctx", "wshard")
small_cost = pl.CostEstimate(flops=1024, bytes_accessed=1024, transcendentals=0)


def nt(left_side, right_side):
    return lax.dot_general(
        left_side, right_side, (((1,), (1,)), ((), ())), preferred_element_type=jnp.float32
    )


def nn(left_side, right_side):
    return jnp.dot(left_side, right_side, preferred_element_type=jnp.float32)


def outer_sum(left_side, right_side):
    return lax.dot_general(
        left_side, right_side, (((0,), (0,)), ((), ())), preferred_element_type=jnp.float32
    )


def block_rows(block):
    return pl.ds(block * BLK, BLK)


def thirds(ref):
    return [ref.at[:, pl.ds(part * PAIR, PAIR)] for part in range(3)]


def attend_pair(blocks, projected, o_ref, lse_ref, between):
    q_ref, k_ref, v_ref = thirds(projected)
    lane = lax.broadcasted_iota(jnp.int32, (1, PAIR), 1)
    masks = [lane < HD, lane >= HD]
    for i in range(blocks):
        between(i)
        rows = block_rows(i)
        queries = q_ref[rows, :]
        outs = []
        for h in range(2):
            masked = jnp.where(masks[h], queries, jnp.zeros_like(queries))
            scores = [nt(masked, k_ref[block_rows(j), :]) * score_scale for j in range(i + 1)]
            top = scores[0]
            for score in scores[1:]:
                top = jnp.maximum(top, score)
            top = jnp.max(top, axis=1, keepdims=True)
            weights = [jnp.exp2(score - top) for score in scores]
            total = weights[0]
            for weight in weights[1:]:
                total = total + weight
            total = jnp.sum(total, axis=1, keepdims=True)
            mixed = nn(weights[0].astype(low), v_ref[block_rows(0), :])
            for j in range(1, i + 1):
                mixed = mixed + nn(weights[j].astype(low), v_ref[block_rows(j), :])
            outs.append(mixed * (1.0 / total))
            logsum = jnp.broadcast_to(top + jnp.log2(total), (BLK, PAIR))
            lse_ref[h : h + 1, rows] = jnp.transpose(logsum)[0:1, :]
        o_ref[rows, :] = jnp.where(masks[0], outs[0], outs[1]).astype(o_ref.dtype)


def attend_back_pair(
    blocks, projected, do_ref, lse_ref, back_ref, turned, key_sum, value_sum, between
):
    q_ref, k_ref, v_ref = thirds(projected)
    dq_ref, dk_ref, dv_ref = thirds(back_ref)
    lane = lax.broadcasted_iota(jnp.int32, (1, PAIR), 1)
    masks = [lane < HD, lane >= HD]
    for j in range(blocks):
        turned[j] = jnp.transpose(k_ref[block_rows(j), :])
    for i in range(blocks):
        between(i)
        rows = block_rows(i)
        queries, upstream = q_ref[rows, :], do_ref[rows, :]
        query_grads = []
        for h in range(2):
            masked = jnp.where(masks[h], queries, jnp.zeros_like(queries))
            pulled = jnp.where(masks[h], upstream, jnp.zeros_like(upstream))
            logsum = lse_ref[h : h + 1, rows]
            weights, pulls, inner = [], [], None
            for j in range(i + 1):
                weight = jnp.exp2(nt(k_ref[block_rows(j), :], masked) * score_scale - logsum)
                pull = nt(v_ref[block_rows(j), :], pulled)
                along = jnp.sum(weight * pull, axis=0, keepdims=True)
                inner = along if inner is None else inner + along
                weights.append(weight)
                pulls.append(pull)
            query_grad = None
            for j in range(i + 1):
                score_grad = (weights[j] * (pulls[j] - inner)).astype(low)
                value_grad = nn(weights[j].astype(low), pulled)
                key_grad = nn(score_grad, masked)
                if i == j and h == 0:
                    value_sum[j] = value_grad
                    key_sum[j] = key_grad
                else:
                    value_sum[j] += value_grad
                    key_sum[j] += key_grad
                piece = nn(turned[j, h * HD : (h + 1) * HD, :], score_grad)
                query_grad = piece if query_grad is None else query_grad + piece
            query_grads.append(query_grad)
        joined = jnp.transpose(jnp.concatenate(query_grads, axis=0))
        dq_ref[rows, :] = (joined * 0.125).astype(dq_ref.dtype)
    for j in range(blocks):
        dk_ref[block_rows(j), :] = (key_sum[j] * 0.125).astype(dk_ref.dtype)
        dv_ref[block_rows(j), :] = value_sum[j].astype(dv_ref.dtype)


def hooks(step, schedule):
    def between(block):
        for when, where, action in schedule:
            if where == block:
                pl.when(step == when)(action)

    return between


any_place = pl.BlockSpec(memory_space=pl.ANY)
whole_vmem = pl.BlockSpec(memory_space=pltpu.VMEM)


MESH = pl.DeviceIdType.MESH


class Spot:
    def __init__(self, sizes):
        self.sizes = sizes
        ctx, shard = lax.axis_index("ctx"), lax.axis_index("wshard")
        self.c = ctx
        self.k = shard % 2
        self.y = (shard // 2) % 2
        self.z = shard // 4

    def device(self, name, by=1):
        c, z, y, k = self.c, self.z, self.y, self.k
        if name == "c":
            c = 1 - c
        if name == "y":
            y = 1 - y
        if name == "k":
            k = 1 - k
        if name == "z":
            z = (z + by) % self.sizes["z"]
        return (c, (z * 2 + y) * 2 + k)

    def meet(self, names):
        barrier = pltpu.get_barrier_semaphore()
        partners = []
        for name in names:
            for by in range(1, self.sizes[name]):
                partners.append(self.device(name, by))
        for partner in partners:
            pl.semaphore_signal(barrier, inc=1, device_id=partner, device_id_type=MESH)
        pl.semaphore_wait(barrier, len(partners))


class Mover:
    def __init__(self, spot, sems):
        self.spot, self.sems, self.count = spot, sems, 0

    def copy(self, source, target, name, by=1):
        number = self.count
        self.count += 1
        return pltpu.make_async_remote_copy(
            src_ref=source,
            dst_ref=target,
            send_sem=self.sems.at[0, number],
            recv_sem=self.sems.at[1, number],
            device_id=self.spot.device(name, by),
            device_id_type=MESH,
        )

    def local(self, source, target):
        number = self.count
        self.count += 1
        return pltpu.make_async_copy(source, target, self.sems.at[0, number])


class Refs:
    def __init__(self, refs):
        self.refs = list(refs)

    def take(self, count):
        taken, self.refs = self.refs[:count], self.refs[count:]
        return taken


def start(copies):
    for copy in copies:
        copy.start()


def wait(copies):
    for copy in copies:
        copy.wait()


def span(first, size):
    return pl.ds(pl.multiple_of(first, 128), size)


class Deep:
    def __init__(self, mover, quad):
        z = mover.spot.z
        self.copies = [
            mover.copy(quad.at[z], quad.at[z], "z", by) for by in range(1, mover.spot.sizes["z"])
        ]


def first_rows(mover, halves, quad):
    spot = mover.spot
    rows = halves.shape[1]
    block = quad.at[spot.z, pl.ds(pl.multiple_of(spot.k * rows, rows), rows)]
    return [
        mover.local(halves.at[spot.k], block),
        mover.copy(halves.at[1 - spot.k], block, "k"),
    ]


class Near:
    def __init__(self, mover, quad, half, offset, cut, core=True):
        spot = mover.spot
        c, z, y = spot.c, spot.z, spot.y
        width = quad.shape[-1]
        every = slice(None)

        def part(ci, yi, first, size):
            return half.at[ci, every, yi, :, span(offset + first, size)]

        self.near, self.far = [mover.local(quad, part(c, y, 0, width))], []
        for first, size, one, two in ((0, cut, "c", "y"), (cut, width - cut, "y", "c")):
            if size == 0:
                continue
            source = quad.at[every, every, pl.ds(first, size)]
            self.near.append(mover.copy(source, part(c, y, first, size), one))
            self.near.append(mover.copy(source, part(c, y, first, size), two))
            block = part(1 - c if one == "c" else c, 1 - y if one == "y" else y, first, size)
            self.far.append(mover.copy(block, block, two))
        self.core = [[], [], []]
        if core:
            self.core[0].append(mover.copy(quad, part(c, y, 0, width), "k"))
            for stage, ci, yi in ((1, 1 - c, y), (1, c, 1 - y), (2, 1 - c, 1 - y)):
                block = part(ci, yi, 0, width)
                self.core[stage].append(mover.copy(block, block, "k"))

    def close(self):
        wait(self.far)
        start(self.core[2])

    def close_core(self):
        for stage in self.core:
            wait(stage)


class ReduceNear:
    def __init__(self, mover, mine, theirs, cut, quad, scratch):
        self.spot = spot = mover.spot
        self.cut, self.quad = cut, quad
        self.total, self.other, self.by_y, self.by_c, self.then_c, self.then_y = scratch
        self.width = width = self.total.shape[-1]
        c, y = spot.c, spot.y
        every, left, right = slice(None), pl.ds(0, cut), pl.ds(cut, width - cut)
        total = self.total
        self.first = [mover.copy(theirs, self.other, "k")]
        if mine is not None:
            self.first.append(mover.local(mine, total))
        self.near = [
            mover.copy(total.at[every, every, 1 - y, every, left], self.by_y, "y"),
            mover.copy(total.at[1 - c, every, every, every, right], self.by_c, "c"),
        ]
        self.far = [
            mover.copy(total.at[1 - c, every, y, every, left], self.then_c, "c"),
            mover.copy(total.at[c, every, 1 - y, every, right], self.then_y, "y"),
        ]

    @staticmethod
    def scratch(sizes, rows, width, cut):
        c, z, y = sizes["c"], sizes["z"], sizes["y"]
        shapes = [
            (c, z, y, rows, width),
            (c, z, y, rows, width),
            (c, z, rows, cut),
            (z, y, rows, width - cut),
            (z, rows, cut),
            (z, rows, width - cut),
        ]
        return [pltpu.VMEM(shape, low) for shape in shapes]

    def add(self, where, extra):
        total = self.total[where].astype(jnp.float32) + extra.astype(jnp.float32)
        return total.astype(low)

    def go_near(self):
        wait(self.first)
        sizes = self.spot.sizes
        for c in range(sizes["c"]):
            for y in range(sizes["y"]):

                @pl.loop(0, sizes["z"])
                def _(z):
                    self.total[c, z, y] = self.add((c, z, y), self.other[c, z, y])

        start(self.near)

    def go_far(self):
        wait(self.near)
        spot, cut = self.spot, self.cut
        left, right = pl.ds(0, cut), pl.ds(cut, self.width - cut)

        @pl.loop(0, spot.sizes["z"])
        def _(z):
            for c in range(spot.sizes["c"]):
                where = (c, z, spot.y, slice(None), left)
                self.total[where] = self.add(where, self.by_y[c, z])
            for y in range(spot.sizes["y"]):
                where = (spot.c, z, y, slice(None), right)
                self.total[where] = self.add(where, self.by_c[z, y])

        start(self.far)

    def close(self):
        wait(self.far)
        spot, cut = self.spot, self.cut
        left, right = pl.ds(0, cut), pl.ds(cut, self.width - cut)

        @pl.loop(0, spot.sizes["z"])
        def _(z):
            for columns, extra in ((left, self.then_c), (right, self.then_y)):
                where = (spot.c, z, spot.y, slice(None), columns)
                self.quad[z, :, columns] = self.add(where, extra[z])


class ReduceDeep:
    def __init__(self, mover, quad, by_z):
        self.spot = spot = mover.spot
        self.quad, self.by_z = quad, by_z
        depth = spot.sizes["z"]
        self.copies = [
            mover.copy(quad.at[(spot.z + by) % depth], by_z.at[by - 1], "z", by)
            for by in range(1, depth)
        ]

    def result(self):
        spot = self.spot
        value = self.quad[spot.z].astype(jnp.float32)
        for by in range(spot.sizes["z"] - 1):
            value = value + self.by_z[by].astype(jnp.float32)
        return value


class Finish:
    def __init__(self, mover, summed, arrived):
        self.k = mover.spot.k
        self.summed, self.arrived = summed, arrived
        rows = arrived.shape[0]
        self.rows = rows
        away = summed.at[pl.ds(pl.multiple_of((1 - self.k) * rows, rows), rows)]
        self.copies = [mover.copy(away, arrived, "k")]

    @staticmethod
    def scratch(rows, width):
        return [pltpu.VMEM((rows, width), jnp.float32), pltpu.VMEM((rows // 2, width), jnp.float32)]

    def write(self, out, columns=slice(None)):
        rows = self.rows
        kept = pl.ds(pl.multiple_of(self.k * rows, rows), rows)
        out[self.k, :, columns] = self.summed[kept, :]
        out[1 - self.k, :, columns] = self.arrived[...]


def core_halves(grad, k, width, first=0, size=None):
    size = width if size is None else size
    every = slice(None)
    return [
        grad.at[every, every, every, every, span(half * width + first, size)]
        for half in (k, 1 - k)
    ]


all_axes = ("k", "c", "y", "z")


def params(number, megabytes):
    return pltpu.CompilerParams(
        collective_id=number, has_side_effects=True, vmem_limit_bytes=megabytes << 20
    )


def low_shape(*dims):
    return jax.ShapeDtypeStruct(dims, low)


def begin_kernel(sizes, *refs):
    refs = Refs(refs)
    joint_halves, table, mixing_halves, expand_halves, shrink = refs.take(5)
    joint, tables, mixing_quad, expand_quad, shrink_quad = refs.take(5)
    joint_quad, table_quad, sems = refs.take(3)
    spot = Spot(sizes)
    mover = Mover(spot, sems)
    width = joint_halves.shape[2]
    joint_first = first_rows(mover, joint_halves, joint_quad)
    rows = table.shape[0]
    spread = table_quad.at[spot.z, pl.ds(pl.multiple_of(spot.k * rows, rows), rows)]
    joint_first += [mover.local(table, spread), mover.copy(table, spread, "k")]
    later_first = first_rows(mover, mixing_halves, mixing_quad)
    later_first += first_rows(mover, expand_halves, expand_quad)
    later_first += [mover.local(shrink, shrink_quad.at[spot.z])]
    now = Deep(mover, joint_quad).copies + Deep(mover, table_quad).copies
    later = [Deep(mover, quad).copies for quad in (mixing_quad, shrink_quad, expand_quad)]
    job = Near(mover, joint_quad, joint, spot.k * width, width // 2)
    thin = Near(mover, table_quad, tables, 0, table.shape[1], core=False)
    spot.meet(all_axes)
    start(joint_first + later_first)
    wait(joint_first)
    start(now)
    wait(later_first)
    wait(now)
    start(thin.near + job.near + job.core[0])
    for copies in later:
        start(copies)
    wait(thin.near + job.near)
    start(thin.far + job.far + job.core[1])
    wait(thin.far)
    job.close()
    for copies in later:
        wait(copies)
    job.close_core()


def begin(sizes, joint_halves, table, mixing_halves, expand_halves, shrink):
    lead = (sizes["c"], sizes["z"], sizes["y"])
    depth, rows = sizes["z"], 2 * table.shape[0]
    width = joint_halves.shape[2]
    return pl.pallas_call(
        functools.partial(begin_kernel, sizes),
        in_specs=[whole_vmem] * 5,
        out_specs=[any_place] * 5,
        out_shape=[
            low_shape(*lead, rows, 2 * width),
            low_shape(*lead, rows, table.shape[1]),
            low_shape(depth, rows, mixing_halves.shape[2]),
            low_shape(depth, rows, expand_halves.shape[2]),
            low_shape(depth, *shrink.shape),
        ],
        scratch_shapes=[
            pltpu.VMEM((depth, rows, width), low),
            pltpu.VMEM((depth, rows, table.shape[1]), low),
            pltpu.SemaphoreType.DMA((2, 48)),
        ],
        compiler_params=params(1, 16),
        cost_estimate=small_cost,
        name="begin",
    )(joint_halves, table, mixing_halves, expand_halves, shrink)


def attend_kernel(sizes, blocks, *refs):
    refs = Refs(refs)
    projected, mixing_quad, expand_quad, shrink_quad, expand_halves, shrink = refs.take(6)
    o_ref, lse_ref, mixing, expand, shrunk, next_expand, next_shrink, sems = refs.take(8)
    spot = Spot(sizes)
    mover = Mover(spot, sems)
    k = spot.k
    half, grown, width = mixing_quad.shape[-1], expand_quad.shape[-1], shrink_quad.shape[-1]
    jobs = [
        Near(mover, mixing_quad, mixing, k * half, half // 2),
        Near(mover, shrink_quad, shrunk.at[k], 0, width // 2),
        Near(mover, expand_quad, expand, k * grown, grown // 2),
    ]
    next_first = first_rows(mover, expand_halves, next_expand)
    next_first += [mover.local(shrink, next_shrink.at[spot.z])]
    deep = Deep(mover, next_expand).copies + Deep(mover, next_shrink).copies

    def open_all():
        spot.meet(all_axes)
        start(next_first)
        for job in jobs:
            start(job.near + job.core[0])

    def next_deep():
        wait(next_first)
        start(deep)

    def far(*some):
        for job in some:
            wait(job.near)
            start(job.far + job.core[1])

    def close_all():
        for job in jobs:
            job.close()
        wait(deep)
        for job in jobs:
            job.close_core()

    step = pl.program_id(0)
    schedule = [
        (0, 0, open_all),
        (1, 0, next_deep),
        (2, 2, lambda: far(jobs[0])),
        (4, 2, lambda: far(jobs[1])),
        (7, 0, lambda: far(jobs[2])),
    ]
    attend_pair(blocks, projected, o_ref, lse_ref, hooks(step, schedule))
    pl.when(step == pl.num_programs(0) - 1)(close_all)


def attend(sizes, blocks, projected, quads, halves, shrink):
    tokens, width = projected.shape[0], projected.shape[1] // 3
    pairs = width // PAIR
    lead = (sizes["c"], sizes["z"], sizes["y"])
    depth, rows, half = quads[0].shape
    grown, full = quads[1].shape[2], quads[2].shape[2]
    return pl.pallas_call(
        functools.partial(attend_kernel, sizes, blocks),
        grid=(pairs,),
        in_specs=[pl.BlockSpec((tokens, 3 * PAIR), lambda g: (0, g))] + [whole_vmem] * 5,
        out_specs=[
            pl.BlockSpec((tokens, PAIR), lambda g: (0, g)),
            pl.BlockSpec((None, 8, tokens), lambda g: (g, 0, 0)),
        ]
        + [any_place] * 5,
        out_shape=[
            low_shape(tokens, width),
            jax.ShapeDtypeStruct((pairs, 8, tokens), jnp.float32),
            low_shape(*lead, rows, 2 * half),
            low_shape(*lead, rows, 2 * grown),
            low_shape(2, *lead, rows, full),
            low_shape(depth, rows, grown),
            low_shape(depth, rows, full),
        ],
        scratch_shapes=[pltpu.SemaphoreType.DMA((2, 64))],
        compiler_params=params(2, 48),
        cost_estimate=small_cost,
        name="attend",
    )(projected, *quads, halves, shrink)


def mlp_tile(first, rows_step, c_ref, dy_ref, we_ref, ws_ref, be_ref, before, outs, scratch, between):
    y_ref, dc_ref, gwe_ref, gws_ref, gbe_ref = outs
    turned, act_all, du_all = scratch[:3]
    tokens = c_ref.shape[0]

    @pl.when(pl.program_id(0) == 0)
    def _():
        turned[...] = jnp.transpose(c_ref[...])
        if first:
            y_ref[...] = jnp.zeros_like(y_ref)
            dc_ref[...] = jnp.zeros_like(dc_ref)
        else:
            sem = scratch[3]
            copies = [
                pltpu.make_async_copy(before[0], y_ref, sem.at[0]),
                pltpu.make_async_copy(before[1], dc_ref, sem.at[1]),
            ]
            start(copies)
            wait(copies)

    we, ws = we_ref[...], ws_ref[...]
    total = None
    for part in range(tokens // rows_step):
        between(part)
        rows = pl.ds(part * rows_step, rows_step)
        hidden = nn(c_ref[rows, :], we) + be_ref[...]
        squared = hidden * hidden
        bent = jnp.tanh(gelu_root * hidden * (1.0 + gelu_cubic * squared))
        gate = 0.5 + 0.5 * bent
        act = (hidden * gate).astype(low)
        slope = gate + (0.5 * gelu_root) * hidden * (1.0 - bent * bent) * (
            1.0 + (3 * gelu_cubic) * squared
        )
        du = (nt(dy_ref[rows, :], ws) * slope).astype(low)
        act_all[rows, :] = act
        du_all[rows, :] = du
        y_ref[rows, :] += nn(act, ws)
        dc_ref[rows, :] += nt(du, we)
        added = jnp.sum(du.astype(jnp.float32), axis=0, keepdims=True)
        total = added if total is None else total + added
    gbe_ref[...] = total
    gwe_ref[...] = nn(turned[...], du_all[...]).astype(gwe_ref.dtype)
    gws_ref[...] = outer_sum(act_all[...], dy_ref[...]).astype(gws_ref.dtype)


def mlp_parts(tokens, width, hidden, tile):
    whole = pl.BlockSpec((tokens, width), lambda t: (0, 0))
    down = pl.BlockSpec((width, tile), lambda t: (0, t))
    across = pl.BlockSpec((tile, width), lambda t: (t, 0))
    thin = pl.BlockSpec((1, tile), lambda t: (0, t))
    return (
        [whole, whole, down, across, thin],
        [whole, whole, down, across, thin],
        [
            jax.ShapeDtypeStruct((tokens, width), jnp.float32),
            jax.ShapeDtypeStruct((tokens, width), jnp.float32),
            low_shape(width, hidden),
            low_shape(hidden, width),
            jax.ShapeDtypeStruct((1, hidden), jnp.float32),
        ],
        [
            pltpu.VMEM((width, tokens), low),
            pltpu.VMEM((tokens, tile), low),
            pltpu.VMEM((tokens, tile), low),
        ],
    )


def mlp_plain_kernel(first, rows_step, *refs):
    refs = Refs(refs)
    inputs = refs.take(5)
    before = [] if first else refs.take(2)
    outs = refs.take(5)
    mlp_tile(first, rows_step, *inputs, before, outs, refs.refs, lambda part: None)


def mlp(c, dy, we, ws, be, before=(), tile=256, rows_step=256):
    in_specs, out_specs, out_shape, scratch = mlp_parts(*c.shape, we.shape[1], tile)
    if before:
        scratch = scratch + [pltpu.SemaphoreType.DMA((2,))]
    return pl.pallas_call(
        functools.partial(mlp_plain_kernel, not before, rows_step),
        grid=(we.shape[1] // tile,),
        in_specs=in_specs + [any_place] * len(before),
        out_specs=out_specs,
        out_shape=out_shape,
        scratch_shapes=scratch,
        compiler_params=pltpu.CompilerParams(vmem_limit_bytes=56 << 20),
        cost_estimate=small_cost,
        name="mlp",
    )(c, dy, we, ws, be, *before)


def mlp_gather_kernel(sizes, rows_step, *refs):
    refs = Refs(refs)
    inputs = refs.take(5)
    expand_quad, shrink_quad = refs.take(2)
    outs = refs.take(5)
    expand, shrunk = refs.take(2)
    scratch, (sems,) = refs.take(3), refs.take(1)
    spot = Spot(sizes)
    mover = Mover(spot, sems)
    grown, width = expand_quad.shape[-1], shrink_quad.shape[-1]
    jobs = [
        Near(mover, shrink_quad, shrunk.at[spot.k], 0, width // 2),
        Near(mover, expand_quad, expand, spot.k * grown, grown // 2),
    ]

    def open_all():
        spot.meet(all_axes)
        for job in jobs:
            start(job.near + job.core[0])

    def far(job):
        wait(job.near)
        start(job.far + job.core[1])

    def close_all():
        jobs[1].close()
        for job in jobs:
            job.close_core()

    step = pl.program_id(0)
    schedule = [
        (0, 0, open_all),
        (3, 0, lambda: far(jobs[0])),
        (5, 2, lambda: far(jobs[1])),
        (7, 0, jobs[0].close),
    ]
    mlp_tile(True, rows_step, *inputs, [], outs, scratch, hooks(step, schedule))
    pl.when(step == pl.num_programs(0) - 1)(close_all)


def mlp_gather(sizes, c, dy, we, ws, be, quads, tile=256, rows_step=256):
    in_specs, out_specs, out_shape, scratch = mlp_parts(*c.shape, we.shape[1], tile)
    lead = (sizes["c"], sizes["z"], sizes["y"])
    rows, grown, full = quads[0].shape[1], quads[0].shape[2], quads[1].shape[2]
    return pl.pallas_call(
        functools.partial(mlp_gather_kernel, sizes, rows_step),
        grid=(we.shape[1] // tile,),
        in_specs=in_specs + [whole_vmem] * 2,
        out_specs=out_specs + [any_place] * 2,
        out_shape=out_shape + [low_shape(*lead, rows, 2 * grown), low_shape(2, *lead, rows, full)],
        scratch_shapes=scratch + [pltpu.SemaphoreType.DMA((2, 32))],
        compiler_params=params(3, 56),
        cost_estimate=small_cost,
        name="mlp_gather",
    )(c, dy, we, ws, be, *quads)


def mlp_reduce_kernel(sizes, rows_step, *refs):
    refs = Refs(refs)
    inputs, before = refs.take(5), refs.take(2)
    expand, shrink = refs.take(2)
    outs = refs.take(5)
    expand_quad, shrink_quad = refs.take(2)
    scratch, (sems,) = refs.take(4), refs.take(1)
    spot = Spot(sizes)
    mover = Mover(spot, sems)
    grown, width = expand_quad.shape[-1], shrink_quad.shape[-1]
    jobs = [
        ReduceNear(
            mover, shrink.at[spot.k], shrink.at[1 - spot.k], width // 2, shrink_quad, refs.take(6)
        ),
        ReduceNear(
            mover, *core_halves(expand, spot.k, grown), grown // 2, expand_quad, refs.take(6)
        ),
    ]

    def open_all():
        spot.meet(all_axes)
        for job in jobs:
            start(job.first)

    def close_all():
        jobs[1].close()

    step = pl.program_id(0)
    schedule = [
        (0, 0, open_all),
        (1, 1, jobs[0].go_near),
        (2, 1, jobs[1].go_near),
        (4, 0, jobs[0].go_far),
        (6, 1, jobs[1].go_far),
        (7, 1, jobs[0].close),
    ]
    mlp_tile(False, rows_step, *inputs, before, outs, scratch, hooks(step, schedule))
    pl.when(step == pl.num_programs(0) - 1)(close_all)


def mlp_reduce(sizes, c, dy, we, ws, be, before, grads, tile=256, rows_step=256):
    in_specs, out_specs, out_shape, scratch = mlp_parts(*c.shape, we.shape[1], tile)
    expand, shrink = grads
    depth, rows = sizes["z"], expand.shape[3]
    grown, full = expand.shape[-1] // 2, shrink.shape[-1]
    scratch = scratch + [pltpu.SemaphoreType.DMA((2,)), pltpu.SemaphoreType.DMA((2, 16))]
    for columns in (full, grown):
        scratch += ReduceNear.scratch(sizes, rows, columns, columns // 2)
    return pl.pallas_call(
        functools.partial(mlp_reduce_kernel, sizes, rows_step),
        grid=(we.shape[1] // tile,),
        in_specs=in_specs + [any_place] * 4,
        out_specs=out_specs + [whole_vmem] * 2,
        out_shape=out_shape + [low_shape(depth, rows, grown), low_shape(depth, rows, full)],
        scratch_shapes=scratch,
        compiler_params=params(4, 60),
        cost_estimate=small_cost,
        name="mlp_reduce",
    )(c, dy, we, ws, be, *before, *grads)


def attend_back_kernel(sizes, blocks, *refs):
    refs = Refs(refs)
    projected, upstream, lse_ref, mixing, expand, shrink, done_expand, done_shrink = refs.take(8)
    back_ref, mixing_quad, expand_quad, shrink_quad, expand_out, shrink_out = refs.take(6)
    turned, key_sum, value_sum, sems = refs.take(4)
    spot = Spot(sizes)
    mover = Mover(spot, sems)
    k = spot.k
    half, grown, width = mixing_quad.shape[-1], expand_quad.shape[-1], shrink_quad.shape[-1]
    jobs = [
        ReduceNear(mover, shrink.at[k], shrink.at[1 - k], width // 2, shrink_quad, refs.take(6)),
        ReduceNear(mover, *core_halves(expand, k, grown), grown // 2, expand_quad, refs.take(6)),
        ReduceNear(mover, *core_halves(mixing, k, half), half // 2, mixing_quad, refs.take(6)),
    ]
    deep = [
        ReduceDeep(mover, done_expand, *refs.take(1)),
        ReduceDeep(mover, done_shrink, *refs.take(1)),
    ]
    ending = Finish(mover, *refs.take(2))

    def open_all():
        spot.meet(all_axes)
        for job in jobs:
            start(job.first)
        for job in deep:
            start(job.copies)

    def finish():
        wait(deep[0].copies)
        ending.summed[...] = deep[0].result()
        start(ending.copies)
        wait(deep[1].copies)
        shrink_out[...] = deep[1].result()

    def close_all():
        wait(ending.copies)
        ending.write(expand_out)
        jobs[1].close()
        jobs[2].close()

    step = pl.program_id(0)
    schedule = [
        (0, 0, open_all),
        (1, 1, jobs[0].go_near),
        (2, 1, jobs[1].go_near),
        (2, 3, jobs[2].go_near),
        (4, 0, jobs[0].go_far),
        (5, 3, finish),
        (6, 2, jobs[1].go_far),
        (7, 2, jobs[2].go_far),
        (7, 3, jobs[0].close),
    ]
    attend_back_pair(
        blocks, projected, upstream, lse_ref, back_ref, turned, key_sum, value_sum,
        hooks(step, schedule),
    )
    pl.when(step == pl.num_programs(0) - 1)(close_all)


def attend_back(sizes, blocks, projected, upstream, lse, grads, quads):
    tokens, width = upstream.shape
    pairs = width // PAIR
    mixing, expand, shrink = grads
    depth, rows = sizes["z"], mixing.shape[3]
    half, grown, full = mixing.shape[-1] // 2, expand.shape[-1] // 2, shrink.shape[-1]
    triple = pl.BlockSpec((tokens, 3 * PAIR), lambda g: (0, g))
    scratch = [
        pltpu.VMEM((blocks, PAIR, BLK), low),
        pltpu.VMEM((blocks, BLK, PAIR), jnp.float32),
        pltpu.VMEM((blocks, BLK, PAIR), jnp.float32),
        pltpu.SemaphoreType.DMA((2, 32)),
    ]
    for columns in (full, grown, half):
        scratch += ReduceNear.scratch(sizes, rows, columns, columns // 2)
    for columns in (grown, full):
        scratch += [pltpu.VMEM((depth - 1, rows, columns), low)]
    scratch += Finish.scratch(rows, grown)
    return pl.pallas_call(
        functools.partial(attend_back_kernel, sizes, blocks),
        grid=(pairs,),
        in_specs=[
            triple,
            pl.BlockSpec((tokens, PAIR), lambda g: (0, g)),
            pl.BlockSpec((None, 8, tokens), lambda g: (g, 0, 0)),
        ]
        + [any_place] * 3
        + [whole_vmem] * 2,
        out_specs=[triple] + [whole_vmem] * 5,
        out_shape=[
            low_shape(*projected.shape),
            low_shape(depth, rows, half),
            low_shape(depth, rows, grown),
            low_shape(depth, rows, full),
            jax.ShapeDtypeStruct((2, rows // 2, grown), jnp.float32),
            jax.ShapeDtypeStruct((rows, full), jnp.float32),
        ],
        scratch_shapes=scratch,
        compiler_params=params(5, 56),
        cost_estimate=small_cost,
        name="attend_back",
    )(projected, upstream, lse, *grads, *quads)


def normal_rows(rows):
    centered = rows - jnp.mean(rows, axis=-1, keepdims=True)
    inverse = lax.rsqrt(jnp.mean(centered * centered, axis=-1, keepdims=True) + norm_eps)
    return centered * inverse, inverse


def norm_pull(upstream, normal, inverse, gain):
    scaled = upstream * gain
    inner = jnp.mean(scaled, axis=-1, keepdims=True)
    along = jnp.mean(scaled * normal, axis=-1, keepdims=True)
    return inverse * (scaled - inner - normal * along)


def end_kernel(sizes, *refs):
    refs = Refs(refs)
    back_ref, back_far, low_far, joint_far, rows_far, middle_far = refs.take(6)
    gain_ref, vector, mixing_quad, expand_quad, shrink_quad = refs.take(5)
    out, vector_out, mixing_out, expand_out, shrink_out, kept, arrived_rows = refs.take(7)
    sems, steps, arrived = refs.take(3)
    grads, low_rows, turned, joint, rows_in, middle, sent = refs.take(7)
    spot = Spot(sizes)
    mover = Mover(spot, sems)
    width = joint.shape[-1] // 2
    part = width // 2
    tile = 256
    loads = [
        mover.local(far, near)
        for far, near in (
            (back_far, grads),
            (low_far, low_rows),
            (joint_far, joint),
            (rows_far, rows_in),
            (middle_far, middle),
        )
    ]
    jobs, deeps, ends, others_half = [], [], [], []
    for number in range(2):
        theirs, quad = refs.take(2)
        others_half.append(theirs)
        jobs.append(ReduceNear(mover, None, theirs, part // 2, quad, refs.take(6)))
        deeps.append(ReduceDeep(mover, quad, *refs.take(1)))
        ends.append(Finish(mover, *refs.take(2)))
    others = [
        ReduceDeep(mover, quad, *refs.take(1))
        for quad in (mixing_quad, expand_quad, shrink_quad)
    ]
    other_ends = [Finish(mover, *refs.take(2)) for _ in range(2)]
    hops = [
        mover.copy(steps.at[number], arrived.at[number], name)
        for number, name in enumerate(("k", "c", "y"))
    ]
    spread = [
        mover.copy(steps.at[3], arrived.at[2 + by], "z", by) for by in range(1, sizes["z"])
    ]
    rows_copy = mover.copy(sent, arrived_rows, "c")

    def gradient(core, number, target):
        @pl.loop(0, part // tile)
        def _(t):
            columns = span(core * width + number * part + t * tile, tile)
            piece = nn(turned[...], grads[:, columns]).astype(low)
            target[..., span(t * tile, tile)] = piece.reshape(*target.shape[:-1], tile)

    sums = {}

    def pull_block(number):
        rows = block_rows(number)
        pulled = grads[rows, :]
        upstream = nt(pulled, joint[...])
        normal, inverse = normal_rows(rows_in[rows, :].astype(jnp.float32))
        middle[rows, :] += norm_pull(upstream, normal, inverse, gain_ref[...])
        for name, value in (
            ("gain", upstream * normal),
            ("shift", upstream),
            ("back", pulled.astype(jnp.float32)),
        ):
            value = jnp.sum(value, axis=0, keepdims=True)
            sums[name] = sums[name] + value if name in sums else value

    def stored_block(place):
        number = jnp.full((1, middle.shape[1]), back_ref[place], jnp.int32)
        value = middle[block_rows(0), :]
        for other in range(1, middle.shape[0] // BLK):
            value = jnp.where(number == other, middle[block_rows(other), :], value)
        return value

    def hop(number):
        wait([hops[number]])
        steps[number + 1] = steps[number] + arrived[number]
        start([hops[number + 1]] if number < 2 else spread)

    start(loads)
    spot.meet(all_axes)
    for job in others:
        start(job.copies)
    wait(loads[:2])
    turned[...] = jnp.transpose(low_rows[...])
    for number, job in enumerate(jobs):
        gradient(1 - spot.k, number, others_half[number])
        start(job.first)
        gradient(spot.k, number, job.total)
        job.go_near()
    wait(loads[2:])
    pull_block(0)
    pull_block(1)
    jobs[0].go_far()
    pull_block(2)
    jobs[1].go_far()
    pull_block(3)
    for place in range(2):
        sent[block_rows(place), :] = stored_block(2 + place).astype(low)
    start([rows_copy])
    for place in range(2):
        kept[block_rows(place), :] = stored_block(place)
    steps[0] = vector[...]
    steps[0, 0:1, :] = sums["gain"]
    steps[0, 1:2, :] = sums["shift"]
    for pair in range(H // 2):
        for row, third in ((2, 0), (3, 2)):
            steps[0, row : row + 1, pair * PAIR : (pair + 1) * PAIR] = sums["back"][
                :, (3 * pair + third) * PAIR : (3 * pair + third + 1) * PAIR
            ]
    start(hops[:1])
    jobs[0].close()
    start(deeps[0].copies)
    hop(0)
    for job, ending in zip(others, other_ends):
        wait(job.copies)
        ending.summed[...] = job.result()
        start(ending.copies)
    wait(others[2].copies)
    shrink_out[...] = others[2].result()
    jobs[1].close()
    start(deeps[1].copies)
    hop(1)
    hop(2)
    for ending, target in zip(other_ends, (mixing_out, expand_out)):
        wait(ending.copies)
        ending.write(target)
    for deep, ending in zip(deeps, ends):
        wait(deep.copies)
        ending.summed[...] = deep.result()
        start(ending.copies)
    wait(spread)
    total = steps[3]
    for by in range(1, sizes["z"]):
        total = total + arrived[2 + by]
    vector_out[...] = total
    for number, ending in enumerate(ends):
        wait(ending.copies)
        ending.write(out, pl.ds(number * part, part))
    wait([rows_copy])


def end(sizes, back, joint_back, first_low, joint, rows_in, middle_grad, gain, vector, quads):
    tokens, model = rows_in.shape
    width = joint.shape[1] // 2
    lead = (sizes["c"], sizes["z"], sizes["y"])
    depth = sizes["z"]
    rows = model // (lead[0] * lead[1] * lead[2])
    part = width // 2
    half, grown, full = [quad.shape[-1] for quad in quads]
    scratch = [
        pltpu.SemaphoreType.DMA((2, 48)),
        pltpu.VMEM((4, *vector.shape), jnp.float32),
        pltpu.VMEM((2 + depth, *vector.shape), jnp.float32),
        pltpu.VMEM(joint_back.shape, low),
        pltpu.VMEM(first_low.shape, low),
        pltpu.VMEM(first_low.shape[::-1], low),
        pltpu.VMEM(joint.shape, low),
        pltpu.VMEM(rows_in.shape, low),
        pltpu.VMEM(middle_grad.shape, jnp.float32),
        pltpu.VMEM((tokens // 2, model), low),
    ]
    for number in range(2):
        scratch += [pltpu.VMEM((*lead, rows, part), low), pltpu.VMEM((depth, rows, part), low)]
        scratch += ReduceNear.scratch(sizes, rows, part, part // 2)
        scratch += [pltpu.VMEM((depth - 1, rows, part), low)]
        scratch += Finish.scratch(rows, part)
    scratch += [pltpu.VMEM((depth - 1, rows, columns), low) for columns in (half, grown, full)]
    for columns in (half, grown):
        scratch += Finish.scratch(rows, columns)
    own = rows // 2
    shapes = [(2, own, width), vector.shape, (2, own, half), (2, own, grown), (rows, full)]
    shapes.append((tokens // 2, model))
    return pl.pallas_call(
        functools.partial(end_kernel, sizes),
        in_specs=[pl.BlockSpec(memory_space=pltpu.SMEM)] + [any_place] * 5 + [whole_vmem] * 5,
        out_specs=[whole_vmem] * 6 + [any_place],
        out_shape=[jax.ShapeDtypeStruct(shape, jnp.float32) for shape in shapes]
        + [low_shape(tokens // 2, model)],
        scratch_shapes=scratch,
        compiler_params=params(6, 60),
        cost_estimate=small_cost,
        name="end",
    )(back, joint_back, first_low, joint, rows_in, middle_grad, gain, vector, *quads)


def give_kernel(back_ref, middle_ref, result_ref, shift_ref, kept_ref, sent_ref):
    value = (middle_ref[...] + result_ref[...] + shift_ref[...]).astype(low)
    step = pl.program_id(0)

    @pl.when(step < 2)
    def _():
        kept_ref[...] = value

    @pl.when(step >= 2)
    def _():
        sent_ref[...] = value


def give(back, middle, result, shift):
    width = middle.shape[1]
    block = pl.BlockSpec((BLK, width), lambda p, back: (back[p], 0))
    return pl.pallas_call(
        give_kernel,
        grid_spec=pltpu.PrefetchScalarGridSpec(
            num_scalar_prefetch=1,
            grid=(back.shape[0],),
            in_specs=[block, block, pl.BlockSpec((1, width), lambda p, back: (0, 0))],
            out_specs=[
                pl.BlockSpec((BLK, width), lambda p, back: (jnp.minimum(p, 1), 0)),
                pl.BlockSpec((BLK, width), lambda p, back: (jnp.maximum(p - 2, 0), 0)),
            ],
        ),
        out_shape=[low_shape(2 * BLK, width)] * 2,
        cost_estimate=small_cost,
        name="give",
    )(back, middle, result, shift)


def take_kernel(place_ref, kept_ref, arrived_ref, out_ref):
    here = place_ref[pl.program_id(0)] < 2

    @pl.when(here)
    def _():
        out_ref[...] = kept_ref[...]

    @pl.when(jnp.logical_not(here))
    def _():
        out_ref[...] = arrived_ref[...]


def take(place, kept, arrived):
    width = kept.shape[1]
    return pl.pallas_call(
        take_kernel,
        grid_spec=pltpu.PrefetchScalarGridSpec(
            num_scalar_prefetch=1,
            grid=(place.shape[0],),
            in_specs=[
                pl.BlockSpec((BLK, width), lambda i, place: (jnp.minimum(place[i], 1), 0)),
                pl.BlockSpec((BLK, width), lambda i, place: (jnp.maximum(place[i] - 2, 0), 0)),
            ],
            out_specs=pl.BlockSpec((BLK, width), lambda i, place: (i, 0)),
        ),
        out_shape=low_shape(4 * BLK, width),
        cost_estimate=small_cost,
        name="take",
    )(place, kept, arrived)


def last_kernel(ctx_ref, *refs):
    refs = Refs(refs)
    joint_part, mixing_part, expand_a, expand_b, shrink_a, shrink_b = refs.take(6)
    kept_grad, far_grad, kept_out, far_out = refs.take(4)
    states = [refs.take(3) for _ in range(4)]
    grad_out, block_out = refs.take(2)
    news = [refs.take(4) for _ in range(4)]
    here = ctx_ref[0]
    grad_out[here] = kept_grad[...]
    grad_out[1 - here] = far_grad[...].astype(jnp.float32)
    block_out[here] = kept_out[...]
    block_out[1 - here] = far_out[...]

    def update(number, where, gradient):
        weight, first, second = [ref[where] for ref in states[number]]
        results = adam_update(weight, first, second, gradient, 0.05, 0.1)
        for ref, value in zip(news[number], (*results, results[0].astype(low))):
            ref[where] = value

    every = slice(None)
    pairs = joint_part.shape[2] // (3 * PAIR)
    for core in range(2):
        for pair in range(pairs):
            for third in range(3):
                first = ((third * 2 + core) * pairs + pair) * PAIR
                source = (pair * 3 + third) * PAIR
                update(
                    0,
                    (every, pl.ds(first, PAIR)),
                    joint_part[core, :, source : source + PAIR],
                )
        half = mixing_part.shape[2]
        update(1, (every, pl.ds(core * half, half)), mixing_part[core])
        lane = lax.broadcasted_iota(jnp.int32, (1, PAIR), 1)
        for chip in range(0, expand_a.shape[2] // HD, 2):
            a = expand_a[core, :, chip * HD : chip * HD + PAIR]
            b = expand_b[core, :, chip * HD : chip * HD + PAIR]
            even = jnp.where(lane < HD, a, pltpu.roll(b, HD, 1))
            odd = jnp.where(lane < HD, pltpu.roll(a, HD, 1), b)
            for number, value in ((chip, even), (chip + 1, odd)):
                update(2, (every, pl.ds((number * 2 + core) * PAIR, PAIR)), value)
    rows = shrink_a.shape[0]
    update(3, (pl.ds(0, rows), every), shrink_a[...])
    update(3, (pl.ds(rows, rows), every), shrink_b[...])


def last(ctx, parts, kept_grad, far_grad, kept_out, far_out, states):
    shapes = [jax.ShapeDtypeStruct((2, *kept_grad.shape), jnp.float32), low_shape(2, *kept_out.shape)]
    for weight, _, _ in states:
        shapes += [jax.ShapeDtypeStruct(weight.shape, jnp.float32)] * 3
        shapes.append(low_shape(*weight.shape))
    flat = [array for state in states for array in state]
    return pl.pallas_call(
        last_kernel,
        in_specs=[pl.BlockSpec(memory_space=pltpu.SMEM)] + [whole_vmem] * (10 + len(flat)),
        out_specs=[whole_vmem] * len(shapes),
        out_shape=shapes,
        compiler_params=pltpu.CompilerParams(vmem_limit_bytes=56 << 20),
        cost_estimate=small_cost,
        name="last",
    )(ctx, *parts, kept_grad, far_grad, kept_out, far_out, *flat)


def layer_norm(values, gain_row, shift_row):
    centered = values - jnp.mean(values, axis=-1, keepdims=True)
    variance = jnp.mean(centered * centered, axis=-1, keepdims=True)
    inverse = lax.rsqrt(variance + norm_eps)
    normal_part = centered * inverse
    return (normal_part * gain_row + shift_row, normal_part, inverse)


def norm_back(upstream, normal_part, inverse, gain_row):
    scaled = upstream * gain_row
    inner_sum = jnp.mean(scaled, axis=-1, keepdims=True)
    along_sum = jnp.mean(scaled * normal_part, axis=-1, keepdims=True)
    values_grad = inverse * (scaled - inner_sum - normal_part * along_sum)
    return (values_grad, jnp.sum(upstream * normal_part, axis=0), jnp.sum(upstream, axis=0))


def adam_update(weight, moment_one, moment_two, gradient, step_rate, decay_rate):
    first_new = 0.5 * moment_one + 0.5 * gradient
    second_new = 0.5 * moment_two + 0.5 * gradient * gradient
    correct = 1.0 - 0.5**STEP
    direction = first_new / correct / (jnp.sqrt(second_new / correct) + adam_eps)
    updated = weight - step_rate * (direction + decay_rate * weight)
    return (updated, first_new, second_new)


def to_groups(matrix):
    row_count = matrix.shape[0]
    return matrix.reshape(row_count, H // group_heads, group_heads, HD).transpose(1, 0, 2, 3)


def from_groups(stacked):
    return stacked.transpose(1, 0, 2, 3).reshape(stacked.shape[1], H * HD)


def tile_scores(queries, key_rows, allowed):
    products = jnp.einsum("rgd,lgd->grl", queries, key_rows, preferred_element_type=jnp.float32)
    return jnp.where(allowed[None], products * 0.125, -1e30)


def tile_forward(queries, key_rows, value_rows, allowed):
    scores = tile_scores(queries, key_rows, allowed)
    largest = jnp.max(scores, axis=-1, keepdims=True)
    exponent = jnp.exp(scores - largest)
    row_total = jnp.sum(exponent, axis=-1, keepdims=True)
    weights = (exponent / row_total).astype(low)
    mixed = jnp.einsum("grl,lgd->rgd", weights, value_rows, preferred_element_type=jnp.float32)
    return (mixed, (largest + jnp.log(row_total))[..., 0])


def tile_backward(queries, key_rows, value_rows, allowed, logsum, upstream):
    scores = tile_scores(queries, key_rows, allowed)
    recomputed = jnp.exp(scores - logsum[..., None])
    value_grad = jnp.einsum(
        "grl,rgd->lgd", recomputed.astype(low), upstream, preferred_element_type=jnp.float32
    )
    weight_grad = jnp.einsum(
        "rgd,lgd->grl", upstream, value_rows, preferred_element_type=jnp.float32
    )
    inner_sum = jnp.sum(recomputed * weight_grad, axis=-1, keepdims=True)
    score_grad = (recomputed * (weight_grad - inner_sum)).astype(low)
    query_grad = (
        jnp.einsum("grl,lgd->rgd", score_grad, key_rows, preferred_element_type=jnp.float32) * 0.125
    )
    key_grad = (
        jnp.einsum("grl,rgd->lgd", score_grad, queries, preferred_element_type=jnp.float32) * 0.125
    )
    return (query_grad, key_grad, value_grad)


def spread_forward(queries, key_value, allowed):
    def one_sequence(pieces):
        queries, key_value, allowed = pieces
        width = queries.shape[1]
        mixed, logsum = lax.map(
            lambda triple: tile_forward(triple[0], triple[1], triple[2], allowed),
            (to_groups(queries), to_groups(key_value[:, :width]), to_groups(key_value[:, width:])),
        )
        return (from_groups(mixed), logsum)

    return lax.map(one_sequence, (queries, key_value, allowed))


def spread_backward(queries, key_value, allowed, logsum, upstream):
    def one_sequence(pieces):
        queries, key_value, allowed, logsum, upstream = pieces
        width = queries.shape[1]
        query_grad, key_grad, value_grad = lax.map(
            lambda member: tile_backward(
                member[0], member[1], member[2], allowed, member[3], member[4]
            ),
            (
                to_groups(queries),
                to_groups(key_value[:, :width]),
                to_groups(key_value[:, width:]),
                logsum,
                to_groups(upstream),
            ),
        )
        return (
            from_groups(query_grad),
            jnp.concatenate([from_groups(key_grad), from_groups(value_grad)], axis=1),
        )

    return lax.map(one_sequence, (queries, key_value, allowed, logsum, upstream))


class Slice:
    def __init__(self, ctx_size, wshard_size):
        rest = wshard_size // 2
        self.sizes = {"c": ctx_size, "z": 4, "y": rest // 4, "k": 2}

    def here(self):
        flat = lax.axis_index(axes)
        found = {}
        for name in ("k", "y", "z", "c"):
            found[name] = flat % self.sizes[name]
            flat = flat // self.sizes[name]
        return found

    def shift(self, value, name, by):
        pairs = []
        sizes = self.sizes
        for c in range(sizes["c"]):
            for z in range(sizes["z"]):
                for y in range(sizes["y"]):
                    for k in range(sizes["k"]):
                        spot = {"c": c, "z": z, "y": y, "k": k}
                        goal = dict(spot)
                        goal[name] = (spot[name] + by) % sizes[name]
                        pairs.append((self.flat(spot), self.flat(goal)))
        return lax.ppermute(value, axes, pairs)

    def flat(self, spot):
        sizes = self.sizes
        return ((spot["c"] * sizes["z"] + spot["z"]) * sizes["y"] + spot["y"]) * sizes["k"] + spot[
            "k"
        ]

    def stack(self, array, name, here):
        size = self.sizes[name]
        parts = [array] + [self.shift(array, name, by) for by in range(1, size)]
        if size > 4:
            ordered = [parts[(-place) % size] for place in range(size)]
            return jnp.roll(jnp.stack(ordered), here[name], axis=0)
        return jnp.stack(
            [lax.select_n((here[name] - place) % size, *parts) if size > 2 else
             jnp.where(here[name] == place, parts[0], parts[1]) for place in range(size)]
        )

    def reach(self, pieces, name):
        grown = list(pieces)
        for by in range(1, self.sizes[name]):
            for array, place in pieces:
                moved = dict(place)
                moved[name] = (place[name] - by) % self.sizes[name]
                grown.append((self.shift(array, name, by), moved))
        return grown

    def gather_split(self, stacked, cut, here):
        sizes = self.sizes
        depth, rows, columns = stacked.shape
        out = jnp.zeros((sizes["c"], depth, sizes["y"], rows, columns), stacked.dtype)
        for low_column, high_column, order in ((0, cut, "cy"), (cut, columns, "yc")):
            pieces = [(stacked[:, :, low_column:high_column], here)]
            for name in order:
                pieces = self.reach(pieces, name)
            for array, place in pieces:
                out = lax.dynamic_update_slice(
                    out, array[None, :, None], (place["c"], 0, place["y"], 0, low_column)
                )
        return out.reshape(-1, columns)

    def send_terms(self, value, name, place, here):
        size = self.sizes[name]
        own = lax.dynamic_index_in_dim(value, here[name], place, False)
        moved = [
            self.shift(
                lax.dynamic_index_in_dim(value, (here[name] + by) % size, place, False), name, by
            )
            for by in range(1, size)
        ]
        return own, moved

    def add_terms(self, terms, kind=low):
        own, moved = terms
        total = own.astype(jnp.float32)
        for other in moved:
            total = total + other.astype(jnp.float32)
        return total.astype(kind)

    def everywhere(self, value):
        for name in ("k", "c", "y", "z"):
            total = value
            for by in range(1, self.sizes[name]):
                total = total + self.shift(value, name, by)
            value = total
        return value


def tie(value, *others):
    return lax.optimization_barrier((value, others))[0]


def by_core(core, first, second, axis):
    return jnp.where(
        core == 0,
        jnp.concatenate([first, second], axis=axis),
        jnp.concatenate([second, first], axis=axis),
    )


def pick(core, array, axis):
    return (
        lax.dynamic_index_in_dim(array, core, axis, False),
        lax.dynamic_index_in_dim(array, 1 - core, axis, False),
    )


def gather_far(grid, here, pieces):
    joint_halves, table, mixing_halves, expand_a, expand_b, shrink_a, shrink_b = pieces
    core = here["k"]

    def chip_rows(halves):
        own, other = pick(core, halves, 0)
        return by_core(core, own, grid.shift(other, "k", 1), 0)

    def everyone(block):
        width = block.shape[1]
        return grid.gather_split(grid.stack(block, "z", here), width // 2, here)

    def both(block, axis):
        own = everyone(block)
        return by_core(core, own, grid.shift(own, "k", 1), axis)

    return (
        both(chip_rows(joint_halves), 1),
        everyone(by_core(core, table, grid.shift(table, "k", 1), 0)),
        both(chip_rows(mixing_halves), 1),
        both(chip_rows(expand_a), 1),
        both(chip_rows(expand_b), 1),
        both(shrink_a, 0),
        both(shrink_b, 0),
    )


def reduce_far(grid, here, gradient, by_rows):
    core = here["k"]
    sizes = grid.sizes
    if by_rows:
        own, other = pick(core, gradient.reshape(2, -1, gradient.shape[1]), 0)
    else:
        own, other = pick(core, gradient.reshape(gradient.shape[0], 2, -1), 1)
    total = grid.add_terms((own, [grid.shift(other, "k", 1)]))
    total = total.reshape(sizes["c"], sizes["z"], sizes["y"], -1, own.shape[-1])
    for name, place in (("y", 2), ("c", 0)):
        total = grid.add_terms(grid.send_terms(total, name, place, here))
    total = grid.add_terms(grid.send_terms(total, "z", 0, here), jnp.float32)
    if by_rows:
        return total
    kept, other = pick(core, total.reshape(2, -1, total.shape[1]), 0)
    return by_core(core, kept[None], grid.shift(other, "k", 1)[None], 0)


def body(
    grid,
    block_input,
    block_order,
    cotangent,
    joint_weight,
    mixing_weight,
    expand_weight,
    shrink_weight,
    vectors,
    joint_first,
    mixing_first,
    expand_first,
    shrink_first,
    vectors_first,
    joint_second,
    mixing_second,
    expand_second,
    shrink_second,
    vectors_second,
):
    here = grid.here()
    sizes = grid.sizes
    ctx, ctx_size = here["c"], sizes["c"]
    seq_count, row_count, width = block_input.shape
    half = width // 2
    pairs = H // 2
    hidden_width = expand_weight.shape[1]
    own_rows = joint_weight.shape[0]
    slot = shrink_weight.shape[0]
    sub = slot // 2
    chips = hidden_width // (2 * slot)
    tokens = seq_count * row_count
    row_blocks = row_count // BLK
    near = ctx_size == 2 and seq_count == 2 and sizes["y"] == 2 and own_rows % 32 == 0

    def exchange(rows):
        sent = lax.dynamic_index_in_dim(rows, 1 - ctx, 0, False)
        return lax.dynamic_index_in_dim(rows, ctx, 0, False), grid.shift(sent, "c", 1)

    def hidden_sets(shard):
        parts = shard.astype(low).reshape(own_rows, chips, 2, 2, sub)
        return [
            parts[:, :, :, number].transpose(2, 0, 1, 3).reshape(2, own_rows, chips * sub)
            for number in range(2)
        ]

    joint_halves = (
        joint_weight.astype(low)
        .reshape(own_rows, 3, 2, pairs // 2, PAIR)
        .transpose(2, 0, 3, 1, 4)
        .reshape(2, own_rows, 3 * half)
    )
    table = jnp.pad(vectors.T.astype(low), ((0, 0), (0, 128 - vectors.shape[0])))
    mixing_halves = mixing_weight.astype(low).reshape(own_rows, 2, half).transpose(1, 0, 2)
    shrink_low = shrink_weight.astype(low)
    pieces = [joint_halves, table, mixing_halves, *hidden_sets(expand_weight)]
    pieces += [shrink_low[:sub], shrink_low[sub:]]
    if near:
        input_parts = exchange(block_input)
        joint_halves, table, mixing_halves, expand_half, next_half, shrink, next_shrink = pieces
        joint, tables, *quads = begin(
            sizes, joint_halves, table, mixing_halves, expand_half, shrink
        )
    else:
        joint, tables, mixing, expand_a, expand_b, shrink_a, shrink_b = gather_far(
            grid, here, pieces
        )
    joint = joint.reshape(width, 3 * width)
    vector_values = (
        tables.reshape(width, -1)[:, : vectors.shape[0]].T.astype(jnp.float32)
    )

    if near:
        order = lax.dynamic_slice_in_dim(block_order, ctx, 1, 0)[0]
        blocks = order.shape[0]
        stored = jnp.arange(blocks, dtype=jnp.int32)
        moved = jnp.where(stored // row_blocks == ctx, 0, row_blocks) + stored % row_blocks
        place = jnp.sum(jnp.where(order[None, :] == stored[:, None], moved[None, :], 0), axis=1)
        back = jnp.sum(jnp.where(moved[None, :] == stored[:, None], order[None, :], 0), axis=1)
        place, back = place.astype(jnp.int32), back.astype(jnp.int32)
        input_low = take(place, *input_parts)
        upstream_parts = exchange(tie(cotangent, tables))
    else:
        input_low = block_input.reshape(tokens, width)
        upstream = cotangent.reshape(tokens, width)
    input_rows = input_low.astype(jnp.float32)
    normed_first, normal_first, inverse_first = layer_norm(
        input_rows, vector_values[0], vector_values[1]
    )
    first_low = normed_first.astype(low)
    joint_shift = jnp.stack(
        [
            vector_values[2].reshape(pairs, PAIR),
            jnp.zeros((pairs, PAIR), jnp.float32),
            vector_values[3].reshape(pairs, PAIR),
        ],
        axis=1,
    ).reshape(-1)
    projected = (nn(first_low, joint) + joint_shift).astype(low)
    if near:
        mixed_low, logsum, mixing, expand_a, shrink_a, *quads = attend(
            sizes, blocks, projected, quads, next_half, next_shrink
        )
    else:
        by_part = projected.reshape(seq_count, row_count, pairs, 3, PAIR)
        queries, keys, values = [
            by_part[:, :, :, part].reshape(seq_count, row_count, width) for part in range(3)
        ]
        key_value = lax.all_gather(
            jnp.concatenate([keys, values], axis=2), "ctx", axis=1, tiled=True
        )
        own_blocks = lax.dynamic_slice_in_dim(block_order, ctx * row_blocks, row_blocks, 1)
        query_block = jnp.repeat(own_blocks, BLK, axis=1, total_repeat_length=row_count)
        key_block = jnp.repeat(block_order, BLK, axis=1, total_repeat_length=key_value.shape[1])
        allowed = key_block[:, None, :] <= query_block[:, :, None]
        mixed, logsum = spread_forward(queries, key_value, allowed)
        mixed_low = mixed.astype(low).reshape(tokens, width)
    mixing = mixing.reshape(width, width)
    middle = input_rows + (nn(mixed_low, mixing) + vector_values[4])
    normed_second, normal_second, inverse_second = layer_norm(
        middle, vector_values[5], vector_values[6]
    )
    second_low = normed_second.astype(low)
    if near:
        upstream = take(place, *upstream_parts)

    lead = (sizes["c"], sizes["z"], sizes["y"])
    hidden_bias = vector_values[8:].reshape(chips, 2, 2, sub).transpose(2, 1, 0, 3).reshape(2, 1, -1)

    def operands(number, expand, shrink):
        return (
            second_low,
            upstream,
            expand.reshape(width, -1),
            shrink.reshape(-1, width),
            hidden_bias[number],
        )

    def by_device(expand_grad, shrink_grad):
        return (
            expand_grad.reshape(*lead, -1, expand_grad.shape[1]),
            shrink_grad.reshape(2, *lead, -1, width),
        )

    if near:
        *before, expand_grad_a, shrink_grad_a, bias_a, expand_b, shrink_b = mlp_gather(
            sizes, *operands(0, expand_a, shrink_a), quads
        )
        result, second_grad, expand_grad_b, shrink_grad_b, bias_b, *quads = mlp_reduce(
            sizes,
            *operands(1, expand_b, shrink_b),
            before,
            by_device(expand_grad_a, shrink_grad_a),
        )
    else:
        *before, expand_grad_a, shrink_grad_a, bias_a = mlp(*operands(0, expand_a, shrink_a))
        result, second_grad, expand_grad_b, shrink_grad_b, bias_b = mlp(
            *operands(1, expand_b, shrink_b), before=before
        )
    hidden_bias_grads = [
        bias.reshape(2, chips, 1, sub).transpose(1, 0, 2, 3) for bias in (bias_a, bias_b)
    ]
    if near:
        kept_out, sent_out = give(back, middle, result, vector_values[7:8])
        far_out = grid.shift(sent_out, "c", 1)
        second_grad = tie(second_grad, sent_out)
    else:
        block_output = (middle + result + vector_values[7]).astype(low).reshape(block_input.shape)

    upstream_float = upstream.astype(jnp.float32)
    middle_part, gain_two, shift_two = norm_back(
        second_grad, normal_second, inverse_second, vector_values[5]
    )
    middle_grad = upstream_float + middle_part
    branch_low = middle_grad.astype(low)
    mixing_grad = outer_sum(mixed_low, branch_low).astype(low)
    mixed_grad = nt(branch_low, mixing).astype(low)
    if near:
        joint_back, *last_quads, expand_part_a, shrink_part_a = attend_back(
            sizes,
            blocks,
            projected,
            mixed_grad,
            logsum,
            (
                mixing_grad.reshape(*lead, -1, width),
                *by_device(expand_grad_b, shrink_grad_b),
            ),
            quads,
        )
    else:
        query_grad, key_value_grad = spread_backward(
            queries, key_value, allowed, logsum, mixed_grad.reshape(seq_count, row_count, width)
        )
        summed = lax.psum_scatter(
            key_value_grad.astype(low), "ctx", scatter_dimension=1, tiled=True
        )
        parts = [query_grad.astype(low), summed[..., :width], summed[..., width:]]
        joint_back = jnp.stack(
            [part.reshape(tokens, pairs, PAIR) for part in parts], axis=2
        ).reshape(tokens, 3 * width)
        mixing_part = reduce_far(grid, here, mixing_grad, False)
        expand_part_a, shrink_part_a, expand_part_b, shrink_part_b = [
            reduce_far(grid, here, grad, number % 2 == 1)
            for number, grad in enumerate(
                (expand_grad_a, shrink_grad_a, expand_grad_b, shrink_grad_b)
            )
        ]

    def column_sum(rows):
        return jnp.sum(rows.astype(jnp.float32), axis=0)

    hidden_bias_grad = jnp.concatenate(hidden_bias_grads, axis=2).reshape(-1, width)
    vector_rows = [column_sum(branch_low), gain_two, shift_two, column_sum(upstream)]
    weights = (joint_weight, mixing_weight, expand_weight, shrink_weight)
    firsts = (joint_first, mixing_first, expand_first, shrink_first)
    seconds = (joint_second, mixing_second, expand_second, shrink_second)
    if near:
        rows = vectors.shape[0]
        vector_grad = jnp.concatenate(
            [jnp.zeros((4, width)), jnp.stack(vector_rows), hidden_bias_grad, jnp.zeros((-rows % 8, width))],
            axis=0,
        )
        joint_part, vector_sum, mixing_part, expand_part_b, shrink_part_b, kept_grad, far_grad = end(
            sizes,
            back,
            joint_back,
            first_low,
            joint,
            input_low,
            middle_grad,
            vector_values[0:1],
            vector_grad,
            last_quads,
        )
        input_gradient, block_output, *news = last(
            ctx.astype(jnp.int32).reshape(1),
            (joint_part, mixing_part, expand_part_a, expand_part_b, shrink_part_a, shrink_part_b),
            kept_grad,
            far_grad,
            kept_out,
            far_out,
            list(zip(weights, firsts, seconds)),
        )
        updated, moments, squares, copies = [news[number::4] for number in range(4)]
    else:
        joint_grad = outer_sum(first_low, joint_back).astype(low)
        first_grad = nt(joint_back, joint)
        input_part, gain_one, shift_one = norm_back(
            first_grad, normal_first, inverse_first, vector_values[0]
        )
        input_gradient = (middle_grad + input_part).reshape(block_input.shape)
        joint_sums = column_sum(joint_back).reshape(pairs, 3, PAIR)
        vector_rows = [
            gain_one,
            shift_one,
            joint_sums[:, 0].reshape(-1),
            joint_sums[:, 2].reshape(-1),
        ] + vector_rows
        joint_part = reduce_far(grid, here, joint_grad, False)
        vector_sum = grid.everywhere(
            jnp.concatenate([jnp.stack(vector_rows), hidden_bias_grad], axis=0)
        )
        joint_sum = (
            joint_part.reshape(2, own_rows, pairs // 2, 3, PAIR)
            .transpose(1, 3, 0, 2, 4)
            .reshape(joint_weight.shape)
        )
        mixing_sum = mixing_part.transpose(1, 0, 2).reshape(mixing_weight.shape)
        expand_sum = jnp.stack(
            [part.reshape(2, own_rows, chips, sub) for part in (expand_part_a, expand_part_b)]
        )
        expand_sum = expand_sum.transpose(2, 3, 1, 0, 4).reshape(expand_weight.shape)
        shrink_sum = jnp.concatenate([shrink_part_a, shrink_part_b], axis=0)
        updated, moments, squares = zip(
            *[
                adam_update(*terms, 0.05, 0.1)
                for terms in zip(
                    weights, firsts, seconds, (joint_sum, mixing_sum, expand_sum, shrink_sum)
                )
            ]
        )
        copies = [array.astype(low) for array in updated]
    vector_sum = lax.dynamic_slice(
        vector_sum, (0, lax.axis_index(axes) * vectors.shape[1]), vectors.shape
    )
    vectors_new, vectors_moment, vectors_square = adam_update(
        vectors, vectors_first, vectors_second, vector_sum, 0.5, 0.0
    )
    return (
        block_output,
        input_gradient,
        *updated,
        vectors_new,
        *moments,
        vectors_moment,
        *squares,
        vectors_square,
        *copies,
        vectors_new.astype(low),
    )


def solution(mesh):
    grid = Slice(mesh.shape["ctx"], mesh.shape["wshard"])
    rows = P("wshard", "ctx", None)
    matrix = P(axes, None)
    table = P(None, axes)
    parameters = (matrix, matrix, matrix, matrix, table)
    return jax.shard_map(
        functools.partial(body, grid),
        mesh=mesh,
        in_specs=(rows, P("wshard", None), rows) + parameters * 3,
        out_specs=(rows, rows) + parameters * 4,
        check_vma=False,
    )
```

time: 608 us -> 442 us (0.73)
  Pallas kernels: 453 us -> 368 us
  other arithmetic: 50.1 us -> 21.7 us
  local copies, waits for them, and re-layouts: 48.1 us -> 20.4 us
  matrix products: 45.9 us -> 20.5 us
    pallas_call x1, Pallas kernels: 125 us -> 55.7 us  [attend_back(): pl.pallas_call(functools.partial(attend_back_kernel, sizes, blocks), grid...]
    pallas_call x7, Pallas kernels: 164 us -> 204 us  [the longest x1 74.3 us: end(): pl.pallas_call(functools.partial(end_kernel, sizes), in_specs=[pl.BlockSp...]
    pallas_call x1, Pallas kernels: 89.6 us -> 50.4 us  [attend(): pl.pallas_call(functools.partial(attend_kernel, sizes, blocks), grid=(pai...]
    pallas_call x1, Pallas kernels: 74.7 us -> 58.1 us  [begin(): pl.pallas_call(functools.partial(begin_kernel, sizes), in_specs=[whole_vm...]
    dot_general x4 -> x3, matrix products: 29.8 us -> 16.8 us  [the longest x2 13.1 us: nn(): return jnp.dot(left_side, right_side, preferred_element_type=jnp.float32)]
    dot_general x2 -> x1, matrix products: 16.1 us -> 3.71 us  [outer_sum(): lax.dot_general(left_side, right_side, (((0,), (0,)), ((), ())), preferre...]
    unnamed x98 -> x59, local copies, waits for them, and re-layouts: 16.3 us -> 7.74 us
    reshape x12 -> x3, local copies, waits for them, and re-layouts: 7.8 us -> 0.24 us  [the longest x2 0.14 us: body(): bias.reshape(2, chips, 1, sub).transpose(1, 0, 2, 3)]
  transfers between devices with their start and end apart: 4 -> 3, of which waited for: 0 -> 0; matrix products, arithmetic and copies ran while one was open for 10% -> 12% of each run, Pallas kernels for 38% -> 55%
where the time goes in v3:
time: 442 us; the launch traced here: 439 us
  Pallas kernels  368 us (83%)
  other arithmetic  21.7 us (5%)
  matrix products  20.5 us (5%)
  local copies, waits for them, and re-layouts  20.4 us (5%)
  starting transfers between devices  6.35 us (1%)
    pallas_call x1, Pallas kernels, end(): pl.pallas_call(functools.partial(end_kernel, sizes), in_specs=[pl.BlockSp...  74.3 us
    pallas_call x1, Pallas kernels, begin(): pl.pallas_call(functools.partial(begin_kernel, sizes), in_specs=[whole_vm...  58.1 us
    pallas_call x1, Pallas kernels, attend_back(): pl.pallas_call(functools.partial(attend_back_kernel, sizes, blocks), grid...  55.7 us
    pallas_call x1, Pallas kernels, mlp_reduce(): pl.pallas_call(functools.partial(mlp_reduce_kernel, sizes, rows_step), gr...  55 us
    pallas_call x1, Pallas kernels, mlp_gather(): pl.pallas_call(functools.partial(mlp_gather_kernel, sizes, rows_step), gr...  50.4 us
    pallas_call x1, Pallas kernels, attend(): pl.pallas_call(functools.partial(attend_kernel, sizes, blocks), grid=(pai...  50.4 us
    dot_general x2, matrix products, nn(): return jnp.dot(left_side, right_side, preferred_element_type=jnp.float32)  13.1 us
    pallas_call x1, Pallas kernels, last(): pl.pallas_call(last_kernel, in_specs=[pl.BlockSpec(memory_space=pltpu.SME...  9.23 us
  transfers between devices with their start and end apart: 3, of which 0 were waited for; matrix products, arithmetic and copies ran while one was open for 12% of the time, Pallas kernels for 55%

profile of v3, /device:TPU:0, one launch (start us, length us, event | category | flops | bytes accessed | tf_op | source)
XLA Modules:
  0.0 439.3 jit_solution(18339147715519496392)
XLA Ops:
  0.8 3.1 dynamic-slice_bitcast_fusion.2
  3.9 2.9 collective-permute-start
  8.1 0.7 fusion.13
  9.1 58.1 %begin.1 = (bf16[2,4,2,64,3072]{4,3,2,1,0:T(8,128)(2,1)S(1)}, bf16[2,4,2,64,128]{4,3,2,1,0:T(8,128)(2,1)S(1)}, bf16[4,64,512]{2,1,0:T(8,128)(2,1)S(1)}, bf16[4,6...) custom-call(bf16[2,32,1536]{2,1,0:T(8,128)(2,1)S(1)} %reshape.176.refs_0_, bf16[32,128]{1,0:T(8,128)(2,1)S(1)} %pad.4.refs_1_, ...), custom_call_target="tpu_custom_call" | custom-call | flops 1024 | bytes 1024 | tf_op jit(solution)/shard_map/begin/pallas_call | solution.py:453
  67.3 2.6 copy-done.2
  70.6 3.1 dynamic-slice_bitcast_fusion
  73.8 2.4 collective-permute-start.1
  79.6 4.6 %take.2.refs_4_ = bf16[1024,1024]{1,0:T(8,128)(2,1)} custom-call(s32[4]{0:T(128)} %get-tuple-element.148.place_ref, bf16[512,1024]{1,0:T(8,128)(2,1)} %get-tuple-element.160.kept_ref, bf16[512,1024]{1,0:T(8,128)(2,1)} %collective-permute-done.arrived_ref), custom_call_target="tpu_custom_call" | custom-call | flops 1024 | bytes 1024 | tf_op jit(solution)/shard_map/take/pallas_call | solution.py:1116
  84.2 2.1 convert_reduce_fusion
  86.3 2.3 fusion.2
  88.6 2.4 fusion.5.refs_2_
  91.0 1.3 copy-done.13
  92.3 8.6 %add_convert_fusion.refs_0_ = bf16[1024,3072]{1,0:T(8,128)(2,1)} fusion(f32[3072]{0:T(1024)S(1)} %add.136, bf16[1024,1024]{1,0:T(8,128)(2,1)S(1)} %fusion.5.refs_2_, bf16[1024,3072]{1,0:T(8,128)(2,1)S(1)} %bitcast.87), kind=kOutput, calls=%fused_computation | convolution fusion | flops 6448742400 | bytes 14692352 | tf_op jit(solution)/shard_map/dot_general | solution.py:34
  101.0 50.4 %attend.1 = (bf16[1024,1024]{1,0:T(8,128)(2,1)S(1)}, f32[8,8,1024]{2,1,0:T(8,128)S(1)}, bf16[2,4,2,64,1024]{4,3,2,1,0:T(8,128)(2,1)}, bf16[2,4,2,64,2048]{4,3,2,...) custom-call(bf16[1024,3072]{1,0:T(8,128)(2,1)} %add_convert_fusion.r, ...), custom_call_target="tpu_custom_call" | custom-call | flops 1024 | bytes 1024 | tf_op jit(solution)/shard_map/attend/pallas_call | solution.py:532
  151.4 4.5 %fusion.17 = (f32[1024]{0:T(1024)S(1)}, f32[1024,1024]{1,0:T(8,128)S(1)}) fusion(f32[1024]{0:T(1024)S(1)} %bitcast.115, bf16[1024,1024]{1,0:T(8,128)(2,1)S(1)} %get-tuple-element.89, bf16[1024,1024]{1,0:T(8,128)(2,1)} %bitcast.116, bf16[1024,1024]{1,0:T(8,128)(2,1)S(1)} %copy-done.10), kind=kOutput, calls=%fused_computation.66 | convolution fusion | flops 2151676928 | bytes 10493952 | tf_op jit(solution)/shard_map/dot_general | solution.py:34
  156.5 1.4 copy-done.8
  157.9 2.1 add_convert_fusion.1.refs_0_
  160.0 4.6 %take.3.refs_1_ = bf16[1024,1024]{1,0:T(8,128)(2,1)} custom-call(s32[4]{0:T(128)} %get-tuple-element.148.place_ref, bf16[512,1024]{1,0:T(8,128)(2,1)} %get-tuple-element.158.kept_ref, bf16[512,1024]{1,0:T(8,128)(2,1)} %collective-permute-done.1.arrived_ref), custom_call_target="tpu_custom_call" | custom-call | flops 1024 | bytes 1024 | tf_op jit(solution)/shard_map/take/pallas_call | solution.py:1116
  164.6 50.4 %mlp_gather.1 = (f32[1024,1024]{1,0:T(8,128)}, f32[1024,1024]{1,0:T(8,128)}, bf16[1024,2048]{1,0:T(8,128)(2,1)}, bf16[2048,1024]{1,0:T(8,128)(2,1)}, f32[1,2048]...) custom-call(bf16[1024,1024]{1,0:T(8,128)(2,1)} %add_convert_fusion.1.refs_0_, ...), custom_call_target="tpu_custom_call" | custom-call | flops 1024 | bytes 1024 | tf_op jit(solution)/shard_map/mlp_gather/pallas_call | solution.py:694
  215.0 55.0 %mlp_reduce.1 = (f32[1024,1024]{1,0:T(8,128)}, f32[1024,1024]{1,0:T(8,128)}, bf16[1024,2048]{1,0:T(8,128)(2,1)}, bf16[2048,1024]{1,0:T(8,128)(2,1)}, f32[1,2048]...) custom-call(bf16[1024,1024]{1,0:T(8,128)(2,1)} %add_convert_fusion.1.refs_0_, ...), custom_call_target="tpu_custom_call" | custom-call | flops 1024 | bytes 1024 | tf_op jit(solution)/shard_map/mlp_reduce/pallas_call | solution.py:755
  270.0 6.2 %give.1 = (bf16[512,1024]{1,0:T(8,128)(2,1)}, bf16[512,1024]{1,0:T(8,128)(2,1)}) custom-call(s32[4]{0:T(128)} %get-tuple-element.149.back_ref.refs_0_, f32[1024,1024]{1,0:T(8,128)} %copy-done.8, f32[1024,1024]{1,0:T(8,128)} %get-tuple-element.102.result_ref, f32[1,1024]{1,0:T(1,128)} %get-tuple-element.165.shift_ref), custom_call_target="tpu_custom_call" | custom-call | flops 1024 | bytes 1024 | tf_op jit(solution)/shard_map/give/pallas_call | solution.py:1085
  276.2 1.0 collective-permute-start.2
  277.2 5.0 %multiply_reduce_fusion = (f32[1024]{0:T(1024)S(1)}, f32[1024]{0:T(1024)S(1)}, f32[1024]{0:T(1024)S(1)}, f32[1024]{0:T(1024)S(1)}) fusion(f32[1024,1024]{1,0:T(8,128)} %get-tuple-element.104, f32[1024,1024]{1,0:T(8,128)} %copy-done.8, f32[1024]{0:T(1024)S(1)} %add_rsqrt_fusion, f32[1024]{0:T(1024)S(1)} %broadcast_multiply_fusion.2, f32[1024]{0:T(1024)S(1)} %bitcast.105), kind=kLoop, calls=%fused_computation.12 | loop fusion | flops 9433088 | bytes 8417280 | tf_op jit(solution)/shard_map/reduce_sum | solution.py:1209
  282.5 3.7 convert_reduce_fusion.2
  286.2 3.7 convolution_convert_fusion.1.refs_1_
  289.9 3.7 convolution_convert_fusion
  293.6 55.7 %attend_back.1 = (bf16[1024,3072]{1,0:T(8,128)(2,1)}, bf16[4,64,512]{2,1,0:T(8,128)(2,1)}, bf16[4,64,1024]{2,1,0:T(8,128)(2,1)}, bf16[4,64,1024]{2,1,0:T(8,128)(...) custom-call(bf16[1024,3072]{1,0:T(8,128)(2,1)} %add_convert_fusion.refs_0_, ...), custom_call_target="tpu_custom_call" | custom-call | flops 1024 | bytes 1024 | tf_op jit(solution)/shard_map/attend_back/pallas_call | solution.py:845
  351.5 1.3 concatenate.7.refs_7_
  352.8 74.3 %end.1 = (f32[2,32,1536]{2,1,0:T(8,128)}, f32[16,1024]{1,0:T(8,128)}, f32[2,32,512]{2,1,0:T(8,128)}, f32[2,32,1024]{2,1,0:T(8,128)}, f32[64,1024]{1,0:T(8,128)},...) custom-call(s32[4]{0:T(128)} %get-tuple-element.149.back_ref.refs_0_, bf16[1024,3072]{1,0:T(8,128)(2,1)} %get-tuple-element.110.refs_1_, ...), custom_call_target="tpu_custom_call" | custom-call | flops 1024 | bytes 1024 | tf_op jit(solution)/shard_map/end/pallas_call | solution.py:1056
  427.1 1.4 fusion.11
  428.5 1.0 copy-done.17
  429.5 9.2 %last.1 = (f32[2,512,1024]{2,1,0:T(8,128)}, bf16[2,512,1024]{2,1,0:T(8,128)(2,1)}, f32[32,3072]{1,0:T(8,128)}, f32[32,3072]{1,0:T(8,128)}, f32[32,3072]{1,0:T(8,...) custom-call(s32[1]{0:T(128)} %bitcast.ctx_ref, ...), custom_call_target="tpu_custom_call" | custom-call | flops 1024 | bytes 1024 | tf_op jit(solution)/shard_map/last/pallas_call | solution.py:1185
  (104 shorter events, 8.6 us)
Async XLA Ops:
  0.7 78.2 %copy-start = (s32[2,4]{1,0:T(2,128)S(1)}, s32[2,4]{1,0:T(2,128)}, u32[]{:S(2)}) copy-start(s32[2,4]{1,0:T(2,128)} %param.19) | copy-start | bytes 100
  0.7 6.2 %copy-start.16 = (f32[32,3072]{1,0:T(8,128)S(1)}, f32[32,3072]{1,0:T(8,128)}, u32[]{:S(2)}) copy-start(f32[32,3072]{1,0:T(8,128)} %refs_10_.1) | copy-start | bytes 1179652
  0.7 6.6 %copy-start.20 = (f32[12,32]{1,0:T(8,128)S(1)}, f32[12,32]{1,0:T(8,128)}, u32[]{:S(2)}) copy-start(f32[12,32]{1,0:T(8,128)} %param.25) | copy-start | bytes 4612
  0.7 6.7 %copy-start.18 = (f32[32,1024]{1,0:T(8,128)S(1)}, f32[32,1024]{1,0:T(8,128)}, u32[]{:S(2)}) copy-start(f32[32,1024]{1,0:T(8,128)} %refs_13_.1) | copy-start | bytes 393220
  0.7 6.8 %copy-start.14 = (f32[32,4096]{1,0:T(8,128)S(1)}, f32[32,4096]{1,0:T(8,128)}, u32[]{:S(2)}) copy-start(f32[32,4096]{1,0:T(8,128)} %refs_16_.1) | copy-start | bytes 1572868
  3.9 5.1 %copy-start.15 = (f32[128,1024]{1,0:T(8,128)S(1)}, f32[128,1024]{1,0:T(8,128)}, u32[]{:S(2)}) copy-start(f32[128,1024]{1,0:T(8,128)} %refs_19_.1) | copy-start | bytes 1572868
  3.9 75.6 %collective-permute-start = (bf16[512,1024]{1,0:T(8,128)(2,1)}, bf16[512,1024]{1,0:T(8,128)(2,1)}, u32[]{:S(2)}, u32[]{:S(2)}) collective-permute-start(bf16[512,1024]{1,0:T(8,128)(2,1)} %get-tuple-element.159), channel_id=1, source_target_pairs={{0,16},{1,17},{2,18},{3,19},{4,20},{5,21},{6,22},{7,23},{8,24},{9,... | collective-permute-start | bytes 3145736 | tf_op jit(solution)/shard_map/ppermute | solution.py:1326
  67.3 2.7 copy-start.2
  69.9 0.7 copy-start.6
  73.8 86.2 %collective-permute-start.1 = (bf16[512,1024]{1,0:T(8,128)(2,1)}, bf16[512,1024]{1,0:T(8,128)(2,1)}, u32[]{:S(2)}, u32[]{:S(2)}) collective-permute-start(bf16[512,1024]{1,0:T(8,128)(2,1)} %get-tuple-element.157), channel_id=1, source_target_pairs={{0,16},{1,17},{2,18},{3,19},{4,20},{5,21},{6,22},{7,23},{8,24},{9,... | collective-permute-start | bytes 3145736 | tf_op jit(solution)/shard_map/ppermute | solution.py:1326
  77.0 11.6 %copy-start.19 = (f32[1,1024]{1,0:T(1,128)}, f32[1,1024]{1,0:T(1,128)S(1)}, u32[]{:S(2)}) copy-start(f32[1,1024]{1,0:T(1,128)S(1)} %get-tuple-element.172.refs_6_) | copy-start | bytes 12292
  77.5 14.9 %slice-start = ((s8[6291456]{0:T(1024)(128)(4,1)}), s8[2097152]{0:T(1024)(128)(4,1)S(1)}, s32[]{:S(2)}) async-start(s8[6291456]{0:T(1024)(128)(4,1)} %bitcast.85), calls=%async_computation | async-start | bytes 4194304
  84.2 8.2 %slice-start.1 = ((s8[6291456]{0:T(1024)(128)(4,1)}), s8[4194304]{0:T(1024)(128)(4,1)S(1)}, s32[]{:S(2)}) async-start(s8[6291456]{0:T(1024)(128)(4,1)} %bitcast.85), calls=%async_computation.1 | async-start | bytes 8388608
  91.0 1.3 copy-start.13
  92.3 8.6 %copy-start.7 = (bf16[4,64,512]{2,1,0:T(8,128)(2,1)S(1)}, bf16[4,64,512]{2,1,0:T(8,128)(2,1)}, u32[]{:S(2)}) copy-start(bf16[4,64,512]{2,1,0:T(8,128)(2,1)} %copy-done.6) | copy-start | bytes 786436
  101.0 50.4 %copy-start.10 = (bf16[1024,1024]{1,0:T(8,128)(2,1)S(1)}, bf16[1024,1024]{1,0:T(8,128)(2,1)}, u32[]{:S(2)}) copy-start(bf16[1024,1024]{1,0:T(8,128)(2,1)} %take.2.refs_4_) | copy-start | bytes 6291460
  151.3 4.5 %copy-start.3 = (bf16[4,64,1024]{2,1,0:T(8,128)(2,1)}, bf16[4,64,1024]{2,1,0:T(8,128)(2,1)S(1)}, u32[]{:S(2)}) copy-start(bf16[4,64,1024]{2,1,0:T(8,128)(2,1)S(1)} %get-tuple-element.93.refs_5_) | copy-start | bytes 1572868
  151.4 4.5 %copy-start.4 = (bf16[4,64,1024]{2,1,0:T(8,128)(2,1)}, bf16[4,64,1024]{2,1,0:T(8,128)(2,1)S(1)}, u32[]{:S(2)}) copy-start(bf16[4,64,1024]{2,1,0:T(8,128)(2,1)S(1)} %get-tuple-element.94.refs_6_) | copy-start | bytes 1572868
  151.4 4.5 %copy-start.5 = (f32[8,8,1024]{2,1,0:T(8,128)}, f32[8,8,1024]{2,1,0:T(8,128)S(1)}, u32[]{:S(2)}) copy-start(f32[8,8,1024]{2,1,0:T(8,128)S(1)} %get-tuple-element.105.refs_2_) | copy-start | bytes 786436
  155.9 2.0 copy-start.8
  276.2 152.4 %collective-permute-start.2 = (bf16[512,1024]{1,0:T(8,128)(2,1)}, bf16[512,1024]{1,0:T(8,128)(2,1)S(1)}, u32[]{:S(2)}, u32[]{:S(2)}) collective-permute-start(bf16[512,1024]{1,0:T(8,128)(2,1)} %get-tuple-element.103), channel_id=1, source_target_pairs={{0,16},{1,17},{2,18},{3,19},{4,20},{5,21},{6,22},{7,23},{8,24},{9,... | collective-permute-start | bytes 3145736 | tf_op jit(solution)/shard_map/ppermute | solution.py:1326
  277.2 5.0 %copy-start.9 = (f32[1024,1024]{1,0:T(8,128)S(1)}, f32[1024,1024]{1,0:T(8,128)}, u32[]{:S(2)}) copy-start(f32[1024,1024]{1,0:T(8,128)} %copy-done.8) | copy-start | bytes 12582916
  277.2 5.3 %copy-start.11 = (bf16[1024,1024]{1,0:T(8,128)(2,1)S(1)}, bf16[1024,1024]{1,0:T(8,128)(2,1)}, u32[]{:S(2)}) copy-start(bf16[1024,1024]{1,0:T(8,128)(2,1)} %take.3.refs_1_) | copy-start | bytes 6291460
  282.5 3.7 copy-start.25
  286.2 3.7 copy-start.12
  293.6 56.2 %copy-start.24 = (f32[1,2048]{1,0:T(1,128)S(1)}, f32[1,2048]{1,0:T(1,128)}, u32[]{:S(2)}) copy-start(f32[1,2048]{1,0:T(1,128)} %get-tuple-element.112) | copy-start | bytes 24580
  293.6 57.0 %copy-start.23 = (f32[1,2048]{1,0:T(1,128)S(1)}, f32[1,2048]{1,0:T(1,128)}, u32[]{:S(2)}) copy-start(f32[1,2048]{1,0:T(1,128)} %get-tuple-element.111) | copy-start | bytes 24580
  352.8 74.3 %copy-start.21 = (f32[12,32]{1,0:T(8,128)S(1)}, f32[12,32]{1,0:T(8,128)}, u32[]{:S(2)}) copy-start(f32[12,32]{1,0:T(8,128)} %param.30) | copy-start | bytes 4612
  352.8 74.3 %copy-start.22 = (f32[12,32]{1,0:T(8,128)S(1)}, f32[12,32]{1,0:T(8,128)}, u32[]{:S(2)}) copy-start(f32[12,32]{1,0:T(8,128)} %param.35) | copy-start | bytes 4612
  428.5 1.0 copy-start.17
  428.5 10.2 %copy-start.1 = (s32[2,4]{1,0:T(2,128)S(1)}, s32[2,4]{1,0:T(2,128)}, u32[]{:S(2)}) copy-start(s32[2,4]{1,0:T(2,128)} %param.19) | copy-start | bytes 100

commit v4 on v3

--- a/solution.py
+++ b/solution.py
@@ -405,15 +405,21 @@
     )
 
 
+def cut_of(width):
+    return max(5 * width // 8 // 128, 1) * 128
+
+
 def low_shape(*dims):
     return jax.ShapeDtypeStruct(dims, low)
 
 
 def begin_kernel(sizes, *refs):
     refs = Refs(refs)
-    joint_halves, table, mixing_halves, expand_halves, shrink = refs.take(5)
-    joint, tables, mixing_quad, expand_quad, shrink_quad = refs.take(5)
-    joint_quad, table_quad, sems = refs.take(3)
+    joint_weight, table, mixing_weight, expand_weight, shrink_weight = refs.take(5)
+    rows_in, upstream = refs.take(2)
+    joint, tables, mixing_quad, expand_quad, shrink_quad, far_rows, far_upstream = refs.take(7)
+    next_expand, next_shrink = refs.take(2)
+    joint_quad, table_quad, sems, joint_halves, mixing_halves, expand_halves, shrink = refs.take(7)
     spot = Spot(sizes)
     mover = Mover(spot, sems)
     width = joint_halves.shape[2]
@@ -426,10 +432,45 @@
     later_first += [mover.local(shrink, shrink_quad.at[spot.z])]
     now = Deep(mover, joint_quad).copies + Deep(mover, table_quad).copies
     later = [Deep(mover, quad).copies for quad in (mixing_quad, shrink_quad, expand_quad)]
-    job = Near(mover, joint_quad, joint, spot.k * width, width // 2)
+    job = Near(mover, joint_quad, joint, spot.k * width, cut_of(width))
     thin = Near(mover, table_quad, tables, 0, table.shape[1], core=False)
+    rows_copies = [
+        mover.copy(rows_in.at[1 - spot.c], far_rows, "c"),
+        mover.copy(upstream.at[1 - spot.c, block_rows(0)], far_upstream, "c"),
+    ]
+    pairs = width // (3 * PAIR)
+    for core in range(2):
+        for pair in range(pairs):
+            for third in range(3):
+                source = ((third * 2 + core) * pairs + pair) * PAIR
+                target = (pair * 3 + third) * PAIR
+                joint_halves[core, :, target : target + PAIR] = joint_weight[
+                    :, source : source + PAIR
+                ].astype(low)
     spot.meet(all_axes)
-    start(joint_first + later_first)
+    start(joint_first)
+    start(rows_copies[:1])
+    half = mixing_halves.shape[2]
+    for core in range(2):
+        mixing_halves[core] = mixing_weight[:, core * half : (core + 1) * half].astype(low)
+    sub = shrink.shape[0]
+    shrink[...] = shrink_weight[:sub, :].astype(low)
+    next_shrink[...] = shrink_weight[sub:, :].astype(low)
+    lane = lax.broadcasted_iota(jnp.int32, (1, PAIR), 1)
+    for core in range(2):
+        for chip in range(0, expand_halves.shape[2] // HD, 2):
+            one, two = [
+                expand_weight[:, (number * 2 + core) * PAIR : (number * 2 + core + 1) * PAIR]
+                for number in (chip, chip + 1)
+            ]
+            columns = pl.ds(chip * HD, PAIR)
+            expand_halves[core, :, columns] = jnp.where(
+                lane < HD, one, pltpu.roll(two, HD, 1)
+            ).astype(low)
+            next_expand[core, :, columns] = jnp.where(
+                lane < HD, pltpu.roll(one, HD, 1), two
+            ).astype(low)
+    start(later_first)
     wait(joint_first)
     start(now)
     wait(later_first)
@@ -439,70 +480,114 @@
         start(copies)
     wait(thin.near + job.near)
     start(thin.far + job.far + job.core[1])
+    start(rows_copies[1:])
     wait(thin.far)
     job.close()
     for copies in later:
         wait(copies)
     job.close_core()
-
-
-def begin(sizes, joint_halves, table, mixing_halves, expand_halves, shrink):
+    wait(rows_copies)
+
+
+def begin(sizes, joint_weight, table, mixing_weight, expand_weight, shrink_weight, rows_in, upstream):
     lead = (sizes["c"], sizes["z"], sizes["y"])
-    depth, rows = sizes["z"], 2 * table.shape[0]
-    width = joint_halves.shape[2]
+    own, model = mixing_weight.shape
+    depth, rows = sizes["z"], 2 * own
+    width, half, grown = 3 * model // 2, model // 2, expand_weight.shape[1] // 4
+    sub = shrink_weight.shape[0] // 2
     return pl.pallas_call(
         functools.partial(begin_kernel, sizes),
-        in_specs=[whole_vmem] * 5,
-        out_specs=[any_place] * 5,
+        in_specs=[whole_vmem] * 5 + [any_place] * 2,
+        out_specs=[any_place] * 7 + [whole_vmem] * 2,
         out_shape=[
             low_shape(*lead, rows, 2 * width),
             low_shape(*lead, rows, table.shape[1]),
-            low_shape(depth, rows, mixing_halves.shape[2]),
-            low_shape(depth, rows, expand_halves.shape[2]),
-            low_shape(depth, *shrink.shape),
+            low_shape(depth, rows, half),
+            low_shape(depth, rows, grown),
+            low_shape(depth, sub, model),
+            low_shape(*rows_in.shape[1:]),
+            low_shape(BLK, model),
+            low_shape(2, own, grown),
+            low_shape(sub, model),
         ],
         scratch_shapes=[
             pltpu.VMEM((depth, rows, width), low),
             pltpu.VMEM((depth, rows, table.shape[1]), low),
             pltpu.SemaphoreType.DMA((2, 48)),
+            pltpu.VMEM((2, own, width), low),
+            pltpu.VMEM((2, own, half), low),
+            pltpu.VMEM((2, own, grown), low),
+            pltpu.VMEM((sub, model), low),
         ],
-        compiler_params=params(1, 16),
+        compiler_params=params(1, 60),
         cost_estimate=small_cost,
         name="begin",
-    )(joint_halves, table, mixing_halves, expand_halves, shrink)
+    )(joint_weight, table, mixing_weight, expand_weight, shrink_weight, rows_in, upstream)
+
+
+def normal_rows(rows):
+    centered = rows - jnp.mean(rows, axis=-1, keepdims=True)
+    inverse = lax.rsqrt(jnp.mean(centered * centered, axis=-1, keepdims=True) + norm_eps)
+    return centered * inverse, inverse
+
+
+def norm_pull(upstream, normal, inverse, gain):
+    scaled = upstream * gain
+    inner = jnp.mean(scaled, axis=-1, keepdims=True)
+    along = jnp.mean(scaled * normal, axis=-1, keepdims=True)
+    return inverse * (scaled - inner - normal * along)
+
+
+def chosen_block(number, source):
+    chosen = jnp.full((1, source.shape[1]), number, jnp.int32)
+    value = source[block_rows(0), :].astype(jnp.float32)
+    for other in range(1, source.shape[0] // BLK):
+        value = jnp.where(chosen == other, source[block_rows(other), :].astype(jnp.float32), value)
+    return value
 
 
 def attend_kernel(sizes, blocks, *refs):
     refs = Refs(refs)
-    projected, mixing_quad, expand_quad, shrink_quad, expand_halves, shrink = refs.take(6)
-    o_ref, lse_ref, mixing, expand, shrunk, next_expand, next_shrink, sems = refs.take(8)
+    place_ref, rows_in, far_rows, joint, norm_ref, shift_ref, upstream = refs.take(7)
+    mixing_quad, expand_quad, shrink_quad, expand_halves, shrink = refs.take(5)
+    o_ref, lse_ref, rows_ref, low_ref, projected_ref = refs.take(5)
+    mixing, expand, shrunk, next_expand, next_shrink, far_upstream = refs.take(6)
+    sems, rows_all, joint_all, projected = refs.take(4)
     spot = Spot(sizes)
     mover = Mover(spot, sems)
     k = spot.k
     half, grown, width = mixing_quad.shape[-1], expand_quad.shape[-1], shrink_quad.shape[-1]
+    loads = [
+        mover.local(rows_in.at[spot.c], rows_all.at[pl.ds(0, 2 * BLK)]),
+        mover.local(far_rows, rows_all.at[pl.ds(2 * BLK, 2 * BLK)]),
+        mover.local(joint, joint_all),
+    ]
     jobs = [
-        Near(mover, mixing_quad, mixing, k * half, half // 2),
-        Near(mover, shrink_quad, shrunk.at[k], 0, width // 2),
-        Near(mover, expand_quad, expand, k * grown, grown // 2),
+        Near(mover, mixing_quad, mixing, k * half, cut_of(half)),
+        Near(mover, shrink_quad, shrunk.at[k], 0, cut_of(width)),
+        Near(mover, expand_quad, expand, k * grown, cut_of(grown)),
     ]
     next_first = first_rows(mover, expand_halves, next_expand)
     next_first += [mover.local(shrink, next_shrink.at[spot.z])]
     deep = Deep(mover, next_expand).copies + Deep(mover, next_shrink).copies
+    upstream_copy = [mover.copy(upstream.at[1 - spot.c, block_rows(1)], far_upstream, "c")]
 
     def open_all():
+        start(loads)
         spot.meet(all_axes)
         start(next_first)
         for job in jobs:
             start(job.near + job.core[0])
+        wait(loads)
 
     def next_deep():
         wait(next_first)
         start(deep)
-
-    def far(*some):
-        for job in some:
-            wait(job.near)
-            start(job.far + job.core[1])
+        start(upstream_copy)
+
+    def far(job):
+        wait(job.near)
+        start(job.far + job.core[1])
 
     def close_all():
         for job in jobs:
@@ -510,70 +595,100 @@
         wait(deep)
         for job in jobs:
             job.close_core()
+        wait(upstream_copy)
 
     step = pl.program_id(0)
-    schedule = [
-        (0, 0, open_all),
-        (1, 0, next_deep),
-        (2, 2, lambda: far(jobs[0])),
-        (4, 2, lambda: far(jobs[1])),
-        (7, 0, lambda: far(jobs[2])),
-    ]
-    attend_pair(blocks, projected, o_ref, lse_ref, hooks(step, schedule))
+    between = hooks(
+        step,
+        [
+            (0, 0, open_all),
+            (2, 0, next_deep),
+            (4, 2, lambda: far(jobs[0])),
+            (6, 2, lambda: far(jobs[1])),
+            (9, 2, lambda: far(jobs[2])),
+        ],
+    )
+    between(0)
+
+    @pl.when(step < blocks)
+    def _():
+        value = chosen_block(place_ref[step], rows_all)
+        rows_ref[...] = value.astype(low)
+        normal, _ = normal_rows(value)
+        normed = (normal * norm_ref[0:1, :] + norm_ref[1:2, :]).astype(low)
+        low_ref[...] = normed
+        rows = pl.ds(pl.multiple_of(step * BLK, BLK), BLK)
+        for first in range(0, joint_all.shape[1], 512):
+            columns = pl.ds(first, 512)
+            projected[rows, columns] = (nn(normed, joint_all[:, columns]) + shift_ref[:, columns]).astype(low)
+
+    @pl.when(step >= blocks)
+    def _():
+        columns = span((step - blocks) * 3 * PAIR, 3 * PAIR)
+        projected_ref[...] = projected[:, columns]
+        attend_pair(blocks, projected_ref, o_ref, lse_ref, lambda block: block > 0 and between(block))
+
     pl.when(step == pl.num_programs(0) - 1)(close_all)
 
 
-def attend(sizes, blocks, projected, quads, halves, shrink):
-    tokens, width = projected.shape[0], projected.shape[1] // 3
-    pairs = width // PAIR
+def attend(sizes, place, rows_in, far_rows, joint, norm, shift, upstream, quads, halves, shrink):
+    model = rows_in.shape[2]
+    blocks = place.shape[0]
+    tokens = blocks * BLK
+    pairs = model // PAIR
     lead = (sizes["c"], sizes["z"], sizes["y"])
     depth, rows, half = quads[0].shape
     grown, full = quads[1].shape[2], quads[2].shape[2]
+    by_rows = pl.BlockSpec((BLK, model), lambda g: (jnp.minimum(g, blocks - 1), 0))
+
+    def pair(g):
+        return jnp.maximum(g - blocks, 0)
+
     return pl.pallas_call(
         functools.partial(attend_kernel, sizes, blocks),
-        grid=(pairs,),
-        in_specs=[pl.BlockSpec((tokens, 3 * PAIR), lambda g: (0, g))] + [whole_vmem] * 5,
+        grid=(blocks + pairs,),
+        in_specs=[pl.BlockSpec(memory_space=pltpu.SMEM)]
+        + [any_place] * 3
+        + [whole_vmem] * 2
+        + [any_place]
+        + [whole_vmem] * 5,
         out_specs=[
-            pl.BlockSpec((tokens, PAIR), lambda g: (0, g)),
-            pl.BlockSpec((None, 8, tokens), lambda g: (g, 0, 0)),
+            pl.BlockSpec((tokens, PAIR), lambda g: (0, pair(g))),
+            pl.BlockSpec((None, 8, tokens), lambda g: (pair(g), 0, 0)),
+            by_rows,
+            by_rows,
+            pl.BlockSpec((tokens, 3 * PAIR), lambda g: (0, pair(g))),
         ]
-        + [any_place] * 5,
+        + [any_place] * 6,
         out_shape=[
-            low_shape(tokens, width),
+            low_shape(tokens, model),
             jax.ShapeDtypeStruct((pairs, 8, tokens), jnp.float32),
+            low_shape(tokens, model),
+            low_shape(tokens, model),
+            low_shape(tokens, 3 * model),
             low_shape(*lead, rows, 2 * half),
             low_shape(*lead, rows, 2 * grown),
             low_shape(2, *lead, rows, full),
             low_shape(depth, rows, grown),
             low_shape(depth, rows, full),
+            low_shape(BLK, model),
         ],
-        scratch_shapes=[pltpu.SemaphoreType.DMA((2, 64))],
-        compiler_params=params(2, 48),
+        scratch_shapes=[
+            pltpu.SemaphoreType.DMA((2, 64)),
+            pltpu.VMEM((tokens, model), low),
+            pltpu.VMEM((model, 3 * model), low),
+            pltpu.VMEM((tokens, 3 * model), low),
+        ],
+        compiler_params=params(2, 56),
         cost_estimate=small_cost,
         name="attend",
-    )(projected, *quads, halves, shrink)
-
-
-def mlp_tile(first, rows_step, c_ref, dy_ref, we_ref, ws_ref, be_ref, before, outs, scratch, between):
+    )(place, rows_in, far_rows, joint, norm, shift, upstream, *quads, halves, shrink)
+
+
+def mlp_tile(rows_step, c_ref, dy_ref, we_ref, ws_ref, be_ref, outs, scratch, between):
     y_ref, dc_ref, gwe_ref, gws_ref, gbe_ref = outs
-    turned, act_all, du_all = scratch[:3]
+    turned, act_all, du_all = scratch
     tokens = c_ref.shape[0]
-
-    @pl.when(pl.program_id(0) == 0)
-    def _():
-        turned[...] = jnp.transpose(c_ref[...])
-        if first:
-            y_ref[...] = jnp.zeros_like(y_ref)
-            dc_ref[...] = jnp.zeros_like(dc_ref)
-        else:
-            sem = scratch[3]
-            copies = [
-                pltpu.make_async_copy(before[0], y_ref, sem.at[0]),
-                pltpu.make_async_copy(before[1], dc_ref, sem.at[1]),
-            ]
-            start(copies)
-            wait(copies)
-
     we, ws = we_ref[...], ws_ref[...]
     total = None
     for part in range(tokens // rows_step):
@@ -622,50 +737,65 @@
     )
 
 
-def mlp_plain_kernel(first, rows_step, *refs):
+def mlp_plain_kernel(rows_step, *refs):
     refs = Refs(refs)
-    inputs = refs.take(5)
-    before = [] if first else refs.take(2)
-    outs = refs.take(5)
-    mlp_tile(first, rows_step, *inputs, before, outs, refs.refs, lambda part: None)
-
-
-def mlp(c, dy, we, ws, be, before=(), tile=256, rows_step=256):
+    c_ref, dy_ref, we_ref, ws_ref, be_ref, y_in, dc_in = refs.take(7)
+    outs, scratch, (sem,) = refs.take(5), refs.take(3), refs.take(1)
+
+    @pl.when(pl.program_id(0) == 0)
+    def _():
+        scratch[0][...] = jnp.transpose(c_ref[...])
+        copies = [
+            pltpu.make_async_copy(y_in, outs[0], sem.at[0]),
+            pltpu.make_async_copy(dc_in, outs[1], sem.at[1]),
+        ]
+        start(copies)
+        wait(copies)
+
+    mlp_tile(rows_step, c_ref, dy_ref, we_ref, ws_ref, be_ref, outs, scratch, lambda part: None)
+
+
+def mlp(c, dy, we, ws, be, before, tile=256, rows_step=256):
     in_specs, out_specs, out_shape, scratch = mlp_parts(*c.shape, we.shape[1], tile)
-    if before:
-        scratch = scratch + [pltpu.SemaphoreType.DMA((2,))]
     return pl.pallas_call(
-        functools.partial(mlp_plain_kernel, not before, rows_step),
+        functools.partial(mlp_plain_kernel, rows_step),
         grid=(we.shape[1] // tile,),
-        in_specs=in_specs + [any_place] * len(before),
+        in_specs=in_specs + [any_place] * 2,
         out_specs=out_specs,
         out_shape=out_shape,
-        scratch_shapes=scratch,
+        scratch_shapes=scratch + [pltpu.SemaphoreType.DMA((2,))],
         compiler_params=pltpu.CompilerParams(vmem_limit_bytes=56 << 20),
         cost_estimate=small_cost,
         name="mlp",
     )(c, dy, we, ws, be, *before)
 
 
-def mlp_gather_kernel(sizes, rows_step, *refs):
+def mlp_gather_kernel(sizes, blocks, rows_step, *refs):
     refs = Refs(refs)
-    inputs = refs.take(5)
-    expand_quad, shrink_quad = refs.take(2)
-    outs = refs.take(5)
+    place_ref, mixed_ref, rows_ref, mixing, vector_ref, we_ref, ws_ref, be_ref = refs.take(8)
+    upstream, far_a, far_b, expand_quad, shrink_quad = refs.take(5)
+    outs, (middle_ref, low_ref, upstream_ref) = refs.take(5), refs.take(3)
     expand, shrunk = refs.take(2)
-    scratch, (sems,) = refs.take(3), refs.take(1)
+    scratch, (sems, raw, c_all, dy_all) = refs.take(3), refs.take(4)
     spot = Spot(sizes)
     mover = Mover(spot, sems)
     grown, width = expand_quad.shape[-1], shrink_quad.shape[-1]
+    loads = [
+        mover.local(upstream.at[spot.c], raw.at[pl.ds(0, 2 * BLK)]),
+        mover.local(far_a, raw.at[pl.ds(2 * BLK, BLK)]),
+        mover.local(far_b, raw.at[pl.ds(3 * BLK, BLK)]),
+    ]
     jobs = [
         Near(mover, shrink_quad, shrunk.at[spot.k], 0, width // 2),
         Near(mover, expand_quad, expand, spot.k * grown, grown // 2),
     ]
 
     def open_all():
+        start(loads)
         spot.meet(all_axes)
         for job in jobs:
             start(job.near + job.core[0])
+        wait(loads)
 
     def far(job):
         wait(job.near)
@@ -677,43 +807,99 @@
             job.close_core()
 
     step = pl.program_id(0)
-    schedule = [
-        (0, 0, open_all),
-        (3, 0, lambda: far(jobs[0])),
-        (5, 2, lambda: far(jobs[1])),
-        (7, 0, jobs[0].close),
-    ]
-    mlp_tile(True, rows_step, *inputs, [], outs, scratch, hooks(step, schedule))
+    between = hooks(
+        step,
+        [
+            (0, 0, open_all),
+            (6, 0, lambda: far(jobs[0])),
+            (8, 2, lambda: far(jobs[1])),
+            (10, 0, jobs[0].close),
+        ],
+    )
+    between(0)
+
+    @pl.when(step < blocks)
+    def _():
+        rows = pl.ds(pl.multiple_of(step * BLK, BLK), BLK)
+        dy = chosen_block(place_ref[step], raw).astype(low)
+        upstream_ref[...] = dy
+        dy_all[rows, :] = dy
+        branch = nn(mixed_ref[...], mixing[...]) + vector_ref[4:5, :]
+        middle = rows_ref[...].astype(jnp.float32) + branch
+        middle_ref[...] = middle
+        normal, _ = normal_rows(middle)
+        second = (normal * vector_ref[5:6, :] + vector_ref[6:7, :]).astype(low)
+        low_ref[...] = second
+        c_all[rows, :] = second
+        outs[0][rows, :] = middle + vector_ref[7:8, :]
+        outs[1][rows, :] = jnp.zeros(middle.shape, jnp.float32)
+
+    @pl.when(step == blocks)
+    def _():
+        scratch[0][...] = jnp.transpose(c_all[...])
+
+    @pl.when(step >= blocks)
+    def _():
+        mlp_tile(
+            rows_step, c_all, dy_all, we_ref, ws_ref, be_ref, outs, scratch,
+            lambda part: part > 0 and between(part),
+        )
+
     pl.when(step == pl.num_programs(0) - 1)(close_all)
 
 
-def mlp_gather(sizes, c, dy, we, ws, be, quads, tile=256, rows_step=256):
-    in_specs, out_specs, out_shape, scratch = mlp_parts(*c.shape, we.shape[1], tile)
+def mlp_gather(sizes, place, mixed, rows_in, mixing, vectors, we, ws, be, upstream, far_a, far_b, quads, tile=256, rows_step=256):
+    tokens, model = mixed.shape
+    blocks = place.shape[0]
+    hidden = we.shape[1]
     lead = (sizes["c"], sizes["z"], sizes["y"])
     rows, grown, full = quads[0].shape[1], quads[0].shape[2], quads[1].shape[2]
+    by_rows = pl.BlockSpec((BLK, model), lambda g: (jnp.minimum(g, blocks - 1), 0))
+    whole = pl.BlockSpec((tokens, model), lambda g: (0, 0))
+
+    def at(g):
+        return jnp.maximum(g - blocks, 0)
+
+    down = pl.BlockSpec((model, tile), lambda g: (0, at(g)))
+    across = pl.BlockSpec((tile, model), lambda g: (at(g), 0))
+    thin = pl.BlockSpec((1, tile), lambda g: (0, at(g)))
+    _, _, out_shape, scratch = mlp_parts(tokens, model, hidden, tile)
     return pl.pallas_call(
-        functools.partial(mlp_gather_kernel, sizes, rows_step),
-        grid=(we.shape[1] // tile,),
-        in_specs=in_specs + [whole_vmem] * 2,
-        out_specs=out_specs + [any_place] * 2,
-        out_shape=out_shape + [low_shape(*lead, rows, 2 * grown), low_shape(2, *lead, rows, full)],
-        scratch_shapes=scratch + [pltpu.SemaphoreType.DMA((2, 32))],
-        compiler_params=params(3, 56),
+        functools.partial(mlp_gather_kernel, sizes, blocks, rows_step),
+        grid=(blocks + hidden // tile,),
+        in_specs=[pl.BlockSpec(memory_space=pltpu.SMEM), by_rows, by_rows, whole_vmem, whole_vmem]
+        + [down, across, thin]
+        + [any_place] * 3
+        + [whole_vmem] * 2,
+        out_specs=[whole, whole, down, across, thin] + [by_rows] * 3 + [any_place] * 2,
+        out_shape=out_shape
+        + [
+            jax.ShapeDtypeStruct((tokens, model), jnp.float32),
+            low_shape(tokens, model),
+            low_shape(tokens, model),
+            low_shape(*lead, rows, 2 * grown),
+            low_shape(2, *lead, rows, full),
+        ],
+        scratch_shapes=scratch
+        + [pltpu.SemaphoreType.DMA((2, 32))]
+        + [pltpu.VMEM((tokens, model), low)] * 3,
+        compiler_params=params(3, 60),
         cost_estimate=small_cost,
         name="mlp_gather",
-    )(c, dy, we, ws, be, *quads)
+    )(place, mixed, rows_in, mixing, vectors, we, ws, be, upstream, far_a, far_b, *quads)
 
 
 def mlp_reduce_kernel(sizes, rows_step, *refs):
     refs = Refs(refs)
-    inputs, before = refs.take(5), refs.take(2)
-    expand, shrink = refs.take(2)
-    outs = refs.take(5)
-    expand_quad, shrink_quad = refs.take(2)
-    scratch, (sems,) = refs.take(4), refs.take(1)
+    back_ref, c_ref, dy_ref, we_ref, ws_ref, be_ref, y_in, dc_in, expand, shrink = refs.take(10)
+    outs = refs.take(4)
+    expand_quad, shrink_quad, kept, sent = refs.take(4)
+    scratch, (sems, y_all) = refs.take(3), refs.take(2)
+    outs = [y_all] + outs
     spot = Spot(sizes)
     mover = Mover(spot, sems)
     grown, width = expand_quad.shape[-1], shrink_quad.shape[-1]
+    loads = [mover.local(y_in, y_all), mover.local(dc_in, outs[1])]
     jobs = [
         ReduceNear(
             mover, shrink.at[spot.k], shrink.at[1 - spot.k], width // 2, shrink_quad, refs.take(6)
@@ -724,11 +910,17 @@
     ]
 
     def open_all():
+        start(loads)
         spot.meet(all_axes)
         for job in jobs:
             start(job.first)
+        scratch[0][...] = jnp.transpose(c_ref[...])
+        wait(loads)
 
     def close_all():
+        for place in range(2):
+            kept[block_rows(place), :] = chosen_block(back_ref[place], y_all).astype(low)
+            sent[block_rows(place), :] = chosen_block(back_ref[2 + place], y_all).astype(low)
         jobs[1].close()
 
     step = pl.program_id(0)
@@ -740,36 +932,43 @@
         (6, 1, jobs[1].go_far),
         (7, 1, jobs[0].close),
     ]
-    mlp_tile(False, rows_step, *inputs, before, outs, scratch, hooks(step, schedule))
+    mlp_tile(
+        rows_step, c_ref, dy_ref, we_ref, ws_ref, be_ref, outs, scratch, hooks(step, schedule)
+    )
     pl.when(step == pl.num_programs(0) - 1)(close_all)
 
 
-def mlp_reduce(sizes, c, dy, we, ws, be, before, grads, tile=256, rows_step=256):
-    in_specs, out_specs, out_shape, scratch = mlp_parts(*c.shape, we.shape[1], tile)
+def mlp_reduce(sizes, back, c, dy, we, ws, be, before, grads, tile=256, rows_step=256):
+    tokens, model = c.shape
+    in_specs, out_specs, out_shape, scratch = mlp_parts(tokens, model, we.shape[1], tile)
     expand, shrink = grads
     depth, rows = sizes["z"], expand.shape[3]
     grown, full = expand.shape[-1] // 2, shrink.shape[-1]
-    scratch = scratch + [pltpu.SemaphoreType.DMA((2,)), pltpu.SemaphoreType.DMA((2, 16))]
+    scratch = scratch + [pltpu.SemaphoreType.DMA((2, 16)), pltpu.VMEM((tokens, model), jnp.float32)]
     for columns in (full, grown):
         scratch += ReduceNear.scratch(sizes, rows, columns, columns // 2)
     return pl.pallas_call(
         functools.partial(mlp_reduce_kernel, sizes, rows_step),
         grid=(we.shape[1] // tile,),
-        in_specs=in_specs + [any_place] * 4,
-        out_specs=out_specs + [whole_vmem] * 2,
-        out_shape=out_shape + [low_shape(depth, rows, grown), low_shape(depth, rows, full)],
+        in_specs=[pl.BlockSpec(memory_space=pltpu.SMEM)] + in_specs + [any_place] * 4,
+        out_specs=out_specs[1:] + [whole_vmem] * 4,
+        out_shape=out_shape[1:]
+        + [low_shape(depth, rows, grown), low_shape(depth, rows, full)]
+        + [low_shape(tokens // 2, model)] * 2,
         scratch_shapes=scratch,
         compiler_params=params(4, 60),
         cost_estimate=small_cost,
         name="mlp_reduce",
-    )(c, dy, we, ws, be, *before, *grads)
+    )(back, c, dy, we, ws, be, *before, *grads)
 
 
 def attend_back_kernel(sizes, blocks, *refs):
     refs = Refs(refs)
-    projected, upstream, lse_ref, mixing, expand, shrink, done_expand, done_shrink = refs.take(8)
-    back_ref, mixing_quad, expand_quad, shrink_quad, expand_out, shrink_out = refs.take(6)
-    turned, key_sum, value_sum, sems = refs.take(4)
+    pulled_ref, middle_ref, upstream_ref, mixed, mixing, gain_ref = refs.take(6)
+    projected, lse_ref, expand, shrink, done_expand, done_shrink, sent = refs.take(7)
+    back_ref, grad_ref, sums_ref, mixing_quad, expand_quad, shrink_quad = refs.take(6)
+    expand_out, shrink_out, far_out = refs.take(3)
+    turned, key_sum, value_sum, sems, branch_all, mixed_grad, theirs = refs.take(7)
     spot = Spot(sizes)
     mover = Mover(spot, sems)
     k = spot.k
@@ -777,18 +976,20 @@
     jobs = [
         ReduceNear(mover, shrink.at[k], shrink.at[1 - k], width // 2, shrink_quad, refs.take(6)),
         ReduceNear(mover, *core_halves(expand, k, grown), grown // 2, expand_quad, refs.take(6)),
-        ReduceNear(mover, *core_halves(mixing, k, half), half // 2, mixing_quad, refs.take(6)),
+        ReduceNear(mover, None, theirs, half // 2, mixing_quad, refs.take(6)),
     ]
     deep = [
         ReduceDeep(mover, done_expand, *refs.take(1)),
         ReduceDeep(mover, done_shrink, *refs.take(1)),
     ]
     ending = Finish(mover, *refs.take(2))
+    rows_copy = [mover.copy(sent.at[block_rows(0)], far_out, "c")]
 
     def open_all():
         spot.meet(all_axes)
-        for job in jobs:
+        for job in jobs[:2]:
             start(job.first)
+        start(rows_copy)
         for job in deep:
             start(job.copies)
 
@@ -804,38 +1005,84 @@
         ending.write(expand_out)
         jobs[1].close()
         jobs[2].close()
+        wait(rows_copy)
 
     step = pl.program_id(0)
-    schedule = [
-        (0, 0, open_all),
-        (1, 1, jobs[0].go_near),
-        (2, 1, jobs[1].go_near),
-        (2, 3, jobs[2].go_near),
-        (4, 0, jobs[0].go_far),
-        (5, 3, finish),
-        (6, 2, jobs[1].go_far),
-        (7, 2, jobs[2].go_far),
-        (7, 3, jobs[0].close),
-    ]
-    attend_back_pair(
-        blocks, projected, upstream, lse_ref, back_ref, turned, key_sum, value_sum,
-        hooks(step, schedule),
+    between = hooks(
+        step,
+        [
+            (0, 0, open_all),
+            (3, 0, jobs[0].go_near),
+            (4, 0, jobs[1].go_near),
+            (4, 2, jobs[2].go_near),
+            (6, 2, jobs[0].go_far),
+            (7, 2, finish),
+            (9, 0, jobs[1].go_far),
+            (10, 0, jobs[2].go_far),
+            (11, 1, jobs[0].close),
+        ],
     )
+    between(0)
+
+    @pl.when(step < blocks)
+    def _():
+        rows = pl.ds(pl.multiple_of(step * BLK, BLK), BLK)
+        pulled = pulled_ref[...]
+        upstream = upstream_ref[...].astype(jnp.float32)
+        normal, inverse = normal_rows(middle_ref[...])
+        total = upstream + norm_pull(pulled, normal, inverse, gain_ref[...])
+        grad_ref[...] = total
+        branch = total.astype(low)
+        branch_all[rows, :] = branch
+        mixed_grad[rows, :] = nt(branch, mixing[...]).astype(low)
+
+        @pl.when(step == 0)
+        def _():
+            sums_ref[...] = jnp.zeros_like(sums_ref)
+
+        for row, value in enumerate((branch.astype(jnp.float32), pulled * normal, pulled, upstream)):
+            sums_ref[row : row + 1, :] += jnp.sum(value, axis=0, keepdims=True)
+
+    @pl.when(step == blocks - 1)
+    def _():
+        for core, target in ((1 - k, theirs), (k, jobs[2].total)):
+            piece = outer_sum(mixed[...], branch_all[:, span(core * half, half)]).astype(low)
+            target[...] = piece.reshape(target.shape)
+        start(jobs[2].first)
+
+    @pl.when(step >= blocks)
+    def _():
+        columns = span((step - blocks) * PAIR, PAIR)
+        attend_back_pair(
+            blocks, projected, mixed_grad.at[:, columns], lse_ref, back_ref, turned, key_sum,
+            value_sum, lambda block: block > 0 and between(block),
+        )
+
     pl.when(step == pl.num_programs(0) - 1)(close_all)
 
 
-def attend_back(sizes, blocks, projected, upstream, lse, grads, quads):
-    tokens, width = upstream.shape
-    pairs = width // PAIR
-    mixing, expand, shrink = grads
-    depth, rows = sizes["z"], mixing.shape[3]
-    half, grown, full = mixing.shape[-1] // 2, expand.shape[-1] // 2, shrink.shape[-1]
-    triple = pl.BlockSpec((tokens, 3 * PAIR), lambda g: (0, g))
+def attend_back(sizes, pulled, middle, upstream, mixed, mixing, gain, projected, lse, grads, quads, sent):
+    tokens, model = upstream.shape
+    pairs = model // PAIR
+    blocks = tokens // BLK
+    expand, shrink = grads
+    depth, rows = sizes["z"], expand.shape[3]
+    lead = (sizes["c"], sizes["z"], sizes["y"])
+    half, grown, full = model // 2, expand.shape[-1] // 2, shrink.shape[-1]
+    by_rows = pl.BlockSpec((BLK, model), lambda g: (jnp.minimum(g, blocks - 1), 0))
+
+    def pair(g):
+        return jnp.maximum(g - blocks, 0)
+
+    triple = pl.BlockSpec((tokens, 3 * PAIR), lambda g: (0, pair(g)))
     scratch = [
         pltpu.VMEM((blocks, PAIR, BLK), low),
         pltpu.VMEM((blocks, BLK, PAIR), jnp.float32),
         pltpu.VMEM((blocks, BLK, PAIR), jnp.float32),
         pltpu.SemaphoreType.DMA((2, 32)),
+        pltpu.VMEM((tokens, model), low),
+        pltpu.VMEM((tokens, model), low),
+        pltpu.VMEM((*lead, rows, half), low),
     ]
     for columns in (full, grown, half):
         scratch += ReduceNear.scratch(sizes, rows, columns, columns // 2)
@@ -844,48 +1091,38 @@
     scratch += Finish.scratch(rows, grown)
     return pl.pallas_call(
         functools.partial(attend_back_kernel, sizes, blocks),
-        grid=(pairs,),
-        in_specs=[
-            triple,
-            pl.BlockSpec((tokens, PAIR), lambda g: (0, g)),
-            pl.BlockSpec((None, 8, tokens), lambda g: (g, 0, 0)),
-        ]
-        + [any_place] * 3
-        + [whole_vmem] * 2,
-        out_specs=[triple] + [whole_vmem] * 5,
+        grid=(blocks + pairs,),
+        in_specs=[by_rows] * 3
+        + [whole_vmem] * 3
+        + [triple, pl.BlockSpec((None, 8, tokens), lambda g: (pair(g), 0, 0))]
+        + [any_place] * 2
+        + [whole_vmem] * 2
+        + [any_place],
+        out_specs=[triple, by_rows] + [whole_vmem] * 6 + [any_place],
         out_shape=[
             low_shape(*projected.shape),
+            jax.ShapeDtypeStruct((tokens, model), jnp.float32),
+            jax.ShapeDtypeStruct((8, model), jnp.float32),
             low_shape(depth, rows, half),
             low_shape(depth, rows, grown),
             low_shape(depth, rows, full),
             jax.ShapeDtypeStruct((2, rows // 2, grown), jnp.float32),
             jax.ShapeDtypeStruct((rows, full), jnp.float32),
+            low_shape(BLK, model),
         ],
         scratch_shapes=scratch,
-        compiler_params=params(5, 56),
+        compiler_params=params(5, 60),
         cost_estimate=small_cost,
         name="attend_back",
-    )(projected, upstream, lse, *grads, *quads)
-
-
-def normal_rows(rows):
-    centered = rows - jnp.mean(rows, axis=-1, keepdims=True)
-    inverse = lax.rsqrt(jnp.mean(centered * centered, axis=-1, keepdims=True) + norm_eps)
-    return centered * inverse, inverse
-
-
-def norm_pull(upstream, normal, inverse, gain):
-    scaled = upstream * gain
-    inner = jnp.mean(scaled, axis=-1, keepdims=True)
-    along = jnp.mean(scaled * normal, axis=-1, keepdims=True)
-    return inverse * (scaled - inner - normal * along)
+    )(pulled, middle, upstream, mixed, mixing, gain, projected, lse, *grads, *quads, sent)
 
 
 def end_kernel(sizes, *refs):
     refs = Refs(refs)
     back_ref, back_far, low_far, joint_far, rows_far, middle_far = refs.take(6)
-    gain_ref, vector, mixing_quad, expand_quad, shrink_quad = refs.take(5)
-    out, vector_out, mixing_out, expand_out, shrink_out, kept, arrived_rows = refs.take(7)
+    gain_ref, vector, mixing_quad, expand_quad, shrink_quad, sent_out = refs.take(6)
+    out, vector_out, mixing_out, expand_out, shrink_out, kept = refs.take(6)
+    arrived_rows, far_out = refs.take(2)
     sems, steps, arrived = refs.take(3)
     grads, low_rows, turned, joint, rows_in, middle, sent = refs.take(7)
     spot = Spot(sizes)
@@ -923,6 +1160,7 @@
         mover.copy(steps.at[3], arrived.at[2 + by], "z", by) for by in range(1, sizes["z"])
     ]
     rows_copy = mover.copy(sent, arrived_rows, "c")
+    out_copy = mover.copy(sent_out.at[block_rows(1)], far_out, "c")
 
     def gradient(core, number, target):
         @pl.loop(0, part // tile)
@@ -947,29 +1185,24 @@
             value = jnp.sum(value, axis=0, keepdims=True)
             sums[name] = sums[name] + value if name in sums else value
 
-    def stored_block(place):
-        number = jnp.full((1, middle.shape[1]), back_ref[place], jnp.int32)
-        value = middle[block_rows(0), :]
-        for other in range(1, middle.shape[0] // BLK):
-            value = jnp.where(number == other, middle[block_rows(other), :], value)
-        return value
-
     def hop(number):
         wait([hops[number]])
         steps[number + 1] = steps[number] + arrived[number]
         start([hops[number + 1]] if number < 2 else spread)
 
-    start(loads)
+    start(loads[:2])
     spot.meet(all_axes)
-    for job in others:
-        start(job.copies)
+    start([out_copy])
     wait(loads[:2])
+    start(loads[2:])
     turned[...] = jnp.transpose(low_rows[...])
     for number, job in enumerate(jobs):
         gradient(1 - spot.k, number, others_half[number])
         start(job.first)
         gradient(spot.k, number, job.total)
         job.go_near()
+    for job in others:
+        start(job.copies)
     wait(loads[2:])
     pull_block(0)
     pull_block(1)
@@ -978,10 +1211,10 @@
     jobs[1].go_far()
     pull_block(3)
     for place in range(2):
-        sent[block_rows(place), :] = stored_block(2 + place).astype(low)
+        sent[block_rows(place), :] = chosen_block(back_ref[2 + place], middle).astype(low)
     start([rows_copy])
     for place in range(2):
-        kept[block_rows(place), :] = stored_block(place)
+        kept[block_rows(place), :] = chosen_block(back_ref[place], middle)
     steps[0] = vector[...]
     steps[0, 0:1, :] = sums["gain"]
     steps[0, 1:2, :] = sums["shift"]
@@ -1019,10 +1252,10 @@
     for number, ending in enumerate(ends):
         wait(ending.copies)
         ending.write(out, pl.ds(number * part, part))
-    wait([rows_copy])
-
-
-def end(sizes, back, joint_back, first_low, joint, rows_in, middle_grad, gain, vector, quads):
+    wait([rows_copy, out_copy])
+
+
+def end(sizes, back, joint_back, first_low, joint, rows_in, middle_grad, gain, vector, quads, sent):
     tokens, model = rows_in.shape
     width = joint.shape[1] // 2
     lead = (sizes["c"], sizes["z"], sizes["y"])
@@ -1055,85 +1288,24 @@
     shapes.append((tokens // 2, model))
     return pl.pallas_call(
         functools.partial(end_kernel, sizes),
-        in_specs=[pl.BlockSpec(memory_space=pltpu.SMEM)] + [any_place] * 5 + [whole_vmem] * 5,
-        out_specs=[whole_vmem] * 6 + [any_place],
+        in_specs=[pl.BlockSpec(memory_space=pltpu.SMEM)]
+        + [any_place] * 5
+        + [whole_vmem] * 5
+        + [any_place],
+        out_specs=[whole_vmem] * 6 + [any_place] * 2,
         out_shape=[jax.ShapeDtypeStruct(shape, jnp.float32) for shape in shapes]
-        + [low_shape(tokens // 2, model)],
+        + [low_shape(tokens // 2, model), low_shape(BLK, model)],
         scratch_shapes=scratch,
         compiler_params=params(6, 60),
         cost_estimate=small_cost,
         name="end",
-    )(back, joint_back, first_low, joint, rows_in, middle_grad, gain, vector, *quads)
-
-
-def give_kernel(back_ref, middle_ref, result_ref, shift_ref, kept_ref, sent_ref):
-    value = (middle_ref[...] + result_ref[...] + shift_ref[...]).astype(low)
-    step = pl.program_id(0)
-
-    @pl.when(step < 2)
-    def _():
-        kept_ref[...] = value
-
-    @pl.when(step >= 2)
-    def _():
-        sent_ref[...] = value
-
-
-def give(back, middle, result, shift):
-    width = middle.shape[1]
-    block = pl.BlockSpec((BLK, width), lambda p, back: (back[p], 0))
-    return pl.pallas_call(
-        give_kernel,
-        grid_spec=pltpu.PrefetchScalarGridSpec(
-            num_scalar_prefetch=1,
-            grid=(back.shape[0],),
-            in_specs=[block, block, pl.BlockSpec((1, width), lambda p, back: (0, 0))],
-            out_specs=[
-                pl.BlockSpec((BLK, width), lambda p, back: (jnp.minimum(p, 1), 0)),
-                pl.BlockSpec((BLK, width), lambda p, back: (jnp.maximum(p - 2, 0), 0)),
-            ],
-        ),
-        out_shape=[low_shape(2 * BLK, width)] * 2,
-        cost_estimate=small_cost,
-        name="give",
-    )(back, middle, result, shift)
-
-
-def take_kernel(place_ref, kept_ref, arrived_ref, out_ref):
-    here = place_ref[pl.program_id(0)] < 2
-
-    @pl.when(here)
-    def _():
-        out_ref[...] = kept_ref[...]
-
-    @pl.when(jnp.logical_not(here))
-    def _():
-        out_ref[...] = arrived_ref[...]
-
-
-def take(place, kept, arrived):
-    width = kept.shape[1]
-    return pl.pallas_call(
-        take_kernel,
-        grid_spec=pltpu.PrefetchScalarGridSpec(
-            num_scalar_prefetch=1,
-            grid=(place.shape[0],),
-            in_specs=[
-                pl.BlockSpec((BLK, width), lambda i, place: (jnp.minimum(place[i], 1), 0)),
-                pl.BlockSpec((BLK, width), lambda i, place: (jnp.maximum(place[i] - 2, 0), 0)),
-            ],
-            out_specs=pl.BlockSpec((BLK, width), lambda i, place: (i, 0)),
-        ),
-        out_shape=low_shape(4 * BLK, width),
-        cost_estimate=small_cost,
-        name="take",
-    )(place, kept, arrived)
+    )(back, joint_back, first_low, joint, rows_in, middle_grad, gain, vector, *quads, sent)
 
 
 def last_kernel(ctx_ref, *refs):
     refs = Refs(refs)
     joint_part, mixing_part, expand_a, expand_b, shrink_a, shrink_b = refs.take(6)
-    kept_grad, far_grad, kept_out, far_out = refs.take(4)
+    kept_grad, far_grad, kept_out, far_one, far_two = refs.take(5)
     states = [refs.take(3) for _ in range(4)]
     grad_out, block_out = refs.take(2)
     news = [refs.take(4) for _ in range(4)]
@@ -1141,7 +1313,8 @@
     grad_out[here] = kept_grad[...]
     grad_out[1 - here] = far_grad[...].astype(jnp.float32)
     block_out[here] = kept_out[...]
-    block_out[1 - here] = far_out[...]
+    block_out[1 - here, :BLK, :] = far_one[...]
+    block_out[1 - here, BLK:, :] = far_two[...]
 
     def update(number, where, gradient):
         weight, first, second = [ref[where] for ref in states[number]]
@@ -1176,7 +1349,7 @@
     update(3, (pl.ds(rows, rows), every), shrink_b[...])
 
 
-def last(ctx, parts, kept_grad, far_grad, kept_out, far_out, states):
+def last(ctx, parts, kept_grad, far_grad, kept_out, far_outs, states):
     shapes = [jax.ShapeDtypeStruct((2, *kept_grad.shape), jnp.float32), low_shape(2, *kept_out.shape)]
     for weight, _, _ in states:
         shapes += [jax.ShapeDtypeStruct(weight.shape, jnp.float32)] * 3
@@ -1184,13 +1357,13 @@
     flat = [array for state in states for array in state]
     return pl.pallas_call(
         last_kernel,
-        in_specs=[pl.BlockSpec(memory_space=pltpu.SMEM)] + [whole_vmem] * (10 + len(flat)),
+        in_specs=[pl.BlockSpec(memory_space=pltpu.SMEM)] + [whole_vmem] * (11 + len(flat)),
         out_specs=[whole_vmem] * len(shapes),
         out_shape=shapes,
         compiler_params=pltpu.CompilerParams(vmem_limit_bytes=56 << 20),
         cost_estimate=small_cost,
         name="last",
-    )(ctx, *parts, kept_grad, far_grad, kept_out, far_out, *flat)
+    )(ctx, *parts, kept_grad, far_grad, kept_out, *far_outs, *flat)
 
 
 def layer_norm(values, gain_row, shift_row):
@@ -1492,10 +1665,6 @@
     row_blocks = row_count // BLK
     near = ctx_size == 2 and seq_count == 2 and sizes["y"] == 2 and own_rows % 32 == 0
 
-    def exchange(rows):
-        sent = lax.dynamic_index_in_dim(rows, 1 - ctx, 0, False)
-        return lax.dynamic_index_in_dim(rows, ctx, 0, False), grid.shift(sent, "c", 1)
-
     def hidden_sets(shard):
         parts = shard.astype(low).reshape(own_rows, chips, 2, 2, sub)
         return [
@@ -1503,24 +1672,29 @@
             for number in range(2)
         ]
 
-    joint_halves = (
-        joint_weight.astype(low)
-        .reshape(own_rows, 3, 2, pairs // 2, PAIR)
-        .transpose(2, 0, 3, 1, 4)
-        .reshape(2, own_rows, 3 * half)
-    )
     table = jnp.pad(vectors.T.astype(low), ((0, 0), (0, 128 - vectors.shape[0])))
-    mixing_halves = mixing_weight.astype(low).reshape(own_rows, 2, half).transpose(1, 0, 2)
-    shrink_low = shrink_weight.astype(low)
-    pieces = [joint_halves, table, mixing_halves, *hidden_sets(expand_weight)]
-    pieces += [shrink_low[:sub], shrink_low[sub:]]
     if near:
-        input_parts = exchange(block_input)
-        joint_halves, table, mixing_halves, expand_half, next_half, shrink, next_shrink = pieces
-        joint, tables, *quads = begin(
-            sizes, joint_halves, table, mixing_halves, expand_half, shrink
+        joint, tables, *quads, far_input, far_upstream, next_half, next_shrink = begin(
+            sizes,
+            joint_weight,
+            table,
+            mixing_weight,
+            expand_weight,
+            shrink_weight,
+            block_input,
+            cotangent,
         )
     else:
+        joint_halves = (
+            joint_weight.astype(low)
+            .reshape(own_rows, 3, 2, pairs // 2, PAIR)
+            .transpose(2, 0, 3, 1, 4)
+            .reshape(2, own_rows, 3 * half)
+        )
+        mixing_halves = mixing_weight.astype(low).reshape(own_rows, 2, half).transpose(1, 0, 2)
+        shrink_low = shrink_weight.astype(low)
+        pieces = [joint_halves, table, mixing_halves, *hidden_sets(expand_weight)]
+        pieces += [shrink_low[:sub], shrink_low[sub:]]
         joint, tables, mixing, expand_a, expand_b, shrink_a, shrink_b = gather_far(
             grid, here, pieces
         )
@@ -1537,16 +1711,6 @@
         place = jnp.sum(jnp.where(order[None, :] == stored[:, None], moved[None, :], 0), axis=1)
         back = jnp.sum(jnp.where(moved[None, :] == stored[:, None], order[None, :], 0), axis=1)
         place, back = place.astype(jnp.int32), back.astype(jnp.int32)
-        input_low = take(place, *input_parts)
-        upstream_parts = exchange(tie(cotangent, tables))
-    else:
-        input_low = block_input.reshape(tokens, width)
-        upstream = cotangent.reshape(tokens, width)
-    input_rows = input_low.astype(jnp.float32)
-    normed_first, normal_first, inverse_first = layer_norm(
-        input_rows, vector_values[0], vector_values[1]
-    )
-    first_low = normed_first.astype(low)
     joint_shift = jnp.stack(
         [
             vector_values[2].reshape(pairs, PAIR),
@@ -1554,13 +1718,67 @@
             vector_values[3].reshape(pairs, PAIR),
         ],
         axis=1,
-    ).reshape(-1)
-    projected = (nn(first_low, joint) + joint_shift).astype(low)
+    ).reshape(1, -1)
+    lead = (sizes["c"], sizes["z"], sizes["y"])
+    hidden_bias = vector_values[8:].reshape(chips, 2, 2, sub).transpose(2, 1, 0, 3).reshape(2, 1, -1)
+
+    def by_device(expand_grad, shrink_grad):
+        return (
+            expand_grad.reshape(*lead, -1, expand_grad.shape[1]),
+            shrink_grad.reshape(2, *lead, -1, width),
+        )
+
     if near:
-        mixed_low, logsum, mixing, expand_a, shrink_a, *quads = attend(
-            sizes, blocks, projected, quads, next_half, next_shrink
+        mixed_low, logsum, input_low, first_low, projected, *gathered = attend(
+            sizes,
+            place,
+            block_input,
+            far_input,
+            joint,
+            vector_values[:2],
+            joint_shift,
+            cotangent,
+            quads,
+            next_half,
+            next_shrink,
+        )
+        mixing, expand_a, shrink_a, *quads, last_upstream = gathered
+        mixing = mixing.reshape(width, width)
+        *before, expand_grad_a, shrink_grad_a, bias_a, middle, second_low, upstream, expand_b, shrink_b = mlp_gather(
+            sizes,
+            place,
+            mixed_low,
+            input_low,
+            mixing,
+            vector_values[:8],
+            expand_a.reshape(width, -1),
+            shrink_a.reshape(-1, width),
+            hidden_bias[0],
+            cotangent,
+            far_upstream,
+            last_upstream,
+            quads,
+        )
+        second_grad, expand_grad_b, shrink_grad_b, bias_b, *quads, kept_out, sent_out = mlp_reduce(
+            sizes,
+            back,
+            second_low,
+            upstream,
+            expand_b.reshape(width, -1),
+            shrink_b.reshape(-1, width),
+            hidden_bias[1],
+            before,
+            by_device(expand_grad_a, shrink_grad_a),
         )
     else:
+        input_low = block_input.reshape(tokens, width)
+        upstream = cotangent.reshape(tokens, width)
+        input_rows = input_low.astype(jnp.float32)
+        normed_first, normal_first, inverse_first = layer_norm(
+            input_rows, vector_values[0], vector_values[1]
+        )
+        first_low = normed_first.astype(low)
+        projected = (nn(first_low, joint) + joint_shift).astype(low)
         by_part = projected.reshape(seq_count, row_count, pairs, 3, PAIR)
         queries, keys, values = [
             by_part[:, :, :, part].reshape(seq_count, row_count, width) for part in range(3)
@@ -1574,80 +1792,57 @@
         allowed = key_block[:, None, :] <= query_block[:, :, None]
         mixed, logsum = spread_forward(queries, key_value, allowed)
         mixed_low = mixed.astype(low).reshape(tokens, width)
-    mixing = mixing.reshape(width, width)
-    middle = input_rows + (nn(mixed_low, mixing) + vector_values[4])
-    normed_second, normal_second, inverse_second = layer_norm(
-        middle, vector_values[5], vector_values[6]
-    )
-    second_low = normed_second.astype(low)
-    if near:
-        upstream = take(place, *upstream_parts)
-
-    lead = (sizes["c"], sizes["z"], sizes["y"])
-    hidden_bias = vector_values[8:].reshape(chips, 2, 2, sub).transpose(2, 1, 0, 3).reshape(2, 1, -1)
-
-    def operands(number, expand, shrink):
-        return (
+        mixing = mixing.reshape(width, width)
+        middle = input_rows + (nn(mixed_low, mixing) + vector_values[4])
+        normed_second, normal_second, inverse_second = layer_norm(
+            middle, vector_values[5], vector_values[6]
+        )
+        second_low = normed_second.astype(low)
+        before = (middle + vector_values[7], jnp.zeros_like(middle))
+        *before, expand_grad_a, shrink_grad_a, bias_a = mlp(
             second_low,
             upstream,
-            expand.reshape(width, -1),
-            shrink.reshape(-1, width),
-            hidden_bias[number],
-        )
-
-    def by_device(expand_grad, shrink_grad):
-        return (
-            expand_grad.reshape(*lead, -1, expand_grad.shape[1]),
-            shrink_grad.reshape(2, *lead, -1, width),
-        )
-
-    if near:
-        *before, expand_grad_a, shrink_grad_a, bias_a, expand_b, shrink_b = mlp_gather(
-            sizes, *operands(0, expand_a, shrink_a), quads
-        )
-        result, second_grad, expand_grad_b, shrink_grad_b, bias_b, *quads = mlp_reduce(
-            sizes,
-            *operands(1, expand_b, shrink_b),
+            expand_a.reshape(width, -1),
+            shrink_a.reshape(-1, width),
+            hidden_bias[0],
             before,
-            by_device(expand_grad_a, shrink_grad_a),
-        )
-    else:
-        *before, expand_grad_a, shrink_grad_a, bias_a = mlp(*operands(0, expand_a, shrink_a))
+        )
         result, second_grad, expand_grad_b, shrink_grad_b, bias_b = mlp(
-            *operands(1, expand_b, shrink_b), before=before
-        )
+            second_low,
+            upstream,
+            expand_b.reshape(width, -1),
+            shrink_b.reshape(-1, width),
+            hidden_bias[1],
+            before,
+        )
+        block_output = result.astype(low).reshape(block_input.shape)
     hidden_bias_grads = [
         bias.reshape(2, chips, 1, sub).transpose(1, 0, 2, 3) for bias in (bias_a, bias_b)
     ]
+
     if near:
-        kept_out, sent_out = give(back, middle, result, vector_values[7:8])
-        far_out = grid.shift(sent_out, "c", 1)
-        second_grad = tie(second_grad, sent_out)
+        joint_back, middle_grad, sums, *last_quads, expand_part_a, shrink_part_a, far_one = attend_back(
+            sizes,
+            second_grad,
+            middle,
+            upstream,
+            mixed_low,
+            mixing,
+            vector_values[5:6],
+            projected,
+            logsum,
+            by_device(expand_grad_b, shrink_grad_b),
+            quads,
+            sent_out,
+        )
     else:
-        block_output = (middle + result + vector_values[7]).astype(low).reshape(block_input.shape)
-
-    upstream_float = upstream.astype(jnp.float32)
-    middle_part, gain_two, shift_two = norm_back(
-        second_grad, normal_second, inverse_second, vector_values[5]
-    )
-    middle_grad = upstream_float + middle_part
-    branch_low = middle_grad.astype(low)
-    mixing_grad = outer_sum(mixed_low, branch_low).astype(low)
-    mixed_grad = nt(branch_low, mixing).astype(low)
-    if near:
-        joint_back, *last_quads, expand_part_a, shrink_part_a = attend_back(
-            sizes,
-            blocks,
-            projected,
-            mixed_grad,
-            logsum,
-            (
-                mixing_grad.reshape(*lead, -1, width),
-                *by_device(expand_grad_b, shrink_grad_b),
-            ),
-            quads,
-        )
-    else:
+        middle_part, gain_two, shift_two = norm_back(
+            second_grad, normal_second, inverse_second, vector_values[5]
+        )
+        middle_grad = upstream.astype(jnp.float32) + middle_part
+        branch_low = middle_grad.astype(low)
+        mixing_grad = outer_sum(mixed_low, branch_low).astype(low)
+        mixed_grad = nt(branch_low, mixing).astype(low)
         query_grad, key_value_grad = spread_backward(
             queries, key_value, allowed, logsum, mixed_grad.reshape(seq_count, row_count, width)
         )
@@ -1670,17 +1865,16 @@
         return jnp.sum(rows.astype(jnp.float32), axis=0)
 
     hidden_bias_grad = jnp.concatenate(hidden_bias_grads, axis=2).reshape(-1, width)
-    vector_rows = [column_sum(branch_low), gain_two, shift_two, column_sum(upstream)]
     weights = (joint_weight, mixing_weight, expand_weight, shrink_weight)
     firsts = (joint_first, mixing_first, expand_first, shrink_first)
     seconds = (joint_second, mixing_second, expand_second, shrink_second)
     if near:
         rows = vectors.shape[0]
         vector_grad = jnp.concatenate(
-            [jnp.zeros((4, width)), jnp.stack(vector_rows), hidden_bias_grad, jnp.zeros((-rows % 8, width))],
+            [jnp.zeros((4, width)), sums[:4], hidden_bias_grad, jnp.zeros((-rows % 8, width))],
             axis=0,
         )
-        joint_part, vector_sum, mixing_part, expand_part_b, shrink_part_b, kept_grad, far_grad = end(
+        joint_part, vector_sum, mixing_part, expand_part_b, shrink_part_b, kept_grad, far_grad, far_two = end(
             sizes,
             back,
             joint_back,
@@ -1691,6 +1885,7 @@
             vector_values[0:1],
             vector_grad,
             last_quads,
+            sent_out,
         )
         input_gradient, block_output, *news = last(
             ctx.astype(jnp.int32).reshape(1),
@@ -1698,7 +1893,7 @@
             kept_grad,
             far_grad,
             kept_out,
-            far_out,
+            (far_one, far_two),
             list(zip(weights, firsts, seconds)),
         )
         updated, moments, squares, copies = [news[number::4] for number in range(4)]
@@ -1715,7 +1910,11 @@
             shift_one,
             joint_sums[:, 0].reshape(-1),
             joint_sums[:, 2].reshape(-1),
-        ] + vector_rows
+            column_sum(branch_low),
+            gain_two,
+            shift_two,
+            column_sum(upstream),
+        ]
         joint_part = reduce_far(grid, here, joint_grad, False)
         vector_sum = grid.everywhere(
             jnp.concatenate([jnp.stack(vector_rows), hidden_bias_grad], axis=0)

time: 442 us -> 409 us (0.925)
  Pallas kernels: 368 us -> 389 us
  matrix products: 20.5 us -> 0 us
  other arithmetic: 21.7 us -> 5.58 us
  local copies, waits for them, and re-layouts: 20.4 us -> 8 us
  starting transfers between devices: 6.35 us -> 0 us
    dot_general x4 -> x0, matrix products: 20.5 us -> none  [the longest x2 13.1 us: nn(): return jnp.dot(left_side, right_side, preferred_element_type=jnp.float32)]
    reduce_sum x5 -> x0, other arithmetic: 13.5 us -> none  [the longest x1 4.97 us: norm_back(): jnp.sum(upstream * normal_part, axis=0)]
    pallas_call x1, Pallas kernels: 58.1 us -> 70.1 us  [begin(): pl.pallas_call(functools.partial(begin_kernel, sizes), in_specs=[whole_vm...]
    pallas_call x1, Pallas kernels: 55.7 us -> 64.8 us  [attend_back(): pl.pallas_call(functools.partial(attend_back_kernel, sizes, blocks), grid...]
    ppermute x3 -> x0, starting transfers between devices: 6.35 us -> none  [shift(): return lax.ppermute(value, axes, pairs)]
    squeeze x4 -> x2, local copies, waits for them, and re-layouts: 7.6 us -> 1.36 us  [the longest x1 0.68 us: body(): hidden_bias[0]]
    unnamed x59 -> x13, local copies, waits for them, and re-layouts: 7.74 us -> 1.71 us
    convert_element_type x6 -> x0, other arithmetic: 4.57 us -> none  [the longest x1 2.41 us: body(): first_low = normed_first.astype(low)]
  transfers between devices with their start and end apart: 3 -> 0, of which waited for: 0 -> 0; matrix products, arithmetic and copies ran while one was open for 12% -> 0% of each run, Pallas kernels for 55% -> 0%
where the time goes in v4:
time: 409 us; the launch traced here: 403 us
  Pallas kernels  389 us (95%)
  local copies, waits for them, and re-layouts  8 us (2%)
  other arithmetic  5.58 us (1%)
    pallas_call x1, Pallas kernels, end(): pl.pallas_call(functools.partial(end_kernel, sizes), in_specs=[pl.BlockSp...  74.6 us
    pallas_call x1, Pallas kernels, begin(): pl.pallas_call(functools.partial(begin_kernel, sizes), in_specs=[whole_vm...  70.1 us
    pallas_call x1, Pallas kernels, attend_back(): pl.pallas_call(functools.partial(attend_back_kernel, sizes, blocks), grid...  64.8 us
    pallas_call x1, Pallas kernels, attend(): pl.pallas_call(functools.partial(attend_kernel, sizes, blocks), grid=(blo...  59.5 us
    pallas_call x1, Pallas kernels, mlp_gather(): pl.pallas_call(functools.partial(mlp_gather_kernel, sizes, blocks, rows_s...  57.8 us
    pallas_call x1, Pallas kernels, mlp_reduce(): pl.pallas_call(functools.partial(mlp_reduce_kernel, sizes, rows_step), gr...  52.3 us
    pallas_call x1, Pallas kernels, last(): pl.pallas_call(last_kernel, in_specs=[pl.BlockSpec(memory_space=pltpu.SME...  9.33 us

profile of v4, /device:TPU:0, one launch (start us, length us, event | category | flops | bytes accessed | tf_op | source)
XLA Modules:
  0.0 403.2 jit_solution(12266042003531829107)
XLA Ops:
  0.7 0.0 copy-start
  0.8 0.6 copy-done
  1.4 0.7 select_reduce_fusion
  2.0 0.7 convert_element_type.17
  2.7 0.1 copy.63
  2.8 0.6 pad.4.refs_1_
  3.4 70.1 %begin.1 = (bf16[2,4,2,64,3072]{4,3,2,1,0:T(8,128)(2,1)}, bf16[2,4,2,64,128]{4,3,2,1,0:T(8,128)(2,1)}, bf16[4,64,512]{2,1,0:T(8,128)(2,1)}, bf16[4,64,1024]{2,1,...) custom-call(f32[32,3072]{1,0:T(8,128)} %refs_11_.1, ...), custom_call_target="tpu_custom_call" | custom-call | flops 1024 | bytes 1024 | tf_op jit(solution)/shard_map/begin/pallas_call | solution.py:498
  73.5 1.1 copy.71
  74.6 0.6 fusion.4
  75.2 0.1 pad.12.clone
  75.3 0.1 pad_maximum_fusion.2
  75.4 0.6 reshape.126.refs_5_
  76.0 0.6 slice.47.refs_4_
  76.6 59.5 %attend.1 = (bf16[1024,1024]{1,0:T(8,128)(2,1)}, f32[8,8,1024]{2,1,0:T(8,128)}, bf16[1024,1024]{1,0:T(8,128)(2,1)}, bf16[1024,1024]{1,0:T(8,128)(2,1)}, bf16[102...) custom-call(s32[4]{0:T(128)} %get-tuple-element.168.refs_0_, ...), custom_call_target="tpu_custom_call" | custom-call | flops 1024 | bytes 1024 | tf_op jit(solution)/shard_map/attend/pallas_call | solution.py:647
  136.1 0.1 reshape.130
  136.3 0.7 squeeze.6.refs_7_
  136.9 0.6 slice.50.refs_4_
  137.6 57.8 %mlp_gather.1 = (f32[1024,1024]{1,0:T(8,128)}, f32[1024,1024]{1,0:T(8,128)}, bf16[1024,2048]{1,0:T(8,128)(2,1)}, bf16[2048,1024]{1,0:T(8,128)(2,1)}, f32[1,2048]...) custom-call(s32[4]{0:T(128)} %get-tuple-element.168.refs_0_, ...), custom_call_target="tpu_custom_call" | custom-call | flops 1024 | bytes 1024 | tf_op jit(solution)/shard_map/mlp_gather/pallas_call | solution.py:867
  195.4 0.7 squeeze.7.refs_5_
  196.1 52.3 %mlp_reduce.1 = (f32[1024,1024]{1,0:T(8,128)}, bf16[1024,2048]{1,0:T(8,128)(2,1)}, bf16[2048,1024]{1,0:T(8,128)(2,1)}, f32[1,2048]{1,0:T(1,128)}, bf16[4,64,1024...) custom-call(s32[4]{0:T(128)} %get-tuple-element.169.refs_0_, ...), custom_call_target="tpu_custom_call" | custom-call | flops 1024 | bytes 1024 | tf_op jit(solution)/shard_map/mlp_reduce/pallas_call | solution.py:950
  248.4 0.5 broadcast.98
  248.9 1.4 reduce.6
  250.3 0.1 reshape.138
  250.4 0.7 reduce.7
  251.1 0.1 reshape.137
  251.2 0.1 reshape.139
  251.3 64.8 %attend_back.1 = (bf16[1024,3072]{1,0:T(8,128)(2,1)}, f32[1024,1024]{1,0:T(8,128)}, f32[8,1024]{1,0:T(8,128)}, bf16[4,64,512]{2,1,0:T(8,128)(2,1)}, bf16[4,64,10...) custom-call(f32[1024,1024]{1,0:T(8,128)} %get-tuple-element.120.refs, ...), custom_call_target="tpu_custom_call" | custom-call | flops 1024 | bytes 1024 | tf_op jit(solution)/shard_map/attend_back/pallas_call | solution.py:1092
  316.1 0.8 slice.45
  316.9 0.7 pad_maximum_fusion.refs_7_
  317.5 74.6 %end.1 = (f32[2,32,1536]{2,1,0:T(8,128)}, f32[16,1024]{1,0:T(8,128)}, f32[2,32,512]{2,1,0:T(8,128)}, f32[2,32,1024]{2,1,0:T(8,128)}, f32[64,1024]{1,0:T(8,128)},...) custom-call(s32[4]{0:T(128)} %get-tuple-element.169.refs_0_, ...), custom_call_target="tpu_custom_call" | custom-call | flops 1024 | bytes 1024 | tf_op jit(solution)/shard_map/end/pallas_call | solution.py:1289
  392.2 9.3 %last.1 = (f32[2,512,1024]{2,1,0:T(8,128)}, bf16[2,512,1024]{2,1,0:T(8,128)(2,1)}, f32[32,3072]{1,0:T(8,128)}, f32[32,3072]{1,0:T(8,128)}, f32[32,3072]{1,0:T(8,...) custom-call(s32[1]{0:T(128)} %bitcast.ctx_ref, ...), custom_call_target="tpu_custom_call" | custom-call | flops 1024 | bytes 1024 | tf_op jit(solution)/shard_map/last/pallas_call | solution.py:1358
  401.6 1.4 fusion.2
  (20 shorter events, 0.2 us)
Async XLA Ops:
  0.7 0.7 copy-start
  196.1 54.3 %copy-start.5 = (f32[1,2048]{1,0:T(1,128)S(1)}, f32[1,2048]{1,0:T(1,128)}, u32[]{:S(2)}) copy-start(f32[1,2048]{1,0:T(1,128)} %get-tuple-element.133) | copy-start | bytes 24580
  392.2 10.8 %copy-start.1 = (s32[2,4]{1,0:T(2,128)S(1)}, s32[2,4]{1,0:T(2,128)}, u32[]{:S(2)}) copy-start(s32[2,4]{1,0:T(2,128)} %param.19) | copy-start | bytes 100
  392.2 9.4 %copy-start.2 = (f32[12,32]{1,0:T(8,128)S(1)}, f32[12,32]{1,0:T(8,128)}, u32[]{:S(2)}) copy-start(f32[12,32]{1,0:T(8,128)} %param.25) | copy-start | bytes 4612
  392.2 9.4 %copy-start.3 = (f32[12,32]{1,0:T(8,128)S(1)}, f32[12,32]{1,0:T(8,128)}, u32[]{:S(2)}) copy-start(f32[12,32]{1,0:T(8,128)} %param.30) | copy-start | bytes 4612
  392.2 9.4 %copy-start.4 = (f32[12,32]{1,0:T(8,128)S(1)}, f32[12,32]{1,0:T(8,128)}, u32[]{:S(2)}) copy-start(f32[12,32]{1,0:T(8,128)} %param.35) | copy-start | bytes 4612

commit v5 on v4

--- a/solution.py
+++ b/solution.py
@@ -48,34 +48,32 @@
     return [ref.at[:, pl.ds(part * PAIR, PAIR)] for part in range(3)]
 
 
+def both_heads(rows):
+    lane = lax.broadcasted_iota(jnp.int32, (1, PAIR), 1)
+    empty = jnp.zeros_like(rows)
+    return jnp.concatenate(
+        [jnp.where(lane < HD, rows, empty), jnp.where(lane < HD, empty, rows)], axis=0
+    )
+
+
 def attend_pair(blocks, projected, o_ref, lse_ref, between):
     q_ref, k_ref, v_ref = thirds(projected)
     lane = lax.broadcasted_iota(jnp.int32, (1, PAIR), 1)
-    masks = [lane < HD, lane >= HD]
     for i in range(blocks):
         between(i)
         rows = block_rows(i)
-        queries = q_ref[rows, :]
-        outs = []
+        queries = both_heads(q_ref[rows, :])
+        upto = pl.ds(0, (i + 1) * BLK)
+        scores = nt(queries, k_ref[upto, :]) * score_scale
+        top = jnp.max(scores, axis=1, keepdims=True)
+        weights = jnp.exp2(scores - top)
+        total = jnp.sum(weights, axis=1, keepdims=True)
+        mixed = nn(weights.astype(low), v_ref[upto, :])
+        mixed = mixed * (1.0 / total)
+        o_ref[rows, :] = jnp.where(lane < HD, mixed[:BLK], mixed[BLK:]).astype(o_ref.dtype)
+        logsum = jnp.transpose(jnp.broadcast_to(top + jnp.log2(total), (2 * BLK, PAIR)))
         for h in range(2):
-            masked = jnp.where(masks[h], queries, jnp.zeros_like(queries))
-            scores = [nt(masked, k_ref[block_rows(j), :]) * score_scale for j in range(i + 1)]
-            top = scores[0]
-            for score in scores[1:]:
-                top = jnp.maximum(top, score)
-            top = jnp.max(top, axis=1, keepdims=True)
-            weights = [jnp.exp2(score - top) for score in scores]
-            total = weights[0]
-            for weight in weights[1:]:
-                total = total + weight
-            total = jnp.sum(total, axis=1, keepdims=True)
-            mixed = nn(weights[0].astype(low), v_ref[block_rows(0), :])
-            for j in range(1, i + 1):
-                mixed = mixed + nn(weights[j].astype(low), v_ref[block_rows(j), :])
-            outs.append(mixed * (1.0 / total))
-            logsum = jnp.broadcast_to(top + jnp.log2(total), (BLK, PAIR))
-            lse_ref[h : h + 1, rows] = jnp.transpose(logsum)[0:1, :]
-        o_ref[rows, :] = jnp.where(masks[0], outs[0], outs[1]).astype(o_ref.dtype)
+            lse_ref[h : h + 1, rows] = logsum[0:1, h * BLK : (h + 1) * BLK]
 
 
 def attend_back_pair(
@@ -83,46 +81,30 @@
 ):
     q_ref, k_ref, v_ref = thirds(projected)
     dq_ref, dk_ref, dv_ref = thirds(back_ref)
-    lane = lax.broadcasted_iota(jnp.int32, (1, PAIR), 1)
-    masks = [lane < HD, lane >= HD]
-    for j in range(blocks):
-        turned[j] = jnp.transpose(k_ref[block_rows(j), :])
+    turned[...] = jnp.transpose(k_ref[...])
     for i in range(blocks):
         between(i)
         rows = block_rows(i)
-        queries, upstream = q_ref[rows, :], do_ref[rows, :]
-        query_grads = []
-        for h in range(2):
-            masked = jnp.where(masks[h], queries, jnp.zeros_like(queries))
-            pulled = jnp.where(masks[h], upstream, jnp.zeros_like(upstream))
-            logsum = lse_ref[h : h + 1, rows]
-            weights, pulls, inner = [], [], None
-            for j in range(i + 1):
-                weight = jnp.exp2(nt(k_ref[block_rows(j), :], masked) * score_scale - logsum)
-                pull = nt(v_ref[block_rows(j), :], pulled)
-                along = jnp.sum(weight * pull, axis=0, keepdims=True)
-                inner = along if inner is None else inner + along
-                weights.append(weight)
-                pulls.append(pull)
-            query_grad = None
-            for j in range(i + 1):
-                score_grad = (weights[j] * (pulls[j] - inner)).astype(low)
-                value_grad = nn(weights[j].astype(low), pulled)
-                key_grad = nn(score_grad, masked)
-                if i == j and h == 0:
-                    value_sum[j] = value_grad
-                    key_sum[j] = key_grad
-                else:
-                    value_sum[j] += value_grad
-                    key_sum[j] += key_grad
-                piece = nn(turned[j, h * HD : (h + 1) * HD, :], score_grad)
-                query_grad = piece if query_grad is None else query_grad + piece
-            query_grads.append(query_grad)
-        joined = jnp.transpose(jnp.concatenate(query_grads, axis=0))
-        dq_ref[rows, :] = (joined * 0.125).astype(dq_ref.dtype)
-    for j in range(blocks):
-        dk_ref[block_rows(j), :] = (key_sum[j] * 0.125).astype(dk_ref.dtype)
-        dv_ref[block_rows(j), :] = value_sum[j].astype(dv_ref.dtype)
+        queries, upstream = both_heads(q_ref[rows, :]), both_heads(do_ref[rows, :])
+        logsum = jnp.concatenate([lse_ref[0:1, rows], lse_ref[1:2, rows]], axis=1)
+        upto = pl.ds(0, (i + 1) * BLK)
+        weights = jnp.exp2(nt(k_ref[upto, :], queries) * score_scale - logsum)
+        pulls = nt(v_ref[upto, :], upstream)
+        inner = jnp.sum(weights * pulls, axis=0, keepdims=True)
+        score_grad = (weights * (pulls - inner)).astype(low)
+        value_grad = nn(weights.astype(low), upstream)
+        key_grad = nn(score_grad, queries)
+        query_grad = nn(turned[:, upto], score_grad)
+        earlier, latest = pl.ds(0, i * BLK), block_rows(i)
+        if i > 0:
+            value_sum[earlier, :] += value_grad[: i * BLK]
+            key_sum[earlier, :] += key_grad[: i * BLK]
+        value_sum[latest, :] = value_grad[i * BLK :]
+        key_sum[latest, :] = key_grad[i * BLK :]
+        joined = jnp.concatenate([query_grad[:HD, :BLK], query_grad[HD:, BLK:]], axis=0)
+        dq_ref[rows, :] = (jnp.transpose(joined) * 0.125).astype(dq_ref.dtype)
+    dk_ref[...] = (key_sum[...] * 0.125).astype(dk_ref.dtype)
+    dv_ref[...] = value_sum[...].astype(dv_ref.dtype)
 
 
 def hooks(step, schedule):
@@ -430,9 +412,15 @@
     later_first = first_rows(mover, mixing_halves, mixing_quad)
     later_first += first_rows(mover, expand_halves, expand_quad)
     later_first += [mover.local(shrink, shrink_quad.at[spot.z])]
-    now = Deep(mover, joint_quad).copies + Deep(mover, table_quad).copies
+    part = width // 2
+    chunks = [joint_quad.at[:, :, pl.ds(first, part)] for first in (0, part)]
+    now = [Deep(mover, chunk).copies for chunk in chunks]
+    thin_deep = Deep(mover, table_quad).copies
     later = [Deep(mover, quad).copies for quad in (mixing_quad, shrink_quad, expand_quad)]
-    job = Near(mover, joint_quad, joint, spot.k * width, cut_of(width))
+    jobs = [
+        Near(mover, chunk, joint, spot.k * width + number * part, part)
+        for number, chunk in enumerate(chunks)
+    ]
     thin = Near(mover, table_quad, tables, 0, table.shape[1], core=False)
     rows_copies = [
         mover.copy(rows_in.at[1 - spot.c], far_rows, "c"),
@@ -450,6 +438,8 @@
     spot.meet(all_axes)
     start(joint_first)
     start(rows_copies[:1])
+    wait(joint_first)
+    start(now[0] + thin_deep)
     half = mixing_halves.shape[2]
     for core in range(2):
         mixing_halves[core] = mixing_weight[:, core * half : (core + 1) * half].astype(low)
@@ -471,21 +461,26 @@
                 lane < HD, pltpu.roll(one, HD, 1), two
             ).astype(low)
     start(later_first)
-    wait(joint_first)
-    start(now)
+    wait(now[0] + thin_deep)
+    start(now[1])
+    start(thin.near + jobs[0].near + jobs[0].core[0])
+    wait(now[1])
+    start(jobs[1].near + jobs[1].core[0])
     wait(later_first)
-    wait(now)
-    start(thin.near + job.near + job.core[0])
     for copies in later:
         start(copies)
-    wait(thin.near + job.near)
-    start(thin.far + job.far + job.core[1])
+    wait(thin.near + jobs[0].near)
+    start(thin.far + jobs[0].far + jobs[0].core[1])
+    wait(jobs[1].near)
+    start(jobs[1].far + jobs[1].core[1])
     start(rows_copies[1:])
     wait(thin.far)
-    job.close()
+    for job in jobs:
+        job.close()
     for copies in later:
         wait(copies)
-    job.close_core()
+    for job in jobs:
+        job.close_core()
     wait(rows_copies)
 
 
@@ -513,7 +508,7 @@
         scratch_shapes=[
             pltpu.VMEM((depth, rows, width), low),
             pltpu.VMEM((depth, rows, table.shape[1]), low),
-            pltpu.SemaphoreType.DMA((2, 48)),
+            pltpu.SemaphoreType.DMA((2, 64)),
             pltpu.VMEM((2, own, width), low),
             pltpu.VMEM((2, own, half), low),
             pltpu.VMEM((2, own, grown), low),
@@ -603,9 +598,9 @@
         [
             (0, 0, open_all),
             (2, 0, next_deep),
-            (4, 2, lambda: far(jobs[0])),
-            (6, 2, lambda: far(jobs[1])),
-            (9, 2, lambda: far(jobs[2])),
+            (9, 0, lambda: far(jobs[0])),
+            (10, 2, lambda: far(jobs[1])),
+            (10, 3, lambda: far(jobs[2])),
         ],
     )
     between(0)
@@ -715,7 +710,7 @@
 
 
 def mlp_parts(tokens, width, hidden, tile):
-    whole = pl.BlockSpec((tokens, width), lambda t: (0, 0))
+    whole = pl.BlockSpec((tokens, width), lambda t: (0, 0), pipeline_mode=pl.Buffered(1))
     down = pl.BlockSpec((width, tile), lambda t: (0, t))
     across = pl.BlockSpec((tile, width), lambda t: (t, 0))
     thin = pl.BlockSpec((1, tile), lambda t: (0, t))
@@ -755,7 +750,7 @@
     mlp_tile(rows_step, c_ref, dy_ref, we_ref, ws_ref, be_ref, outs, scratch, lambda part: None)
 
 
-def mlp(c, dy, we, ws, be, before, tile=256, rows_step=256):
+def mlp(c, dy, we, ws, be, before, tile=512, rows_step=512):
     in_specs, out_specs, out_shape, scratch = mlp_parts(*c.shape, we.shape[1], tile)
     return pl.pallas_call(
         functools.partial(mlp_plain_kernel, rows_step),
@@ -812,8 +807,8 @@
         [
             (0, 0, open_all),
             (6, 0, lambda: far(jobs[0])),
-            (8, 2, lambda: far(jobs[1])),
-            (10, 0, jobs[0].close),
+            (6, 1, lambda: far(jobs[1])),
+            (7, 1, jobs[0].close),
         ],
     )
     between(0)
@@ -848,14 +843,14 @@
     pl.when(step == pl.num_programs(0) - 1)(close_all)
 
 
-def mlp_gather(sizes, place, mixed, rows_in, mixing, vectors, we, ws, be, upstream, far_a, far_b, quads, tile=256, rows_step=256):
+def mlp_gather(sizes, place, mixed, rows_in, mixing, vectors, we, ws, be, upstream, far_a, far_b, quads, tile=512, rows_step=512):
     tokens, model = mixed.shape
     blocks = place.shape[0]
     hidden = we.shape[1]
     lead = (sizes["c"], sizes["z"], sizes["y"])
     rows, grown, full = quads[0].shape[1], quads[0].shape[2], quads[1].shape[2]
     by_rows = pl.BlockSpec((BLK, model), lambda g: (jnp.minimum(g, blocks - 1), 0))
-    whole = pl.BlockSpec((tokens, model), lambda g: (0, 0))
+    whole = pl.BlockSpec((tokens, model), lambda g: (0, 0), pipeline_mode=pl.Buffered(1))
 
     def at(g):
         return jnp.maximum(g - blocks, 0)
@@ -912,25 +907,28 @@
     def open_all():
         start(loads)
         spot.meet(all_axes)
-        for job in jobs:
-            start(job.first)
+        start(jobs[0].first)
         scratch[0][...] = jnp.transpose(c_ref[...])
         wait(loads)
+
+    def shrink_near():
+        start(jobs[1].first)
+        jobs[0].go_near()
 
     def close_all():
         for place in range(2):
             kept[block_rows(place), :] = chosen_block(back_ref[place], y_all).astype(low)
             sent[block_rows(place), :] = chosen_block(back_ref[2 + place], y_all).astype(low)
-        jobs[1].close()
+        for job in jobs:
+            job.close()
 
     step = pl.program_id(0)
     schedule = [
         (0, 0, open_all),
-        (1, 1, jobs[0].go_near),
-        (2, 1, jobs[1].go_near),
-        (4, 0, jobs[0].go_far),
-        (6, 1, jobs[1].go_far),
-        (7, 1, jobs[0].close),
+        (0, 1, shrink_near),
+        (1, 0, jobs[1].go_near),
+        (3, 0, jobs[0].go_far),
+        (3, 1, jobs[1].go_far),
     ]
     mlp_tile(
         rows_step, c_ref, dy_ref, we_ref, ws_ref, be_ref, outs, scratch, hooks(step, schedule)
@@ -938,7 +936,7 @@
     pl.when(step == pl.num_programs(0) - 1)(close_all)
 
 
-def mlp_reduce(sizes, back, c, dy, we, ws, be, before, grads, tile=256, rows_step=256):
+def mlp_reduce(sizes, back, c, dy, we, ws, be, before, grads, tile=512, rows_step=512):
     tokens, model = c.shape
     in_specs, out_specs, out_shape, scratch = mlp_parts(tokens, model, we.shape[1], tile)
     expand, shrink = grads
@@ -1015,11 +1013,11 @@
             (3, 0, jobs[0].go_near),
             (4, 0, jobs[1].go_near),
             (4, 2, jobs[2].go_near),
-            (6, 2, jobs[0].go_far),
-            (7, 2, finish),
-            (9, 0, jobs[1].go_far),
-            (10, 0, jobs[2].go_far),
-            (11, 1, jobs[0].close),
+            (7, 0, finish),
+            (10, 0, jobs[0].go_far),
+            (10, 2, jobs[1].go_far),
+            (11, 0, jobs[2].go_far),
+            (11, 3, jobs[0].close),
         ],
     )
     between(0)
@@ -1045,8 +1043,9 @@
 
     @pl.when(step == blocks - 1)
     def _():
+        across = jnp.transpose(mixed[...])
         for core, target in ((1 - k, theirs), (k, jobs[2].total)):
-            piece = outer_sum(mixed[...], branch_all[:, span(core * half, half)]).astype(low)
+            piece = nn(across, branch_all[:, span(core * half, half)]).astype(low)
             target[...] = piece.reshape(target.shape)
         start(jobs[2].first)
 
@@ -1076,9 +1075,9 @@
 
     triple = pl.BlockSpec((tokens, 3 * PAIR), lambda g: (0, pair(g)))
     scratch = [
-        pltpu.VMEM((blocks, PAIR, BLK), low),
-        pltpu.VMEM((blocks, BLK, PAIR), jnp.float32),
-        pltpu.VMEM((blocks, BLK, PAIR), jnp.float32),
+        pltpu.VMEM((PAIR, tokens), low),
+        pltpu.VMEM((tokens, PAIR), jnp.float32),
+        pltpu.VMEM((tokens, PAIR), jnp.float32),
         pltpu.SemaphoreType.DMA((2, 32)),
         pltpu.VMEM((tokens, model), low),
         pltpu.VMEM((tokens, model), low),
@@ -1193,6 +1192,8 @@
     start(loads[:2])
     spot.meet(all_axes)
     start([out_copy])
+    for job in others:
+        start(job.copies)
     wait(loads[:2])
     start(loads[2:])
     turned[...] = jnp.transpose(low_rows[...])
@@ -1201,8 +1202,6 @@
         start(job.first)
         gradient(spot.k, number, job.total)
         job.go_near()
-    for job in others:
-        start(job.copies)
     wait(loads[2:])
     pull_block(0)
     pull_block(1)
@@ -1210,11 +1209,6 @@
     pull_block(2)
     jobs[1].go_far()
     pull_block(3)
-    for place in range(2):
-        sent[block_rows(place), :] = chosen_block(back_ref[2 + place], middle).astype(low)
-    start([rows_copy])
-    for place in range(2):
-        kept[block_rows(place), :] = chosen_block(back_ref[place], middle)
     steps[0] = vector[...]
     steps[0, 0:1, :] = sums["gain"]
     steps[0, 1:2, :] = sums["shift"]
@@ -1224,9 +1218,14 @@
                 :, (3 * pair + third) * PAIR : (3 * pair + third + 1) * PAIR
             ]
     start(hops[:1])
+    for place in range(2):
+        sent[block_rows(place), :] = chosen_block(back_ref[2 + place], middle).astype(low)
+    hop(0)
+    start([rows_copy])
     jobs[0].close()
     start(deeps[0].copies)
-    hop(0)
+    for place in range(2):
+        kept[block_rows(place), :] = chosen_block(back_ref[place], middle)
     for job, ending in zip(others, other_ends):
         wait(job.copies)
         ending.summed[...] = job.result()

time: 409 us -> 393 us (0.961)
  Pallas kernels: 389 us -> 372 us
    pallas_call x1, Pallas kernels: 57.8 us -> 51.4 us  [mlp_gather(): pl.pallas_call(functools.partial(mlp_gather_kernel, sizes, blocks, rows_s...]
    pallas_call x1, Pallas kernels: 74.6 us -> 68.4 us  [end(): pl.pallas_call(functools.partial(end_kernel, sizes), in_specs=[pl.BlockSp...]
    pallas_call x1, Pallas kernels: 70.1 us -> 64.6 us  [begin(): pl.pallas_call(functools.partial(begin_kernel, sizes), in_specs=[whole_vm...]
where the time goes in v5:
time: 393 us; the launch traced here: 387 us
  Pallas kernels  372 us (95%)
  local copies, waits for them, and re-layouts  8 us (2%)
  other arithmetic  5.58 us (1%)
    pallas_call x1, Pallas kernels, end(): pl.pallas_call(functools.partial(end_kernel, sizes), in_specs=[pl.BlockSp...  68.4 us
    pallas_call x1, Pallas kernels, attend_back(): pl.pallas_call(functools.partial(attend_back_kernel, sizes, blocks), grid...  66.2 us
    pallas_call x1, Pallas kernels, begin(): pl.pallas_call(functools.partial(begin_kernel, sizes), in_specs=[whole_vm...  64.6 us
    pallas_call x1, Pallas kernels, attend(): pl.pallas_call(functools.partial(attend_kernel, sizes, blocks), grid=(blo...  61.1 us
    pallas_call x1, Pallas kernels, mlp_gather(): pl.pallas_call(functools.partial(mlp_gather_kernel, sizes, blocks, rows_s...  51.4 us
    pallas_call x1, Pallas kernels, mlp_reduce(): pl.pallas_call(functools.partial(mlp_reduce_kernel, sizes, rows_step), gr...  50.9 us
    pallas_call x1, Pallas kernels, last(): pl.pallas_call(last_kernel, in_specs=[pl.BlockSpec(memory_space=pltpu.SME...  9.33 us

profile of v5, /device:TPU:0, one launch (start us, length us, event | category | flops | bytes accessed | tf_op | source)
XLA Modules:
  0.0 386.6 jit_solution(5235777293738886297)
XLA Ops:
  0.7 0.0 copy-start
  0.8 0.6 copy-done
  1.4 0.7 select_reduce_fusion
  2.0 0.7 convert_element_type.17
  2.7 0.1 copy.63
  2.8 0.6 pad.4.refs_1_
  3.4 64.6 %begin.1 = (bf16[2,4,2,64,3072]{4,3,2,1,0:T(8,128)(2,1)}, bf16[2,4,2,64,128]{4,3,2,1,0:T(8,128)(2,1)}, bf16[4,64,512]{2,1,0:T(8,128)(2,1)}, bf16[4,64,1024]{2,1,...) custom-call(f32[32,3072]{1,0:T(8,128)} %refs_11_.1, ...), custom_call_target="tpu_custom_call" | custom-call | flops 1024 | bytes 1024 | tf_op jit(solution)/shard_map/begin/pallas_call | solution.py:493
  68.0 1.1 copy.71
  69.1 0.6 fusion.4
  69.7 0.1 pad.12.clone
  69.8 0.1 pad_maximum_fusion.2
  69.9 0.6 reshape.126.refs_5_
  70.5 0.6 slice.47.refs_4_
  71.1 61.1 %attend.1 = (bf16[1024,1024]{1,0:T(8,128)(2,1)}, f32[8,8,1024]{2,1,0:T(8,128)}, bf16[1024,1024]{1,0:T(8,128)(2,1)}, bf16[1024,1024]{1,0:T(8,128)(2,1)}, bf16[102...) custom-call(s32[4]{0:T(128)} %get-tuple-element.168.refs_0_, ...), custom_call_target="tpu_custom_call" | custom-call | flops 1024 | bytes 1024 | tf_op jit(solution)/shard_map/attend/pallas_call | solution.py:642
  132.2 0.1 reshape.130
  132.3 0.7 squeeze.6.refs_7_
  133.0 0.6 slice.50.refs_4_
  133.6 51.4 %mlp_gather.1 = (f32[1024,1024]{1,0:T(8,128)}, f32[1024,1024]{1,0:T(8,128)}, bf16[1024,2048]{1,0:T(8,128)(2,1)}, bf16[2048,1024]{1,0:T(8,128)(2,1)}, f32[1,2048]...) custom-call(s32[4]{0:T(128)} %get-tuple-element.168.refs_0_, ...), custom_call_target="tpu_custom_call" | custom-call | flops 1024 | bytes 1024 | tf_op jit(solution)/shard_map/mlp_gather/pallas_call | solution.py:862
  185.0 0.7 squeeze.7.refs_5_
  185.7 50.9 %mlp_reduce.1 = (f32[1024,1024]{1,0:T(8,128)}, bf16[1024,2048]{1,0:T(8,128)(2,1)}, bf16[2048,1024]{1,0:T(8,128)(2,1)}, f32[1,2048]{1,0:T(1,128)}, bf16[4,64,1024...) custom-call(s32[4]{0:T(128)} %get-tuple-element.169.refs_0_, ...), custom_call_target="tpu_custom_call" | custom-call | flops 1024 | bytes 1024 | tf_op jit(solution)/shard_map/mlp_reduce/pallas_call | solution.py:948
  236.7 0.5 broadcast.98
  237.2 1.4 reduce.6
  238.5 0.1 reshape.138
  238.6 0.7 reduce.7
  239.3 0.1 reshape.137
  239.4 0.1 reshape.139
  239.5 66.2 %attend_back.1 = (bf16[1024,3072]{1,0:T(8,128)(2,1)}, f32[1024,1024]{1,0:T(8,128)}, f32[8,1024]{1,0:T(8,128)}, bf16[4,64,512]{2,1,0:T(8,128)(2,1)}, bf16[4,64,10...) custom-call(f32[1024,1024]{1,0:T(8,128)} %get-tuple-element.120.refs, ...), custom_call_target="tpu_custom_call" | custom-call | flops 1024 | bytes 1024 | tf_op jit(solution)/shard_map/attend_back/pallas_call | solution.py:1091
  305.7 0.8 slice.45
  306.5 0.7 pad_maximum_fusion.refs_7_
  307.2 68.4 %end.1 = (f32[2,32,1536]{2,1,0:T(8,128)}, f32[16,1024]{1,0:T(8,128)}, f32[2,32,512]{2,1,0:T(8,128)}, f32[2,32,1024]{2,1,0:T(8,128)}, f32[64,1024]{1,0:T(8,128)},...) custom-call(s32[4]{0:T(128)} %get-tuple-element.169.refs_0_, ...), custom_call_target="tpu_custom_call" | custom-call | flops 1024 | bytes 1024 | tf_op jit(solution)/shard_map/end/pallas_call | solution.py:1288
  375.6 9.3 %last.1 = (f32[2,512,1024]{2,1,0:T(8,128)}, bf16[2,512,1024]{2,1,0:T(8,128)(2,1)}, f32[32,3072]{1,0:T(8,128)}, f32[32,3072]{1,0:T(8,128)}, f32[32,3072]{1,0:T(8,...) custom-call(s32[1]{0:T(128)} %bitcast.ctx_ref, ...), custom_call_target="tpu_custom_call" | custom-call | flops 1024 | bytes 1024 | tf_op jit(solution)/shard_map/last/pallas_call | solution.py:1357
  385.0 1.4 fusion.2
  (20 shorter events, 0.2 us)
Async XLA Ops:
  0.7 0.7 copy-start
  185.7 52.9 %copy-start.5 = (f32[1,2048]{1,0:T(1,128)S(1)}, f32[1,2048]{1,0:T(1,128)}, u32[]{:S(2)}) copy-start(f32[1,2048]{1,0:T(1,128)} %get-tuple-element.133) | copy-start | bytes 24580
  375.5 10.8 %copy-start.1 = (s32[2,4]{1,0:T(2,128)S(1)}, s32[2,4]{1,0:T(2,128)}, u32[]{:S(2)}) copy-start(s32[2,4]{1,0:T(2,128)} %param.19) | copy-start | bytes 100
  375.6 9.4 %copy-start.2 = (f32[12,32]{1,0:T(8,128)S(1)}, f32[12,32]{1,0:T(8,128)}, u32[]{:S(2)}) copy-start(f32[12,32]{1,0:T(8,128)} %param.25) | copy-start | bytes 4612
  375.6 9.4 %copy-start.3 = (f32[12,32]{1,0:T(8,128)S(1)}, f32[12,32]{1,0:T(8,128)}, u32[]{:S(2)}) copy-start(f32[12,32]{1,0:T(8,128)} %param.30) | copy-start | bytes 4612
  375.6 9.4 %copy-start.4 = (f32[12,32]{1,0:T(8,128)S(1)}, f32[12,32]{1,0:T(8,128)}, u32[]{:S(2)}) copy-start(f32[12,32]{1,0:T(8,128)} %param.35) | copy-start | bytes 4612

commit v6 on v5

--- a/solution.py
+++ b/solution.py
@@ -423,7 +423,8 @@
     ]
     thin = Near(mover, table_quad, tables, 0, table.shape[1], core=False)
     rows_copies = [
-        mover.copy(rows_in.at[1 - spot.c], far_rows, "c"),
+        mover.copy(rows_in.at[1 - spot.c, block_rows(0)], far_rows.at[block_rows(0)], "c"),
+        mover.copy(rows_in.at[1 - spot.c, block_rows(1)], far_rows.at[block_rows(1)], "c"),
         mover.copy(upstream.at[1 - spot.c, block_rows(0)], far_upstream, "c"),
     ]
     pairs = width // (3 * PAIR)
@@ -471,9 +472,10 @@
         start(copies)
     wait(thin.near + jobs[0].near)
     start(thin.far + jobs[0].far + jobs[0].core[1])
+    start(rows_copies[1:2])
     wait(jobs[1].near)
     start(jobs[1].far + jobs[1].core[1])
-    start(rows_copies[1:])
+    start(rows_copies[2:])
     wait(thin.far)
     for job in jobs:
         job.close()
@@ -541,13 +543,25 @@
     return value
 
 
+def hidden_pairs(width, columns):
+    chips = columns // 2 // HD
+    for core in range(2):
+        for chip in range(0, chips, 2):
+            places = []
+            for number in (chip, chip + 1):
+                row, first = divmod((number * 2 + core) * PAIR, width)
+                places.append((slice(8 + row, 9 + row), slice(first, first + PAIR)))
+            first = core * (columns // 2) + chip * HD
+            yield places, slice(first, first + PAIR)
+
+
 def attend_kernel(sizes, blocks, *refs):
     refs = Refs(refs)
-    place_ref, rows_in, far_rows, joint, norm_ref, shift_ref, upstream = refs.take(7)
+    place_ref, rows_in, far_rows, joint, table, upstream = refs.take(6)
     mixing_quad, expand_quad, shrink_quad, expand_halves, shrink = refs.take(5)
-    o_ref, lse_ref, rows_ref, low_ref, projected_ref = refs.take(5)
+    o_ref, lse_ref, rows_ref, low_ref, projected_ref, vectors, bias_a, bias_b = refs.take(8)
     mixing, expand, shrunk, next_expand, next_shrink, far_upstream = refs.take(6)
-    sems, rows_all, joint_all, projected = refs.take(4)
+    sems, rows_all, joint_all, projected, shift_ref = refs.take(5)
     spot = Spot(sizes)
     mover = Mover(spot, sems)
     k = spot.k
@@ -573,12 +587,26 @@
         start(next_first)
         for job in jobs:
             start(job.near + job.core[0])
+        vector_rows()
         wait(loads)
 
     def next_deep():
         wait(next_first)
         start(deep)
         start(upstream_copy)
+
+    def vector_rows():
+        vectors[...] = jnp.transpose(table[...].astype(jnp.float32))[: vectors.shape[0]]
+        shift_ref[...] = jnp.zeros_like(shift_ref)
+        for pair in range(H // 2):
+            for row, third in ((2, 0), (3, 2)):
+                columns = pl.ds((3 * pair + third) * PAIR, PAIR)
+                shift_ref[:, columns] = vectors[row : row + 1, pair * PAIR : (pair + 1) * PAIR]
+        lane = lax.broadcasted_iota(jnp.int32, (1, PAIR), 1)
+        for (one, two), target in hidden_pairs(vectors.shape[1], bias_a.shape[1]):
+            one, two = vectors[one], vectors[two]
+            bias_a[:, target] = jnp.where(lane < HD, one, pltpu.roll(two, HD, 1))
+            bias_b[:, target] = jnp.where(lane < HD, pltpu.roll(one, HD, 1), two)
 
     def far(job):
         wait(job.near)
@@ -610,7 +638,7 @@
         value = chosen_block(place_ref[step], rows_all)
         rows_ref[...] = value.astype(low)
         normal, _ = normal_rows(value)
-        normed = (normal * norm_ref[0:1, :] + norm_ref[1:2, :]).astype(low)
+        normed = (normal * vectors[0:1, :] + vectors[1:2, :]).astype(low)
         low_ref[...] = normed
         rows = pl.ds(pl.multiple_of(step * BLK, BLK), BLK)
         for first in range(0, joint_all.shape[1], 512):
@@ -626,7 +654,7 @@
     pl.when(step == pl.num_programs(0) - 1)(close_all)
 
 
-def attend(sizes, place, rows_in, far_rows, joint, norm, shift, upstream, quads, halves, shrink):
+def attend(sizes, place, rows_in, far_rows, joint, table, upstream, quads, halves, shrink):
     model = rows_in.shape[2]
     blocks = place.shape[0]
     tokens = blocks * BLK
@@ -644,8 +672,7 @@
         grid=(blocks + pairs,),
         in_specs=[pl.BlockSpec(memory_space=pltpu.SMEM)]
         + [any_place] * 3
-        + [whole_vmem] * 2
-        + [any_place]
+        + [whole_vmem, any_place]
         + [whole_vmem] * 5,
         out_specs=[
             pl.BlockSpec((tokens, PAIR), lambda g: (0, pair(g))),
@@ -654,6 +681,7 @@
             by_rows,
             pl.BlockSpec((tokens, 3 * PAIR), lambda g: (0, pair(g))),
         ]
+        + [whole_vmem] * 3
         + [any_place] * 6,
         out_shape=[
             low_shape(tokens, model),
@@ -661,6 +689,9 @@
             low_shape(tokens, model),
             low_shape(tokens, model),
             low_shape(tokens, 3 * model),
+            jax.ShapeDtypeStruct((16, model), jnp.float32),
+            jax.ShapeDtypeStruct((1, 2 * grown), jnp.float32),
+            jax.ShapeDtypeStruct((1, 2 * grown), jnp.float32),
             low_shape(*lead, rows, 2 * half),
             low_shape(*lead, rows, 2 * grown),
             low_shape(2, *lead, rows, full),
@@ -673,11 +704,12 @@
             pltpu.VMEM((tokens, model), low),
             pltpu.VMEM((model, 3 * model), low),
             pltpu.VMEM((tokens, 3 * model), low),
+            pltpu.VMEM((1, 3 * model), jnp.float32),
         ],
-        compiler_params=params(2, 56),
+        compiler_params=params(2, 60),
         cost_estimate=small_cost,
         name="attend",
-    )(place, rows_in, far_rows, joint, norm, shift, upstream, *quads, halves, shrink)
+    )(place, rows_in, far_rows, joint, table, upstream, *quads, halves, shrink)
 
 
 def mlp_tile(rows_step, c_ref, dy_ref, we_ref, ws_ref, be_ref, outs, scratch, between):
@@ -985,8 +1017,7 @@
 
     def open_all():
         spot.meet(all_axes)
-        for job in jobs[:2]:
-            start(job.first)
+        start(jobs[0].first)
         start(rows_copy)
         for job in deep:
             start(job.copies)
@@ -1010,7 +1041,8 @@
         step,
         [
             (0, 0, open_all),
-            (3, 0, jobs[0].go_near),
+            (1, 0, lambda: start(jobs[1].first)),
+            (2, 0, jobs[0].go_near),
             (4, 0, jobs[1].go_near),
             (4, 2, jobs[2].go_near),
             (7, 0, finish),
@@ -1028,7 +1060,7 @@
         pulled = pulled_ref[...]
         upstream = upstream_ref[...].astype(jnp.float32)
         normal, inverse = normal_rows(middle_ref[...])
-        total = upstream + norm_pull(pulled, normal, inverse, gain_ref[...])
+        total = upstream + norm_pull(pulled, normal, inverse, gain_ref[5:6, :])
         grad_ref[...] = total
         branch = total.astype(low)
         branch_all[rows, :] = branch
@@ -1116,19 +1148,22 @@
     )(pulled, middle, upstream, mixed, mixing, gain, projected, lse, *grads, *quads, sent)
 
 
+end_chunks = 4
+
+
 def end_kernel(sizes, *refs):
     refs = Refs(refs)
     back_ref, back_far, low_far, joint_far, rows_far, middle_far = refs.take(6)
-    gain_ref, vector, mixing_quad, expand_quad, shrink_quad, sent_out = refs.take(6)
+    gain_ref, row_sums, bias_a, bias_b, mixing_quad, expand_quad, shrink_quad, sent_out = refs.take(8)
     out, vector_out, mixing_out, expand_out, shrink_out, kept = refs.take(6)
     arrived_rows, far_out = refs.take(2)
     sems, steps, arrived = refs.take(3)
     grads, low_rows, turned, joint, rows_in, middle, sent = refs.take(7)
     spot = Spot(sizes)
     mover = Mover(spot, sems)
-    width = joint.shape[-1] // 2
-    part = width // 2
-    tile = 256
+    width, tokens = joint.shape[-1] // 2, rows_in.shape[0]
+    part = width // end_chunks
+    tile = 384
     loads = [
         mover.local(far, near)
         for far, near in (
@@ -1140,10 +1175,10 @@
         )
     ]
     jobs, deeps, ends, others_half = [], [], [], []
-    for number in range(2):
+    for number in range(end_chunks):
         theirs, quad = refs.take(2)
         others_half.append(theirs)
-        jobs.append(ReduceNear(mover, None, theirs, part // 2, quad, refs.take(6)))
+        jobs.append(ReduceNear(mover, None, theirs, 2 * part // 3, quad, refs.take(6)))
         deeps.append(ReduceDeep(mover, quad, *refs.take(1)))
         ends.append(Finish(mover, *refs.take(2)))
     others = [
@@ -1175,7 +1210,7 @@
         pulled = grads[rows, :]
         upstream = nt(pulled, joint[...])
         normal, inverse = normal_rows(rows_in[rows, :].astype(jnp.float32))
-        middle[rows, :] += norm_pull(upstream, normal, inverse, gain_ref[...])
+        middle[rows, :] += norm_pull(upstream, normal, inverse, gain_ref[0:1, :])
         for name, value in (
             ("gain", upstream * normal),
             ("shift", upstream),
@@ -1203,13 +1238,16 @@
         gradient(spot.k, number, job.total)
         job.go_near()
     wait(loads[2:])
-    pull_block(0)
-    pull_block(1)
-    jobs[0].go_far()
-    pull_block(2)
-    jobs[1].go_far()
-    pull_block(3)
-    steps[0] = vector[...]
+    for number in range(tokens // BLK):
+        pull_block(number)
+        jobs[number].go_far()
+    steps[0] = jnp.zeros(steps.shape[1:], jnp.float32)
+    steps[0, 4:8, :] = row_sums[:4, :]
+    lane = lax.broadcasted_iota(jnp.int32, (1, PAIR), 1)
+    for (one, two), source in hidden_pairs(steps.shape[2], bias_a.shape[1]):
+        a, b = bias_a[:, source], bias_b[:, source]
+        steps[(0, *one)] = jnp.where(lane < HD, a, pltpu.roll(b, HD, 1))
+        steps[(0, *two)] = jnp.where(lane < HD, pltpu.roll(a, HD, 1), b)
     steps[0, 0:1, :] = sums["gain"]
     steps[0, 1:2, :] = sums["shift"]
     for pair in range(H // 2):
@@ -1222,8 +1260,9 @@
         sent[block_rows(place), :] = chosen_block(back_ref[2 + place], middle).astype(low)
     hop(0)
     start([rows_copy])
-    jobs[0].close()
-    start(deeps[0].copies)
+    for job, deep in zip(jobs[:2], deeps[:2]):
+        job.close()
+        start(deep.copies)
     for place in range(2):
         kept[block_rows(place), :] = chosen_block(back_ref[place], middle)
     for job, ending in zip(others, other_ends):
@@ -1232,8 +1271,9 @@
         start(ending.copies)
     wait(others[2].copies)
     shrink_out[...] = others[2].result()
-    jobs[1].close()
-    start(deeps[1].copies)
+    for job, deep in zip(jobs[2:], deeps[2:]):
+        job.close()
+        start(deep.copies)
     hop(1)
     hop(2)
     for ending, target in zip(other_ends, (mixing_out, expand_out)):
@@ -1254,18 +1294,18 @@
     wait([rows_copy, out_copy])
 
 
-def end(sizes, back, joint_back, first_low, joint, rows_in, middle_grad, gain, vector, quads, sent):
+def end(sizes, back, joint_back, first_low, joint, rows_in, middle_grad, gain, row_sums, bias_a, bias_b, quads, sent):
     tokens, model = rows_in.shape
     width = joint.shape[1] // 2
     lead = (sizes["c"], sizes["z"], sizes["y"])
     depth = sizes["z"]
     rows = model // (lead[0] * lead[1] * lead[2])
-    part = width // 2
+    part = width // end_chunks
     half, grown, full = [quad.shape[-1] for quad in quads]
     scratch = [
-        pltpu.SemaphoreType.DMA((2, 48)),
-        pltpu.VMEM((4, *vector.shape), jnp.float32),
-        pltpu.VMEM((2 + depth, *vector.shape), jnp.float32),
+        pltpu.SemaphoreType.DMA((2, 80)),
+        pltpu.VMEM((4, *gain.shape), jnp.float32),
+        pltpu.VMEM((2 + depth, *gain.shape), jnp.float32),
         pltpu.VMEM(joint_back.shape, low),
         pltpu.VMEM(first_low.shape, low),
         pltpu.VMEM(first_low.shape[::-1], low),
@@ -1274,22 +1314,22 @@
         pltpu.VMEM(middle_grad.shape, jnp.float32),
         pltpu.VMEM((tokens // 2, model), low),
     ]
-    for number in range(2):
+    for number in range(end_chunks):
         scratch += [pltpu.VMEM((*lead, rows, part), low), pltpu.VMEM((depth, rows, part), low)]
-        scratch += ReduceNear.scratch(sizes, rows, part, part // 2)
+        scratch += ReduceNear.scratch(sizes, rows, part, 2 * part // 3)
         scratch += [pltpu.VMEM((depth - 1, rows, part), low)]
         scratch += Finish.scratch(rows, part)
     scratch += [pltpu.VMEM((depth - 1, rows, columns), low) for columns in (half, grown, full)]
     for columns in (half, grown):
         scratch += Finish.scratch(rows, columns)
     own = rows // 2
-    shapes = [(2, own, width), vector.shape, (2, own, half), (2, own, grown), (rows, full)]
+    shapes = [(2, own, width), gain.shape, (2, own, half), (2, own, grown), (rows, full)]
     shapes.append((tokens // 2, model))
     return pl.pallas_call(
         functools.partial(end_kernel, sizes),
         in_specs=[pl.BlockSpec(memory_space=pltpu.SMEM)]
         + [any_place] * 5
-        + [whole_vmem] * 5
+        + [whole_vmem] * 7
         + [any_place],
         out_specs=[whole_vmem] * 6 + [any_place] * 2,
         out_shape=[jax.ShapeDtypeStruct(shape, jnp.float32) for shape in shapes]
@@ -1298,16 +1338,17 @@
         compiler_params=params(6, 60),
         cost_estimate=small_cost,
         name="end",
-    )(back, joint_back, first_low, joint, rows_in, middle_grad, gain, vector, *quads, sent)
+    )(back, joint_back, first_low, joint, rows_in, middle_grad, gain, row_sums, bias_a, bias_b, *quads, sent)
 
 
 def last_kernel(ctx_ref, *refs):
     refs = Refs(refs)
     joint_part, mixing_part, expand_a, expand_b, shrink_a, shrink_b = refs.take(6)
     kept_grad, far_grad, kept_out, far_one, far_two = refs.take(5)
-    states = [refs.take(3) for _ in range(4)]
+    (vector_sum,) = refs.take(1)
+    states = [refs.take(3) for _ in range(5)]
     grad_out, block_out = refs.take(2)
-    news = [refs.take(4) for _ in range(4)]
+    news = [refs.take(4) for _ in range(5)]
     here = ctx_ref[0]
     grad_out[here] = kept_grad[...]
     grad_out[1 - here] = far_grad[...].astype(jnp.float32)
@@ -1315,9 +1356,9 @@
     block_out[1 - here, :BLK, :] = far_one[...]
     block_out[1 - here, BLK:, :] = far_two[...]
 
-    def update(number, where, gradient):
+    def update(number, where, gradient, rate=0.05, decay=0.1):
         weight, first, second = [ref[where] for ref in states[number]]
-        results = adam_update(weight, first, second, gradient, 0.05, 0.1)
+        results = adam_update(weight, first, second, gradient, rate, decay)
         for ref, value in zip(news[number], (*results, results[0].astype(low))):
             ref[where] = value
 
@@ -1346,9 +1387,12 @@
     rows = shrink_a.shape[0]
     update(3, (pl.ds(0, rows), every), shrink_a[...])
     update(3, (pl.ds(rows, rows), every), shrink_b[...])
-
-
-def last(ctx, parts, kept_grad, far_grad, kept_out, far_outs, states):
+    table_rows, columns = states[4][0].shape
+    moved = pltpu.roll(vector_sum[...], vector_sum.shape[1] - ctx_ref[1] * columns, 1)
+    update(4, (every, every), moved[:table_rows, :columns], 0.5, 0.0)
+
+
+def last(ctx, parts, kept_grad, far_grad, kept_out, far_outs, vector_sum, states):
     shapes = [jax.ShapeDtypeStruct((2, *kept_grad.shape), jnp.float32), low_shape(2, *kept_out.shape)]
     for weight, _, _ in states:
         shapes += [jax.ShapeDtypeStruct(weight.shape, jnp.float32)] * 3
@@ -1356,13 +1400,13 @@
     flat = [array for state in states for array in state]
     return pl.pallas_call(
         last_kernel,
-        in_specs=[pl.BlockSpec(memory_space=pltpu.SMEM)] + [whole_vmem] * (11 + len(flat)),
+        in_specs=[pl.BlockSpec(memory_space=pltpu.SMEM)] + [whole_vmem] * (12 + len(flat)),
         out_specs=[whole_vmem] * len(shapes),
         out_shape=shapes,
         compiler_params=pltpu.CompilerParams(vmem_limit_bytes=56 << 20),
         cost_estimate=small_cost,
         name="last",
-    )(ctx, *parts, kept_grad, far_grad, kept_out, *far_outs, *flat)
+    )(ctx, *parts, kept_grad, far_grad, kept_out, *far_outs, vector_sum, *flat)
 
 
 def layer_norm(values, gain_row, shift_row):
@@ -1698,10 +1742,6 @@
             grid, here, pieces
         )
     joint = joint.reshape(width, 3 * width)
-    vector_values = (
-        tables.reshape(width, -1)[:, : vectors.shape[0]].T.astype(jnp.float32)
-    )
-
     if near:
         order = lax.dynamic_slice_in_dim(block_order, ctx, 1, 0)[0]
         blocks = order.shape[0]
@@ -1710,17 +1750,7 @@
         place = jnp.sum(jnp.where(order[None, :] == stored[:, None], moved[None, :], 0), axis=1)
         back = jnp.sum(jnp.where(moved[None, :] == stored[:, None], order[None, :], 0), axis=1)
         place, back = place.astype(jnp.int32), back.astype(jnp.int32)
-    joint_shift = jnp.stack(
-        [
-            vector_values[2].reshape(pairs, PAIR),
-            jnp.zeros((pairs, PAIR), jnp.float32),
-            vector_values[3].reshape(pairs, PAIR),
-        ],
-        axis=1,
-    ).reshape(1, -1)
     lead = (sizes["c"], sizes["z"], sizes["y"])
-    hidden_bias = vector_values[8:].reshape(chips, 2, 2, sub).transpose(2, 1, 0, 3).reshape(2, 1, -1)
-
     def by_device(expand_grad, shrink_grad):
         return (
             expand_grad.reshape(*lead, -1, expand_grad.shape[1]),
@@ -1728,14 +1758,13 @@
         )
 
     if near:
-        mixed_low, logsum, input_low, first_low, projected, *gathered = attend(
+        mixed_low, logsum, input_low, first_low, projected, vector_values, hidden_a, hidden_b, *gathered = attend(
             sizes,
             place,
             block_input,
             far_input,
             joint,
-            vector_values[:2],
-            joint_shift,
+            tables.reshape(width, -1),
             cotangent,
             quads,
             next_half,
@@ -1749,10 +1778,10 @@
             mixed_low,
             input_low,
             mixing,
-            vector_values[:8],
+            vector_values,
             expand_a.reshape(width, -1),
             shrink_a.reshape(-1, width),
-            hidden_bias[0],
+            hidden_a,
             cotangent,
             far_upstream,
             last_upstream,
@@ -1765,11 +1794,23 @@
             upstream,
             expand_b.reshape(width, -1),
             shrink_b.reshape(-1, width),
-            hidden_bias[1],
+            hidden_b,
             before,
             by_device(expand_grad_a, shrink_grad_a),
         )
     else:
+        vector_values = (
+            tables.reshape(width, -1)[:, : vectors.shape[0]].T.astype(jnp.float32)
+        )
+        joint_shift = jnp.stack(
+            [
+                vector_values[2].reshape(pairs, PAIR),
+                jnp.zeros((pairs, PAIR), jnp.float32),
+                vector_values[3].reshape(pairs, PAIR),
+            ],
+            axis=1,
+        ).reshape(1, -1)
+        hidden_bias = vector_values[8:].reshape(chips, 2, 2, sub).transpose(2, 1, 0, 3).reshape(2, 1, -1)
         input_low = block_input.reshape(tokens, width)
         upstream = cotangent.reshape(tokens, width)
         input_rows = input_low.astype(jnp.float32)
@@ -1815,10 +1856,6 @@
             before,
         )
         block_output = result.astype(low).reshape(block_input.shape)
-    hidden_bias_grads = [
-        bias.reshape(2, chips, 1, sub).transpose(1, 0, 2, 3) for bias in (bias_a, bias_b)
-    ]
-
     if near:
         joint_back, middle_grad, sums, *last_quads, expand_part_a, shrink_part_a, far_one = attend_back(
             sizes,
@@ -1827,7 +1864,7 @@
             upstream,
             mixed_low,
             mixing,
-            vector_values[5:6],
+            vector_values,
             projected,
             logsum,
             by_device(expand_grad_b, shrink_grad_b),
@@ -1863,16 +1900,10 @@
     def column_sum(rows):
         return jnp.sum(rows.astype(jnp.float32), axis=0)
 
-    hidden_bias_grad = jnp.concatenate(hidden_bias_grads, axis=2).reshape(-1, width)
     weights = (joint_weight, mixing_weight, expand_weight, shrink_weight)
     firsts = (joint_first, mixing_first, expand_first, shrink_first)
     seconds = (joint_second, mixing_second, expand_second, shrink_second)
     if near:
-        rows = vectors.shape[0]
-        vector_grad = jnp.concatenate(
-            [jnp.zeros((4, width)), sums[:4], hidden_bias_grad, jnp.zeros((-rows % 8, width))],
-            axis=0,
-        )
         joint_part, vector_sum, mixing_part, expand_part_b, shrink_part_b, kept_grad, far_grad, far_two = end(
             sizes,
             back,
@@ -1881,22 +1912,33 @@
             joint,
             input_low,
             middle_grad,
-            vector_values[0:1],
-            vector_grad,
+            vector_values,
+            sums,
+            bias_a,
+            bias_b,
             last_quads,
             sent_out,
         )
         input_gradient, block_output, *news = last(
-            ctx.astype(jnp.int32).reshape(1),
+            jnp.stack([ctx, lax.axis_index(axes)]).astype(jnp.int32),
             (joint_part, mixing_part, expand_part_a, expand_part_b, shrink_part_a, shrink_part_b),
             kept_grad,
             far_grad,
             kept_out,
             (far_one, far_two),
-            list(zip(weights, firsts, seconds)),
+            vector_sum,
+            list(
+                zip(
+                    (*weights, vectors), (*firsts, vectors_first), (*seconds, vectors_second)
+                )
+            ),
         )
         updated, moments, squares, copies = [news[number::4] for number in range(4)]
     else:
+        hidden_bias_grads = [
+            bias.reshape(2, chips, 1, sub).transpose(1, 0, 2, 3) for bias in (bias_a, bias_b)
+        ]
+        hidden_bias_grad = jnp.concatenate(hidden_bias_grads, axis=2).reshape(-1, width)
         joint_grad = outer_sum(first_low, joint_back).astype(low)
         first_grad = nt(joint_back, joint)
         input_part, gain_one, shift_one = norm_back(
@@ -1938,24 +1980,22 @@
             ]
         )
         copies = [array.astype(low) for array in updated]
-    vector_sum = lax.dynamic_slice(
-        vector_sum, (0, lax.axis_index(axes) * vectors.shape[1]), vectors.shape
-    )
-    vectors_new, vectors_moment, vectors_square = adam_update(
-        vectors, vectors_first, vectors_second, vector_sum, 0.5, 0.0
-    )
-    return (
-        block_output,
-        input_gradient,
-        *updated,
-        vectors_new,
-        *moments,
-        vectors_moment,
-        *squares,
-        vectors_square,
-        *copies,
-        vectors_new.astype(low),
-    )
+        vector_sum = lax.dynamic_slice(
+            vector_sum, (0, lax.axis_index(axes) * vectors.shape[1]), vectors.shape
+        )
+        vectors_new, vectors_moment, vectors_square = adam_update(
+            vectors, vectors_first, vectors_second, vector_sum, 0.5, 0.0
+        )
+        updated, moments, squares = [
+            (*arrays, array)
+            for arrays, array in (
+                (updated, vectors_new),
+                (moments, vectors_moment),
+                (squares, vectors_square),
+            )
+        ]
+        copies.append(vectors_new.astype(low))
+    return (block_output, input_gradient, *updated, *moments, *squares, *copies)
 
 
 def solution(mesh):

time: 393 us -> 379 us (0.964)
  local copies, waits for them, and re-layouts: 8 us -> 0.73 us
where the time goes in v6:
time: 379 us; the launch traced here: 373 us
  Pallas kernels  369 us (97%)
    pallas_call x1, Pallas kernels, attend_back(): pl.pallas_call(functools.partial(attend_back_kernel, sizes, blocks), grid...  67 us
    pallas_call x1, Pallas kernels, end(): pl.pallas_call(functools.partial(end_kernel, sizes), in_specs=[pl.BlockSp...  65.1 us
    pallas_call x1, Pallas kernels, begin(): pl.pallas_call(functools.partial(begin_kernel, sizes), in_specs=[whole_vm...  63.4 us
    pallas_call x1, Pallas kernels, attend(): pl.pallas_call(functools.partial(attend_kernel, sizes, blocks), grid=(blo...  62.3 us
    pallas_call x1, Pallas kernels, mlp_gather(): pl.pallas_call(functools.partial(mlp_gather_kernel, sizes, blocks, rows_s...  51.7 us
    pallas_call x1, Pallas kernels, mlp_reduce(): pl.pallas_call(functools.partial(mlp_reduce_kernel, sizes, rows_step), gr...  50.3 us
    pallas_call x1, Pallas kernels, last(): pl.pallas_call(last_kernel, in_specs=[pl.BlockSpec(memory_space=pltpu.SME...  9.49 us

profile of v6, /device:TPU:0, one launch (start us, length us, event | category | flops | bytes accessed | tf_op | source)
XLA Modules:
  0.0 373.2 jit_solution(12336993870216848001)
XLA Ops:
  0.7 0.0 copy-start
  0.8 0.6 pad_add_fusion.ctx_ref
  1.3 0.0 copy-done
  1.4 0.7 select_reduce_fusion
  2.0 0.7 convert_element_type.8
  2.7 0.1 copy.42
  2.8 0.6 pad.4.refs_1_
  3.4 63.4 %begin.1 = (bf16[2,4,2,64,3072]{4,3,2,1,0:T(8,128)(2,1)}, bf16[2,4,2,64,128]{4,3,2,1,0:T(8,128)(2,1)}, bf16[4,64,512]{2,1,0:T(8,128)(2,1)}, bf16[4,64,1024]{2,1,...) custom-call(f32[32,3072]{1,0:T(8,128)} %refs_12_.1, ...), custom_call_target="tpu_custom_call" | custom-call | flops 1024 | bytes 1024 | tf_op jit(solution)/shard_map/begin/pallas_call | solution.py:495
  66.8 62.3 %attend.1 = (bf16[1024,1024]{1,0:T(8,128)(2,1)}, f32[8,8,1024]{2,1,0:T(8,128)}, bf16[1024,1024]{1,0:T(8,128)(2,1)}, bf16[1024,1024]{1,0:T(8,128)(2,1)}, bf16[102...) custom-call(s32[4]{0:T(128)} %get-tuple-element.182.refs_0_, ...), custom_call_target="tpu_custom_call" | custom-call | flops 1024 | bytes 1024 | tf_op jit(solution)/shard_map/attend/pallas_call | solution.py:670
  129.1 51.7 %mlp_gather.1 = (f32[1024,1024]{1,0:T(8,128)}, f32[1024,1024]{1,0:T(8,128)}, bf16[1024,2048]{1,0:T(8,128)(2,1)}, bf16[2048,1024]{1,0:T(8,128)(2,1)}, f32[1,2048]...) custom-call(s32[4]{0:T(128)} %get-tuple-element.182.refs_0_, ...), custom_call_target="tpu_custom_call" | custom-call | flops 1024 | bytes 1024 | tf_op jit(solution)/shard_map/mlp_gather/pallas_call | solution.py:894
  180.8 50.3 %mlp_reduce.1 = (f32[1024,1024]{1,0:T(8,128)}, bf16[1024,2048]{1,0:T(8,128)(2,1)}, bf16[2048,1024]{1,0:T(8,128)(2,1)}, f32[1,2048]{1,0:T(1,128)}, bf16[4,64,1024...) custom-call(s32[4]{0:T(128)} %get-tuple-element.183.refs_0_, ...), custom_call_target="tpu_custom_call" | custom-call | flops 1024 | bytes 1024 | tf_op jit(solution)/shard_map/mlp_reduce/pallas_call | solution.py:980
  231.1 67.0 %attend_back.1 = (bf16[1024,3072]{1,0:T(8,128)(2,1)}, f32[1024,1024]{1,0:T(8,128)}, f32[8,1024]{1,0:T(8,128)}, bf16[4,64,512]{2,1,0:T(8,128)(2,1)}, bf16[4,64,10...) custom-call(f32[1024,1024]{1,0:T(8,128)} %get-tuple-element.130.refs, ...), custom_call_target="tpu_custom_call" | custom-call | flops 1024 | bytes 1024 | tf_op jit(solution)/shard_map/attend_back/pallas_call | solution.py:1123
  298.1 65.1 %end.1 = (f32[2,32,1536]{2,1,0:T(8,128)}, f32[16,1024]{1,0:T(8,128)}, f32[2,32,512]{2,1,0:T(8,128)}, f32[2,32,1024]{2,1,0:T(8,128)}, f32[64,1024]{1,0:T(8,128)},...) custom-call(s32[4]{0:T(128)} %get-tuple-element.183.refs_0_, ...), custom_call_target="tpu_custom_call" | custom-call | flops 1024 | bytes 1024 | tf_op jit(solution)/shard_map/end/pallas_call | solution.py:1328
  363.2 0.0 copy-start.1
  363.2 9.5 %last.1 = (f32[2,512,1024]{2,1,0:T(8,128)}, bf16[2,512,1024]{2,1,0:T(8,128)(2,1)}, f32[32,3072]{1,0:T(8,128)}, f32[32,3072]{1,0:T(8,128)}, f32[32,3072]{1,0:T(8,...) custom-call(s32[2]{0:T(128)} %pad_add_fusion.ctx_ref, ...), custom_call_target="tpu_custom_call" | custom-call | flops 1024 | bytes 1024 | tf_op jit(solution)/shard_map/last/pallas_call | solution.py:1401
  372.7 0.0 copy-done.1
  (2 shorter events, 0.0 us)
Async XLA Ops:
  0.7 0.7 copy-start
  363.2 9.5 %copy-start.1 = (s32[2,4]{1,0:T(2,128)S(1)}, s32[2,4]{1,0:T(2,128)}, u32[]{:S(2)}) copy-start(s32[2,4]{1,0:T(2,128)} %param.19) | copy-start | bytes 100

commit v7 on v6

--- a/solution.py
+++ b/solution.py
@@ -626,9 +626,9 @@
         [
             (0, 0, open_all),
             (2, 0, next_deep),
-            (9, 0, lambda: far(jobs[0])),
-            (10, 2, lambda: far(jobs[1])),
-            (10, 3, lambda: far(jobs[2])),
+            (7, 2, lambda: far(jobs[0])),
+            (8, 2, lambda: far(jobs[1])),
+            (9, 2, lambda: far(jobs[2])),
         ],
     )
     between(0)
@@ -1046,10 +1046,10 @@
             (4, 0, jobs[1].go_near),
             (4, 2, jobs[2].go_near),
             (7, 0, finish),
-            (10, 0, jobs[0].go_far),
-            (10, 2, jobs[1].go_far),
-            (11, 0, jobs[2].go_far),
-            (11, 3, jobs[0].close),
+            (8, 2, jobs[0].go_far),
+            (9, 1, jobs[1].go_far),
+            (9, 3, jobs[2].go_far),
+            (11, 0, jobs[0].close),
         ],
     )
     between(0)

time: 379 us -> 375 us (0.989)
  Pallas kernels: 369 us -> 365 us
where the time goes in v7:
time: 375 us; the launch traced here: 369 us
  Pallas kernels  365 us (97%)
    pallas_call x1, Pallas kernels, end(): pl.pallas_call(functools.partial(end_kernel, sizes), in_specs=[pl.BlockSp...  65.6 us
    pallas_call x1, Pallas kernels, attend_back(): pl.pallas_call(functools.partial(attend_back_kernel, sizes, blocks), grid...  63.9 us
    pallas_call x1, Pallas kernels, begin(): pl.pallas_call(functools.partial(begin_kernel, sizes), in_specs=[whole_vm...  63.4 us
    pallas_call x1, Pallas kernels, attend(): pl.pallas_call(functools.partial(attend_kernel, sizes, blocks), grid=(blo...  59.7 us
    pallas_call x1, Pallas kernels, mlp_gather(): pl.pallas_call(functools.partial(mlp_gather_kernel, sizes, blocks, rows_s...  51.9 us
    pallas_call x1, Pallas kernels, mlp_reduce(): pl.pallas_call(functools.partial(mlp_reduce_kernel, sizes, rows_step), gr...  51.3 us
    pallas_call x1, Pallas kernels, last(): pl.pallas_call(last_kernel, in_specs=[pl.BlockSpec(memory_space=pltpu.SME...  9.49 us

profile of v7, /device:TPU:0, one launch (start us, length us, event | category | flops | bytes accessed | tf_op | source)
XLA Modules:
  0.0 369.3 jit_solution(13945735471201624261)
XLA Ops:
  0.7 0.0 copy-start
  0.8 0.6 pad_add_fusion.ctx_ref
  1.3 0.0 copy-done
  1.4 0.7 select_reduce_fusion
  2.0 0.7 convert_element_type.8
  2.7 0.1 copy.42
  2.8 0.6 pad.4.refs_1_
  3.4 63.4 %begin.1 = (bf16[2,4,2,64,3072]{4,3,2,1,0:T(8,128)(2,1)}, bf16[2,4,2,64,128]{4,3,2,1,0:T(8,128)(2,1)}, bf16[4,64,512]{2,1,0:T(8,128)(2,1)}, bf16[4,64,1024]{2,1,...) custom-call(f32[32,3072]{1,0:T(8,128)} %refs_12_.1, ...), custom_call_target="tpu_custom_call" | custom-call | flops 1024 | bytes 1024 | tf_op jit(solution)/shard_map/begin/pallas_call | solution.py:495
  66.8 59.7 %attend.1 = (bf16[1024,1024]{1,0:T(8,128)(2,1)}, f32[8,8,1024]{2,1,0:T(8,128)}, bf16[1024,1024]{1,0:T(8,128)(2,1)}, bf16[1024,1024]{1,0:T(8,128)(2,1)}, bf16[102...) custom-call(s32[4]{0:T(128)} %get-tuple-element.182.refs_0_, ...), custom_call_target="tpu_custom_call" | custom-call | flops 1024 | bytes 1024 | tf_op jit(solution)/shard_map/attend/pallas_call | solution.py:670
  126.5 51.9 %mlp_gather.1 = (f32[1024,1024]{1,0:T(8,128)}, f32[1024,1024]{1,0:T(8,128)}, bf16[1024,2048]{1,0:T(8,128)(2,1)}, bf16[2048,1024]{1,0:T(8,128)(2,1)}, f32[1,2048]...) custom-call(s32[4]{0:T(128)} %get-tuple-element.182.refs_0_, ...), custom_call_target="tpu_custom_call" | custom-call | flops 1024 | bytes 1024 | tf_op jit(solution)/shard_map/mlp_gather/pallas_call | solution.py:894
  178.4 51.3 %mlp_reduce.1 = (f32[1024,1024]{1,0:T(8,128)}, bf16[1024,2048]{1,0:T(8,128)(2,1)}, bf16[2048,1024]{1,0:T(8,128)(2,1)}, f32[1,2048]{1,0:T(1,128)}, bf16[4,64,1024...) custom-call(s32[4]{0:T(128)} %get-tuple-element.183.refs_0_, ...), custom_call_target="tpu_custom_call" | custom-call | flops 1024 | bytes 1024 | tf_op jit(solution)/shard_map/mlp_reduce/pallas_call | solution.py:980
  229.7 63.9 %attend_back.1 = (bf16[1024,3072]{1,0:T(8,128)(2,1)}, f32[1024,1024]{1,0:T(8,128)}, f32[8,1024]{1,0:T(8,128)}, bf16[4,64,512]{2,1,0:T(8,128)(2,1)}, bf16[4,64,10...) custom-call(f32[1024,1024]{1,0:T(8,128)} %get-tuple-element.130.refs, ...), custom_call_target="tpu_custom_call" | custom-call | flops 1024 | bytes 1024 | tf_op jit(solution)/shard_map/attend_back/pallas_call | solution.py:1123
  293.6 65.6 %end.1 = (f32[2,32,1536]{2,1,0:T(8,128)}, f32[16,1024]{1,0:T(8,128)}, f32[2,32,512]{2,1,0:T(8,128)}, f32[2,32,1024]{2,1,0:T(8,128)}, f32[64,1024]{1,0:T(8,128)},...) custom-call(s32[4]{0:T(128)} %get-tuple-element.183.refs_0_, ...), custom_call_target="tpu_custom_call" | custom-call | flops 1024 | bytes 1024 | tf_op jit(solution)/shard_map/end/pallas_call | solution.py:1328
  359.3 0.0 copy-start.1
  359.3 9.5 %last.1 = (f32[2,512,1024]{2,1,0:T(8,128)}, bf16[2,512,1024]{2,1,0:T(8,128)(2,1)}, f32[32,3072]{1,0:T(8,128)}, f32[32,3072]{1,0:T(8,128)}, f32[32,3072]{1,0:T(8,...) custom-call(s32[2]{0:T(128)} %pad_add_fusion.ctx_ref, ...), custom_call_target="tpu_custom_call" | custom-call | flops 1024 | bytes 1024 | tf_op jit(solution)/shard_map/last/pallas_call | solution.py:1401
  368.8 0.0 copy-done.1
  (2 shorter events, 0.0 us)
Async XLA Ops:
  0.7 0.7 copy-start
  359.3 9.5 %copy-start.1 = (s32[2,4]{1,0:T(2,128)S(1)}, s32[2,4]{1,0:T(2,128)}, u32[]{:S(2)}) copy-start(s32[2,4]{1,0:T(2,128)} %param.19) | copy-start | bytes 100
